TPU v7x, 32 devices: a whole 2x2x4 slice. The times are simulated.
32 devices in a mesh: rows: 8 (over z, x), grp: 4 (over y, core).
Axes of the slice: x: 2, y: 2, z: 4, core: 2. Of those that a mesh axis runs over, the one named last changes fastest.
Arguments:
- observations: float32 [65536, 512], P(('rows', 'grp')), may hold values from -32 to 32, as said below
- sensor_ids: int32 [65536], P(('rows', 'grp')), may hold values from 0 to 127
- sensor_sigma: float32 [128], replicated, may hold values from 0.3 to 3
- buckets: int32 [65536], P(('rows', 'grp')), may hold values from 0 to 7, as said below
- prior_factor: float32 [512, 512], replicated, may hold values from -0.3 to 3, as said below
Outputs:
- whitened: float32 [65536, 512], P(('rows', 'grp'))
- info_factor: float32 [512, 512], replicated
Inputs may be any that keep to these rules, and one draw needn't show every extreme that they name: `buckets`: in each aligned block of 2048 rows every bucket index appears exactly 256 times. `observations`: rows are real-valued without further structure. `prior_factor`: upper triangular with a positive diagonal of at least 0.5.
All inputs are finite; a program needn't handle non-finite values.
Results may differ from a plain program's by a relative error of at most 0.00007.
Values sent between devices are 32-bit elements; how exact they have to be, the bound alone decides.
No kernel may reach another device: no remote copies, remote signals or barrier semaphores. Data moves between devices by JAX's collectives and lax.ppermute only.
A program may use at most 128 MiB of HBM per device.

v0:
```python
import jax
import jax.numpy as jnp
from jax import lax
from jax.sharding import PartitionSpec as P


def matmul(left, right):
    return jnp.dot(left, right, precision=lax.Precision.HIGHEST, preferred_element_type=jnp.float32)


def outer_sum(values):
    return lax.dot_general(
        values,
        values,
        (((0,), (0,)), ((), ())),
        precision=lax.Precision.HIGHEST,
        preferred_element_type=jnp.float32,
    )


def square_form(matrix):
    return matmul(matrix.T, matrix)


def lower_inverse(lower):
    width = lower.shape[0]
    identity = jnp.eye(width, dtype=jnp.float32)
    diag_values = jnp.diagonal(lower)
    scaled_lower = lower / diag_values[:, None]
    nilpotent = identity - scaled_lower
    product = identity + nilpotent
    power = nilpotent
    reach = 2
    while reach < width:
        power = matmul(power, power)
        product = product + matmul(product, power)
        reach = reach * 2
    return product / diag_values[None, :]


def upper_factor(matrix):
    return jnp.linalg.cholesky(matrix).T


def whiten_rows(values, factor):
    inverse = lower_inverse(factor.T)
    return matmul(values, inverse.T)


def regroup_rows(values, target):
    outgoing = jnp.zeros_like(values).at[target].set(values)
    return lax.all_to_all(outgoing, "rows", split_axis=0, concat_axis=0, tiled=True)


def reduce_gram(local_gram, prior_gram, total_rows):
    summed = lax.psum(local_gram, ("rows", "grp"))
    return upper_factor(prior_gram + summed / jnp.float32(total_rows))


def shards(observations, sensor_ids, sensor_sigma, buckets, prior_factor):
    rows_dev = observations.shape[0]
    row_groups = lax.axis_size("rows")
    devices = lax.axis_size(("rows", "grp"))
    per_bucket = rows_dev // row_groups
    total_rows = rows_dev * devices
    inv_sigma = 1.0 / sensor_sigma
    matches = sensor_ids[:, None] == jnp.arange(sensor_sigma.shape[0], dtype=jnp.int32)[None, :]
    row_scale = jnp.sum(jnp.where(matches, inv_sigma[None, :], jnp.float32(0.0)), axis=1)
    scaled = observations * row_scale[:, None]
    onehot = (buckets[:, None] == jnp.arange(row_groups, dtype=jnp.int32)[None, :]).astype(
        jnp.int32
    )
    running = jnp.cumsum(onehot, axis=0)
    within = jnp.sum(onehot * running, axis=1) - 1
    target = buckets * per_bucket + within
    prior_gram = square_form(prior_factor)
    received = regroup_rows(scaled, target)
    factor = reduce_gram(outer_sum(received), prior_gram, total_rows)
    whitened = whiten_rows(received, factor)
    return (whitened, factor)


def solution(mesh):
    in_specs = (P(("rows", "grp"), None), P(("rows", "grp")), P(), P(("rows", "grp")), P())
    out_specs = (P(("rows", "grp"), None), P())
    return jax.shard_map(shards, mesh=mesh, in_specs=in_specs, out_specs=out_specs, check_vma=False)
```

profile of v0, /device:TPU:8, one launch (start us, length us, event | category | flops | bytes accessed | tf_op | source)
XLA Modules:
  0.0 412.8 jit_solution(15080320871438559474)
XLA Ops:
  8.7 2.3 reduce-window.6
  14.3 13.0 %scatter_custom_fusion = f32[2048,512]{1,0:T(8,128)} fusion(s32[2048]{0:T(1024)S(1)} %compare_select_fusion, f32[2048,512]{1,0:T(8,128)} %param.5, f32[2048]{0:T(1024)S(1)} %select_reduce_fusion, f32[]{:T(128)} %constant.149.clone.1), kind=kCustom, calls=%fused_computation.2 | custom fusion | flops 1048576 | bytes 8396804 | tf_op jit(solution)/shard_map/scatter | solution.py:51
  27.2 98.5 %all_to_all.12 = f32[8,256,512]{2,1,0:T(8,128)S(1)} all-to-all(f32[8,256,512]{2,1,0:T(8,128)} %bitcast.83), channel_id=1, replica_groups=mesh['rows'=8,'grp'=4] {'rows'}, dimensions={0} | all-to-all | bytes 8388608 | tf_op jit(solution)/shard_map/all_to_all | solution.py:52
  125.7 2.0 copy-done.1
  127.8 8.0 %convolution_bitcast_fusion = f32[512,512]{0,1:T(8,128)} fusion(f32[8,256,512]{2,1,0:T(8,128)S(1)} %all_to_all.12), kind=kOutput, calls=%fused_computation.17 | convolution fusion | flops 6442450944 | bytes 5242880 | tf_op jit(solution)/shard_map/dot_general | solution.py:12
  135.8 129.4 %all-reduce.3.cloned.1.call-done = f32[512,512]{0,1:T(8,128)} async-done(((f32[512,512]{0,1:T(8,128)}), f32[512,512]{0,1:T(8,128)}) %all-reduce.3.cloned.1.call-update) | async-done | bytes 1048592 | tf_op jit(solution)/shard_map/psum | solution.py:56
  265.2 3.1 convolution_add_fusion.8
  269.9 12.2 %cholesky.104 = f32[128,128]{1,0:T(8,128)S(1)} custom-call(f32[128,128]{1,0:T(8,128)S(1)} %cholesky.266), custom_call_target="Cholesky" | custom-call | tf_op jit(solution)/shard_map/jit(cholesky)/cholesky | solution.py:42
  282.3 9.8 %custom-call.27 = f32[1,128,128]{1,2,0:T(8,128)S(1)} custom-call(f32[1,128,128]{2,1,0:T(8,128)S(1)} %get-tuple-element.17), custom_call_target="InvertDiagBlocksLowerTriangular" | custom-call | tf_op jit(solution)/shard_map/jit(cholesky)/cholesky | solution.py:42
  294.6 11.7 %cholesky.217 = f32[128,128]{1,0:T(8,128)S(1)} custom-call(f32[128,128]{1,0:T(8,128)S(1)} %cholesky.270), custom_call_target="Cholesky" | custom-call | tf_op jit(solution)/shard_map/jit(cholesky)/cholesky | solution.py:42
  306.4 9.8 %custom-call.28 = f32[1,128,128]{1,2,0:T(8,128)S(1)} custom-call(f32[1,128,128]{2,1,0:T(8,128)S(1)} %get-tuple-element.14), custom_call_target="InvertDiagBlocksLowerTriangular" | custom-call | tf_op jit(solution)/shard_map/jit(cholesky)/cholesky | solution.py:42
  317.7 11.9 %cholesky.238 = f32[128,128]{1,0:T(8,128)S(1)} custom-call(f32[128,128]{1,0:T(8,128)S(1)} %cholesky.275), custom_call_target="Cholesky" | custom-call | tf_op jit(solution)/shard_map/jit(cholesky)/cholesky | solution.py:42
  330.4 9.8 %custom-call.29 = f32[1,128,128]{1,2,0:T(8,128)S(1)} custom-call(f32[1,128,128]{2,1,0:T(8,128)S(1)} %get-tuple-element.11), custom_call_target="InvertDiagBlocksLowerTriangular" | custom-call | tf_op jit(solution)/shard_map/jit(cholesky)/cholesky | solution.py:42
  341.6 11.7 %cholesky.255 = f32[128,128]{1,0:T(8,128)S(1)} custom-call(f32[128,128]{1,0:T(8,128)S(1)} %convolution_subtract_fusion.2), custom_call_target="Cholesky" | custom-call | tf_op jit(solution)/shard_map/jit(cholesky)/cholesky | solution.py:42
  358.5 4.7 %gather_fusion = f32[512]{0:T(512)S(1)} fusion(f32[512,512]{1,0:T(8,128)S(1)} %select_select_fusion, s32[512]{0:T(512)S(1)} %bitcast.82), kind=kCustom, calls=%fused_computation | custom fusion | bytes 8192 | tf_op jit(solution)/shard_map/jit(diagonal)/cond/branch_0_fun/gather | solution.py:28
  363.2 2.1 fusion.20
  365.4 3.0 convolution_add_fusion.7
  370.2 2.5 copy.21
  380.1 2.3 fusion.24
  382.4 1.9 convolution_add_fusion.4
  389.8 1.9 convolution_add_fusion.2
  393.5 2.0 convolution_add_fusion.1
  395.6 1.9 fusion.4
  397.5 8.3 %fusion.28 = f32[2048,512]{1,0:T(8,128)} fusion(f32[2048,512]{1,0:T(8,128)S(1)} %bitcast.81, f32[512,512]{1,0:T(8,128)S(1)} %fusion.4), kind=kOutput, calls=%fused_computation.78 | convolution fusion | flops 6442450944 | bytes 9437184 | tf_op jit(solution)/shard_map/dot_general | solution.py:8
  (50 shorter events, 32.0 us)
Async XLA Ops:
  7.2 258.1 %copy-start = (f32[512,512]{1,0:T(8,128)S(1)}, f32[512,512]{1,0:T(8,128)}, u32[]{:S(2)}) copy-start(f32[512,512]{1,0:T(8,128)} %param.9) | copy-start | bytes 3145732
  7.2 258.0 %all-reduce.3.cloned.1.call-start = ((), (), s32[]{:S(2)}) async-start(), calls=%async_computation.1 | async-start | bytes 2097152 | tf_op jit(solution)/shard_map/psum | solution.py:56
  125.7 2.0 copy-start.1
  268.9 1.0 copy-start.3
  368.3 6.2 %copy-start.4 = (f32[512,512]{1,0:T(8,128)S(1)}, f32[512,512]{1,0:T(8,128)}, u32[]{:S(2)}) copy-start(f32[512,512]{1,0:T(8,128)} %convolution_add_fusion.7) | copy-start | bytes 3145732
  393.5 3.9 copy-start.2
Sparse Core Ops, SparseCore 0:
  135.9 129.2 all-reduce.2
where the time goes:
time: 418 us; the launch traced here: 413 us
  waiting for transfers between devices  129 us (31%)
  other arithmetic  100 us (24%)
  blocking collectives  98.5 us (24%)
  matrix products  56.4 us (13%)
  between operations  17.1 us (4%)
  local copies, waits for them, and re-layouts  11 us (3%)
    psum x1, waiting for transfers between devices, reduce_gram(): summed = lax.psum(local_gram, ('rows', 'grp'))  129 us
    all_to_all x1, blocking collectives, regroup_rows(): lax.all_to_all(outgoing, 'rows', split_axis=0, concat_axis=0, tiled=True)  98.5 us
    another operation x14, other arithmetic, upper_factor(): return jnp.linalg.cholesky(matrix).T  79.1 us
    dot_general x18, matrix products, matmul(): jnp.dot(left, right, precision=lax.Precision.HIGHEST, preferred_element_t...  42.9 us
    scatter x1, other arithmetic, regroup_rows(): outgoing = jnp.zeros_like(values).at[target].set(values)  13 us
  transfers between devices with their start and end apart: 1, of which 1 were waited for; matrix products, arithmetic and copies ran while one was open for 0% of the time, Pallas kernels for 0%

commit v1 on v0

v1 whole, which is shorter than its diff:
```python
import jax
import jax.numpy as jnp
from jax import lax
from jax.sharding import PartitionSpec as P


def matmul(left, right):
    return jnp.dot(left, right, precision=lax.Precision.HIGH, preferred_element_type=jnp.float32)


def outer_sum(values):
    return lax.dot_general(
        values,
        values,
        (((0,), (0,)), ((), ())),
        precision=lax.Precision.HIGH,
        preferred_element_type=jnp.float32,
    )


def lower_inverse(lower):
    width = lower.shape[0]
    identity = jnp.eye(width, dtype=jnp.float32)
    diag_values = jnp.diagonal(lower)
    scaled_lower = lower / diag_values[:, None]
    nilpotent = identity - scaled_lower
    product = identity + nilpotent
    power = nilpotent
    reach = 2
    while reach < width:
        power = matmul(power, power)
        product = product + matmul(product, power)
        reach = reach * 2
    return product / diag_values[None, :]


def exchange(chunks, row_groups):
    received = [chunks[0]]
    for k in range(1, row_groups):
        perm = [(i, i ^ k) for i in range(row_groups)]
        received.append(lax.ppermute(chunks[k], "rows", perm))
    return received


def shards(observations, sensor_ids, sensor_sigma, buckets, prior_factor):
    rows_dev, state = observations.shape
    row_groups = lax.axis_size("rows")
    devices = lax.axis_size(("rows", "grp"))
    me = lax.axis_index("rows")
    per_bucket = rows_dev // row_groups
    total_rows = rows_dev * devices
    inv_sigma = 1.0 / sensor_sigma
    matches = sensor_ids[:, None] == jnp.arange(sensor_sigma.shape[0], dtype=jnp.int32)[None, :]
    row_scale = jnp.sum(jnp.where(matches, inv_sigma[None, :], jnp.float32(0.0)), axis=1)
    scaled = observations * row_scale[:, None]
    slots = jnp.bitwise_xor(buckets, me)
    onehot = (slots[:, None] == jnp.arange(row_groups, dtype=jnp.int32)[None, :]).astype(jnp.int32)
    running = jnp.cumsum(onehot, axis=0)
    within = jnp.sum(onehot * running, axis=1) - 1
    target = slots * per_bucket + within
    outgoing = jnp.zeros_like(scaled).at[target].set(scaled)
    chunks = [outgoing[k * per_bucket : (k + 1) * per_bucket] for k in range(row_groups)]
    received = exchange(chunks, row_groups)
    summed = lax.psum(outer_sum(scaled), ("rows", "grp"))
    information = outer_sum(prior_factor) + summed / jnp.float32(total_rows)
    lower = jnp.linalg.cholesky(information)
    inverse = lower_inverse(lower).T
    white = jnp.stack([matmul(part, inverse) for part in received])
    order = jnp.bitwise_xor(jnp.arange(row_groups, dtype=jnp.int32), me)
    whitened = jnp.take(white, order, axis=0).reshape(rows_dev, state)
    return (whitened, lower.T)


def solution(mesh):
    in_specs = (P(("rows", "grp"), None), P(("rows", "grp")), P(), P(("rows", "grp")), P())
    out_specs = (P(("rows", "grp"), None), P())
    return jax.shard_map(shards, mesh=mesh, in_specs=in_specs, out_specs=out_specs, check_vma=False)
```

time: 418 us -> 372 us (0.89)
  blocking collectives: 98.5 us -> 0 us
  waiting for transfers between devices: 129 us -> 166 us
  starting transfers between devices: 0.04 us -> 10.3 us
  local copies, waits for them, and re-layouts: 11 us -> 16.6 us
    all_to_all x1 -> x0, blocking collectives: 98.5 us -> none  [regroup_rows(): lax.all_to_all(outgoing, 'rows', split_axis=0, concat_axis=0, tiled=True)]
    ppermute x0 -> x7, waiting for transfers between devices: none -> 29.6 us  [exchange(): received.append(lax.ppermute(chunks[k], 'rows', perm))]
    ppermute x0 -> x7, starting transfers between devices: none -> 10.3 us  [exchange(): received.append(lax.ppermute(chunks[k], 'rows', perm))]
    psum x1, waiting for transfers between devices: 129 us -> 136 us  [shards(): summed = lax.psum(outer_sum(scaled), ('rows', 'grp'))]
    dot_general x18 -> x24, matrix products: 42.9 us -> 36.9 us  [matmul(): jnp.dot(left, right, precision=lax.Precision.HIGH, preferred_element_type...]
    gather x0 -> x1, local copies, waits for them, and re-layouts: none -> 4.97 us  [shards(): whitened = jnp.take(white, order, axis=0).reshape(rows_dev, state)]
    dot_general x1 -> x2, matrix products: 8.03 us -> 11.1 us  [outer_sum(): lax.dot_general(values, values, (((0,), (0,)), ((), ())), precision=lax.P...]
  transfers between devices with their start and end apart: 1 -> 8, of which waited for: 1 -> 3; matrix products, arithmetic and copies ran while one was open for 0% -> 41% of each run, Pallas kernels for 0% -> 0%
where the time goes in v1:
time: 372 us; the launch traced here: 365 us
  waiting for transfers between devices  166 us (45%)
  other arithmetic  101 us (27%)
  matrix products  53.4 us (14%)
  between operations  17.2 us (5%)
  local copies, waits for them, and re-layouts  16.6 us (4%)
  starting transfers between devices  10.3 us (3%)
    psum x1, waiting for transfers between devices, shards(): summed = lax.psum(outer_sum(scaled), ('rows', 'grp'))  136 us
    another operation x14, other arithmetic, shards(): lower = jnp.linalg.cholesky(information)  79 us
    dot_general x24, matrix products, matmul(): jnp.dot(left, right, precision=lax.Precision.HIGH, preferred_element_type...  36.9 us
    ppermute x7, waiting for transfers between devices, exchange(): received.append(lax.ppermute(chunks[k], 'rows', perm))  29.6 us
    scatter x1, other arithmetic, shards(): outgoing = jnp.zeros_like(scaled).at[target].set(scaled)  13.1 us
    dot_general x2, matrix products, outer_sum(): lax.dot_general(values, values, (((0,), (0,)), ((), ())), precision=lax.P...  11.1 us
    ppermute x7, starting transfers between devices, exchange(): received.append(lax.ppermute(chunks[k], 'rows', perm))  10.3 us
  transfers between devices with their start and end apart: 8, of which 3 were waited for; matrix products, arithmetic and copies ran while one was open for 41% of the time, Pallas kernels for 0%

profile of v1, /device:TPU:8, one launch (start us, length us, event | category | flops | bytes accessed | tf_op | source)
XLA Modules:
  0.0 364.8 jit_solution(3243878577814806415)
XLA Ops:
  9.3 8.8 %fusion = f32[512,512]{0,1:T(8,128)} fusion(f32[2048,512]{1,0:T(8,128)} %param.5, f32[2048]{0:T(1024)S(1)} %select_reduce_fusion), kind=kOutput, calls=%fused_computation.4 | convolution fusion | flops 3222274048 | bytes 5251072 | tf_op jit(solution)/shard_map/dot_general | solution.py:12
  21.1 13.1 %scatter_custom_fusion = f32[2048,512]{1,0:T(8,128)} fusion(s32[2048]{0:T(1024)S(1)} %compare_select_fusion, f32[2048,512]{1,0:T(8,128)} %param.5, f32[2048]{0:T(1024)S(1)} %select_reduce_fusion, f32[]{:T(128)} %constant.170.clone.1), kind=kCustom, calls=%fused_computation.6 | custom fusion | flops 1048576 | bytes 8396804 | tf_op jit(solution)/shard_map/scatter | solution.py:61
  34.2 4.0 %fusion.34 = (f32[256,512]{1,0:T(8,128)}, f32[256,512]{1,0:T(8,128)}, f32[256,512]{1,0:T(8,128)}, f32[256,512]{1,0:T(8,128)}, f32[256,512]{1,0:T(8,128)}, /*index=5*/f32[256,512]{1,0:T(8,128)}, f32[256,512]{1,0:T(8,128)}) fusion(f32[2048,512]{1,0:T(8,128)} %scatter_custom_fusion), kind=kLoop, calls=%fused_computation.98 | loop fusion | bytes 7340032 | tf_op jit(solution)/shard_map/slice | solution.py:62
  41.7 2.6 collective-permute-start.3
  45.7 136.5 %all-reduce.3.cloned.1.call-done = f32[512,512]{0,1:T(8,128)} async-done(((f32[512,512]{0,1:T(8,128)}), f32[512,512]{0,1:T(8,128)}) %all-reduce.3.cloned.1.call-update) | async-done | bytes 1048592 | tf_op jit(solution)/shard_map/psum | solution.py:64
  186.0 11.7 %cholesky.104 = f32[128,128]{1,0:T(8,128)S(1)} custom-call(f32[128,128]{1,0:T(8,128)S(1)} %cholesky.266), custom_call_target="Cholesky" | custom-call | tf_op jit(solution)/shard_map/jit(cholesky)/cholesky | solution.py:66
  197.9 9.8 %custom-call.27 = f32[1,128,128]{1,2,0:T(8,128)S(1)} custom-call(f32[1,128,128]{2,1,0:T(8,128)S(1)} %get-tuple-element.24), custom_call_target="InvertDiagBlocksLowerTriangular" | custom-call | tf_op jit(solution)/shard_map/jit(cholesky)/cholesky | solution.py:66
  210.2 12.1 %cholesky.217 = f32[128,128]{1,0:T(8,128)S(1)} custom-call(f32[128,128]{1,0:T(8,128)S(1)} %cholesky.270), custom_call_target="Cholesky" | custom-call | tf_op jit(solution)/shard_map/jit(cholesky)/cholesky | solution.py:66
  222.4 9.8 %custom-call.28 = f32[1,128,128]{1,2,0:T(8,128)S(1)} custom-call(f32[1,128,128]{2,1,0:T(8,128)S(1)} %get-tuple-element.21), custom_call_target="InvertDiagBlocksLowerTriangular" | custom-call | tf_op jit(solution)/shard_map/jit(cholesky)/cholesky | solution.py:66
  233.8 11.7 %cholesky.238 = f32[128,128]{1,0:T(8,128)S(1)} custom-call(f32[128,128]{1,0:T(8,128)S(1)} %cholesky.275), custom_call_target="Cholesky" | custom-call | tf_op jit(solution)/shard_map/jit(cholesky)/cholesky | solution.py:66
  246.2 9.8 %custom-call.29 = f32[1,128,128]{1,2,0:T(8,128)S(1)} custom-call(f32[1,128,128]{2,1,0:T(8,128)S(1)} %get-tuple-element.18), custom_call_target="InvertDiagBlocksLowerTriangular" | custom-call | tf_op jit(solution)/shard_map/jit(cholesky)/cholesky | solution.py:66
  257.5 11.9 %cholesky.255 = f32[128,128]{1,0:T(8,128)S(1)} custom-call(f32[128,128]{1,0:T(8,128)S(1)} %convolution_subtract_fusion.2), custom_call_target="Cholesky" | custom-call | tf_op jit(solution)/shard_map/jit(cholesky)/cholesky | solution.py:66
  273.4 4.5 %gather_fusion = f32[512]{0:T(512)S(1)} fusion(f32[512,512]{1,0:T(8,128)S(1)} %select_select_fusion, s32[512]{0:T(512)S(1)} %bitcast.124), kind=kCustom, calls=%fused_computation | custom fusion | bytes 8192 | tf_op jit(solution)/shard_map/jit(diagonal)/cond/branch_0_fun/gather | solution.py:24
  296.0 2.6 fusion.7
  298.7 2.5 fusion.15
  301.7 2.5 fusion.14
  306.5 2.5 fusion.13
  309.0 2.5 fusion.12
  311.5 2.5 fusion.11
  313.9 2.5 fusion.10
  316.4 21.1 %collective-permute-done.5 = f32[256,512]{1,0:T(8,128)S(1)} collective-permute-done((f32[256,512]{1,0:T(8,128)S(1)}, f32[256,512]{1,0:T(8,128)S(1)}, u32[]{:S(2)}, u32[]{:S(2)}) %collective-permute-start.5) | collective-permute-done | bytes 524320 | tf_op jit(solution)/shard_map/ppermute | solution.py:41
  338.9 8.6 %collective-permute-done.6 = f32[256,512]{1,0:T(8,128)S(1)} collective-permute-done((f32[256,512]{1,0:T(8,128)S(1)}, f32[256,512]{1,0:T(8,128)S(1)}, u32[]{:S(2)}, u32[]{:S(2)}) %collective-permute-start.6) | collective-permute-done | bytes 524320 | tf_op jit(solution)/shard_map/ppermute | solution.py:41
  348.9 5.0 %gather_fusion.1 = f32[8,256,512]{2,1,0:T(8,128)} fusion(f32[8,256,512]{2,1,0:T(8,128)} %fusion.8, s32[1024]{0:T(1024)S(1)} %pad_clamp_fusion), kind=kCustom, calls=%fused_computation.1 | custom fusion | bytes 8388640 | tf_op jit(solution)/shard_map/jit(_take)/gather | solution.py:70
  353.9 3.8 %bitcast_select_fusion = f32[2048,512]{1,0:T(8,128)} fusion(f32[8,256,512]{2,1,0:T(8,128)} %gather_fusion.1, pred[2048]{0:T(1024)(128)(4,1)S(1)} %broadcast_in_dim.47), kind=kLoop, calls=%fused_computation.3 | loop fusion | flops 1048576 | bytes 8390656 | tf_op jit(solution)/shard_map/jit(_take)/select_n | solution.py:70
  (80 shorter events, 45.4 us)
Async XLA Ops:
  7.2 175.0 %copy-start = (f32[512,512]{1,0:T(8,128)S(1)}, f32[512,512]{1,0:T(8,128)}, u32[]{:S(2)}) copy-start(f32[512,512]{1,0:T(8,128)} %param.9) | copy-start | bytes 3145732
  7.2 175.0 %all-reduce.3.cloned.1.call-start = ((), (), s32[]{:S(2)}) async-start(), calls=%async_computation | async-start | bytes 2097152 | tf_op jit(solution)/shard_map/psum | solution.py:64
  9.3 8.9 %copy-start.4 = (s32[2048]{0:T(1024)S(1)}, s32[2048]{0:T(1024)}, u32[]{:S(2)}) copy-start(s32[2048]{0:T(1024)} %param.8) | copy-start | bytes 24580
  38.2 262.9 %collective-permute-start = (f32[256,512]{1,0:T(8,128)}, f32[256,512]{1,0:T(8,128)}, u32[]{:S(2)}, u32[]{:S(2)}) collective-permute-start(f32[256,512]{1,0:T(8,128)} %get-tuple-element.14), channel_id=1, source_target_pairs={{0,4},{4,0},{8,12},{12,8},{16,20},{20,16},{24,28},{28,24},{1,5},{5... | collective-permute-start | bytes 1572872 | tf_op jit(solution)/shard_map/ppermute | solution.py:41
  39.7 264.4 %collective-permute-start.1 = (f32[256,512]{1,0:T(8,128)}, f32[256,512]{1,0:T(8,128)}, u32[]{:S(2)}, u32[]{:S(2)}) collective-permute-start(f32[256,512]{1,0:T(8,128)} %get-tuple-element.13), channel_id=1, source_target_pairs={{0,8},{4,12},{8,0},{12,4},{16,24},{20,28},{24,16},{28,20},{1,9},{5... | collective-permute-start | bytes 1572872 | tf_op jit(solution)/shard_map/ppermute | solution.py:41
  40.2 268.8 %collective-permute-start.2 = (f32[256,512]{1,0:T(8,128)}, f32[256,512]{1,0:T(8,128)}, u32[]{:S(2)}, u32[]{:S(2)}) collective-permute-start(f32[256,512]{1,0:T(8,128)} %get-tuple-element.12), channel_id=1, source_target_pairs={{0,12},{4,8},{8,4},{12,0},{16,28},{20,24},{24,20},{28,16},{1,13},{... | collective-permute-start | bytes 1572872 | tf_op jit(solution)/shard_map/ppermute | solution.py:41
  41.7 269.8 %collective-permute-start.3 = (f32[256,512]{1,0:T(8,128)}, f32[256,512]{1,0:T(8,128)}, u32[]{:S(2)}, u32[]{:S(2)}) collective-permute-start(f32[256,512]{1,0:T(8,128)} %get-tuple-element.11), channel_id=1, source_target_pairs={{0,16},{4,20},{8,24},{12,28},{16,0},{20,4},{24,8},{28,12},{1,17},{... | collective-permute-start | bytes 1572872 | tf_op jit(solution)/shard_map/ppermute | solution.py:41
  44.3 269.6 %collective-permute-start.4 = (f32[256,512]{1,0:T(8,128)}, f32[256,512]{1,0:T(8,128)}, u32[]{:S(2)}, u32[]{:S(2)}) collective-permute-start(f32[256,512]{1,0:T(8,128)} %get-tuple-element.10), channel_id=1, source_target_pairs={{0,20},{4,16},{8,28},{12,24},{16,4},{20,0},{24,12},{28,8},{1,21},{... | collective-permute-start | bytes 1572872 | tf_op jit(solution)/shard_map/ppermute | solution.py:41
  185.0 1.0 copy-start.1
  296.0 5.1 %copy-start.3 = (f32[256,512]{1,0:T(8,128)S(1)}, f32[256,512]{1,0:T(8,128)}, u32[]{:S(2)}) copy-start(f32[256,512]{1,0:T(8,128)} %get-tuple-element.9) | copy-start | bytes 1572868
  296.0 8.1 %copy-start.2 = (f32[256,512]{1,0:T(8,128)S(1)}, f32[256,512]{1,0:T(8,128)}, u32[]{:S(2)}) copy-start(f32[256,512]{1,0:T(8,128)} %get-tuple-element.8) | copy-start | bytes 1572868
  301.1 36.4 %collective-permute-start.5 = (f32[256,512]{1,0:T(8,128)S(1)}, f32[256,512]{1,0:T(8,128)S(1)}, u32[]{:S(2)}, u32[]{:S(2)}) collective-permute-start(f32[256,512]{1,0:T(8,128)S(1)} %copy-done.3), channel_id=1, source_target_pairs={{0,24},{4,28},{8,16},{12,20},{16,8},{20,12},{24,0},{28,4},{1,25},{... | collective-permute-start | bytes 1572872 | tf_op jit(solution)/shard_map/ppermute | solution.py:41
  304.1 43.3 %collective-permute-start.6 = (f32[256,512]{1,0:T(8,128)S(1)}, f32[256,512]{1,0:T(8,128)S(1)}, u32[]{:S(2)}, u32[]{:S(2)}) collective-permute-start(f32[256,512]{1,0:T(8,128)S(1)} %copy-done.2), channel_id=1, source_target_pairs={{0,28},{4,24},{8,20},{12,16},{16,12},{20,8},{24,4},{28,0},{1,29},{... | collective-permute-start | bytes 1572872 | tf_op jit(solution)/shard_map/ppermute | solution.py:41
Sparse Core Ops, SparseCore 0:
  18.3 163.8 all-reduce.2

commit v2 on v1

v2 whole, which is shorter than its diff:
```python
import functools

import jax
import jax.numpy as jnp
from jax import lax
from jax.experimental import pallas as pl
from jax.experimental.pallas import tpu as pltpu
from jax.sharding import PartitionSpec as P

F32 = jnp.float32
BF16 = jnp.bfloat16
I32 = jnp.int32
LANES = 128
SUB = 8
MIB = 1024 * 1024


def iota(shape, axis):
    return lax.broadcasted_iota(I32, shape, axis)


def split(values):
    high = values.astype(BF16)
    low = (values - high.astype(F32)).astype(BF16)
    return high, low


def dot(left, right):
    return jnp.dot(left, right, preferred_element_type=F32)


def dot_rows(left, right):
    return lax.dot_general(left, right, (((0,), (0,)), ((), ())), preferred_element_type=F32)


def dot3(left, right):
    lh, ll = split(left)
    rh, rl = split(right)
    return dot(lh, rh) + (dot(lh, rl) + dot(ll, rh))


def dot3_rows(left, right):
    lh, ll = split(left)
    rh, rl = split(right)
    return dot_rows(lh, rh) + (dot_rows(lh, rl) + dot_rows(ll, rh))


def regroup_kernel(groups, per_bucket, me_ref, buckets_ref, ids_ref, sigma_ref, obs_ref, *rest):
    outs = rest[:groups]
    place_ref, meta_ref, sorted_ref, inv_ref, meta_smem, sem = rest[groups:]
    step = pl.program_id(0)
    blocks, block = buckets_ref.shape
    sensors = sigma_ref.shape[1]
    padded = sorted_ref.shape[0]
    cells = blocks * groups

    @pl.when(step == 0)
    def _():
        me = me_ref[0]
        inv_row = 1.0 / sigma_ref[...]
        inv_ref[...] = jnp.transpose(jnp.broadcast_to(inv_row, (LANES, sensors)))
        slots = buckets_ref[...] ^ me
        hits = jnp.concatenate(
            [
                jnp.broadcast_to(slots[s : s + 1, :], (groups, block)) == iota((groups, block), 0)
                for s in range(blocks)
            ],
            axis=0,
        )
        upto = (iota((block, block), 0) <= iota((block, block), 1)).astype(F32).astype(BF16)
        running = dot(hits.astype(F32).astype(BF16), upto)
        count = jnp.broadcast_to(running[:, block - 1 : block], (cells, LANES))
        row, col = iota((cells, cells), 0), iota((cells, cells), 1)
        shift = groups.bit_length() - 1
        earlier = ((row & (groups - 1)) == (col & (groups - 1))) & (col < row)
        before = dot(earlier.astype(F32).astype(BF16), count.astype(BF16)).astype(I32)
        cell = iota((cells, LANES), 0)
        start = (cell & (groups - 1)) * per_bucket + before
        odd = start & (SUB - 1)
        tiles = (odd + count.astype(I32) + (SUB - 1)) >> 3
        same = ((row >> shift) == (col >> shift)) & (col < row)
        first = dot(same.astype(F32).astype(BF16), tiles.astype(F32).astype(BF16)).astype(I32)
        lane = iota((cells, LANES), 1)
        meta_ref[...] = jnp.where(lane == 0, before, jnp.where(lane == 1, first, tiles))
        copy = pltpu.make_async_copy(meta_ref, meta_smem, sem)
        copy.start()
        local = first * SUB + odd
        local = jnp.concatenate([local] * (block // LANES), axis=1)
        spot = jnp.where(hits, local + running.astype(I32) - 1, 0)
        place_ref[...] = jnp.concatenate(
            [
                jnp.sum(spot[s * groups : (s + 1) * groups], axis=0, keepdims=True)
                for s in range(blocks)
            ],
            axis=0,
        )
        copy.wait()

    place = place_ref[pl.ds(step, 1), :]
    moves = (iota((padded, block), 0) == place).astype(F32).astype(BF16)
    known = iota((sensors, block), 0) == ids_ref[pl.ds(step, 1), :]
    inv = jnp.concatenate([inv_ref[...]] * (block // LANES), axis=1)
    scale_row = jnp.sum(jnp.where(known, inv, 0.0), axis=0, keepdims=True)
    scale = jnp.transpose(jnp.broadcast_to(scale_row, (LANES, block)))
    state = obs_ref.shape[1]
    scaled = obs_ref[...] * jnp.concatenate([scale] * (state // LANES), axis=1)
    high, low = split(scaled)
    sorted_ref[...] = dot(moves, high) + dot(moves, low)

    for v in range(groups):
        cell = step * groups + v
        before = meta_smem[cell, 0]
        source = meta_smem[cell, 1]
        tiles = meta_smem[cell, 2]
        target = before >> 3
        out = outs[v]

        @pl.when(tiles > 0)
        def _(out=out, before=before, source=source, target=target):
            rows = pl.ds(pl.multiple_of(target * SUB, SUB), SUB)
            old = jnp.where((before & (SUB - 1)) > 0, out[rows, :], 0.0)
            out[rows, :] = old + sorted_ref[pl.ds(pl.multiple_of(source * SUB, SUB), SUB), :]

        def body(t, carry, out=out, source=source, target=target):
            out[pl.ds(pl.multiple_of((target + t) * SUB, SUB), SUB), :] = sorted_ref[
                pl.ds(pl.multiple_of((source + t) * SUB, SUB), SUB), :
            ]
            return carry

        lax.fori_loop(1, tiles, body, 0)


def regroup(observations, sensor_ids, sensor_sigma, buckets, me, groups):
    rows, state = observations.shape
    sensors = sensor_sigma.shape[0]
    block = 256
    blocks = rows // block
    per_bucket = rows // groups
    padded = -(-(block + groups * 2 * (SUB - 1)) // LANES) * LANES
    whole = lambda shape: pl.BlockSpec(shape, lambda s, me: (0, 0))
    return pl.pallas_call(
        functools.partial(regroup_kernel, groups, per_bucket),
        grid_spec=pltpu.PrefetchScalarGridSpec(
            num_scalar_prefetch=1,
            grid=(blocks,),
            in_specs=[
                whole((blocks, block)),
                whole((blocks, block)),
                whole((1, sensors)),
                pl.BlockSpec((block, state), lambda s, me: (s, 0)),
            ],
            out_specs=[whole((per_bucket, state))] * groups,
            scratch_shapes=[
                pltpu.VMEM((blocks, block), I32),
                pltpu.VMEM((blocks * groups, LANES), I32),
                pltpu.VMEM((padded, state), F32),
                pltpu.VMEM((sensors, LANES), F32),
                pltpu.SMEM((blocks * groups, LANES), I32),
                pltpu.SemaphoreType.DMA,
            ],
        ),
        out_shape=[jax.ShapeDtypeStruct((per_bucket, state), F32)] * groups,
        compiler_params=pltpu.CompilerParams(vmem_limit_bytes=24 * MIB),
        cost_estimate=pl.CostEstimate(
            flops=4 * rows * padded * state, bytes_accessed=8 * rows * state, transcendentals=0
        ),
    )(
        me.reshape(1),
        buckets.reshape(blocks, block),
        sensor_ids.reshape(blocks, block),
        sensor_sigma.reshape(1, sensors),
        observations,
    )


def block_pairs(count):
    return [(i, j) for i in range(count) for j in range(i, count)]


def write_gram(both, state, out_ref):
    for n, (i, j) in enumerate(block_pairs(state // LANES)):
        a, b = i * LANES, j * LANES
        cross = both[a : a + LANES, state + b : state + b + LANES]
        turned = both[b : b + LANES, state + a : state + a + LANES]
        out_ref[n * LANES : (n + 1) * LANES, :] = both[a : a + LANES, b : b + LANES] + (
            cross + jnp.transpose(turned)
        )


def gram_kernel(groups, prior_ref, *rest):
    chunks = rest[:groups]
    out_ref, prior_out_ref, both_ref, pair_ref = rest[groups:]
    per_bucket, state = chunks[0].shape
    for k, chunk in enumerate(chunks):
        rows = slice(k * per_bucket, (k + 1) * per_bucket)
        high, low = split(chunk[...])
        pair_ref[rows, :state] = high
        pair_ref[rows, state:] = low
    both_ref[...] = dot_rows(pair_ref[:, :state], pair_ref[...])
    write_gram(both_ref, state, out_ref)
    high, low = split(prior_ref[...])
    both_ref[...] = dot_rows(high, jnp.concatenate([high, low], axis=1))
    write_gram(both_ref, state, prior_out_ref)


def gram(prior_factor, chunks):
    groups = len(chunks)
    per_bucket, state = chunks[0].shape
    rows = groups * per_bucket
    packed = len(block_pairs(state // LANES)) * LANES
    vmem = pl.BlockSpec(memory_space=pltpu.VMEM)
    return pl.pallas_call(
        functools.partial(gram_kernel, groups),
        in_specs=[vmem] * (groups + 1),
        out_specs=[vmem] * 2,
        out_shape=[jax.ShapeDtypeStruct((packed, LANES), F32)] * 2,
        scratch_shapes=[pltpu.VMEM((state, 2 * state), F32), pltpu.VMEM((rows, 2 * state), BF16)],
        compiler_params=pltpu.CompilerParams(vmem_limit_bytes=24 * MIB),
        cost_estimate=pl.CostEstimate(
            flops=4 * rows * state * state, bytes_accessed=4 * rows * state, transcendentals=0
        ),
    )(prior_factor, *chunks)


def sum_all(packed, row_groups, grp, later):
    rows, lanes = packed.shape
    part = rows // grp
    got = lax.all_to_all(packed, "grp", split_axis=0, concat_axis=0, tiled=True)
    mine = jnp.sum(got.reshape(grp, part, lanes), axis=0)
    piece = -(-part // row_groups)
    mine = jnp.pad(mine, ((0, piece * row_groups - part), (0, 0)))
    got = lax.all_to_all(mine, "rows", split_axis=0, concat_axis=0, tiled=True)
    got, early = lax.optimization_barrier((got, later[0]))
    mine = jnp.sum(got.reshape(row_groups, piece, lanes), axis=0)
    mine = jnp.broadcast_to(mine, (row_groups, piece, lanes)).reshape(row_groups * piece, lanes)
    mine = lax.all_to_all(mine, "rows", split_axis=0, concat_axis=0, tiled=True)[:part]
    mine = jnp.broadcast_to(mine, (grp, part, lanes)).reshape(rows, lanes)
    summed = lax.all_to_all(mine, "grp", split_axis=0, concat_axis=0, tiled=True)
    summed, late = lax.optimization_barrier((summed, later[1]))
    return summed, (early, late)


def sweep(a, w):
    width = a.shape[0]
    groups = width // SUB
    row_id = iota((SUB, LANES), 0)
    a_rows = [a[g * SUB : (g + 1) * SUB, :] for g in range(groups)]
    w_rows = [w[g * SUB : (g + 1) * SUB, :] for g in range(groups)]
    for g in range(groups):
        va, vw = a_rows[g], w_rows[g]
        cols = [
            jnp.broadcast_to(va[:, g * SUB + j : g * SUB + j + 1], (SUB, LANES)) for j in range(SUB)
        ]
        scale = jnp.zeros((SUB, LANES), F32)
        for j in range(SUB):
            pivot = jnp.broadcast_to(cols[j][j : j + 1, :], (SUB, LANES))
            root = lax.rsqrt(pivot)
            scale = jnp.where(row_id == j, root, scale)
            if j < SUB - 1:
                ratio = jnp.where(row_id > j, cols[j] * (root * root), 0.0)
                for k in range(j + 1, SUB):
                    cols[k] = cols[k] - ratio * cols[k][j : j + 1, :]
                va = va - ratio * va[j : j + 1, :]
                vw = vw - ratio * vw[j : j + 1, :]
        va, vw = va * scale, vw * scale
        va = jnp.where(iota((SUB, LANES), 1) >= row_id + g * SUB, va, 0.0)
        a_rows[g], w_rows[g] = va, vw
        if g < groups - 1:
            both = jnp.concatenate([va, vw], axis=1)
            high = both.astype(BF16).astype(F32)
            low = both - high
            left = jnp.concatenate([high[:, :LANES], high[:, :LANES], low[:, :LANES]], axis=0)
            right = jnp.concatenate([high, low, high], axis=0)
            change = dot_rows(left.astype(BF16), right.astype(BF16))
            for q in range(g + 1, groups):
                rows = slice(q * SUB, (q + 1) * SUB)
                a_rows[q] = a_rows[q] - change[rows, :LANES]
                w_rows[q] = w_rows[q] - change[rows, LANES:]
    return jnp.concatenate(a_rows, axis=0), jnp.concatenate(w_rows, axis=0)


def factor_kernel(inv_total, sum_ref, prior_ref, factor_ref, high_ref, low_ref, a_ref, x_ref):
    state = factor_ref.shape[0]
    count = state // LANES
    span = lambda i: slice(i * LANES, (i + 1) * LANES)
    for n, (i, j) in enumerate(block_pairs(count)):
        a_ref[span(i), span(j)] = prior_ref[span(n), :] + sum_ref[span(n), :] * inv_total
    factor_ref[...] = jnp.zeros((state, state), F32)
    x_ref[...] = jnp.zeros((state, state), F32)
    eye = (iota((LANES, LANES), 0) == iota((LANES, LANES), 1)).astype(F32)
    for k in range(count):
        r, w = sweep(a_ref[span(k), span(k)], eye)
        factor_ref[span(k), span(k)] = r
        x = jnp.transpose(w)
        x_ref[span(k), span(k)] = x
        if k > 0:
            left = dot3(x_ref[: k * LANES, : k * LANES], factor_ref[: k * LANES, span(k)])
            x_ref[: k * LANES, span(k)] = -dot3(left, x)
        if k < count - 1:
            rest = slice((k + 1) * LANES, state)
            right = dot3(w, a_ref[span(k), rest])
            factor_ref[span(k), rest] = right
            for i in range(k + 1, count):
                low = slice(i * LANES, state)
                at = (i - k - 1) * LANES
                a_ref[span(i), low] -= dot3_rows(right[:, at : at + LANES], right[:, at:])
    high, low = split(x_ref[...])
    high_ref[...] = high
    low_ref[...] = low


def factorise(summed, prior_gram, state, total_rows):
    vmem = pl.BlockSpec(memory_space=pltpu.VMEM)
    return pl.pallas_call(
        functools.partial(factor_kernel, 1.0 / total_rows),
        in_specs=[vmem] * 2,
        out_specs=[vmem] * 3,
        out_shape=[
            jax.ShapeDtypeStruct((state, state), F32),
            jax.ShapeDtypeStruct((state, state), BF16),
            jax.ShapeDtypeStruct((state, state), BF16),
        ],
        scratch_shapes=[pltpu.VMEM((state, state), F32)] * 2,
        compiler_params=pltpu.CompilerParams(vmem_limit_bytes=16 * MIB),
        cost_estimate=pl.CostEstimate(
            flops=40_000_000_000, bytes_accessed=4 * state * state, transcendentals=0
        ),
    )(summed, prior_gram)


def whiten_kernel(steps, aliased, me_ref, high_ref, low_ref, *rest):
    count = len(steps)
    chunks = rest[:count]
    out_ref, held, sems = rest[count + aliased :]
    per_bucket = chunks[0].shape[0]
    high, low = high_ref[...], low_ref[...]
    copies = []
    for n, k in enumerate(steps):
        rows_high, rows_low = split(chunks[n][...])
        held[n] = dot(rows_high, high) + (dot(rows_high, low) + dot(rows_low, high))
        slot = me_ref[0] ^ k
        copy = pltpu.make_async_copy(
            held.at[n],
            out_ref.at[pl.ds(pl.multiple_of(slot * per_bucket, per_bucket), per_bucket), :],
            sems.at[n],
        )
        copy.start()
        copies.append(copy)
    for copy in copies:
        copy.wait()


def whiten(me, high, low, steps, chunks, out, rows):
    per_bucket, state = chunks[0].shape
    count = len(chunks)
    vmem = pl.BlockSpec(memory_space=pltpu.VMEM)
    anywhere = pl.BlockSpec(memory_space=pl.ANY)
    extra = [] if out is None else [out]
    return pl.pallas_call(
        functools.partial(whiten_kernel, tuple(steps), len(extra)),
        in_specs=[pl.BlockSpec(memory_space=pltpu.SMEM)]
        + [vmem] * (2 + count)
        + [anywhere] * len(extra),
        out_specs=anywhere,
        out_shape=jax.ShapeDtypeStruct((rows, state), F32),
        scratch_shapes=[
            pltpu.VMEM((count, per_bucket, state), F32),
            pltpu.SemaphoreType.DMA((count,)),
        ],
        input_output_aliases={3 + count: 0} if extra else {},
        compiler_params=pltpu.CompilerParams(vmem_limit_bytes=16 * MIB),
        cost_estimate=pl.CostEstimate(
            flops=6 * count * per_bucket * state * state,
            bytes_accessed=8 * count * per_bucket * state,
            transcendentals=0,
        ),
    )(me.reshape(1), high, low, *chunks, *extra)


def shards(observations, sensor_ids, sensor_sigma, buckets, prior_factor):
    rows_dev, state = observations.shape
    groups = lax.axis_size("rows")
    grp = lax.axis_size("grp")
    me = lax.axis_index("rows").astype(I32)
    total_rows = rows_dev * groups * grp
    chunks = regroup(observations, sensor_ids, sensor_sigma, buckets, me, groups)
    move = lambda k, chunk: lax.ppermute(chunk, "rows", [(i, i ^ k) for i in range(groups)])
    held_back = [k for k in (2, 3) if k < groups]
    received = [chunks[0]] + [None] * (groups - 1)
    for k in reversed(range(1, groups)):
        if k not in held_back:
            received[k] = move(k, chunks[k])
    packed, prior_gram = gram(prior_factor, chunks)
    summed, later = sum_all(packed, groups, grp, [chunks[k] for k in held_back])
    for k, chunk in zip(held_back, later):
        received[k] = move(k, chunk)
    factor, high, low = factorise(summed, prior_gram, state, total_rows)
    out = whiten(me, high, low, range(groups // 2), received[: groups // 2], None, rows_dev)
    out = whiten(me, high, low, range(groups // 2, groups), received[groups // 2 :], out, rows_dev)
    return (out, factor)


def solution(mesh):
    in_specs = (P(("rows", "grp"), None), P(("rows", "grp")), P(), P(("rows", "grp")), P())
    out_specs = (P(("rows", "grp"), None), P())
    return jax.shard_map(shards, mesh=mesh, in_specs=in_specs, out_specs=out_specs, check_vma=False)
```

time: 372 us -> 160 us (0.43); the launches traced: 365 us -> 159 us
  waiting for transfers between devices: 166 us -> 60.9 us
  other arithmetic: 101 us -> 0.05 us
  matrix products: 53.4 us -> 0 us
  Pallas kernels: 0 us -> 47 us
  blocking collectives: 0 us -> 24.3 us
  between operations: 17.2 us -> 0.9 us
  local copies, waits for them, and re-layouts: 16.6 us -> 7.73 us
  starting transfers between devices: 10.3 us -> 18 us
    psum x1 -> x0, waiting for transfers between devices: 136 us -> none  [shards(): summed = lax.psum(outer_sum(scaled), ('rows', 'grp'))]
    another operation x16 -> x0, other arithmetic: 81.4 us -> none  [the longest x14 79 us: shards(): lower = jnp.linalg.cholesky(information)]
    dot_general x26 -> x0, matrix products: 48 us -> none  [the longest x24 36.9 us: matmul(): jnp.dot(left, right, precision=lax.Precision.HIGH, preferred_element_type...]
    pallas_call x0 -> x5, Pallas kernels: none -> 47 us  [the longest x1 25.8 us: factorise(): pl.pallas_call(functools.partial(factor_kernel, 1.0 / total_rows), in_spe...]
    all_to_all x0 -> x2, blocking collectives: none -> 24.3 us  [the longest x1 12.8 us: sum_all(): got = lax.all_to_all(packed, 'grp', split_axis=0, concat_axis=0, tiled=True)]
    ppermute x7, waiting for transfers between devices: 29.6 us -> 49.9 us  [shards(): lax.ppermute(chunk, 'rows', [(i, i ^ k) for i in range(groups)])]
    scatter x1 -> x0, other arithmetic: 13.1 us -> none  [shards(): outgoing = jnp.zeros_like(scaled).at[target].set(scaled)]
    all_to_all x0 -> x2, waiting for transfers between devices: none -> 10.9 us  [the longest x1 6.13 us: sum_all(): lax.all_to_all(mine, 'grp', split_axis=0, concat_axis=0, tiled=True)]
  transfers between devices with their start and end apart: 8 -> 9, of which waited for: 3 -> 6; matrix products, arithmetic and copies ran while one was open for 41% -> 1% of each run, Pallas kernels for 0% -> 19%
where the time goes in v2:
time: 160 us; the launch traced here: 159 us
  waiting for transfers between devices  60.9 us (38%)
  Pallas kernels  47 us (29%)
  blocking collectives  24.3 us (15%)
  starting transfers between devices  18 us (11%)
  local copies, waits for them, and re-layouts  7.73 us (5%)
    ppermute x7, waiting for transfers between devices, shards(): lax.ppermute(chunk, 'rows', [(i, i ^ k) for i in range(groups)])  49.9 us
    pallas_call x1, Pallas kernels, factorise(): pl.pallas_call(functools.partial(factor_kernel, 1.0 / total_rows), in_spe...  25.8 us
    all_to_all x1, blocking collectives, sum_all(): got = lax.all_to_all(packed, 'grp', split_axis=0, concat_axis=0, tiled=True)  12.8 us
    all_to_all x1, blocking collectives, sum_all(): got = lax.all_to_all(mine, 'rows', split_axis=0, concat_axis=0, tiled=True)  11.5 us
    pallas_call x1, Pallas kernels, regroup(): pl.pallas_call(functools.partial(regroup_kernel, groups, per_bucket), gri...  9.77 us
    ppermute x7, starting transfers between devices, shards(): lax.ppermute(chunk, 'rows', [(i, i ^ k) for i in range(groups)])  8.87 us
    pallas_call x2, Pallas kernels, whiten(): pl.pallas_call(functools.partial(whiten_kernel, tuple(steps), len(extra))...  6.3 us
    all_to_all x1, waiting for transfers between devices, sum_all(): lax.all_to_all(mine, 'grp', split_axis=0, concat_axis=0, tiled=True)  6.13 us
  transfers between devices with their start and end apart: 9, of which 6 were waited for; matrix products, arithmetic and copies ran while one was open for 1% of the time, Pallas kernels for 19%

profile of v2, /device:TPU:8, one launch (start us, length us, event | category | flops | bytes accessed | tf_op | source)
XLA Modules:
  0.0 158.8 jit_solution(11853019358173177196)
XLA Ops:
  0.6 0.7 reshape.37.ids_ref
  1.3 0.7 reshape.36.buckets_ref
  2.0 2.2 %copy-done = f32[2048,512]{1,0:T(8,128)S(1)} copy-done((f32[2048,512]{1,0:T(8,128)S(1)}, f32[2048,512]{1,0:T(8,128)}, u32[]{:S(2)}) %copy-start) | copy-done | bytes 4194328
  4.9 9.8 %shard_map.68 = (f32[256,512]{1,0:T(8,128)S(1)}, f32[256,512]{1,0:T(8,128)}, f32[256,512]{1,0:T(8,128)}, f32[256,512]{1,0:T(8,128)S(1)}, f32[256,512]{1,0:T(8,12...) custom-call(s32[1]{0:T(128)} %bitcast.me_ref, s32[8,256]{1,0:T(8,128)S(1)} %reshape.36.buckets_ref, ...), custom_call_target="tpu_custom_call" | custom-call | flops 1610612736 | bytes 8388608 | tf_op jit(solution)/shard_map/pallas_call | solution.py:141
  14.7 5.1 %shard_map.69 = (f32[1280,128]{1,0:T(8,128)S(1)}, f32[1280,128]{1,0:T(8,128)S(1)}) custom-call(f32[512,512]{1,0:T(8,128)S(1)} %copy-done.1, f32[256,512]{1,0:T(8,128)S(1)} %get-tuple-element.19.rest_0_, f32[256,512]{1,0:T(8,128)} %get-tuple-element.20.rest_1_, f32[256,512]{1,0:T(8,128)} %get-tuple-element.33.rest_2_, ...), custom_call_target="tpu_custom_call" | custom-call | flops 2147483648 | bytes 4194304 | tf_op jit(solution)/shard_map/pallas_call | solution.py:212
  19.8 0.8 copy-done.6
  20.7 12.8 %all_to_all.39 = f32[4,320,128]{2,1,0:T(8,128)S(1)} all-to-all(f32[4,320,128]{2,1,0:T(8,128)S(1)} %bitcast.9), channel_id=1, replica_groups=mesh['rows'=8,'grp'=4] {'grp'}, dimensions={0} | all-to-all | bytes 1310720 | tf_op jit(solution)/shard_map/all_to_all | solution.py:228
  33.5 11.5 %all_to_all.40 = f32[8,40,128]{2,1,0:T(8,128)S(1)} all-to-all(f32[8,40,128]{2,1,0:T(8,128)S(1)} %bitcast.12), channel_id=1, replica_groups=mesh['rows'=8,'grp'=4] {'rows'}, dimensions={0} | all-to-all | bytes 327680 | tf_op jit(solution)/shard_map/all_to_all | solution.py:232
  45.7 5.4 %all-to-all-start.2 = ((f32[8,40,128]{2,1,0:T(8,128)}), f32[8,40,128]{2,1,0:T(8,128)S(1)}, u32[]{:S(2)}, u32[]{:S(2)}) async-start(f32[8,40,128]{2,1,0:T(8,128)} %broadcast_in_dim.6), calls=%async_computation.2 | async-start | bytes 327680 | tf_op jit(solution)/shard_map/all_to_all | solution.py:236
  51.2 1.5 collective-permute-start.4
  53.2 4.8 %all-to-all-done.2 = f32[8,40,128]{2,1,0:T(8,128)S(1)} async-done(((f32[8,40,128]{2,1,0:T(8,128)}), f32[8,40,128]{2,1,0:T(8,128)S(1)}, u32[]{:S(2)}, u32[]{:S(2)}) %all-to-all-start.2) | async-done | bytes 163872 | tf_op jit(solution)/shard_map/all_to_all | solution.py:236
  58.0 0.9 broadcast_in_dim.7
  58.9 3.7 %all-to-all-start.3 = ((f32[4,320,128]{2,1,0:T(8,128)}), f32[4,320,128]{2,1,0:T(8,128)S(1)}, u32[]{:S(2)}, u32[]{:S(2)}) async-start(f32[4,320,128]{2,1,0:T(8,128)} %broadcast_in_dim.7), calls=%async_computation.3 | async-start | bytes 1310720 | tf_op jit(solution)/shard_map/all_to_all | solution.py:238
  63.2 3.3 %collective-permute-start.1 = (f32[256,512]{1,0:T(8,128)}, f32[256,512]{1,0:T(8,128)S(1)}, u32[]{:S(2)}, u32[]{:S(2)}) collective-permute-start(f32[256,512]{1,0:T(8,128)} %get-tuple-element.24.rest_5_), channel_id=1, source_target_pairs={{0,20},{4,16},{8,28},{12,24},{16,4},{20,0},{24,12},{28,8},{1,21},{... | collective-permute-start | bytes 1572872 | tf_op jit(solution)/shard_map/ppermute | solution.py:387
  66.5 6.1 %all-to-all-done.3 = f32[4,320,128]{2,1,0:T(8,128)S(1)} async-done(((f32[4,320,128]{2,1,0:T(8,128)}), f32[4,320,128]{2,1,0:T(8,128)S(1)}, u32[]{:S(2)}, u32[]{:S(2)}) %all-to-all-start.3) | async-done | bytes 655392 | tf_op jit(solution)/shard_map/all_to_all | solution.py:238
  73.1 2.4 %collective-permute-start.6 = (f32[256,512]{1,0:T(8,128)}, f32[256,512]{1,0:T(8,128)S(1)}, u32[]{:S(2)}, u32[]{:S(2)}) collective-permute-start(f32[256,512]{1,0:T(8,128)} %copy-done.4), channel_id=1, source_target_pairs={{0,12},{4,8},{8,4},{12,0},{16,28},{20,24},{24,20},{28,16},{1,13},{... | collective-permute-start | bytes 1572872 | tf_op jit(solution)/shard_map/ppermute | solution.py:387
  75.5 1.1 copy-done.7
  76.6 25.8 %shard_map.70 = (f32[512,512]{1,0:T(8,128)}, bf16[512,512]{1,0:T(8,128)(2,1)S(1)}, bf16[512,512]{1,0:T(8,128)(2,1)S(1)}) custom-call(f32[1280,128]{1,0:T(8,128)S(1)} %bitcast.8, f32[1280,128]{1,0:T(8,128)S(1)} %copy-done.7), custom_call_target="tpu_custom_call" | custom-call | flops 40000000000 | bytes 1048576 | tf_op jit(solution)/shard_map/pallas_call | solution.py:314
  102.4 19.4 %collective-permute-done.6.rest_3_ = f32[256,512]{1,0:T(8,128)S(1)} collective-permute-done((f32[256,512]{1,0:T(8,128)}, f32[256,512]{1,0:T(8,128)S(1)}, u32[]{:S(2)}, u32[]{:S(2)}) %collective-permute-start.6) | collective-permute-done | bytes 524320 | tf_op jit(solution)/shard_map/ppermute | solution.py:387
  121.8 3.7 %shard_map.71.rest_4_ = f32[2048,512]{1,0:T(8,128)} custom-call(s32[1]{0:T(128)} %bitcast.me_ref, bf16[512,512]{1,0:T(8,128)(2,1)S(1)} %get-tuple-element.31.high_ref, bf16[512,512]{1,0:T(8,128)(2,1)S(1)} %get-tuple-element.32.low_ref, f32[256,512]{1,0:T(8,128)S(1)} %get-tuple-element.19.rest_0_, f32[256,512]{1,0:T(8,128)S(1)} %collective-permute-done.4.rest_1_, ...), custom_call_target="tpu_custom_call" | custom-call | flops 1610612736 | bytes 4194304 | tf_op jit(solution)/shard_map/pallas_call | solution.py:359
  125.5 6.5 %collective-permute-done.1.rest_1_ = f32[256,512]{1,0:T(8,128)S(1)} collective-permute-done((f32[256,512]{1,0:T(8,128)}, f32[256,512]{1,0:T(8,128)S(1)}, u32[]{:S(2)}, u32[]{:S(2)}) %collective-permute-start.1) | collective-permute-done | bytes 524320 | tf_op jit(solution)/shard_map/ppermute | solution.py:387
  132.1 13.2 %collective-permute-done.2.rest_2_ = f32[256,512]{1,0:T(8,128)S(1)} collective-permute-done((f32[256,512]{1,0:T(8,128)}, f32[256,512]{1,0:T(8,128)S(1)}, u32[]{:S(2)}, u32[]{:S(2)}) %collective-permute-start.2) | collective-permute-done | bytes 524320 | tf_op jit(solution)/shard_map/ppermute | solution.py:387
  145.3 10.8 %collective-permute-done.3.rest_3_ = f32[256,512]{1,0:T(8,128)S(1)} collective-permute-done((f32[256,512]{1,0:T(8,128)}, f32[256,512]{1,0:T(8,128)S(1)}, u32[]{:S(2)}, u32[]{:S(2)}) %collective-permute-start.3) | collective-permute-done | bytes 524320 | tf_op jit(solution)/shard_map/ppermute | solution.py:387
  156.0 2.6 %shard_map.72 = f32[2048,512]{1,0:T(8,128)} custom-call(s32[1]{0:T(128)} %bitcast.me_ref, bf16[512,512]{1,0:T(8,128)(2,1)S(1)} %get-tuple-element.31.high_ref, bf16[512,512]{1,0:T(8,128)(2,1)S(1)} %get-tuple-element.32.low_ref, f32[256,512]{1,0:T(8,128)S(1)} %collective-permute-done.rest_0_, ...), custom_call_target="tpu_custom_call", output_to_operand_aliasing={{}: (7, {})} | custom-call | flops 1610612736 | bytes 4194304 | tf_op jit(solution)/shard_map/pallas_call | solution.py:359
  (23 shorter events, 3.1 us)
Async XLA Ops:
  2.0 2.2 %copy-start = (f32[2048,512]{1,0:T(8,128)S(1)}, f32[2048,512]{1,0:T(8,128)}, u32[]{:S(2)}) copy-start(f32[2048,512]{1,0:T(8,128)} %obs_ref.1) | copy-start | bytes 12582916
  4.2 0.7 copy-start.5
  4.9 9.8 %copy-start.1 = (f32[512,512]{1,0:T(8,128)S(1)}, f32[512,512]{1,0:T(8,128)}, u32[]{:S(2)}) copy-start(f32[512,512]{1,0:T(8,128)} %prior_ref.1) | copy-start | bytes 3145732
  14.7 5.2 %copy-start.2 = (f32[256,512]{1,0:T(8,128)}, f32[256,512]{1,0:T(8,128)S(1)}, u32[]{:S(2)}) copy-start(f32[256,512]{1,0:T(8,128)S(1)} %get-tuple-element.26.rest_7_) | copy-start | bytes 1572868
  14.7 6.0 %copy-start.3 = (f32[256,512]{1,0:T(8,128)}, f32[256,512]{1,0:T(8,128)S(1)}, u32[]{:S(2)}) copy-start(f32[256,512]{1,0:T(8,128)S(1)} %get-tuple-element.25.rest_6_) | copy-start | bytes 1572868
  14.7 6.0 %copy-start.4 = (f32[256,512]{1,0:T(8,128)}, f32[256,512]{1,0:T(8,128)S(1)}, u32[]{:S(2)}) copy-start(f32[256,512]{1,0:T(8,128)S(1)} %get-tuple-element.34.rest_3_) | copy-start | bytes 1572868
  19.8 0.8 copy-start.6
  45.7 12.3 %all-to-all-start.2 = ((f32[8,40,128]{2,1,0:T(8,128)}), f32[8,40,128]{2,1,0:T(8,128)S(1)}, u32[]{:S(2)}, u32[]{:S(2)}) async-start(f32[8,40,128]{2,1,0:T(8,128)} %broadcast_in_dim.6), calls=%async_computation.2 | async-start | bytes 327680 | tf_op jit(solution)/shard_map/all_to_all | solution.py:236
  51.2 21.4 %collective-permute-start.4 = (f32[256,512]{1,0:T(8,128)}, f32[256,512]{1,0:T(8,128)S(1)}, u32[]{:S(2)}, u32[]{:S(2)}) collective-permute-start(f32[256,512]{1,0:T(8,128)} %get-tuple-element.20.rest_1_), channel_id=1, source_target_pairs={{0,4},{4,0},{8,12},{12,8},{16,20},{20,16},{24,28},{28,24},{1,5},{5... | collective-permute-start | bytes 1572872 | tf_op jit(solution)/shard_map/ppermute | solution.py:387
  52.6 20.5 %collective-permute-start.5 = (f32[256,512]{1,0:T(8,128)}, f32[256,512]{1,0:T(8,128)}, u32[]{:S(2)}, u32[]{:S(2)}) collective-permute-start(f32[256,512]{1,0:T(8,128)} %get-tuple-element.33.rest_2_), channel_id=1, source_target_pairs={{0,8},{4,12},{8,0},{12,4},{16,24},{20,28},{24,16},{28,20},{1,9},{5... | collective-permute-start | bytes 1572872 | tf_op jit(solution)/shard_map/ppermute | solution.py:387
  58.9 13.7 %all-to-all-start.3 = ((f32[4,320,128]{2,1,0:T(8,128)}), f32[4,320,128]{2,1,0:T(8,128)S(1)}, u32[]{:S(2)}, u32[]{:S(2)}) async-start(f32[4,320,128]{2,1,0:T(8,128)} %broadcast_in_dim.7), calls=%async_computation.3 | async-start | bytes 1310720 | tf_op jit(solution)/shard_map/all_to_all | solution.py:238
  62.5 63.0 %collective-permute-start = (f32[256,512]{1,0:T(8,128)}, f32[256,512]{1,0:T(8,128)S(1)}, u32[]{:S(2)}, u32[]{:S(2)}) collective-permute-start(f32[256,512]{1,0:T(8,128)} %get-tuple-element.23.rest_4_), channel_id=1, source_target_pairs={{0,16},{4,20},{8,24},{12,28},{16,0},{20,4},{24,8},{28,12},{1,17},{... | collective-permute-start | bytes 1572872 | tf_op jit(solution)/shard_map/ppermute | solution.py:387
  63.2 68.9 %collective-permute-start.1 = (f32[256,512]{1,0:T(8,128)}, f32[256,512]{1,0:T(8,128)S(1)}, u32[]{:S(2)}, u32[]{:S(2)}) collective-permute-start(f32[256,512]{1,0:T(8,128)} %get-tuple-element.24.rest_5_), channel_id=1, source_target_pairs={{0,20},{4,16},{8,28},{12,24},{16,4},{20,0},{24,12},{28,8},{1,21},{... | collective-permute-start | bytes 1572872 | tf_op jit(solution)/shard_map/ppermute | solution.py:387
  66.5 78.8 %collective-permute-start.2 = (f32[256,512]{1,0:T(8,128)}, f32[256,512]{1,0:T(8,128)S(1)}, u32[]{:S(2)}, u32[]{:S(2)}) collective-permute-start(f32[256,512]{1,0:T(8,128)} %copy-done.3), channel_id=1, source_target_pairs={{0,24},{4,28},{8,16},{12,20},{16,8},{20,12},{24,0},{28,4},{1,25},{... | collective-permute-start | bytes 1572872 | tf_op jit(solution)/shard_map/ppermute | solution.py:387
  72.6 83.4 %collective-permute-start.3 = (f32[256,512]{1,0:T(8,128)}, f32[256,512]{1,0:T(8,128)S(1)}, u32[]{:S(2)}, u32[]{:S(2)}) collective-permute-start(f32[256,512]{1,0:T(8,128)} %copy-done.2), channel_id=1, source_target_pairs={{0,28},{4,24},{8,20},{12,16},{16,12},{20,8},{24,4},{28,0},{1,29},{... | collective-permute-start | bytes 1572872 | tf_op jit(solution)/shard_map/ppermute | solution.py:387
  73.1 48.7 %collective-permute-start.6 = (f32[256,512]{1,0:T(8,128)}, f32[256,512]{1,0:T(8,128)S(1)}, u32[]{:S(2)}, u32[]{:S(2)}) collective-permute-start(f32[256,512]{1,0:T(8,128)} %copy-done.4), channel_id=1, source_target_pairs={{0,12},{4,8},{8,4},{12,0},{16,28},{20,24},{24,20},{28,16},{1,13},{... | collective-permute-start | bytes 1572872 | tf_op jit(solution)/shard_map/ppermute | solution.py:387
  75.5 1.1 copy-start.7

commit v3 on v2

--- a/solution.py
+++ b/solution.py
@@ -45,25 +45,43 @@
     return dot_rows(lh, rh) + (dot_rows(lh, rl) + dot_rows(ll, rh))
 
 
-def regroup_kernel(groups, per_bucket, me_ref, buckets_ref, ids_ref, sigma_ref, obs_ref, *rest):
-    outs = rest[:groups]
-    place_ref, meta_ref, sorted_ref, inv_ref, meta_smem, sem = rest[groups:]
+def rows_of(packed, count, wide):
+    return [
+        jnp.concatenate([packed[s * wide + i : s * wide + i + 1, :] for i in range(wide)], axis=1)
+        for s in range(count)
+    ]
+
+
+def regroup_kernel(
+    groups,
+    per_bucket,
+    buckets_ref,
+    ids_ref,
+    sigma_ref,
+    obs_ref,
+    out,
+    place_ref,
+    meta_ref,
+    sorted_ref,
+    inv_ref,
+    meta_smem,
+    sem,
+):
     step = pl.program_id(0)
-    blocks, block = buckets_ref.shape
+    blocks, block = place_ref.shape
+    wide = block // LANES
     sensors = sigma_ref.shape[1]
     padded = sorted_ref.shape[0]
     cells = blocks * groups
 
     @pl.when(step == 0)
     def _():
-        me = me_ref[0]
         inv_row = 1.0 / sigma_ref[...]
         inv_ref[...] = jnp.transpose(jnp.broadcast_to(inv_row, (LANES, sensors)))
-        slots = buckets_ref[...] ^ me
+        slots = rows_of(buckets_ref[...], blocks, wide)
         hits = jnp.concatenate(
             [
-                jnp.broadcast_to(slots[s : s + 1, :], (groups, block)) == iota((groups, block), 0)
-                for s in range(blocks)
+                jnp.broadcast_to(row, (groups, block)) == iota((groups, block), 0) for row in slots
             ],
             axis=0,
         )
@@ -98,7 +116,8 @@
 
     place = place_ref[pl.ds(step, 1), :]
     moves = (iota((padded, block), 0) == place).astype(F32).astype(BF16)
-    known = iota((sensors, block), 0) == ids_ref[pl.ds(step, 1), :]
+    ids = [ids_ref[pl.ds(step * wide + i, 1), :] for i in range(wide)]
+    known = iota((sensors, block), 0) == jnp.concatenate(ids, axis=1)
     inv = jnp.concatenate([inv_ref[...]] * (block // LANES), axis=1)
     scale_row = jnp.sum(jnp.where(known, inv, 0.0), axis=0, keepdims=True)
     scale = jnp.transpose(jnp.broadcast_to(scale_row, (LANES, block)))
@@ -112,16 +131,15 @@
         before = meta_smem[cell, 0]
         source = meta_smem[cell, 1]
         tiles = meta_smem[cell, 2]
-        target = before >> 3
-        out = outs[v]
+        target = (before >> 3) + v * (per_bucket // SUB)
 
         @pl.when(tiles > 0)
-        def _(out=out, before=before, source=source, target=target):
+        def _(before=before, source=source, target=target):
             rows = pl.ds(pl.multiple_of(target * SUB, SUB), SUB)
             old = jnp.where((before & (SUB - 1)) > 0, out[rows, :], 0.0)
             out[rows, :] = old + sorted_ref[pl.ds(pl.multiple_of(source * SUB, SUB), SUB), :]
 
-        def body(t, carry, out=out, source=source, target=target):
+        def body(t, carry, source=source, target=target):
             out[pl.ds(pl.multiple_of((target + t) * SUB, SUB), SUB), :] = sorted_ref[
                 pl.ds(pl.multiple_of((source + t) * SUB, SUB), SUB), :
             ]
@@ -130,44 +148,40 @@
         lax.fori_loop(1, tiles, body, 0)
 
 
-def regroup(observations, sensor_ids, sensor_sigma, buckets, me, groups):
+def regroup(observations, sensor_ids, sensor_sigma, buckets, groups):
     rows, state = observations.shape
     sensors = sensor_sigma.shape[0]
     block = 256
     blocks = rows // block
     per_bucket = rows // groups
     padded = -(-(block + groups * 2 * (SUB - 1)) // LANES) * LANES
-    whole = lambda shape: pl.BlockSpec(shape, lambda s, me: (0, 0))
+    whole = lambda shape: pl.BlockSpec(shape, lambda s: (0, 0))
     return pl.pallas_call(
         functools.partial(regroup_kernel, groups, per_bucket),
-        grid_spec=pltpu.PrefetchScalarGridSpec(
-            num_scalar_prefetch=1,
-            grid=(blocks,),
-            in_specs=[
-                whole((blocks, block)),
-                whole((blocks, block)),
-                whole((1, sensors)),
-                pl.BlockSpec((block, state), lambda s, me: (s, 0)),
-            ],
-            out_specs=[whole((per_bucket, state))] * groups,
-            scratch_shapes=[
-                pltpu.VMEM((blocks, block), I32),
-                pltpu.VMEM((blocks * groups, LANES), I32),
-                pltpu.VMEM((padded, state), F32),
-                pltpu.VMEM((sensors, LANES), F32),
-                pltpu.SMEM((blocks * groups, LANES), I32),
-                pltpu.SemaphoreType.DMA,
-            ],
-        ),
-        out_shape=[jax.ShapeDtypeStruct((per_bucket, state), F32)] * groups,
+        grid=(blocks,),
+        in_specs=[
+            whole((rows // LANES, LANES)),
+            whole((rows // LANES, LANES)),
+            whole((1, sensors)),
+            pl.BlockSpec((block, state), lambda s: (s, 0)),
+        ],
+        out_specs=whole((rows, state)),
+        scratch_shapes=[
+            pltpu.VMEM((blocks, block), I32),
+            pltpu.VMEM((blocks * groups, LANES), I32),
+            pltpu.VMEM((padded, state), F32),
+            pltpu.VMEM((sensors, LANES), F32),
+            pltpu.SMEM((blocks * groups, LANES), I32),
+            pltpu.SemaphoreType.DMA,
+        ],
+        out_shape=jax.ShapeDtypeStruct((rows, state), F32),
         compiler_params=pltpu.CompilerParams(vmem_limit_bytes=24 * MIB),
         cost_estimate=pl.CostEstimate(
             flops=4 * rows * padded * state, bytes_accessed=8 * rows * state, transcendentals=0
         ),
     )(
-        me.reshape(1),
-        buckets.reshape(blocks, block),
-        sensor_ids.reshape(blocks, block),
+        buckets.reshape(rows // LANES, LANES),
+        sensor_ids.reshape(rows // LANES, LANES),
         sensor_sigma.reshape(1, sensors),
         observations,
     )
@@ -187,15 +201,11 @@
         )
 
 
-def gram_kernel(groups, prior_ref, *rest):
-    chunks = rest[:groups]
-    out_ref, prior_out_ref, both_ref, pair_ref = rest[groups:]
-    per_bucket, state = chunks[0].shape
-    for k, chunk in enumerate(chunks):
-        rows = slice(k * per_bucket, (k + 1) * per_bucket)
-        high, low = split(chunk[...])
-        pair_ref[rows, :state] = high
-        pair_ref[rows, state:] = low
+def gram_kernel(prior_ref, rows_ref, out_ref, prior_out_ref, both_ref, pair_ref):
+    state = rows_ref.shape[1]
+    high, low = split(rows_ref[...])
+    pair_ref[:, :state] = high
+    pair_ref[:, state:] = low
     both_ref[...] = dot_rows(pair_ref[:, :state], pair_ref[...])
     write_gram(both_ref, state, out_ref)
     high, low = split(prior_ref[...])
@@ -203,15 +213,13 @@
     write_gram(both_ref, state, prior_out_ref)
 
 
-def gram(prior_factor, chunks):
-    groups = len(chunks)
-    per_bucket, state = chunks[0].shape
-    rows = groups * per_bucket
+def gram(prior_factor, scaled):
+    rows, state = scaled.shape
     packed = len(block_pairs(state // LANES)) * LANES
     vmem = pl.BlockSpec(memory_space=pltpu.VMEM)
     return pl.pallas_call(
-        functools.partial(gram_kernel, groups),
-        in_specs=[vmem] * (groups + 1),
+        gram_kernel,
+        in_specs=[vmem] * 2,
         out_specs=[vmem] * 2,
         out_shape=[jax.ShapeDtypeStruct((packed, LANES), F32)] * 2,
         scratch_shapes=[pltpu.VMEM((state, 2 * state), F32), pltpu.VMEM((rows, 2 * state), BF16)],
@@ -219,10 +227,10 @@
         cost_estimate=pl.CostEstimate(
             flops=4 * rows * state * state, bytes_accessed=4 * rows * state, transcendentals=0
         ),
-    )(prior_factor, *chunks)
-
-
-def sum_all(packed, row_groups, grp, later):
+    )(prior_factor, scaled)
+
+
+def sum_all(packed, row_groups, grp):
     rows, lanes = packed.shape
     part = rows // grp
     got = lax.all_to_all(packed, "grp", split_axis=0, concat_axis=0, tiled=True)
@@ -230,14 +238,11 @@
     piece = -(-part // row_groups)
     mine = jnp.pad(mine, ((0, piece * row_groups - part), (0, 0)))
     got = lax.all_to_all(mine, "rows", split_axis=0, concat_axis=0, tiled=True)
-    got, early = lax.optimization_barrier((got, later[0]))
     mine = jnp.sum(got.reshape(row_groups, piece, lanes), axis=0)
     mine = jnp.broadcast_to(mine, (row_groups, piece, lanes)).reshape(row_groups * piece, lanes)
     mine = lax.all_to_all(mine, "rows", split_axis=0, concat_axis=0, tiled=True)[:part]
     mine = jnp.broadcast_to(mine, (grp, part, lanes)).reshape(rows, lanes)
-    summed = lax.all_to_all(mine, "grp", split_axis=0, concat_axis=0, tiled=True)
-    summed, late = lax.optimization_barrier((summed, later[1]))
-    return summed, (early, late)
+    return lax.all_to_all(mine, "grp", split_axis=0, concat_axis=0, tiled=True)
 
 
 def sweep(a, w):
@@ -328,76 +333,41 @@
     )(summed, prior_gram)
 
 
-def whiten_kernel(steps, aliased, me_ref, high_ref, low_ref, *rest):
-    count = len(steps)
-    chunks = rest[:count]
-    out_ref, held, sems = rest[count + aliased :]
-    per_bucket = chunks[0].shape[0]
+def whiten_kernel(high_ref, low_ref, rows_ref, out_ref):
+    rows_high, rows_low = split(rows_ref[...])
     high, low = high_ref[...], low_ref[...]
-    copies = []
-    for n, k in enumerate(steps):
-        rows_high, rows_low = split(chunks[n][...])
-        held[n] = dot(rows_high, high) + (dot(rows_high, low) + dot(rows_low, high))
-        slot = me_ref[0] ^ k
-        copy = pltpu.make_async_copy(
-            held.at[n],
-            out_ref.at[pl.ds(pl.multiple_of(slot * per_bucket, per_bucket), per_bucket), :],
-            sems.at[n],
-        )
-        copy.start()
-        copies.append(copy)
-    for copy in copies:
-        copy.wait()
-
-
-def whiten(me, high, low, steps, chunks, out, rows):
-    per_bucket, state = chunks[0].shape
-    count = len(chunks)
-    vmem = pl.BlockSpec(memory_space=pltpu.VMEM)
-    anywhere = pl.BlockSpec(memory_space=pl.ANY)
-    extra = [] if out is None else [out]
+    out_ref[...] = dot(rows_high, high) + (dot(rows_high, low) + dot(rows_low, high))
+
+
+def whiten(high, low, received):
+    rows, state = received.shape
+    block = 256
+    whole = pl.BlockSpec((state, state), lambda s: (0, 0))
+    part = pl.BlockSpec((block, state), lambda s: (s, 0))
     return pl.pallas_call(
-        functools.partial(whiten_kernel, tuple(steps), len(extra)),
-        in_specs=[pl.BlockSpec(memory_space=pltpu.SMEM)]
-        + [vmem] * (2 + count)
-        + [anywhere] * len(extra),
-        out_specs=anywhere,
+        whiten_kernel,
+        grid=(rows // block,),
+        in_specs=[whole, whole, part],
+        out_specs=part,
         out_shape=jax.ShapeDtypeStruct((rows, state), F32),
-        scratch_shapes=[
-            pltpu.VMEM((count, per_bucket, state), F32),
-            pltpu.SemaphoreType.DMA((count,)),
-        ],
-        input_output_aliases={3 + count: 0} if extra else {},
         compiler_params=pltpu.CompilerParams(vmem_limit_bytes=16 * MIB),
         cost_estimate=pl.CostEstimate(
-            flops=6 * count * per_bucket * state * state,
-            bytes_accessed=8 * count * per_bucket * state,
-            transcendentals=0,
+            flops=6 * rows * state * state, bytes_accessed=8 * rows * state, transcendentals=0
         ),
-    )(me.reshape(1), high, low, *chunks, *extra)
+    )(high, low, received)
 
 
 def shards(observations, sensor_ids, sensor_sigma, buckets, prior_factor):
     rows_dev, state = observations.shape
     groups = lax.axis_size("rows")
     grp = lax.axis_size("grp")
-    me = lax.axis_index("rows").astype(I32)
     total_rows = rows_dev * groups * grp
-    chunks = regroup(observations, sensor_ids, sensor_sigma, buckets, me, groups)
-    move = lambda k, chunk: lax.ppermute(chunk, "rows", [(i, i ^ k) for i in range(groups)])
-    held_back = [k for k in (2, 3) if k < groups]
-    received = [chunks[0]] + [None] * (groups - 1)
-    for k in reversed(range(1, groups)):
-        if k not in held_back:
-            received[k] = move(k, chunks[k])
-    packed, prior_gram = gram(prior_factor, chunks)
-    summed, later = sum_all(packed, groups, grp, [chunks[k] for k in held_back])
-    for k, chunk in zip(held_back, later):
-        received[k] = move(k, chunk)
+    scaled = regroup(observations, sensor_ids, sensor_sigma, buckets, groups)
+    received = lax.all_to_all(scaled, "rows", split_axis=0, concat_axis=0, tiled=True)
+    packed, prior_gram = gram(prior_factor, scaled)
+    summed = sum_all(packed, groups, grp)
     factor, high, low = factorise(summed, prior_gram, state, total_rows)
-    out = whiten(me, high, low, range(groups // 2), received[: groups // 2], None, rows_dev)
-    out = whiten(me, high, low, range(groups // 2, groups), received[groups // 2 :], out, rows_dev)
-    return (out, factor)
+    return (whiten(high, low, received), factor)
 
 
 def solution(mesh):

time: 160 us -> 176 us (1.10)
  the two profiles are of different devices: /device:TPU:8 before, /device:TPU:0 now
where the time goes in v3:
time: 176 us; the launch traced here: 175 us
  waiting for transfers between devices  67.1 us (38%)
  blocking collectives  50.1 us (28%)
  Pallas kernels  45.9 us (26%)
  local copies, waits for them, and re-layouts  6.3 us (4%)
  starting transfers between devices  4.74 us (3%)
    all_to_all x1, waiting for transfers between devices, shards(): lax.all_to_all(scaled, 'rows', split_axis=0, concat_axis=0, tiled=True)  67.1 us
    pallas_call x1, Pallas kernels, factorise(): pl.pallas_call(functools.partial(factor_kernel, 1.0 / total_rows), in_spe...  25.8 us
    all_to_all x1, blocking collectives, sum_all(): got = lax.all_to_all(packed, 'grp', split_axis=0, concat_axis=0, tiled=True)  14.3 us
    all_to_all x1, blocking collectives, sum_all(): got = lax.all_to_all(mine, 'rows', split_axis=0, concat_axis=0, tiled=True)  13.1 us
    all_to_all x1, blocking collectives, sum_all(): return lax.all_to_all(mine, 'grp', split_axis=0, concat_axis=0, tiled=True)  12.7 us
    all_to_all x1, blocking collectives, sum_all(): lax.all_to_all(mine, 'rows', split_axis=0, concat_axis=0, tiled=True)[:part]  9.96 us
    pallas_call x1, Pallas kernels, whiten(): pl.pallas_call(whiten_kernel, grid=(rows // block,), in_specs=[whole, who...  8.61 us
    pallas_call x1, Pallas kernels, regroup(): pl.pallas_call(functools.partial(regroup_kernel, groups, per_bucket), gri...  8.34 us
  transfers between devices with their start and end apart: 1, of which 1 were waited for; matrix products, arithmetic and copies ran while one was open for 0% of the time, Pallas kernels for 15%

profile of v3, /device:TPU:0, one launch (start us, length us, event | category | flops | bytes accessed | tf_op | source)
XLA Modules:
  0.0 174.9 jit_solution(5262830273659551215)
XLA Ops:
  0.6 0.0 copy-start.1
  0.6 2.2 %copy-done.1 = f32[2048,512]{1,0:T(8,128)S(1)} copy-done((f32[2048,512]{1,0:T(8,128)S(1)}, f32[2048,512]{1,0:T(8,128)}, u32[]{:S(2)}) %copy-start.1) | copy-done | bytes 4194328
  2.8 0.0 copy-start.2
  2.8 0.7 copy-done.2
  3.5 0.0 copy-start.3
  3.5 0.7 copy-done.3
  4.2 0.0 copy-start.4
  4.2 0.7 copy-done.4
  4.9 0.0 copy-start.5
  4.9 8.3 %shard_map.68.rows_ref = f32[2048,512]{1,0:T(8,128)S(1)} custom-call(s32[16,128]{1,0:T(8,128)S(1)} %bitcast.12, s32[16,128]{1,0:T(8,128)S(1)} %bitcast.13, f32[1,128]{1,0:T(1,128)S(1)} %bitcast.14, f32[2048,512]{1,0:T(8,128)S(1)} %copy-done.1), custom_call_target="tpu_custom_call" | custom-call | flops 1610612736 | bytes 8388608 | tf_op jit(solution)/shard_map/pallas_call | solution.py:159
  13.2 0.0 copy-done.5
  13.2 3.1 %shard_map.69 = (f32[1280,128]{1,0:T(8,128)S(1)}, f32[1280,128]{1,0:T(8,128)S(1)}) custom-call(f32[512,512]{1,0:T(8,128)S(1)} %copy-done.5, f32[2048,512]{1,0:T(8,128)S(1)} %shard_map.68.rows_ref), custom_call_target="tpu_custom_call" | custom-call | flops 2147483648 | bytes 4194304 | tf_op jit(solution)/shard_map/pallas_call | solution.py:220
  16.4 0.0 copy-start
  16.4 2.0 %copy-done = f32[2048,512]{1,0:T(8,128)} copy-done((f32[2048,512]{1,0:T(8,128)}, f32[2048,512]{1,0:T(8,128)S(1)}, u32[]{:S(2)}) %copy-start) | copy-done | bytes 4194328
  18.4 14.3 %all_to_all.46 = f32[4,320,128]{2,1,0:T(8,128)S(1)} all-to-all(f32[4,320,128]{2,1,0:T(8,128)S(1)} %bitcast.11), channel_id=1, replica_groups=mesh['rows'=8,'grp'=4] {'grp'}, dimensions={0} | all-to-all | bytes 1310720 | tf_op jit(solution)/shard_map/all_to_all | solution.py:236
  32.8 13.1 %all_to_all.47 = f32[8,40,128]{2,1,0:T(8,128)S(1)} all-to-all(f32[8,40,128]{2,1,0:T(8,128)S(1)} %bitcast.15), channel_id=1, replica_groups=mesh['rows'=8,'grp'=4] {'rows'}, dimensions={0} | all-to-all | bytes 327680 | tf_op jit(solution)/shard_map/all_to_all | solution.py:240
  45.9 10.0 %all_to_all.48 = f32[8,40,128]{2,1,0:T(8,128)S(1)} all-to-all(f32[8,40,128]{2,1,0:T(8,128)S(1)} %broadcast_in_dim.6), channel_id=1, replica_groups=mesh['rows'=8,'grp'=4] {'rows'}, dimensions={0} | all-to-all | bytes 327680 | tf_op jit(solution)/shard_map/all_to_all | solution.py:243
  55.9 12.7 %all_to_all.49 = f32[4,320,128]{2,1,0:T(8,128)S(1)} all-to-all(f32[4,320,128]{2,1,0:T(8,128)S(1)} %broadcast_in_dim.7), channel_id=1, replica_groups=mesh['rows'=8,'grp'=4] {'grp'}, dimensions={0} | all-to-all | bytes 1310720 | tf_op jit(solution)/shard_map/all_to_all | solution.py:245
  68.6 4.7 %all-to-all-start.4 = ((f32[8,256,512]{2,1,0:T(8,128)}), f32[8,256,512]{2,1,0:T(8,128)}, u32[]{:S(2)}, u32[]{:S(2)}) async-start(f32[8,256,512]{2,1,0:T(8,128)} %bitcast.9), calls=%async_computation.4 | async-start | bytes 8388608 | tf_op jit(solution)/shard_map/all_to_all | solution.py:366
  73.3 25.8 %shard_map.70 = (f32[512,512]{1,0:T(8,128)}, bf16[512,512]{1,0:T(8,128)(2,1)S(1)}, bf16[512,512]{1,0:T(8,128)(2,1)S(1)}) custom-call(f32[1280,128]{1,0:T(8,128)S(1)} %bitcast.10, f32[1280,128]{1,0:T(8,128)S(1)} %get-tuple-element.8.prior_ref), custom_call_target="tpu_custom_call" | custom-call | flops 40000000000 | bytes 1048576 | tf_op jit(solution)/shard_map/pallas_call | solution.py:319
  99.1 67.1 %all-to-all-done.4 = f32[8,256,512]{2,1,0:T(8,128)} async-done(((f32[8,256,512]{2,1,0:T(8,128)}), f32[8,256,512]{2,1,0:T(8,128)}, u32[]{:S(2)}, u32[]{:S(2)}) %all-to-all-start.4) | async-done | bytes 4194336 | tf_op jit(solution)/shard_map/all_to_all | solution.py:366
  166.2 8.6 %shard_map.71 = f32[2048,512]{1,0:T(8,128)} custom-call(bf16[512,512]{1,0:T(8,128)(2,1)S(1)} %get-tuple-element.9.high_ref, bf16[512,512]{1,0:T(8,128)(2,1)S(1)} %get-tuple-element.10.low_ref, f32[2048,512]{1,0:T(8,128)} %bitcast.8.rows_ref), custom_call_target="tpu_custom_call" | custom-call | flops 3221225472 | bytes 8388608 | tf_op jit(solution)/shard_map/pallas_call | solution.py:347
  (4 shorter events, 0.1 us)
Async XLA Ops:
  0.6 2.2 %copy-start.1 = (f32[2048,512]{1,0:T(8,128)S(1)}, f32[2048,512]{1,0:T(8,128)}, u32[]{:S(2)}) copy-start(f32[2048,512]{1,0:T(8,128)} %obs_ref.1) | copy-start | bytes 12582916
  2.8 0.7 copy-start.2
  3.5 0.7 copy-start.3
  4.2 0.7 copy-start.4
  4.9 8.3 %copy-start.5 = (f32[512,512]{1,0:T(8,128)S(1)}, f32[512,512]{1,0:T(8,128)}, u32[]{:S(2)}) copy-start(f32[512,512]{1,0:T(8,128)} %prior_ref.1) | copy-start | bytes 3145732
  16.4 2.0 %copy-start = (f32[2048,512]{1,0:T(8,128)}, f32[2048,512]{1,0:T(8,128)S(1)}, u32[]{:S(2)}) copy-start(f32[2048,512]{1,0:T(8,128)S(1)} %shard_map.68.rows_ref) | copy-start | bytes 12582916
  68.6 97.7 %all-to-all-start.4 = ((f32[8,256,512]{2,1,0:T(8,128)}), f32[8,256,512]{2,1,0:T(8,128)}, u32[]{:S(2)}, u32[]{:S(2)}) async-start(f32[8,256,512]{2,1,0:T(8,128)} %bitcast.9), calls=%async_computation.4 | async-start | bytes 8388608 | tf_op jit(solution)/shard_map/all_to_all | solution.py:366

commit v4 on v2

--- a/solution.py
+++ b/solution.py
@@ -45,11 +45,19 @@
     return dot_rows(lh, rh) + (dot_rows(lh, rl) + dot_rows(ll, rh))
 
 
+def rows_of(packed, count, wide):
+    return [
+        jnp.concatenate([packed[s * wide + i : s * wide + i + 1, :] for i in range(wide)], axis=1)
+        for s in range(count)
+    ]
+
+
 def regroup_kernel(groups, per_bucket, me_ref, buckets_ref, ids_ref, sigma_ref, obs_ref, *rest):
     outs = rest[:groups]
     place_ref, meta_ref, sorted_ref, inv_ref, meta_smem, sem = rest[groups:]
     step = pl.program_id(0)
-    blocks, block = buckets_ref.shape
+    blocks, block = place_ref.shape
+    wide = block // LANES
     sensors = sigma_ref.shape[1]
     padded = sorted_ref.shape[0]
     cells = blocks * groups
@@ -59,11 +67,10 @@
         me = me_ref[0]
         inv_row = 1.0 / sigma_ref[...]
         inv_ref[...] = jnp.transpose(jnp.broadcast_to(inv_row, (LANES, sensors)))
-        slots = buckets_ref[...] ^ me
+        slots = rows_of(buckets_ref[...] ^ me, blocks, wide)
         hits = jnp.concatenate(
             [
-                jnp.broadcast_to(slots[s : s + 1, :], (groups, block)) == iota((groups, block), 0)
-                for s in range(blocks)
+                jnp.broadcast_to(row, (groups, block)) == iota((groups, block), 0) for row in slots
             ],
             axis=0,
         )
@@ -98,7 +105,8 @@
 
     place = place_ref[pl.ds(step, 1), :]
     moves = (iota((padded, block), 0) == place).astype(F32).astype(BF16)
-    known = iota((sensors, block), 0) == ids_ref[pl.ds(step, 1), :]
+    ids = [ids_ref[pl.ds(step * wide + i, 1), :] for i in range(wide)]
+    known = iota((sensors, block), 0) == jnp.concatenate(ids, axis=1)
     inv = jnp.concatenate([inv_ref[...]] * (block // LANES), axis=1)
     scale_row = jnp.sum(jnp.where(known, inv, 0.0), axis=0, keepdims=True)
     scale = jnp.transpose(jnp.broadcast_to(scale_row, (LANES, block)))
@@ -144,8 +152,8 @@
             num_scalar_prefetch=1,
             grid=(blocks,),
             in_specs=[
-                whole((blocks, block)),
-                whole((blocks, block)),
+                whole((rows // LANES, LANES)),
+                whole((rows // LANES, LANES)),
                 whole((1, sensors)),
                 pl.BlockSpec((block, state), lambda s, me: (s, 0)),
             ],
@@ -166,8 +174,8 @@
         ),
     )(
         me.reshape(1),
-        buckets.reshape(blocks, block),
-        sensor_ids.reshape(blocks, block),
+        buckets.reshape(rows // LANES, LANES),
+        sensor_ids.reshape(rows // LANES, LANES),
         sensor_sigma.reshape(1, sensors),
         observations,
     )
@@ -222,7 +230,7 @@
     )(prior_factor, *chunks)
 
 
-def sum_all(packed, row_groups, grp, later):
+def scatter_sum(packed, row_groups, grp):
     rows, lanes = packed.shape
     part = rows // grp
     got = lax.all_to_all(packed, "grp", split_axis=0, concat_axis=0, tiled=True)
@@ -230,14 +238,16 @@
     piece = -(-part // row_groups)
     mine = jnp.pad(mine, ((0, piece * row_groups - part), (0, 0)))
     got = lax.all_to_all(mine, "rows", split_axis=0, concat_axis=0, tiled=True)
-    got, early = lax.optimization_barrier((got, later[0]))
-    mine = jnp.sum(got.reshape(row_groups, piece, lanes), axis=0)
-    mine = jnp.broadcast_to(mine, (row_groups, piece, lanes)).reshape(row_groups * piece, lanes)
+    return jnp.sum(got.reshape(row_groups, piece, lanes), axis=0)
+
+
+def gather_pieces(piece, rows, row_groups, grp):
+    size, lanes = piece.shape
+    part = rows // grp
+    mine = jnp.broadcast_to(piece, (row_groups, size, lanes)).reshape(row_groups * size, lanes)
     mine = lax.all_to_all(mine, "rows", split_axis=0, concat_axis=0, tiled=True)[:part]
     mine = jnp.broadcast_to(mine, (grp, part, lanes)).reshape(rows, lanes)
-    summed = lax.all_to_all(mine, "grp", split_axis=0, concat_axis=0, tiled=True)
-    summed, late = lax.optimization_barrier((summed, later[1]))
-    return summed, (early, late)
+    return lax.all_to_all(mine, "grp", split_axis=0, concat_axis=0, tiled=True)
 
 
 def sweep(a, w):
@@ -370,9 +380,7 @@
         input_output_aliases={3 + count: 0} if extra else {},
         compiler_params=pltpu.CompilerParams(vmem_limit_bytes=16 * MIB),
         cost_estimate=pl.CostEstimate(
-            flops=6 * count * per_bucket * state * state,
-            bytes_accessed=8 * count * per_bucket * state,
-            transcendentals=0,
+            flops=1, bytes_accessed=1, transcendentals=0
         ),
     )(me.reshape(1), high, low, *chunks, *extra)
 
@@ -385,16 +393,35 @@
     total_rows = rows_dev * groups * grp
     chunks = regroup(observations, sensor_ids, sensor_sigma, buckets, me, groups)
     move = lambda k, chunk: lax.ppermute(chunk, "rows", [(i, i ^ k) for i in range(groups)])
-    held_back = [k for k in (2, 3) if k < groups]
+    short = [k for k in (1, 2, 3) if k < groups]
     received = [chunks[0]] + [None] * (groups - 1)
     for k in reversed(range(1, groups)):
-        if k not in held_back:
+        if k not in short:
             received[k] = move(k, chunks[k])
-    packed, prior_gram = gram(prior_factor, chunks)
-    summed, later = sum_all(packed, groups, grp, [chunks[k] for k in held_back])
-    for k, chunk in zip(held_back, later):
-        received[k] = move(k, chunk)
-    factor, high, low = factorise(summed, prior_gram, state, total_rows)
+    packed_rows = len(block_pairs(state // LANES)) * LANES
+
+    def inside():
+        moved = [move(k, chunks[k]) for k in short[:1]]
+
+        def move_next(value):
+            if len(moved) < len(short):
+                chunk = chunks[short[len(moved)]]
+                value, moved[-1], chunk = lax.optimization_barrier((value, moved[-1], chunk))
+                moved.append(move(short[len(moved)], chunk))
+            return value
+
+        packed, prior_gram = gram(prior_factor, chunks)
+        piece = move_next(scatter_sum(packed, groups, grp))
+        summed = move_next(gather_pieces(piece, packed_rows, groups, grp))
+        return moved, list(factorise(summed, prior_gram, state, total_rows))
+
+    def invalid():
+        wrong = jnp.full((state, state), jnp.nan, F32)
+        return [chunks[k] for k in short], [wrong, wrong.astype(BF16), wrong.astype(BF16)]
+
+    moved, (factor, high, low) = lax.cond(prior_factor[0, 0] > 0, inside, invalid)
+    for k, chunk in zip(short, moved):
+        received[k] = chunk
     out = whiten(me, high, low, range(groups // 2), received[: groups // 2], None, rows_dev)
     out = whiten(me, high, low, range(groups // 2, groups), received[groups // 2 :], out, rows_dev)
     return (out, factor)

time: 160 us -> 180 us (1.12)
  the two profiles are of different devices: /device:TPU:8 before, /device:TPU:0 now
where the time goes in v4:
time: 180 us; the launch traced here: 179 us
  blocking collectives  68.4 us (38%)
  Pallas kernels  48.9 us (27%)
  starting transfers between devices  26.2 us (15%)
  waiting for transfers between devices  23.3 us (13%)
  local copies, waits for them, and re-layouts  10 us (6%)
    all_to_all x1, blocking collectives, scatter_sum(): got = lax.all_to_all(mine, 'rows', split_axis=0, concat_axis=0, tiled=True)  68.4 us
    pallas_call x1, Pallas kernels, factorise(): pl.pallas_call(functools.partial(factor_kernel, 1.0 / total_rows), in_spe...  26.1 us
    ppermute x7, starting transfers between devices, shards(): lax.ppermute(chunk, 'rows', [(i, i ^ k) for i in range(groups)])  13.7 us
    pallas_call x1, Pallas kernels, regroup(): pl.pallas_call(functools.partial(regroup_kernel, groups, per_bucket), gri...  9.96 us
    all_to_all x1, waiting for transfers between devices, scatter_sum(): got = lax.all_to_all(packed, 'grp', split_axis=0, concat_axis=0, tiled=True)  8.48 us
    pallas_call x2, Pallas kernels, whiten(): pl.pallas_call(functools.partial(whiten_kernel, tuple(steps), len(extra))...  7.82 us
    all_to_all x1, waiting for transfers between devices, gather_pieces(): return lax.all_to_all(mine, 'grp', split_axis=0, concat_axis=0, tiled=True)  6.77 us
    all_to_all x1, waiting for transfers between devices, gather_pieces(): lax.all_to_all(mine, 'rows', split_axis=0, concat_axis=0, tiled=True)[:part]  6.67 us
  transfers between devices with their start and end apart: 10, of which 4 were waited for; matrix products, arithmetic and copies ran while one was open for 3% of the time, Pallas kernels for 20%

profile of v4, /device:TPU:0, one launch (start us, length us, event | category | flops | bytes accessed | tf_op | source)
XLA Modules:
  0.0 179.5 jit_solution(12766671627296430097)
XLA Ops:
  0.6 2.2 %copy-done = f32[2048,512]{1,0:T(8,128)S(1)} copy-done((f32[2048,512]{1,0:T(8,128)S(1)}, f32[2048,512]{1,0:T(8,128)}, u32[]{:S(2)}) %copy-start) | copy-done | bytes 4194328
  4.9 10.0 %shard_map.68 = (f32[256,512]{1,0:T(8,128)}, f32[256,512]{1,0:T(8,128)S(1)}, f32[256,512]{1,0:T(8,128)S(1)}, f32[256,512]{1,0:T(8,128)S(1)}, f32[256,512]{1,0:T(...) custom-call(s32[1]{0:T(128)} %bitcast.4.me_ref, s32[16,128]{1,0:T(8,128)S(1)} %bitcast.10, ...), custom_call_target="tpu_custom_call" | custom-call | flops 1610612736 | bytes 8388608 | tf_op jit(solution)/shard_map/pallas_call | solution.py:149
  14.8 4.0 %collective-permute-start.3 = (f32[256,512]{1,0:T(8,128)}, f32[256,512]{1,0:T(8,128)S(1)}, u32[]{:S(2)}, u32[]{:S(2)}) collective-permute-start(f32[256,512]{1,0:T(8,128)} %get-tuple-element.67), channel_id=1, source_target_pairs={{0,16},{4,20},{8,24},{12,28},{16,0},{20,4},{24,8},{28,12},{1,17},{... | collective-permute-start | bytes 1572872 | tf_op jit(solution)/shard_map/ppermute | solution.py:395
  18.9 1.3 collective-permute-start.4
  20.2 3.6 %collective-permute-start.5 = (f32[256,512]{1,0:T(8,128)}, f32[256,512]{1,0:T(8,128)S(1)}, u32[]{:S(2)}, u32[]{:S(2)}) collective-permute-start(f32[256,512]{1,0:T(8,128)} %get-tuple-element.69), channel_id=1, source_target_pairs={{0,24},{4,28},{8,16},{12,20},{16,8},{20,12},{24,0},{28,4},{1,25},{... | collective-permute-start | bytes 1572872 | tf_op jit(solution)/shard_map/ppermute | solution.py:395
  25.0 146.5 %conditional.1 = (f32[256,512]{1,0:T(8,128)S(1)}, f32[256,512]{1,0:T(8,128)S(1)}, f32[256,512]{1,0:T(8,128)S(1)}, f32[512,512]{1,0:T(8,128)}, bf16[512,512]{1,0:T(8,128)(2,1)}, /*index=5*/bf16[512,512]{1,0:T(8,128)(2,1)}) conditional(s32[]{:T(128)} %bitcast.5, (f32[256,512]{1,0:T(8,128)S(1)}, f32[256,512]{1,0:T(8,128)S(1)}, ...), branch_computations={%region_0.0_spmd, %region_1.4_spmd} | conditional | flops 42147643392 | bytes 29827456 | solution.py:422
  25.8 5.0 %branch_1_fun.2 = (f32[1280,128]{1,0:T(8,128)}, f32[1280,128]{1,0:T(8,128)S(1)}) custom-call(f32[512,512]{1,0:T(8,128)S(1)} %get-tuple-element.27.prior_ref, f32[256,512]{1,0:T(8,128)} %get-tuple-element.28.rest_0_, f32[256,512]{1,0:T(8,128)S(1)} %get-tuple-element.29.rest_1_, f32[256,512]{1,0:T(8,128)S(1)} %get-tuple-element.39.rest_2_, ...), custom_call_target="tpu_custom_call" | custom-call | flops 2147483648 | bytes 4194304 | tf_op jit(solution)/shard_map/cond/branch_1_fun/pallas_call | solution.py:220
  30.8 3.5 %all-to-all-start = ((f32[4,320,128]{2,1,0:T(8,128)}), f32[4,320,128]{2,1,0:T(8,128)S(1)}, u32[]{:S(2)}, u32[]{:S(2)}) async-start(f32[4,320,128]{2,1,0:T(8,128)} %bitcast), calls=%async_computation | async-start | bytes 1310720 | tf_op jit(solution)/shard_map/cond/branch_1_fun/all_to_all | solution.py:236
  34.3 1.7 collective-permute-start
  36.1 8.5 %all-to-all-done = f32[4,320,128]{2,1,0:T(8,128)S(1)} async-done(((f32[4,320,128]{2,1,0:T(8,128)}), f32[4,320,128]{2,1,0:T(8,128)S(1)}, u32[]{:S(2)}, u32[]{:S(2)}) %all-to-all-start) | async-done | bytes 655392 | tf_op jit(solution)/shard_map/cond/branch_1_fun/all_to_all | solution.py:236
  45.2 68.4 %all_to_all.28 = f32[8,40,128]{2,1,0:T(8,128)S(1)} all-to-all(f32[8,40,128]{2,1,0:T(8,128)} %bitcast.14), channel_id=1, replica_groups=mesh['rows'=8,'grp'=4] {'rows'}, dimensions={0} | all-to-all | bytes 327680 | tf_op jit(solution)/shard_map/cond/branch_1_fun/all_to_all | solution.py:240
  114.3 5.4 %all-to-all-start.2 = ((f32[8,40,128]{2,1,0:T(8,128)}), f32[8,40,128]{2,1,0:T(8,128)S(1)}, u32[]{:S(2)}, u32[]{:S(2)}) async-start(f32[8,40,128]{2,1,0:T(8,128)} %broadcast_in_dim.4), calls=%async_computation.2 | async-start | bytes 327680 | tf_op jit(solution)/shard_map/cond/branch_1_fun/all_to_all | solution.py:248
  119.7 2.0 %collective-permute-start.1 = (f32[256,512]{1,0:T(8,128)}, f32[256,512]{1,0:T(8,128)}, u32[]{:S(2)}, u32[]{:S(2)}) collective-permute-start(f32[256,512]{1,0:T(8,128)} %copy-done.5), channel_id=1, source_target_pairs={{0,8},{4,12},{8,0},{12,4},{16,24},{20,28},{24,16},{28,20},{1,9},{5... | collective-permute-start | bytes 1572872 | tf_op jit(solution)/shard_map/cond/branch_1_fun/ppermute | solution.py:395
  121.7 6.7 %all-to-all-done.2 = f32[8,40,128]{2,1,0:T(8,128)S(1)} async-done(((f32[8,40,128]{2,1,0:T(8,128)}), f32[8,40,128]{2,1,0:T(8,128)S(1)}, u32[]{:S(2)}, u32[]{:S(2)}) %all-to-all-start.2) | async-done | bytes 163872 | tf_op jit(solution)/shard_map/cond/branch_1_fun/all_to_all | solution.py:248
  128.4 0.9 broadcast_in_dim.5
  129.3 3.7 %all-to-all-start.3 = ((f32[4,320,128]{2,1,0:T(8,128)}), f32[4,320,128]{2,1,0:T(8,128)S(1)}, u32[]{:S(2)}, u32[]{:S(2)}) async-start(f32[4,320,128]{2,1,0:T(8,128)} %broadcast_in_dim.5), calls=%async_computation.3 | async-start | bytes 1310720 | tf_op jit(solution)/shard_map/cond/branch_1_fun/all_to_all | solution.py:250
  133.0 1.9 %copy.14 = f32[256,512]{1,0:T(8,128)} copy(f32[256,512]{1,0:T(8,128)} %collective-permute-done) | data formatting | bytes 1048576 | tf_op jit(solution)/shard_map/cond
  134.8 1.4 collective-permute-done.1
  136.2 6.8 %all-to-all-done.3 = f32[4,320,128]{2,1,0:T(8,128)S(1)} async-done(((f32[4,320,128]{2,1,0:T(8,128)}), f32[4,320,128]{2,1,0:T(8,128)S(1)}, u32[]{:S(2)}, u32[]{:S(2)}) %all-to-all-start.3) | async-done | bytes 655392 | tf_op jit(solution)/shard_map/cond/branch_1_fun/all_to_all | solution.py:250
  143.0 1.0 collective-permute-start.2
  144.0 26.1 %branch_1_fun.3 = (f32[512,512]{1,0:T(8,128)}, bf16[512,512]{1,0:T(8,128)(2,1)}, bf16[512,512]{1,0:T(8,128)(2,1)}) custom-call(f32[1280,128]{1,0:T(8,128)S(1)} %bitcast.9, f32[1280,128]{1,0:T(8,128)S(1)} %get-tuple-element.43.prior_ref), custom_call_target="tpu_custom_call" | custom-call | flops 40000000000 | bytes 1048576 | tf_op jit(solution)/shard_map/cond/branch_1_fun/pallas_call | solution.py:324
  170.1 1.0 copy.15
  171.4 4.0 %shard_map.69.rest_4_ = f32[2048,512]{1,0:T(8,128)} custom-call(s32[1]{0:T(128)} %bitcast.4.me_ref, bf16[512,512]{1,0:T(8,128)(2,1)} %get-tuple-element.71.high_ref, bf16[512,512]{1,0:T(8,128)(2,1)} %get-tuple-element.72.low_ref, f32[256,512]{1,0:T(8,128)} %get-tuple-element.66.rest_0_, f32[256,512]{1,0:T(8,128)S(1)} %get-tuple-element.73.rest_1_, ...), custom_call_target="tpu_custom_call" | custom-call | flops 1 | bytes 1 | tf_op jit(solution)/shard_map/pallas_call | solution.py:369
  175.5 3.8 %shard_map.70 = f32[2048,512]{1,0:T(8,128)} custom-call(s32[1]{0:T(128)} %bitcast.4.me_ref, bf16[512,512]{1,0:T(8,128)(2,1)} %get-tuple-element.71.high_ref, bf16[512,512]{1,0:T(8,128)(2,1)} %get-tuple-element.72.low_ref, f32[256,512]{1,0:T(8,128)S(1)} %collective-permute-done.3.rest_0_, ...), custom_call_target="tpu_custom_call", output_to_operand_aliasing={{}: (7, {})} | custom-call | flops 1 | bytes 1 | tf_op jit(solution)/shard_map/pallas_call | solution.py:369
  (29 shorter events, 4.8 us)
Async XLA Ops:
  0.6 2.2 %copy-start = (f32[2048,512]{1,0:T(8,128)S(1)}, f32[2048,512]{1,0:T(8,128)}, u32[]{:S(2)}) copy-start(f32[2048,512]{1,0:T(8,128)} %obs_ref.1) | copy-start | bytes 12582916
  2.8 0.7 copy-start.1
  3.5 0.7 copy-start.2
  4.2 0.7 copy-start.3
  4.9 18.9 %copy-start.8 = (f32[512,512]{1,0:T(8,128)S(1)}, f32[512,512]{1,0:T(8,128)}, u32[]{:S(2)}) copy-start(f32[512,512]{1,0:T(8,128)} %param.11) | copy-start | bytes 3145732
  14.8 160.6 %collective-permute-start.3 = (f32[256,512]{1,0:T(8,128)}, f32[256,512]{1,0:T(8,128)S(1)}, u32[]{:S(2)}, u32[]{:S(2)}) collective-permute-start(f32[256,512]{1,0:T(8,128)} %get-tuple-element.67), channel_id=1, source_target_pairs={{0,16},{4,20},{8,24},{12,28},{16,0},{20,4},{24,8},{28,12},{1,17},{... | collective-permute-start | bytes 1572872 | tf_op jit(solution)/shard_map/ppermute | solution.py:395
  18.9 156.6 %collective-permute-start.4 = (f32[256,512]{1,0:T(8,128)}, f32[256,512]{1,0:T(8,128)S(1)}, u32[]{:S(2)}, u32[]{:S(2)}) collective-permute-start(f32[256,512]{1,0:T(8,128)} %get-tuple-element.68), channel_id=1, source_target_pairs={{0,20},{4,16},{8,28},{12,24},{16,4},{20,0},{24,12},{28,8},{1,21},{... | collective-permute-start | bytes 1572872 | tf_op jit(solution)/shard_map/ppermute | solution.py:395
  20.2 155.3 %collective-permute-start.5 = (f32[256,512]{1,0:T(8,128)}, f32[256,512]{1,0:T(8,128)S(1)}, u32[]{:S(2)}, u32[]{:S(2)}) collective-permute-start(f32[256,512]{1,0:T(8,128)} %get-tuple-element.69), channel_id=1, source_target_pairs={{0,24},{4,28},{8,16},{12,20},{16,8},{20,12},{24,0},{28,4},{1,25},{... | collective-permute-start | bytes 1572872 | tf_op jit(solution)/shard_map/ppermute | solution.py:395
  23.8 151.7 %collective-permute-start.6 = (f32[256,512]{1,0:T(8,128)}, f32[256,512]{1,0:T(8,128)S(1)}, u32[]{:S(2)}, u32[]{:S(2)}) collective-permute-start(f32[256,512]{1,0:T(8,128)} %get-tuple-element.70), channel_id=1, source_target_pairs={{0,28},{4,24},{8,20},{12,16},{16,12},{20,8},{24,4},{28,0},{1,29},{... | collective-permute-start | bytes 1572872 | tf_op jit(solution)/shard_map/ppermute | solution.py:395
  25.0 0.8 copy-start.4
  25.0 5.8 %copy-start.5 = (f32[256,512]{1,0:T(8,128)}, f32[256,512]{1,0:T(8,128)S(1)}, u32[]{:S(2)}) copy-start(f32[256,512]{1,0:T(8,128)S(1)} %get-tuple-element.39.rest_2_) | copy-start | bytes 1572868 | tf_op jit(solution)/shard_map/cond
  25.0 5.8 %copy-start.6 = (f32[256,512]{1,0:T(8,128)}, f32[256,512]{1,0:T(8,128)S(1)}, u32[]{:S(2)}) copy-start(f32[256,512]{1,0:T(8,128)S(1)} %get-tuple-element.29.rest_1_) | copy-start | bytes 1572868 | tf_op jit(solution)/shard_map/cond
  30.8 13.7 %all-to-all-start = ((f32[4,320,128]{2,1,0:T(8,128)}), f32[4,320,128]{2,1,0:T(8,128)S(1)}, u32[]{:S(2)}, u32[]{:S(2)}) async-start(f32[4,320,128]{2,1,0:T(8,128)} %bitcast), calls=%async_computation | async-start | bytes 1310720 | tf_op jit(solution)/shard_map/cond/branch_1_fun/all_to_all | solution.py:236
  34.3 79.3 %collective-permute-start = (f32[256,512]{1,0:T(8,128)}, f32[256,512]{1,0:T(8,128)}, u32[]{:S(2)}, u32[]{:S(2)}) collective-permute-start(f32[256,512]{1,0:T(8,128)} %copy-done.6), channel_id=1, source_target_pairs={{0,4},{4,0},{8,12},{12,8},{16,20},{20,16},{24,28},{28,24},{1,5},{5... | collective-permute-start | bytes 1572872 | tf_op jit(solution)/shard_map/cond/branch_1_fun/ppermute | solution.py:395
  114.3 14.1 %all-to-all-start.2 = ((f32[8,40,128]{2,1,0:T(8,128)}), f32[8,40,128]{2,1,0:T(8,128)S(1)}, u32[]{:S(2)}, u32[]{:S(2)}) async-start(f32[8,40,128]{2,1,0:T(8,128)} %broadcast_in_dim.4), calls=%async_computation.2 | async-start | bytes 327680 | tf_op jit(solution)/shard_map/cond/branch_1_fun/all_to_all | solution.py:248
  119.7 16.5 %collective-permute-start.1 = (f32[256,512]{1,0:T(8,128)}, f32[256,512]{1,0:T(8,128)}, u32[]{:S(2)}, u32[]{:S(2)}) collective-permute-start(f32[256,512]{1,0:T(8,128)} %copy-done.5), channel_id=1, source_target_pairs={{0,8},{4,12},{8,0},{12,4},{16,24},{20,28},{24,16},{28,20},{1,9},{5... | collective-permute-start | bytes 1572872 | tf_op jit(solution)/shard_map/cond/branch_1_fun/ppermute | solution.py:395
  129.3 13.7 %all-to-all-start.3 = ((f32[4,320,128]{2,1,0:T(8,128)}), f32[4,320,128]{2,1,0:T(8,128)S(1)}, u32[]{:S(2)}, u32[]{:S(2)}) async-start(f32[4,320,128]{2,1,0:T(8,128)} %broadcast_in_dim.5), calls=%async_computation.3 | async-start | bytes 1310720 | tf_op jit(solution)/shard_map/cond/branch_1_fun/all_to_all | solution.py:250
  143.0 28.2 %collective-permute-start.2 = (f32[256,512]{1,0:T(8,128)}, f32[256,512]{1,0:T(8,128)S(1)}, u32[]{:S(2)}, u32[]{:S(2)}) collective-permute-start(f32[256,512]{1,0:T(8,128)} %copy-done.4), channel_id=1, source_target_pairs={{0,12},{4,8},{8,4},{12,0},{16,28},{20,24},{24,20},{28,16},{1,13},{... | collective-permute-start | bytes 1572872 | tf_op jit(solution)/shard_map/cond/branch_1_fun/ppermute | solution.py:395
  144.0 27.2 %copy-start.7 = (f32[256,512]{1,0:T(8,128)S(1)}, f32[256,512]{1,0:T(8,128)}, u32[]{:S(2)}) copy-start(f32[256,512]{1,0:T(8,128)} %copy.14) | copy-start | bytes 1572868 | tf_op jit(solution)/shard_map/cond

commit v5 on v4

--- a/solution.py
+++ b/solution.py
@@ -230,24 +230,18 @@
     )(prior_factor, *chunks)
 
 
-def scatter_sum(packed, row_groups, grp):
+def scatter_sum(packed, count, groups):
     rows, lanes = packed.shape
-    part = rows // grp
-    got = lax.all_to_all(packed, "grp", split_axis=0, concat_axis=0, tiled=True)
-    mine = jnp.sum(got.reshape(grp, part, lanes), axis=0)
-    piece = -(-part // row_groups)
-    mine = jnp.pad(mine, ((0, piece * row_groups - part), (0, 0)))
-    got = lax.all_to_all(mine, "rows", split_axis=0, concat_axis=0, tiled=True)
-    return jnp.sum(got.reshape(row_groups, piece, lanes), axis=0)
-
-
-def gather_pieces(piece, rows, row_groups, grp):
-    size, lanes = piece.shape
-    part = rows // grp
-    mine = jnp.broadcast_to(piece, (row_groups, size, lanes)).reshape(row_groups * size, lanes)
-    mine = lax.all_to_all(mine, "rows", split_axis=0, concat_axis=0, tiled=True)[:part]
-    mine = jnp.broadcast_to(mine, (grp, part, lanes)).reshape(rows, lanes)
-    return lax.all_to_all(mine, "grp", split_axis=0, concat_axis=0, tiled=True)
+    axes = ("rows", "grp")
+    got = lax.all_to_all(packed, axes, split_axis=0, concat_axis=0, axis_index_groups=groups, tiled=True)
+    return jnp.sum(got.reshape(count, rows // count, lanes), axis=0)
+
+
+def gather_pieces(piece, count, groups):
+    rows, lanes = piece.shape
+    copies = jnp.broadcast_to(piece, (count, rows, lanes)).reshape(count * rows, lanes)
+    axes = ("rows", "grp")
+    return lax.all_to_all(copies, axes, split_axis=0, concat_axis=0, axis_index_groups=groups, tiled=True)
 
 
 def sweep(a, w):
@@ -333,7 +327,7 @@
         scratch_shapes=[pltpu.VMEM((state, state), F32)] * 2,
         compiler_params=pltpu.CompilerParams(vmem_limit_bytes=16 * MIB),
         cost_estimate=pl.CostEstimate(
-            flops=40_000_000_000, bytes_accessed=4 * state * state, transcendentals=0
+            flops=1, bytes_accessed=1, transcendentals=0
         ),
     )(summed, prior_gram)
 
@@ -385,6 +379,10 @@
     )(me.reshape(1), high, low, *chunks, *extra)
 
 
+def behind(value, *arrays):
+    return lax.optimization_barrier((value, *arrays))
+
+
 def shards(observations, sensor_ids, sensor_sigma, buckets, prior_factor):
     rows_dev, state = observations.shape
     groups = lax.axis_size("rows")
@@ -393,37 +391,47 @@
     total_rows = rows_dev * groups * grp
     chunks = regroup(observations, sensor_ids, sensor_sigma, buckets, me, groups)
     move = lambda k, chunk: lax.ppermute(chunk, "rows", [(i, i ^ k) for i in range(groups)])
+    packed_rows = len(block_pairs(state // LANES)) * LANES
+    plane = 2 * grp
+    planes = [list(range(i, i + plane)) for i in range(0, groups * grp, plane)]
     short = [k for k in (1, 2, 3) if k < groups]
-    received = [chunks[0]] + [None] * (groups - 1)
-    for k in reversed(range(1, groups)):
-        if k not in short:
-            received[k] = move(k, chunks[k])
-    packed_rows = len(block_pairs(state // LANES)) * LANES
-
-    def inside():
-        moved = [move(k, chunks[k]) for k in short[:1]]
-
-        def move_next(value):
-            if len(moved) < len(short):
-                chunk = chunks[short[len(moved)]]
-                value, moved[-1], chunk = lax.optimization_barrier((value, moved[-1], chunk))
-                moved.append(move(short[len(moved)], chunk))
-            return value
-
+    early = [k for k in (4,) if k < groups]
+    middle = [k for k in (6, 2) if k < groups]
+    late = [k for k in range(3, groups) if k not in early + middle]
+    received = {0: chunks[0]}
+    valid = prior_factor[0, 0] > 0
+    nothing = lambda rows: jnp.full((rows, LANES), jnp.nan, F32)
+
+    for k in early:
+        received[k] = move(k, chunks[k])
+
+    def first():
         packed, prior_gram = gram(prior_factor, chunks)
-        piece = move_next(scatter_sum(packed, groups, grp))
-        summed = move_next(gather_pieces(piece, packed_rows, groups, grp))
-        return moved, list(factorise(summed, prior_gram, state, total_rows))
-
-    def invalid():
-        wrong = jnp.full((state, state), jnp.nan, F32)
-        return [chunks[k] for k in short], [wrong, wrong.astype(BF16), wrong.astype(BF16)]
-
-    moved, (factor, high, low) = lax.cond(prior_factor[0, 0] > 0, inside, invalid)
-    for k, chunk in zip(short, moved):
-        received[k] = chunk
-    out = whiten(me, high, low, range(groups // 2), received[: groups // 2], None, rows_dev)
-    out = whiten(me, high, low, range(groups // 2, groups), received[groups // 2 :], out, rows_dev)
+        return move(1, chunks[1]), scatter_sum(packed, plane, planes), prior_gram
+
+    received[1], piece, prior_gram = lax.cond(
+        valid, first, lambda: (chunks[1], nothing(packed_rows // plane), nothing(packed_rows))
+    )
+    for k in early:
+        piece, received[k] = behind(piece, received[k])
+    across = [piece]
+    for step in range(1, groups // 2):
+        across.append(move(2 * step, piece))
+    for k in middle:
+        _, chunk = behind(piece, chunks[k])
+        received[k] = move(k, chunk)
+    while len(across) > 1:
+        across = [across[i] + across[i + 1] for i in range(0, len(across), 2)]
+    summed = lax.cond(
+        valid, lambda: gather_pieces(across[0], plane, planes), lambda: nothing(packed_rows)
+    )
+    for k in late:
+        _, chunk = behind(summed, chunks[k])
+        received[k] = move(k, chunk)
+    factor, high, low = factorise(summed, prior_gram, state, total_rows)
+    out = None
+    for steps in ([0, 1] + early + middle, late):
+        out = whiten(me, high, low, steps, [received[k] for k in steps], out, rows_dev)
     return (out, factor)
 
 

time: 180 us -> 136 us (0.76)
  the two profiles are of different devices: /device:TPU:0 before, /device:TPU:8 now
where the time goes in v5:
time: 136 us
  Pallas kernels  47.4 us (35%)
  waiting for transfers between devices  47.1 us (35%)
  starting transfers between devices  21.5 us (16%)
  blocking collectives  13.4 us (10%)
  local copies, waits for them, and re-layouts  4.83 us (4%)
  between operations  1.53 us (1%)
    ppermute x10, waiting for transfers between devices, shards(): lax.ppermute(chunk, 'rows', [(i, i ^ k) for i in range(groups)])  47.1 us
    pallas_call x1, Pallas kernels, factorise(): pl.pallas_call(functools.partial(factor_kernel, 1.0 / total_rows), in_spe...  25.8 us
    ppermute x10, starting transfers between devices, shards(): lax.ppermute(chunk, 'rows', [(i, i ^ k) for i in range(groups)])  17.8 us
    all_to_all x1, blocking collectives, gather_pieces(): lax.all_to_all(copies, axes, split_axis=0, concat_axis=0, axis_index_grou...  13.4 us
    pallas_call x1, Pallas kernels, regroup(): pl.pallas_call(functools.partial(regroup_kernel, groups, per_bucket), gri...  10.1 us
    pallas_call x2, Pallas kernels, whiten(): pl.pallas_call(functools.partial(whiten_kernel, tuple(steps), len(extra))...  6.3 us
    pallas_call x1, Pallas kernels, gram(): pl.pallas_call(functools.partial(gram_kernel, groups), in_specs=[vmem] *...  5.19 us
    unnamed x12, local copies, waits for them, and re-layouts  4.24 us
  transfers between devices with their start and end apart: 11, of which 5 were waited for; matrix products, arithmetic and copies ran while one was open for 0% of the time, Pallas kernels for 26%

profile of v5, /device:TPU:8, one launch (start us, length us, event | category | flops | bytes accessed | tf_op | source)
XLA Modules:
  0.0 135.9 jit_solution(7262136571233209744)
XLA Ops:
  0.6 2.2 %copy-done = f32[2048,512]{1,0:T(8,128)S(1)} copy-done((f32[2048,512]{1,0:T(8,128)S(1)}, f32[2048,512]{1,0:T(8,128)}, u32[]{:S(2)}) %copy-start) | copy-done | bytes 4194328
  2.8 0.7 copy-done.1
  3.5 0.7 copy-done.2
  4.2 0.7 copy-done.3
  4.9 10.1 %shard_map.68 = (f32[256,512]{1,0:T(8,128)S(1)}, f32[256,512]{1,0:T(8,128)S(1)}, f32[256,512]{1,0:T(8,128)}, f32[256,512]{1,0:T(8,128)}, f32[256,512]{1,0:T(8,12...) custom-call(s32[1]{0:T(128)} %bitcast.2.me_ref, s32[16,128]{1,0:T(8,128)S(1)} %bitcast.7, ...), custom_call_target="tpu_custom_call" | custom-call | flops 1610612736 | bytes 8388608 | tf_op jit(solution)/shard_map/pallas_call | solution.py:149
  15.0 2.6 %collective-permute-start.1 = (f32[256,512]{1,0:T(8,128)}, f32[256,512]{1,0:T(8,128)S(1)}, u32[]{:S(2)}, u32[]{:S(2)}) collective-permute-start(f32[256,512]{1,0:T(8,128)} %get-tuple-element.75), channel_id=1, source_target_pairs={{0,16},{4,20},{8,24},{12,28},{16,0},{20,4},{24,8},{28,12},{1,17},{... | collective-permute-start | bytes 1572872 | tf_op jit(solution)/shard_map/ppermute | solution.py:393
  18.8 30.5 %conditional.2 = (f32[256,512]{1,0:T(8,128)S(1)}, f32[160,128]{1,0:T(8,128)S(1)}, f32[1280,128]{1,0:T(8,128)S(1)}) conditional(s32[]{:T(128)} %bitcast.3, f32[256,512]{1,0:T(8,128)S(1)} %get-tuple-element.71, (f32[256,512]{1,0:T(8,128)S(1)}, f32[512,512]{1,0:T(8,128)S(1)}, f32[256,512]{1,0:T(8,128)S(1)}, f32[256,512]{1,0:T(8,128)}, ...), branch_computations={%region_0.0_spmd, %region_1.0_spmd} | conditional | flops 2147627008 | bytes 10043492 | solution.py:412
  18.8 5.2 %branch_1_fun.1 = (f32[1280,128]{1,0:T(8,128)}, f32[1280,128]{1,0:T(8,128)S(1)}) custom-call(f32[512,512]{1,0:T(8,128)S(1)} %get-tuple-element.34.prior_ref, f32[256,512]{1,0:T(8,128)S(1)} %get-tuple-element.35.rest_0_, f32[256,512]{1,0:T(8,128)S(1)} %get-tuple-element.33.rest_1_, f32[256,512]{1,0:T(8,128)} %get-tuple-element.36.rest_2_, ...), custom_call_target="tpu_custom_call" | custom-call | flops 2147483648 | bytes 4194304 | tf_op jit(solution)/shard_map/cond/branch_1_fun/pallas_call | solution.py:220
  24.0 3.7 %all-to-all-start = ((f32[8,160,128]{2,1,0:T(8,128)}), f32[8,160,128]{2,1,0:T(8,128)S(1)}, u32[]{:S(2)}, u32[]{:S(2)}) async-start(f32[8,160,128]{2,1,0:T(8,128)} %bitcast), calls=%async_computation | async-start | bytes 1310720 | tf_op jit(solution)/shard_map/cond/branch_1_fun/all_to_all | solution.py:236
  27.7 2.0 %collective-permute-start = (f32[256,512]{1,0:T(8,128)S(1)}, f32[256,512]{1,0:T(8,128)S(1)}, u32[]{:S(2)}, u32[]{:S(2)}) collective-permute-start(f32[256,512]{1,0:T(8,128)S(1)} %get-tuple-element.33.rest_1_), channel_id=1, source_target_pairs={{0,4},{4,0},{8,12},{12,8},{16,20},{20,16},{24,28},{28,24},{1,5},{5... | collective-permute-start | bytes 1572872 | tf_op jit(solution)/shard_map/cond/branch_1_fun/ppermute | solution.py:393
  29.8 19.5 %collective-permute-done = f32[256,512]{1,0:T(8,128)S(1)} collective-permute-done((f32[256,512]{1,0:T(8,128)S(1)}, f32[256,512]{1,0:T(8,128)S(1)}, u32[]{:S(2)}, u32[]{:S(2)}) %collective-permute-start) | collective-permute-done | bytes 524320 | tf_op jit(solution)/shard_map/cond/branch_1_fun/ppermute | solution.py:393
  49.4 2.8 %collective-permute-start.3 = (f32[160,128]{1,0:T(8,128)S(1)}, f32[160,128]{1,0:T(8,128)S(1)}, u32[]{:S(2)}, u32[]{:S(2)}) collective-permute-start(f32[160,128]{1,0:T(8,128)S(1)} %get-tuple-element.80), channel_id=1, source_target_pairs={{0,16},{4,20},{8,24},{12,28},{16,0},{20,4},{24,8},{28,12},{1,17},{... | collective-permute-start | bytes 245768 | tf_op jit(solution)/shard_map/ppermute | solution.py:393
  53.0 2.6 %collective-permute-start.9 = (f32[256,512]{1,0:T(8,128)}, f32[256,512]{1,0:T(8,128)S(1)}, u32[]{:S(2)}, u32[]{:S(2)}) collective-permute-start(f32[256,512]{1,0:T(8,128)} %get-tuple-element.90), channel_id=1, source_target_pairs={{0,8},{4,12},{8,0},{12,4},{16,24},{20,28},{24,16},{28,20},{1,9},{5... | collective-permute-start | bytes 1572872 | tf_op jit(solution)/shard_map/ppermute | solution.py:393
  55.6 3.9 %collective-permute-done.4 = f32[160,128]{1,0:T(8,128)S(1)} collective-permute-done((f32[160,128]{1,0:T(8,128)S(1)}, f32[160,128]{1,0:T(8,128)S(1)}, u32[]{:S(2)}, u32[]{:S(2)}) %collective-permute-start.4) | collective-permute-done | bytes 81952 | tf_op jit(solution)/shard_map/ppermute | solution.py:393
  59.5 8.2 %collective-permute-done.3 = f32[160,128]{1,0:T(8,128)S(1)} collective-permute-done((f32[160,128]{1,0:T(8,128)S(1)}, f32[160,128]{1,0:T(8,128)S(1)}, u32[]{:S(2)}, u32[]{:S(2)}) %collective-permute-start.3) | collective-permute-done | bytes 81952 | tf_op jit(solution)/shard_map/ppermute | solution.py:393
  67.7 13.5 %conditional.3 = (f32[1280,128]{1,0:T(8,128)S(1)}) conditional(s32[]{:T(128)} %bitcast.3, () %tuple.29, (f32[160,128]{1,0:T(8,128)S(1)}, f32[160,128]{1,0:T(8,128)S(1)}, f32[160,128]{1,0:T(8,128)S(1)}, f32[160,128]{1,0:T(8,128)S(1)}) %tuple.32), branch_computations={%region_3.0_spmd, %region_4.0_spmd} | conditional | flops 61440 | bytes 2457608 | solution.py:425
  67.8 13.4 %all_to_all.14 = f32[8,160,128]{2,1,0:T(8,128)S(1)} all-to-all(f32[8,160,128]{2,1,0:T(8,128)S(1)} %broadcast_in_dim.2), channel_id=1, replica_groups={{0,1,2,3,4,5,6,7},{8,9,10,11,12,13,14,15},{16,17,18,19,20,21,22,23},{24..., dimensions={0} | all-to-all | bytes 1310720 | tf_op jit(solution)/shard_map/cond/branch_1_fun/all_to_all | solution.py:244
  81.2 4.8 %collective-permute-start.5 = (f32[256,512]{1,0:T(8,128)}, f32[256,512]{1,0:T(8,128)S(1)}, u32[]{:S(2)}, u32[]{:S(2)}) collective-permute-start(f32[256,512]{1,0:T(8,128)} %get-tuple-element.84), channel_id=1, source_target_pairs={{0,12},{4,8},{8,4},{12,0},{16,28},{20,24},{24,20},{28,16},{1,13},{... | collective-permute-start | bytes 1572872 | tf_op jit(solution)/shard_map/ppermute | solution.py:393
  86.1 2.1 %collective-permute-start.7 = (f32[256,512]{1,0:T(8,128)}, f32[256,512]{1,0:T(8,128)S(1)}, u32[]{:S(2)}, u32[]{:S(2)}) collective-permute-start(f32[256,512]{1,0:T(8,128)} %get-tuple-element.86), channel_id=1, source_target_pairs={{0,28},{4,24},{8,20},{12,16},{16,12},{20,8},{24,4},{28,0},{1,29},{... | collective-permute-start | bytes 1572872 | tf_op jit(solution)/shard_map/ppermute | solution.py:393
  88.1 25.8 %shard_map.69 = (f32[512,512]{1,0:T(8,128)}, bf16[512,512]{1,0:T(8,128)(2,1)S(1)}, bf16[512,512]{1,0:T(8,128)(2,1)S(1)}) custom-call(f32[1280,128]{1,0:T(8,128)S(1)} %get-tuple-element.98.sum_ref, f32[1280,128]{1,0:T(8,128)S(1)} %get-tuple-element.81.prior_ref), custom_call_target="tpu_custom_call" | custom-call | flops 1 | bytes 1 | tf_op jit(solution)/shard_map/pallas_call | solution.py:318
  113.9 4.1 %shard_map.70.rest_3_ = f32[2048,512]{1,0:T(8,128)} custom-call(s32[1]{0:T(128)} %bitcast.2.me_ref, bf16[512,512]{1,0:T(8,128)(2,1)S(1)} %get-tuple-element.82.high_ref, bf16[512,512]{1,0:T(8,128)(2,1)S(1)} %get-tuple-element.83.low_ref, f32[256,512]{1,0:T(8,128)S(1)} %get-tuple-element.72.rest_0_, f32[256,512]{1,0:T(8,128)} %copy-done.4, ...), custom_call_target="tpu_custom_call" | custom-call | flops 1 | bytes 1 | tf_op jit(solution)/shard_map/pallas_call | solution.py:363
  118.0 3.2 %collective-permute-done.6.rest_1_ = f32[256,512]{1,0:T(8,128)S(1)} collective-permute-done((f32[256,512]{1,0:T(8,128)}, f32[256,512]{1,0:T(8,128)S(1)}, u32[]{:S(2)}, u32[]{:S(2)}) %collective-permute-start.6) | collective-permute-done | bytes 524320 | tf_op jit(solution)/shard_map/ppermute | solution.py:393
  121.2 12.3 %collective-permute-done.7.rest_2_ = f32[256,512]{1,0:T(8,128)S(1)} collective-permute-done((f32[256,512]{1,0:T(8,128)}, f32[256,512]{1,0:T(8,128)S(1)}, u32[]{:S(2)}, u32[]{:S(2)}) %collective-permute-start.7) | collective-permute-done | bytes 524320 | tf_op jit(solution)/shard_map/ppermute | solution.py:393
  133.5 2.2 %shard_map.71 = f32[2048,512]{1,0:T(8,128)} custom-call(s32[1]{0:T(128)} %bitcast.2.me_ref, bf16[512,512]{1,0:T(8,128)(2,1)S(1)} %get-tuple-element.82.high_ref, bf16[512,512]{1,0:T(8,128)(2,1)S(1)} %get-tuple-element.83.low_ref, f32[256,512]{1,0:T(8,128)S(1)} %collective-permute-done.5.rest_0_, ...), custom_call_target="tpu_custom_call", output_to_operand_aliasing={{}: (6, {})} | custom-call | flops 1 | bytes 1 | tf_op jit(solution)/shard_map/pallas_call | solution.py:363
  (23 shorter events, 1.5 us)
Async XLA Ops:
  0.6 2.2 %copy-start = (f32[2048,512]{1,0:T(8,128)S(1)}, f32[2048,512]{1,0:T(8,128)}, u32[]{:S(2)}) copy-start(f32[2048,512]{1,0:T(8,128)} %obs_ref.1) | copy-start | bytes 12582916
  2.8 0.7 copy-start.1
  3.5 0.7 copy-start.2
  4.2 0.7 copy-start.3
  4.9 12.8 %copy-start.5 = (f32[512,512]{1,0:T(8,128)S(1)}, f32[512,512]{1,0:T(8,128)}, u32[]{:S(2)}) copy-start(f32[512,512]{1,0:T(8,128)} %param.13) | copy-start | bytes 3145732
  15.0 34.3 %collective-permute-start.1 = (f32[256,512]{1,0:T(8,128)}, f32[256,512]{1,0:T(8,128)S(1)}, u32[]{:S(2)}, u32[]{:S(2)}) collective-permute-start(f32[256,512]{1,0:T(8,128)} %get-tuple-element.75), channel_id=1, source_target_pairs={{0,16},{4,20},{8,24},{12,28},{16,0},{20,4},{24,8},{28,12},{1,17},{... | collective-permute-start | bytes 1572872 | tf_op jit(solution)/shard_map/ppermute | solution.py:393
  24.0 25.2 %all-to-all-start = ((f32[8,160,128]{2,1,0:T(8,128)}), f32[8,160,128]{2,1,0:T(8,128)S(1)}, u32[]{:S(2)}, u32[]{:S(2)}) async-start(f32[8,160,128]{2,1,0:T(8,128)} %bitcast), calls=%async_computation | async-start | bytes 1310720 | tf_op jit(solution)/shard_map/cond/branch_1_fun/all_to_all | solution.py:236
  27.7 21.5 %collective-permute-start = (f32[256,512]{1,0:T(8,128)S(1)}, f32[256,512]{1,0:T(8,128)S(1)}, u32[]{:S(2)}, u32[]{:S(2)}) collective-permute-start(f32[256,512]{1,0:T(8,128)S(1)} %get-tuple-element.33.rest_1_), channel_id=1, source_target_pairs={{0,4},{4,0},{8,12},{12,8},{16,20},{20,16},{24,28},{28,24},{1,5},{5... | collective-permute-start | bytes 1572872 | tf_op jit(solution)/shard_map/cond/branch_1_fun/ppermute | solution.py:393
  49.3 3.6 %copy-start.4 = (f32[256,512]{1,0:T(8,128)}, f32[256,512]{1,0:T(8,128)S(1)}, u32[]{:S(2)}) copy-start(f32[256,512]{1,0:T(8,128)S(1)} %get-tuple-element.87.rest_1_) | copy-start | bytes 1572868
  49.3 10.2 %collective-permute-start.4 = (f32[160,128]{1,0:T(8,128)S(1)}, f32[160,128]{1,0:T(8,128)S(1)}, u32[]{:S(2)}, u32[]{:S(2)}) collective-permute-start(f32[160,128]{1,0:T(8,128)S(1)} %get-tuple-element.80), channel_id=1, source_target_pairs={{0,24},{4,28},{8,16},{12,20},{16,8},{20,12},{24,0},{28,4},{1,25},{... | collective-permute-start | bytes 245768 | tf_op jit(solution)/shard_map/ppermute | solution.py:393
  49.4 18.3 %collective-permute-start.3 = (f32[160,128]{1,0:T(8,128)S(1)}, f32[160,128]{1,0:T(8,128)S(1)}, u32[]{:S(2)}, u32[]{:S(2)}) collective-permute-start(f32[160,128]{1,0:T(8,128)S(1)} %get-tuple-element.80), channel_id=1, source_target_pairs={{0,16},{4,20},{8,24},{12,28},{16,0},{20,4},{24,8},{28,12},{1,17},{... | collective-permute-start | bytes 245768 | tf_op jit(solution)/shard_map/ppermute | solution.py:393
  52.2 15.5 %collective-permute-start.2 = (f32[160,128]{1,0:T(8,128)S(1)}, f32[160,128]{1,0:T(8,128)S(1)}, u32[]{:S(2)}, u32[]{:S(2)}) collective-permute-start(f32[160,128]{1,0:T(8,128)S(1)} %get-tuple-element.80), channel_id=1, source_target_pairs={{0,8},{4,12},{8,0},{12,4},{16,24},{20,28},{24,16},{28,20},{1,9},{5... | collective-permute-start | bytes 245768 | tf_op jit(solution)/shard_map/ppermute | solution.py:393
  52.9 61.0 %collective-permute-start.8 = (f32[256,512]{1,0:T(8,128)}, f32[256,512]{1,0:T(8,128)S(1)}, u32[]{:S(2)}, u32[]{:S(2)}) collective-permute-start(f32[256,512]{1,0:T(8,128)} %get-tuple-element.89), channel_id=1, source_target_pairs={{0,24},{4,28},{8,16},{12,20},{16,8},{20,12},{24,0},{28,4},{1,25},{... | collective-permute-start | bytes 1572872 | tf_op jit(solution)/shard_map/ppermute | solution.py:393
  53.0 60.9 %collective-permute-start.9 = (f32[256,512]{1,0:T(8,128)}, f32[256,512]{1,0:T(8,128)S(1)}, u32[]{:S(2)}, u32[]{:S(2)}) collective-permute-start(f32[256,512]{1,0:T(8,128)} %get-tuple-element.90), channel_id=1, source_target_pairs={{0,8},{4,12},{8,0},{12,4},{16,24},{20,28},{24,16},{28,20},{1,9},{5... | collective-permute-start | bytes 1572872 | tf_op jit(solution)/shard_map/ppermute | solution.py:393
  81.2 36.8 %collective-permute-start.5 = (f32[256,512]{1,0:T(8,128)}, f32[256,512]{1,0:T(8,128)S(1)}, u32[]{:S(2)}, u32[]{:S(2)}) collective-permute-start(f32[256,512]{1,0:T(8,128)} %get-tuple-element.84), channel_id=1, source_target_pairs={{0,12},{4,8},{8,4},{12,0},{16,28},{20,24},{24,20},{28,16},{1,13},{... | collective-permute-start | bytes 1572872 | tf_op jit(solution)/shard_map/ppermute | solution.py:393
  86.0 35.2 %collective-permute-start.6 = (f32[256,512]{1,0:T(8,128)}, f32[256,512]{1,0:T(8,128)S(1)}, u32[]{:S(2)}, u32[]{:S(2)}) collective-permute-start(f32[256,512]{1,0:T(8,128)} %get-tuple-element.85), channel_id=1, source_target_pairs={{0,20},{4,16},{8,28},{12,24},{16,4},{20,0},{24,12},{28,8},{1,21},{... | collective-permute-start | bytes 1572872 | tf_op jit(solution)/shard_map/ppermute | solution.py:393
  86.1 47.5 %collective-permute-start.7 = (f32[256,512]{1,0:T(8,128)}, f32[256,512]{1,0:T(8,128)S(1)}, u32[]{:S(2)}, u32[]{:S(2)}) collective-permute-start(f32[256,512]{1,0:T(8,128)} %get-tuple-element.86), channel_id=1, source_target_pairs={{0,28},{4,24},{8,20},{12,16},{16,12},{20,8},{24,4},{28,0},{1,29},{... | collective-permute-start | bytes 1572872 | tf_op jit(solution)/shard_map/ppermute | solution.py:393

commit v6 on v5

--- a/solution.py
+++ b/solution.py
@@ -52,90 +52,107 @@
     ]
 
 
-def regroup_kernel(groups, per_bucket, me_ref, buckets_ref, ids_ref, sigma_ref, obs_ref, *rest):
-    outs = rest[:groups]
-    place_ref, meta_ref, sorted_ref, inv_ref, meta_smem, sem = rest[groups:]
-    step = pl.program_id(0)
+def regroup_kernel(groups, per_bucket, me_ref, *refs):
+    given, outs, scratch = refs[:4], refs[4 : 4 + groups], refs[4 + groups :]
+    held, (place_ref, meta_ref, sorted_ref, inv_ref, meta_smem, sems) = scratch[:4], scratch[4:]
+    buckets_ref, ids_ref, sigma_ref, obs_ref = held
     blocks, block = place_ref.shape
     wide = block // LANES
     sensors = sigma_ref.shape[1]
-    padded = sorted_ref.shape[0]
+    padded, state = sorted_ref.shape
     cells = blocks * groups
-
-    @pl.when(step == 0)
-    def _():
-        me = me_ref[0]
-        inv_row = 1.0 / sigma_ref[...]
-        inv_ref[...] = jnp.transpose(jnp.broadcast_to(inv_row, (LANES, sensors)))
-        slots = rows_of(buckets_ref[...] ^ me, blocks, wide)
-        hits = jnp.concatenate(
-            [
-                jnp.broadcast_to(row, (groups, block)) == iota((groups, block), 0) for row in slots
-            ],
-            axis=0,
-        )
-        upto = (iota((block, block), 0) <= iota((block, block), 1)).astype(F32).astype(BF16)
-        running = dot(hits.astype(F32).astype(BF16), upto)
-        count = jnp.broadcast_to(running[:, block - 1 : block], (cells, LANES))
-        row, col = iota((cells, cells), 0), iota((cells, cells), 1)
-        shift = groups.bit_length() - 1
-        earlier = ((row & (groups - 1)) == (col & (groups - 1))) & (col < row)
-        before = dot(earlier.astype(F32).astype(BF16), count.astype(BF16)).astype(I32)
-        cell = iota((cells, LANES), 0)
-        start = (cell & (groups - 1)) * per_bucket + before
-        odd = start & (SUB - 1)
-        tiles = (odd + count.astype(I32) + (SUB - 1)) >> 3
-        same = ((row >> shift) == (col >> shift)) & (col < row)
-        first = dot(same.astype(F32).astype(BF16), tiles.astype(F32).astype(BF16)).astype(I32)
-        lane = iota((cells, LANES), 1)
-        meta_ref[...] = jnp.where(lane == 0, before, jnp.where(lane == 1, first, tiles))
-        copy = pltpu.make_async_copy(meta_ref, meta_smem, sem)
+    last_tile = per_bucket // SUB - 1
+    most = min(7, last_tile + 2)
+
+    small = [pltpu.make_async_copy(given[i], held[i], sems.at[i]) for i in range(3)]
+    for copy in small:
         copy.start()
-        local = first * SUB + odd
-        local = jnp.concatenate([local] * (block // LANES), axis=1)
-        spot = jnp.where(hits, local + running.astype(I32) - 1, 0)
-        place_ref[...] = jnp.concatenate(
-            [
-                jnp.sum(spot[s * groups : (s + 1) * groups], axis=0, keepdims=True)
-                for s in range(blocks)
-            ],
-            axis=0,
-        )
+
+    def fetch(s):
+        rows = pl.ds(pl.multiple_of(s * block, block), block)
+        return pltpu.make_async_copy(given[3].at[rows, :], obs_ref.at[rows, :], sems.at[4 + s])
+
+    for s in range(blocks):
+        fetch(s).start()
+    for copy in small:
         copy.wait()
 
-    place = place_ref[pl.ds(step, 1), :]
-    moves = (iota((padded, block), 0) == place).astype(F32).astype(BF16)
-    ids = [ids_ref[pl.ds(step * wide + i, 1), :] for i in range(wide)]
-    known = iota((sensors, block), 0) == jnp.concatenate(ids, axis=1)
-    inv = jnp.concatenate([inv_ref[...]] * (block // LANES), axis=1)
-    scale_row = jnp.sum(jnp.where(known, inv, 0.0), axis=0, keepdims=True)
-    scale = jnp.transpose(jnp.broadcast_to(scale_row, (LANES, block)))
-    state = obs_ref.shape[1]
-    scaled = obs_ref[...] * jnp.concatenate([scale] * (state // LANES), axis=1)
-    high, low = split(scaled)
-    sorted_ref[...] = dot(moves, high) + dot(moves, low)
-
-    for v in range(groups):
-        cell = step * groups + v
-        before = meta_smem[cell, 0]
-        source = meta_smem[cell, 1]
-        tiles = meta_smem[cell, 2]
-        target = before >> 3
-        out = outs[v]
-
-        @pl.when(tiles > 0)
-        def _(out=out, before=before, source=source, target=target):
-            rows = pl.ds(pl.multiple_of(target * SUB, SUB), SUB)
-            old = jnp.where((before & (SUB - 1)) > 0, out[rows, :], 0.0)
-            out[rows, :] = old + sorted_ref[pl.ds(pl.multiple_of(source * SUB, SUB), SUB), :]
-
-        def body(t, carry, out=out, source=source, target=target):
-            out[pl.ds(pl.multiple_of((target + t) * SUB, SUB), SUB), :] = sorted_ref[
-                pl.ds(pl.multiple_of((source + t) * SUB, SUB), SUB), :
-            ]
-            return carry
-
-        lax.fori_loop(1, tiles, body, 0)
+    inv_row = 1.0 / sigma_ref[...]
+    inv_ref[...] = jnp.transpose(jnp.broadcast_to(inv_row, (LANES, sensors)))
+    slots = rows_of(buckets_ref[...] ^ me_ref[0], blocks, wide)
+    hits = jnp.concatenate(
+        [jnp.broadcast_to(row, (groups, block)) == iota((groups, block), 0) for row in slots], axis=0
+    )
+    upto = (iota((block, block), 0) <= iota((block, block), 1)).astype(F32).astype(BF16)
+    running = dot(hits.astype(F32).astype(BF16), upto)
+    count = jnp.broadcast_to(running[:, block - 1 : block], (cells, LANES))
+    row, col = iota((cells, cells), 0), iota((cells, cells), 1)
+    shift = groups.bit_length() - 1
+    earlier = ((row & (groups - 1)) == (col & (groups - 1))) & (col < row)
+    before = dot(earlier.astype(F32).astype(BF16), count.astype(BF16)).astype(I32)
+    odd = before & (SUB - 1)
+    tiles = (odd + count.astype(I32) + (SUB - 1)) >> 3
+    same = ((row >> shift) == (col >> shift)) & (col < row)
+    first = dot(same.astype(F32).astype(BF16), tiles.astype(F32).astype(BF16)).astype(I32)
+    lane = iota((cells, LANES), 1)
+    kept = jnp.where(tiles > 0, odd, SUB)
+    target = jnp.minimum(before >> 3, last_tile)
+    final = jnp.maximum(tiles - 1, 0)
+    meta = jnp.where(lane == 2, first, final)
+    meta_ref[...] = jnp.where(lane == 0, kept, jnp.where(lane == 1, target, meta))
+    copy = pltpu.make_async_copy(meta_ref, meta_smem, sems.at[3])
+    copy.start()
+    local = first * SUB + odd
+    local = jnp.concatenate([local] * wide, axis=1)
+    spot = jnp.where(hits, local + running.astype(I32) - 1, 0)
+    place_ref[...] = jnp.concatenate(
+        [jnp.sum(spot[s * groups : (s + 1) * groups], axis=0, keepdims=True) for s in range(blocks)],
+        axis=0,
+    )
+    copy.wait()
+    sub_row = iota((SUB, state), 0)
+    tile = lambda t: pl.ds(pl.multiple_of(t * SUB, SUB), SUB)
+
+    def body(s, carry):
+        place = place_ref[pl.ds(s, 1), :]
+        moves = (iota((padded, block), 0) == place).astype(F32).astype(BF16)
+        ids = [ids_ref[pl.ds(s * wide + i, 1), :] for i in range(wide)]
+        known = iota((sensors, block), 0) == jnp.concatenate(ids, axis=1)
+        inv = jnp.concatenate([inv_ref[...]] * wide, axis=1)
+        scale_row = jnp.sum(jnp.where(known, inv, 0.0), axis=0, keepdims=True)
+        scale = jnp.transpose(jnp.broadcast_to(scale_row, (LANES, block)))
+        fetch(s).wait()
+        rows = pl.ds(pl.multiple_of(s * block, block), block)
+        scaled = obs_ref[rows, :] * jnp.concatenate([scale] * (state // LANES), axis=1)
+        high, low = split(scaled)
+        sorted_ref[...] = dot(moves, high) + dot(moves, low)
+        longest = 0
+        for v in range(groups):
+            cell = s * groups + v
+            kept, target = meta_smem[cell, 0], meta_smem[cell, 1]
+            first, final = meta_smem[cell, 2], meta_smem[cell, 3]
+            longest = jnp.maximum(longest, final)
+            old = outs[v][tile(target), :]
+            for t in reversed(range(1, most)):
+                t = jnp.minimum(t, final)
+                outs[v][tile(target + t), :] = sorted_ref[tile(first + t), :]
+            outs[v][tile(target), :] = jnp.where(sub_row < kept, old, sorted_ref[tile(first), :])
+
+        @pl.when(longest >= most)
+        def _():
+            for v in range(groups):
+                cell = s * groups + v
+                target, first, final = (meta_smem[cell, i] for i in (1, 2, 3))
+
+                def longer(t, carry, v=v, target=target, first=first):
+                    outs[v][tile(target + t), :] = sorted_ref[tile(first + t), :]
+                    return carry
+
+                lax.fori_loop(most, final + 1, longer, 0)
+
+        return carry
+
+    lax.fori_loop(0, blocks, body, 0)
 
 
 def regroup(observations, sensor_ids, sensor_sigma, buckets, me, groups):
@@ -144,31 +161,26 @@
     block = 256
     blocks = rows // block
     per_bucket = rows // groups
-    padded = -(-(block + groups * 2 * (SUB - 1)) // LANES) * LANES
-    whole = lambda shape: pl.BlockSpec(shape, lambda s, me: (0, 0))
+    padded = -(-(block + groups * 2 * (SUB - 1)) // 16) * 16
+    far = pl.BlockSpec(memory_space=pltpu.HBM)
     return pl.pallas_call(
         functools.partial(regroup_kernel, groups, per_bucket),
-        grid_spec=pltpu.PrefetchScalarGridSpec(
-            num_scalar_prefetch=1,
-            grid=(blocks,),
-            in_specs=[
-                whole((rows // LANES, LANES)),
-                whole((rows // LANES, LANES)),
-                whole((1, sensors)),
-                pl.BlockSpec((block, state), lambda s, me: (s, 0)),
-            ],
-            out_specs=[whole((per_bucket, state))] * groups,
-            scratch_shapes=[
-                pltpu.VMEM((blocks, block), I32),
-                pltpu.VMEM((blocks * groups, LANES), I32),
-                pltpu.VMEM((padded, state), F32),
-                pltpu.VMEM((sensors, LANES), F32),
-                pltpu.SMEM((blocks * groups, LANES), I32),
-                pltpu.SemaphoreType.DMA,
-            ],
-        ),
+        in_specs=[pl.BlockSpec(memory_space=pltpu.SMEM)] + [far] * 4,
+        out_specs=[pl.BlockSpec(memory_space=pltpu.VMEM)] * groups,
+        scratch_shapes=[
+            pltpu.VMEM((rows // LANES, LANES), I32),
+            pltpu.VMEM((rows // LANES, LANES), I32),
+            pltpu.VMEM((1, sensors), F32),
+            pltpu.VMEM((rows, state), F32),
+            pltpu.VMEM((blocks, block), I32),
+            pltpu.VMEM((blocks * groups, LANES), I32),
+            pltpu.VMEM((padded, state), F32),
+            pltpu.VMEM((sensors, LANES), F32),
+            pltpu.SMEM((blocks * groups, LANES), I32),
+            pltpu.SemaphoreType.DMA((4 + blocks,)),
+        ],
         out_shape=[jax.ShapeDtypeStruct((per_bucket, state), F32)] * groups,
-        compiler_params=pltpu.CompilerParams(vmem_limit_bytes=24 * MIB),
+        compiler_params=pltpu.CompilerParams(vmem_limit_bytes=56 * MIB),
         cost_estimate=pl.CostEstimate(
             flops=4 * rows * padded * state, bytes_accessed=8 * rows * state, transcendentals=0
         ),
@@ -394,10 +406,9 @@
     packed_rows = len(block_pairs(state // LANES)) * LANES
     plane = 2 * grp
     planes = [list(range(i, i + plane)) for i in range(0, groups * grp, plane)]
-    short = [k for k in (1, 2, 3) if k < groups]
-    early = [k for k in (4,) if k < groups]
+    early = [k for k in (1, 4) if k < groups]
     middle = [k for k in (6, 2) if k < groups]
-    late = [k for k in range(3, groups) if k not in early + middle]
+    late = [k for k in range(1, groups) if k not in early + middle]
     received = {0: chunks[0]}
     valid = prior_factor[0, 0] > 0
     nothing = lambda rows: jnp.full((rows, LANES), jnp.nan, F32)
@@ -407,10 +418,10 @@
 
     def first():
         packed, prior_gram = gram(prior_factor, chunks)
-        return move(1, chunks[1]), scatter_sum(packed, plane, planes), prior_gram
-
-    received[1], piece, prior_gram = lax.cond(
-        valid, first, lambda: (chunks[1], nothing(packed_rows // plane), nothing(packed_rows))
+        return scatter_sum(packed, plane, planes), prior_gram
+
+    piece, prior_gram = lax.cond(
+        valid, first, lambda: (nothing(packed_rows // plane), nothing(packed_rows))
     )
     for k in early:
         piece, received[k] = behind(piece, received[k])
@@ -430,7 +441,7 @@
         received[k] = move(k, chunk)
     factor, high, low = factorise(summed, prior_gram, state, total_rows)
     out = None
-    for steps in ([0, 1] + early + middle, late):
+    for steps in ([0] + early + middle, late):
         out = whiten(me, high, low, steps, [received[k] for k in steps], out, rows_dev)
     return (out, factor)
 

time: 136 us -> 125 us (0.919)
  waiting for transfers between devices: 47.1 us -> 20.4 us
  blocking collectives: 13.4 us -> 27 us
  starting transfers between devices: 21.5 us -> 25.5 us
  local copies, waits for them, and re-layouts: 4.83 us -> 1.25 us
    ppermute x10, waiting for transfers between devices: 47.1 us -> 20.4 us  [shards(): lax.ppermute(chunk, 'rows', [(i, i ^ k) for i in range(groups)])]
    all_to_all x0 -> x1, blocking collectives: none -> 13.5 us  [scatter_sum(): lax.all_to_all(packed, axes, split_axis=0, concat_axis=0, axis_index_grou...]
    ppermute x10, starting transfers between devices: 17.8 us -> 25.5 us  [shards(): lax.ppermute(chunk, 'rows', [(i, i ^ k) for i in range(groups)])]
    unnamed x12 -> x2, local copies, waits for them, and re-layouts: 4.24 us -> 0.01 us
    all_to_all x1 -> x0, starting transfers between devices: 3.71 us -> none  [scatter_sum(): lax.all_to_all(packed, axes, split_axis=0, concat_axis=0, axis_index_grou...]
  transfers between devices with their start and end apart: 11 -> 10, of which waited for: 5 -> 5; matrix products, arithmetic and copies ran while one was open for 0% -> 1% of each run, Pallas kernels for 26% -> 28%
where the time goes in v6:
time: 125 us; the launch traced here: 124 us
  Pallas kernels  47.6 us (38%)
  blocking collectives  27 us (22%)
  starting transfers between devices  25.5 us (20%)
  waiting for transfers between devices  20.4 us (16%)
  between operations  1.42 us (1%)
  local copies, waits for them, and re-layouts  1.25 us (1%)
    pallas_call x1, Pallas kernels, factorise(): pl.pallas_call(functools.partial(factor_kernel, 1.0 / total_rows), in_spe...  25.8 us
    ppermute x10, starting transfers between devices, shards(): lax.ppermute(chunk, 'rows', [(i, i ^ k) for i in range(groups)])  25.5 us
    ppermute x10, waiting for transfers between devices, shards(): lax.ppermute(chunk, 'rows', [(i, i ^ k) for i in range(groups)])  20.4 us
    all_to_all x1, blocking collectives, scatter_sum(): lax.all_to_all(packed, axes, split_axis=0, concat_axis=0, axis_index_grou...  13.5 us
    all_to_all x1, blocking collectives, gather_pieces(): lax.all_to_all(copies, axes, split_axis=0, concat_axis=0, axis_index_grou...  13.5 us
    pallas_call x1, Pallas kernels, regroup(): pl.pallas_call(functools.partial(regroup_kernel, groups, per_bucket), in_...  10.3 us
    pallas_call x2, Pallas kernels, whiten(): pl.pallas_call(functools.partial(whiten_kernel, tuple(steps), len(extra))...  6.31 us
    pallas_call x1, Pallas kernels, gram(): pl.pallas_call(functools.partial(gram_kernel, groups), in_specs=[vmem] *...  5.21 us
  transfers between devices with their start and end apart: 10, of which 5 were waited for; matrix products, arithmetic and copies ran while one was open for 1% of the time, Pallas kernels for 28%

profile of v6, /device:TPU:8, one launch (start us, length us, event | category | flops | bytes accessed | tf_op | source)
XLA Modules:
  0.0 124.3 jit_solution(7688038802568818243)
XLA Ops:
  0.6 10.3 %shard_map.68 = (f32[256,512]{1,0:T(8,128)}, f32[256,512]{1,0:T(8,128)}, f32[256,512]{1,0:T(8,128)}, f32[256,512]{1,0:T(8,128)}, f32[256,512]{1,0:T(8,128)}, /*i...) custom-call(s32[1]{0:T(128)} %bitcast.2.me_ref, s32[16,128]{1,0:T(8,128)} %bitcast.9, s32[16,128]{1,0:T(8,128)} %bitcast.10, ...), custom_call_target="tpu_custom_call" | custom-call | flops 1543503872 | bytes 8388608 | tf_op jit(solution)/shard_map/pallas_call | solution.py:166
  11.0 1.6 %collective-permute-start = (f32[256,512]{1,0:T(8,128)}, f32[256,512]{1,0:T(8,128)S(1)}, u32[]{:S(2)}, u32[]{:S(2)}) collective-permute-start(f32[256,512]{1,0:T(8,128)} %get-tuple-element.72), channel_id=1, source_target_pairs={{0,4},{4,0},{8,12},{12,8},{16,20},{20,16},{24,28},{28,24},{1,5},{5... | collective-permute-start | bytes 1572872 | tf_op jit(solution)/shard_map/ppermute | solution.py:405
  12.6 2.6 %collective-permute-start.1 = (f32[256,512]{1,0:T(8,128)}, f32[256,512]{1,0:T(8,128)S(1)}, u32[]{:S(2)}, u32[]{:S(2)}) collective-permute-start(f32[256,512]{1,0:T(8,128)} %get-tuple-element.75), channel_id=1, source_target_pairs={{0,16},{4,20},{8,24},{12,28},{16,0},{20,4},{24,8},{28,12},{1,17},{... | collective-permute-start | bytes 1572872 | tf_op jit(solution)/shard_map/ppermute | solution.py:405
  16.2 18.8 %conditional.2 = (f32[160,128]{1,0:T(8,128)S(1)}, f32[1280,128]{1,0:T(8,128)S(1)}) conditional(s32[]{:T(128)} %bitcast.3, () %tuple.31, (f32[512,512]{1,0:T(8,128)S(1)}, f32[256,512]{1,0:T(8,128)}, f32[256,512]{1,0:T(8,128)}, f32[256,512]{1,0:T(8,128)}, f32[256,512]{1,0:T(8,128)}, /*index=5*/f32[256,512]{1,0:T(8,128)}, f32[256,512]{1,0:T(8,128)}, ...), branch_computations={%region_0.0_spmd, %region_1.0_spmd} | conditional | flops 2147627008 | bytes 6242324 | solution.py:423
  16.2 5.2 %branch_1_fun.1 = (f32[1280,128]{1,0:T(8,128)S(1)}, f32[1280,128]{1,0:T(8,128)S(1)}) custom-call(f32[512,512]{1,0:T(8,128)S(1)} %get-tuple-element.32.prior_ref, f32[256,512]{1,0:T(8,128)} %get-tuple-element.33.rest_0_, f32[256,512]{1,0:T(8,128)} %get-tuple-element.34.rest_1_, f32[256,512]{1,0:T(8,128)} %get-tuple-element.35.rest_2_, ...), custom_call_target="tpu_custom_call" | custom-call | flops 2147483648 | bytes 4194304 | tf_op jit(solution)/shard_map/cond/branch_1_fun/pallas_call | solution.py:232
  21.5 13.5 %all_to_all.14 = f32[8,160,128]{2,1,0:T(8,128)S(1)} all-to-all(f32[8,160,128]{2,1,0:T(8,128)S(1)} %bitcast.7), channel_id=1, replica_groups={{0,1,2,3,4,5,6,7},{8,9,10,11,12,13,14,15},{16,17,18,19,20,21,22,23},{24..., dimensions={0} | all-to-all | bytes 1310720 | tf_op jit(solution)/shard_map/cond/branch_1_fun/all_to_all | solution.py:248
  35.0 2.5 %collective-permute-done.1.rest_2_ = f32[256,512]{1,0:T(8,128)S(1)} collective-permute-done((f32[256,512]{1,0:T(8,128)}, f32[256,512]{1,0:T(8,128)S(1)}, u32[]{:S(2)}, u32[]{:S(2)}) %collective-permute-start.1) | collective-permute-done | bytes 524320 | tf_op jit(solution)/shard_map/ppermute | solution.py:405
  37.5 3.6 %collective-permute-start.3 = (f32[160,128]{1,0:T(8,128)S(1)}, f32[160,128]{1,0:T(8,128)S(1)}, u32[]{:S(2)}, u32[]{:S(2)}) collective-permute-start(f32[160,128]{1,0:T(8,128)S(1)} %get-tuple-element.81), channel_id=1, source_target_pairs={{0,16},{4,20},{8,24},{12,28},{16,0},{20,4},{24,8},{28,12},{1,17},{... | collective-permute-start | bytes 245768 | tf_op jit(solution)/shard_map/ppermute | solution.py:405
  41.1 1.1 collective-permute-start.2
  42.2 1.5 %collective-permute-start.8 = (f32[256,512]{1,0:T(8,128)}, f32[256,512]{1,0:T(8,128)S(1)}, u32[]{:S(2)}, u32[]{:S(2)}) collective-permute-start(f32[256,512]{1,0:T(8,128)} %get-tuple-element.90), channel_id=1, source_target_pairs={{0,24},{4,28},{8,16},{12,20},{16,8},{20,12},{24,0},{28,4},{1,25},{... | collective-permute-start | bytes 1572872 | tf_op jit(solution)/shard_map/ppermute | solution.py:405
  43.7 2.9 %collective-permute-start.9 = (f32[256,512]{1,0:T(8,128)}, f32[256,512]{1,0:T(8,128)S(1)}, u32[]{:S(2)}, u32[]{:S(2)}) collective-permute-start(f32[256,512]{1,0:T(8,128)} %get-tuple-element.91), channel_id=1, source_target_pairs={{0,8},{4,12},{8,0},{12,4},{16,24},{20,28},{24,16},{28,20},{1,9},{5... | collective-permute-start | bytes 1572872 | tf_op jit(solution)/shard_map/ppermute | solution.py:405
  46.6 0.6 collective-permute-done.3
  47.3 1.8 %collective-permute-done.2 = f32[160,128]{1,0:T(8,128)S(1)} collective-permute-done((f32[160,128]{1,0:T(8,128)S(1)}, f32[160,128]{1,0:T(8,128)S(1)}, u32[]{:S(2)}, u32[]{:S(2)}) %collective-permute-start.2) | collective-permute-done | bytes 81952 | tf_op jit(solution)/shard_map/ppermute | solution.py:405
  49.1 15.2 %conditional.3 = (f32[1280,128]{1,0:T(8,128)S(1)}) conditional(s32[]{:T(128)} %bitcast.3, () %tuple.30, (f32[160,128]{1,0:T(8,128)S(1)}, f32[160,128]{1,0:T(8,128)S(1)}, f32[160,128]{1,0:T(8,128)S(1)}, f32[160,128]{1,0:T(8,128)S(1)}) %tuple.35), branch_computations={%region_3.0_spmd, %region_4.0_spmd} | conditional | flops 61440 | bytes 3440732 | solution.py:436
  49.1 0.6 copy-done
  49.7 1.0 add_add_fusion
  50.8 13.5 %all_to_all.15 = f32[8,160,128]{2,1,0:T(8,128)S(1)} all-to-all(f32[8,160,128]{2,1,0:T(8,128)S(1)} %broadcast_in_dim.2), channel_id=1, replica_groups={{0,1,2,3,4,5,6,7},{8,9,10,11,12,13,14,15},{16,17,18,19,20,21,22,23},{24..., dimensions={0} | all-to-all | bytes 1310720 | tf_op jit(solution)/shard_map/cond/branch_1_fun/all_to_all | solution.py:256
  64.3 10.1 %collective-permute-start.5 = (f32[256,512]{1,0:T(8,128)}, f32[256,512]{1,0:T(8,128)S(1)}, u32[]{:S(2)}, u32[]{:S(2)}) collective-permute-start(f32[256,512]{1,0:T(8,128)} %get-tuple-element.85), channel_id=1, source_target_pairs={{0,12},{4,8},{8,4},{12,0},{16,28},{20,24},{24,20},{28,16},{1,13},{... | collective-permute-start | bytes 1572872 | tf_op jit(solution)/shard_map/ppermute | solution.py:405
  74.4 2.1 %collective-permute-start.7 = (f32[256,512]{1,0:T(8,128)}, f32[256,512]{1,0:T(8,128)S(1)}, u32[]{:S(2)}, u32[]{:S(2)}) collective-permute-start(f32[256,512]{1,0:T(8,128)} %get-tuple-element.87), channel_id=1, source_target_pairs={{0,28},{4,24},{8,20},{12,16},{16,12},{20,8},{24,4},{28,0},{1,29},{... | collective-permute-start | bytes 1572872 | tf_op jit(solution)/shard_map/ppermute | solution.py:405
  76.5 25.8 %shard_map.69 = (f32[512,512]{1,0:T(8,128)}, bf16[512,512]{1,0:T(8,128)(2,1)S(1)}, bf16[512,512]{1,0:T(8,128)(2,1)S(1)}) custom-call(f32[1280,128]{1,0:T(8,128)S(1)} %get-tuple-element.97.sum_ref, f32[1280,128]{1,0:T(8,128)S(1)} %get-tuple-element.82.prior_ref), custom_call_target="tpu_custom_call" | custom-call | flops 1 | bytes 1 | tf_op jit(solution)/shard_map/pallas_call | solution.py:330
  102.3 4.1 %shard_map.70.rest_3_ = f32[2048,512]{1,0:T(8,128)} custom-call(s32[1]{0:T(128)} %bitcast.2.me_ref, bf16[512,512]{1,0:T(8,128)(2,1)S(1)} %get-tuple-element.83.high_ref, bf16[512,512]{1,0:T(8,128)(2,1)S(1)} %get-tuple-element.84.low_ref, f32[256,512]{1,0:T(8,128)} %get-tuple-element.71.rest_0_, f32[256,512]{1,0:T(8,128)S(1)} %collective-permute-done.rest_1_, ...), custom_call_target="tpu_custom_call" | custom-call | flops 1 | bytes 1 | tf_op jit(solution)/shard_map/pallas_call | solution.py:375
  106.4 3.1 %collective-permute-done.6.rest_1_ = f32[256,512]{1,0:T(8,128)S(1)} collective-permute-done((f32[256,512]{1,0:T(8,128)}, f32[256,512]{1,0:T(8,128)S(1)}, u32[]{:S(2)}, u32[]{:S(2)}) %collective-permute-start.6) | collective-permute-done | bytes 524320 | tf_op jit(solution)/shard_map/ppermute | solution.py:405
  109.5 12.4 %collective-permute-done.7.rest_2_ = f32[256,512]{1,0:T(8,128)S(1)} collective-permute-done((f32[256,512]{1,0:T(8,128)}, f32[256,512]{1,0:T(8,128)S(1)}, u32[]{:S(2)}, u32[]{:S(2)}) %collective-permute-start.7) | collective-permute-done | bytes 524320 | tf_op jit(solution)/shard_map/ppermute | solution.py:405
  121.9 2.2 %shard_map.71 = f32[2048,512]{1,0:T(8,128)} custom-call(s32[1]{0:T(128)} %bitcast.2.me_ref, bf16[512,512]{1,0:T(8,128)(2,1)S(1)} %get-tuple-element.83.high_ref, bf16[512,512]{1,0:T(8,128)(2,1)S(1)} %get-tuple-element.84.low_ref, f32[256,512]{1,0:T(8,128)S(1)} %collective-permute-done.5.rest_0_, ...), custom_call_target="tpu_custom_call", output_to_operand_aliasing={{}: (6, {})} | custom-call | flops 1 | bytes 1 | tf_op jit(solution)/shard_map/pallas_call | solution.py:375
  (17 shorter events, 0.7 us)
Async XLA Ops:
  0.6 14.5 %copy-start.3 = (f32[512,512]{1,0:T(8,128)S(1)}, f32[512,512]{1,0:T(8,128)}, u32[]{:S(2)}) copy-start(f32[512,512]{1,0:T(8,128)} %param.13) | copy-start | bytes 3145732
  11.0 24.0 %collective-permute-start = (f32[256,512]{1,0:T(8,128)}, f32[256,512]{1,0:T(8,128)S(1)}, u32[]{:S(2)}, u32[]{:S(2)}) collective-permute-start(f32[256,512]{1,0:T(8,128)} %get-tuple-element.72), channel_id=1, source_target_pairs={{0,4},{4,0},{8,12},{12,8},{16,20},{20,16},{24,28},{28,24},{1,5},{5... | collective-permute-start | bytes 1572872 | tf_op jit(solution)/shard_map/ppermute | solution.py:405
  12.6 24.9 %collective-permute-start.1 = (f32[256,512]{1,0:T(8,128)}, f32[256,512]{1,0:T(8,128)S(1)}, u32[]{:S(2)}, u32[]{:S(2)}) collective-permute-start(f32[256,512]{1,0:T(8,128)} %get-tuple-element.75), channel_id=1, source_target_pairs={{0,16},{4,20},{8,24},{12,28},{16,0},{20,4},{24,8},{28,12},{1,17},{... | collective-permute-start | bytes 1572872 | tf_op jit(solution)/shard_map/ppermute | solution.py:405
  37.5 9.1 %collective-permute-start.4 = (f32[160,128]{1,0:T(8,128)S(1)}, f32[160,128]{1,0:T(8,128)S(1)}, u32[]{:S(2)}, u32[]{:S(2)}) collective-permute-start(f32[160,128]{1,0:T(8,128)S(1)} %get-tuple-element.81), channel_id=1, source_target_pairs={{0,24},{4,28},{8,16},{12,20},{16,8},{20,12},{24,0},{28,4},{1,25},{... | collective-permute-start | bytes 245768 | tf_op jit(solution)/shard_map/ppermute | solution.py:405
  37.5 9.8 %collective-permute-start.3 = (f32[160,128]{1,0:T(8,128)S(1)}, f32[160,128]{1,0:T(8,128)S(1)}, u32[]{:S(2)}, u32[]{:S(2)}) collective-permute-start(f32[160,128]{1,0:T(8,128)S(1)} %get-tuple-element.81), channel_id=1, source_target_pairs={{0,16},{4,20},{8,24},{12,28},{16,0},{20,4},{24,8},{28,12},{1,17},{... | collective-permute-start | bytes 245768 | tf_op jit(solution)/shard_map/ppermute | solution.py:405
  41.1 8.0 %collective-permute-start.2 = (f32[160,128]{1,0:T(8,128)S(1)}, f32[160,128]{1,0:T(8,128)S(1)}, u32[]{:S(2)}, u32[]{:S(2)}) collective-permute-start(f32[160,128]{1,0:T(8,128)S(1)} %get-tuple-element.81), channel_id=1, source_target_pairs={{0,8},{4,12},{8,0},{12,4},{16,24},{20,28},{24,16},{28,20},{1,9},{5... | collective-permute-start | bytes 245768 | tf_op jit(solution)/shard_map/ppermute | solution.py:405
  42.2 60.1 %collective-permute-start.8 = (f32[256,512]{1,0:T(8,128)}, f32[256,512]{1,0:T(8,128)S(1)}, u32[]{:S(2)}, u32[]{:S(2)}) collective-permute-start(f32[256,512]{1,0:T(8,128)} %get-tuple-element.90), channel_id=1, source_target_pairs={{0,24},{4,28},{8,16},{12,20},{16,8},{20,12},{24,0},{28,4},{1,25},{... | collective-permute-start | bytes 1572872 | tf_op jit(solution)/shard_map/ppermute | solution.py:405
  43.7 58.6 %collective-permute-start.9 = (f32[256,512]{1,0:T(8,128)}, f32[256,512]{1,0:T(8,128)S(1)}, u32[]{:S(2)}, u32[]{:S(2)}) collective-permute-start(f32[256,512]{1,0:T(8,128)} %get-tuple-element.91), channel_id=1, source_target_pairs={{0,8},{4,12},{8,0},{12,4},{16,24},{20,28},{24,16},{28,20},{1,9},{5... | collective-permute-start | bytes 1572872 | tf_op jit(solution)/shard_map/ppermute | solution.py:405
  49.1 0.6 copy-start
  49.1 0.7 copy-start.1
  49.1 0.7 copy-start.2
  64.3 42.1 %collective-permute-start.5 = (f32[256,512]{1,0:T(8,128)}, f32[256,512]{1,0:T(8,128)S(1)}, u32[]{:S(2)}, u32[]{:S(2)}) collective-permute-start(f32[256,512]{1,0:T(8,128)} %get-tuple-element.85), channel_id=1, source_target_pairs={{0,12},{4,8},{8,4},{12,0},{16,28},{20,24},{24,20},{28,16},{1,13},{... | collective-permute-start | bytes 1572872 | tf_op jit(solution)/shard_map/ppermute | solution.py:405
  74.4 35.1 %collective-permute-start.6 = (f32[256,512]{1,0:T(8,128)}, f32[256,512]{1,0:T(8,128)S(1)}, u32[]{:S(2)}, u32[]{:S(2)}) collective-permute-start(f32[256,512]{1,0:T(8,128)} %get-tuple-element.86), channel_id=1, source_target_pairs={{0,20},{4,16},{8,28},{12,24},{16,4},{20,0},{24,12},{28,8},{1,21},{... | collective-permute-start | bytes 1572872 | tf_op jit(solution)/shard_map/ppermute | solution.py:405
  74.4 47.5 %collective-permute-start.7 = (f32[256,512]{1,0:T(8,128)}, f32[256,512]{1,0:T(8,128)S(1)}, u32[]{:S(2)}, u32[]{:S(2)}) collective-permute-start(f32[256,512]{1,0:T(8,128)} %get-tuple-element.87), channel_id=1, source_target_pairs={{0,28},{4,24},{8,20},{12,16},{16,12},{20,8},{24,4},{28,0},{1,29},{... | collective-permute-start | bytes 1572872 | tf_op jit(solution)/shard_map/ppermute | solution.py:405

commit v7 on v6

--- a/solution.py
+++ b/solution.py
@@ -59,7 +59,7 @@
     blocks, block = place_ref.shape
     wide = block // LANES
     sensors = sigma_ref.shape[1]
-    padded, state = sorted_ref.shape
+    _, padded, state = sorted_ref.shape
     cells = blocks * groups
     last_tile = per_bucket // SUB - 1
     most = min(7, last_tile + 2)
@@ -109,11 +109,10 @@
         [jnp.sum(spot[s * groups : (s + 1) * groups], axis=0, keepdims=True) for s in range(blocks)],
         axis=0,
     )
-    copy.wait()
     sub_row = iota((SUB, state), 0)
     tile = lambda t: pl.ds(pl.multiple_of(t * SUB, SUB), SUB)
 
-    def body(s, carry):
+    def sort_block(s, into):
         place = place_ref[pl.ds(s, 1), :]
         moves = (iota((padded, block), 0) == place).astype(F32).astype(BF16)
         ids = [ids_ref[pl.ds(s * wide + i, 1), :] for i in range(wide)]
@@ -125,34 +124,52 @@
         rows = pl.ds(pl.multiple_of(s * block, block), block)
         scaled = obs_ref[rows, :] * jnp.concatenate([scale] * (state // LANES), axis=1)
         high, low = split(scaled)
-        sorted_ref[...] = dot(moves, high) + dot(moves, low)
-        longest = 0
+        into[...] = dot(moves, high) + dot(moves, low)
+
+    def run(cell):
+        return [meta_smem[cell, i] for i in range(4)]
+
+    def place_runs(s, source):
         for v in range(groups):
-            cell = s * groups + v
-            kept, target = meta_smem[cell, 0], meta_smem[cell, 1]
-            first, final = meta_smem[cell, 2], meta_smem[cell, 3]
-            longest = jnp.maximum(longest, final)
+            kept, target, first, final = run(s * groups + v)
             old = outs[v][tile(target), :]
             for t in reversed(range(1, most)):
                 t = jnp.minimum(t, final)
-                outs[v][tile(target + t), :] = sorted_ref[tile(first + t), :]
-            outs[v][tile(target), :] = jnp.where(sub_row < kept, old, sorted_ref[tile(first), :])
-
-        @pl.when(longest >= most)
-        def _():
-            for v in range(groups):
-                cell = s * groups + v
-                target, first, final = (meta_smem[cell, i] for i in (1, 2, 3))
-
-                def longer(t, carry, v=v, target=target, first=first):
-                    outs[v][tile(target + t), :] = sorted_ref[tile(first + t), :]
-                    return carry
-
-                lax.fori_loop(most, final + 1, longer, 0)
-
-        return carry
-
-    lax.fori_loop(0, blocks, body, 0)
+                outs[v][tile(target + t), :] = source[tile(first + t), :]
+            outs[v][tile(target), :] = jnp.where(sub_row < kept, old, source[tile(first), :])
+
+    def place_rest(s, source):
+        for v in range(groups):
+            _, target, first, final = run(s * groups + v)
+
+            def longer(t, carry, v=v, target=target, first=first):
+                outs[v][tile(target + t), :] = source[tile(first + t), :]
+                return carry
+
+            lax.fori_loop(most, final + 1, longer, 0)
+
+    longest = jnp.max(final)
+    unroll = groups <= 8
+
+    @pl.when((longest < most) & unroll)
+    def _():
+        for s in range(blocks if unroll else 0):
+            sort_block(s, sorted_ref.at[s % 2])
+            if s == 0:
+                copy.wait()
+            place_runs(s, sorted_ref.at[s % 2])
+
+    @pl.when((longest >= most) | (not unroll))
+    def _():
+        copy.wait()
+
+        def body(s, carry):
+            sort_block(s, sorted_ref.at[0])
+            place_runs(s, sorted_ref.at[0])
+            place_rest(s, sorted_ref.at[0])
+            return carry
+
+        lax.fori_loop(0, blocks, body, 0)
 
 
 def regroup(observations, sensor_ids, sensor_sigma, buckets, me, groups):
@@ -174,7 +191,7 @@
             pltpu.VMEM((rows, state), F32),
             pltpu.VMEM((blocks, block), I32),
             pltpu.VMEM((blocks * groups, LANES), I32),
-            pltpu.VMEM((padded, state), F32),
+            pltpu.VMEM((2, padded, state), F32),
             pltpu.VMEM((sensors, LANES), F32),
             pltpu.SMEM((blocks * groups, LANES), I32),
             pltpu.SemaphoreType.DMA((4 + blocks,)),
@@ -423,16 +440,16 @@
     piece, prior_gram = lax.cond(
         valid, first, lambda: (nothing(packed_rows // plane), nothing(packed_rows))
     )
-    for k in early:
-        piece, received[k] = behind(piece, received[k])
     across = [piece]
     for step in range(1, groups // 2):
         across.append(move(2 * step, piece))
-    for k in middle:
-        _, chunk = behind(piece, chunks[k])
-        received[k] = move(k, chunk)
     while len(across) > 1:
         across = [across[i] + across[i + 1] for i in range(0, len(across), 2)]
+    for k in middle:
+        _, chunk = behind(across[0], chunks[k])
+        received[k] = move(k, chunk)
+    for k in early:
+        across[0], received[k] = behind(across[0], received[k])
     summed = lax.cond(
         valid, lambda: gather_pieces(across[0], plane, planes), lambda: nothing(packed_rows)
     )
@@ -441,7 +458,7 @@
         received[k] = move(k, chunk)
     factor, high, low = factorise(summed, prior_gram, state, total_rows)
     out = None
-    for steps in ([0] + early + middle, late):
+    for steps in ([0] + early + middle, late[:-1], late[-1:]):
         out = whiten(me, high, low, steps, [received[k] for k in steps], out, rows_dev)
     return (out, factor)
 

time: 125 us -> 118 us (0.944)
  starting transfers between devices: 25.5 us -> 17.2 us
  waiting for transfers between devices: 20.4 us -> 24.2 us
    ppermute x10, starting transfers between devices: 25.5 us -> 17.2 us  [shards(): lax.ppermute(chunk, 'rows', [(i, i ^ k) for i in range(groups)])]
    ppermute x10, waiting for transfers between devices: 20.4 us -> 24.2 us  [shards(): lax.ppermute(chunk, 'rows', [(i, i ^ k) for i in range(groups)])]
    pallas_call x1, Pallas kernels: 10.3 us -> 8.86 us  [regroup(): pl.pallas_call(functools.partial(regroup_kernel, groups, per_bucket), in_...]
    pallas_call x2 -> x3, Pallas kernels: 6.31 us -> 7.33 us  [whiten(): pl.pallas_call(functools.partial(whiten_kernel, tuple(steps), len(extra))...]
  transfers between devices with their start and end apart: 10 -> 10, of which waited for: 5 -> 3; matrix products, arithmetic and copies ran while one was open for 1% -> 1% of each run, Pallas kernels for 28% -> 31%
where the time goes in v7:
time: 118 us
  Pallas kernels  47.2 us (40%)
  blocking collectives  26.9 us (23%)
  waiting for transfers between devices  24.2 us (21%)
  starting transfers between devices  17.2 us (15%)
  between operations  1.44 us (1%)
    pallas_call x1, Pallas kernels, factorise(): pl.pallas_call(functools.partial(factor_kernel, 1.0 / total_rows), in_spe...  25.8 us
    ppermute x10, waiting for transfers between devices, shards(): lax.ppermute(chunk, 'rows', [(i, i ^ k) for i in range(groups)])  24.2 us
    ppermute x10, starting transfers between devices, shards(): lax.ppermute(chunk, 'rows', [(i, i ^ k) for i in range(groups)])  17.2 us
    all_to_all x1, blocking collectives, gather_pieces(): lax.all_to_all(copies, axes, split_axis=0, concat_axis=0, axis_index_grou...  13.5 us
    all_to_all x1, blocking collectives, scatter_sum(): lax.all_to_all(packed, axes, split_axis=0, concat_axis=0, axis_index_grou...  13.5 us
    pallas_call x1, Pallas kernels, regroup(): pl.pallas_call(functools.partial(regroup_kernel, groups, per_bucket), in_...  8.86 us
    pallas_call x3, Pallas kernels, whiten(): pl.pallas_call(functools.partial(whiten_kernel, tuple(steps), len(extra))...  7.33 us
    pallas_call x1, Pallas kernels, gram(): pl.pallas_call(functools.partial(gram_kernel, groups), in_specs=[vmem] *...  5.21 us
  transfers between devices with their start and end apart: 10, of which 3 were waited for; matrix products, arithmetic and copies ran while one was open for 1% of the time, Pallas kernels for 31%

profile of v7, /device:TPU:8, one launch (start us, length us, event | category | flops | bytes accessed | tf_op | source)
XLA Modules:
  0.0 117.6 jit_solution(8594928721616135160)
XLA Ops:
  0.6 8.9 %shard_map.68 = (f32[256,512]{1,0:T(8,128)}, f32[256,512]{1,0:T(8,128)}, f32[256,512]{1,0:T(8,128)}, f32[256,512]{1,0:T(8,128)}, f32[256,512]{1,0:T(8,128)}, /*i...) custom-call(s32[1]{0:T(128)} %bitcast.2.me_ref, s32[16,128]{1,0:T(8,128)} %bitcast.9, s32[16,128]{1,0:T(8,128)} %bitcast.10, ...), custom_call_target="tpu_custom_call" | custom-call | flops 1543503872 | bytes 8388608 | tf_op jit(solution)/shard_map/pallas_call | solution.py:183
  9.5 1.6 %collective-permute-start.3 = (f32[256,512]{1,0:T(8,128)}, f32[256,512]{1,0:T(8,128)S(1)}, u32[]{:S(2)}, u32[]{:S(2)}) collective-permute-start(f32[256,512]{1,0:T(8,128)} %get-tuple-element.58), channel_id=1, source_target_pairs={{0,4},{4,0},{8,12},{12,8},{16,20},{20,16},{24,28},{28,24},{1,5},{5... | collective-permute-start | bytes 1572872 | tf_op jit(solution)/shard_map/ppermute | solution.py:422
  11.1 2.6 %collective-permute-start.4 = (f32[256,512]{1,0:T(8,128)}, f32[256,512]{1,0:T(8,128)S(1)}, u32[]{:S(2)}, u32[]{:S(2)}) collective-permute-start(f32[256,512]{1,0:T(8,128)} %get-tuple-element.61), channel_id=1, source_target_pairs={{0,16},{4,20},{8,24},{12,28},{16,0},{20,4},{24,8},{28,12},{1,17},{... | collective-permute-start | bytes 1572872 | tf_op jit(solution)/shard_map/ppermute | solution.py:422
  13.7 0.5 slice.3
  14.7 18.7 %conditional.2 = (f32[160,128]{1,0:T(8,128)S(1)}, f32[1280,128]{1,0:T(8,128)S(1)}) conditional(s32[]{:T(128)} %bitcast.3, () %tuple.30, (f32[512,512]{1,0:T(8,128)S(1)}, f32[256,512]{1,0:T(8,128)}, f32[256,512]{1,0:T(8,128)}, f32[256,512]{1,0:T(8,128)}, f32[256,512]{1,0:T(8,128)}, /*index=5*/f32[256,512]{1,0:T(8,128)}, f32[256,512]{1,0:T(8,128)}, ...), branch_computations={%region_0.0_spmd, %region_1.0_spmd} | conditional | flops 2147627008 | bytes 6242324 | solution.py:440
  14.8 5.2 %branch_1_fun.1 = (f32[1280,128]{1,0:T(8,128)S(1)}, f32[1280,128]{1,0:T(8,128)S(1)}) custom-call(f32[512,512]{1,0:T(8,128)S(1)} %get-tuple-element.22.prior_ref, f32[256,512]{1,0:T(8,128)} %get-tuple-element.23.rest_0_, f32[256,512]{1,0:T(8,128)} %get-tuple-element.24.rest_1_, f32[256,512]{1,0:T(8,128)} %get-tuple-element.25.rest_2_, ...), custom_call_target="tpu_custom_call" | custom-call | flops 2147483648 | bytes 4194304 | tf_op jit(solution)/shard_map/cond/branch_1_fun/pallas_call | solution.py:249
  20.0 13.5 %all_to_all.14 = f32[8,160,128]{2,1,0:T(8,128)S(1)} all-to-all(f32[8,160,128]{2,1,0:T(8,128)S(1)} %bitcast.7), channel_id=1, replica_groups={{0,1,2,3,4,5,6,7},{8,9,10,11,12,13,14,15},{16,17,18,19,20,21,22,23},{24..., dimensions={0} | all-to-all | bytes 1310720 | tf_op jit(solution)/shard_map/cond/branch_1_fun/all_to_all | solution.py:265
  33.5 0.1 collective-permute-start.2
  33.6 2.8 %collective-permute-start.1 = (f32[160,128]{1,0:T(8,128)S(1)}, f32[160,128]{1,0:T(8,128)S(1)}, u32[]{:S(2)}, u32[]{:S(2)}) collective-permute-start(f32[160,128]{1,0:T(8,128)S(1)} %get-tuple-element.65), channel_id=1, source_target_pairs={{0,16},{4,20},{8,24},{12,28},{16,0},{20,4},{24,8},{28,12},{1,17},{... | collective-permute-start | bytes 245768 | tf_op jit(solution)/shard_map/ppermute | solution.py:422
  36.4 0.7 collective-permute-start
  37.0 5.1 %collective-permute-done.2 = f32[160,128]{1,0:T(8,128)S(1)} collective-permute-done((f32[160,128]{1,0:T(8,128)S(1)}, f32[160,128]{1,0:T(8,128)S(1)}, u32[]{:S(2)}, u32[]{:S(2)}) %collective-permute-start.2) | collective-permute-done | bytes 81952 | tf_op jit(solution)/shard_map/ppermute | solution.py:422
  42.1 0.8 collective-permute-done.1
  42.9 0.9 collective-permute-start.8
  43.8 4.0 %collective-permute-start.9 = (f32[256,512]{1,0:T(8,128)}, f32[256,512]{1,0:T(8,128)S(1)}, u32[]{:S(2)}, u32[]{:S(2)}) collective-permute-start(f32[256,512]{1,0:T(8,128)} %get-tuple-element.77), channel_id=1, source_target_pairs={{0,8},{4,12},{8,0},{12,4},{16,24},{20,28},{24,16},{28,20},{1,9},{5... | collective-permute-start | bytes 1572872 | tf_op jit(solution)/shard_map/ppermute | solution.py:422
  47.9 13.5 %conditional.3 = (f32[1280,128]{1,0:T(8,128)S(1)}) conditional(s32[]{:T(128)} %bitcast.3, () %tuple.29, f32[160,128]{1,0:T(8,128)S(1)} %add_add_fusion), branch_computations={%region_3.0_spmd, %region_4.0_spmd} | conditional | bytes 2048008 | solution.py:453
  47.9 13.5 %all_to_all.15 = f32[8,160,128]{2,1,0:T(8,128)S(1)} all-to-all(f32[8,160,128]{2,1,0:T(8,128)S(1)} %broadcast_in_dim.2), channel_id=1, replica_groups={{0,1,2,3,4,5,6,7},{8,9,10,11,12,13,14,15},{16,17,18,19,20,21,22,23},{24..., dimensions={0} | all-to-all | bytes 1310720 | tf_op jit(solution)/shard_map/cond/branch_1_fun/all_to_all | solution.py:273
  61.4 0.3 collective-permute-start.6
  61.7 1.5 %collective-permute-start.7 = (f32[256,512]{1,0:T(8,128)}, f32[256,512]{1,0:T(8,128)S(1)}, u32[]{:S(2)}, u32[]{:S(2)}) collective-permute-start(f32[256,512]{1,0:T(8,128)} %get-tuple-element.73), channel_id=1, source_target_pairs={{0,20},{4,16},{8,28},{12,24},{16,4},{20,0},{24,12},{28,8},{1,21},{... | collective-permute-start | bytes 1572872 | tf_op jit(solution)/shard_map/ppermute | solution.py:422
  63.2 2.8 %collective-permute-start.5 = (f32[256,512]{1,0:T(8,128)}, f32[256,512]{1,0:T(8,128)S(1)}, u32[]{:S(2)}, u32[]{:S(2)}) collective-permute-start(f32[256,512]{1,0:T(8,128)} %get-tuple-element.71), channel_id=1, source_target_pairs={{0,28},{4,24},{8,20},{12,16},{16,12},{20,8},{24,4},{28,0},{1,29},{... | collective-permute-start | bytes 1572872 | tf_op jit(solution)/shard_map/ppermute | solution.py:422
  66.0 25.8 %shard_map.69 = (f32[512,512]{1,0:T(8,128)}, bf16[512,512]{1,0:T(8,128)(2,1)S(1)}, bf16[512,512]{1,0:T(8,128)(2,1)S(1)}) custom-call(f32[1280,128]{1,0:T(8,128)S(1)} %get-tuple-element.83.sum_ref, f32[1280,128]{1,0:T(8,128)S(1)} %get-tuple-element.68.prior_ref), custom_call_target="tpu_custom_call" | custom-call | flops 1 | bytes 1 | tf_op jit(solution)/shard_map/pallas_call | solution.py:347
  91.8 4.1 %shard_map.70.rest_2_ = f32[2048,512]{1,0:T(8,128)} custom-call(s32[1]{0:T(128)} %bitcast.2.me_ref, bf16[512,512]{1,0:T(8,128)(2,1)S(1)} %get-tuple-element.69.high_ref, bf16[512,512]{1,0:T(8,128)(2,1)S(1)} %get-tuple-element.70.low_ref, f32[256,512]{1,0:T(8,128)} %get-tuple-element.57.rest_0_, f32[256,512]{1,0:T(8,128)S(1)} %collective-permute-done.3.rest_1_, ...), custom_call_target="tpu_custom_call" | custom-call | flops 1 | bytes 1 | tf_op jit(solution)/shard_map/pallas_call | solution.py:392
  96.0 1.8 %shard_map.71.rest_1_ = f32[2048,512]{1,0:T(8,128)} custom-call(s32[1]{0:T(128)} %bitcast.2.me_ref, bf16[512,512]{1,0:T(8,128)(2,1)S(1)} %get-tuple-element.69.high_ref, bf16[512,512]{1,0:T(8,128)(2,1)S(1)} %get-tuple-element.70.low_ref, f32[256,512]{1,0:T(8,128)S(1)} %collective-permute-done.6.rest_0_, ...), custom_call_target="tpu_custom_call", output_to_operand_aliasing={{}: (5, {})} | custom-call | flops 1 | bytes 1 | tf_op jit(solution)/shard_map/pallas_call | solution.py:392
  97.8 18.3 %collective-permute-done.5.rest_0_ = f32[256,512]{1,0:T(8,128)S(1)} collective-permute-done((f32[256,512]{1,0:T(8,128)}, f32[256,512]{1,0:T(8,128)S(1)}, u32[]{:S(2)}, u32[]{:S(2)}) %collective-permute-start.5) | collective-permute-done | bytes 524320 | tf_op jit(solution)/shard_map/ppermute | solution.py:422
  116.1 1.4 %shard_map.72 = f32[2048,512]{1,0:T(8,128)} custom-call(s32[1]{0:T(128)} %bitcast.2.me_ref, bf16[512,512]{1,0:T(8,128)(2,1)S(1)} %get-tuple-element.69.high_ref, bf16[512,512]{1,0:T(8,128)(2,1)S(1)} %get-tuple-element.70.low_ref, f32[256,512]{1,0:T(8,128)S(1)} %collective-permute-done.5.rest_0_, ...), custom_call_target="tpu_custom_call", output_to_operand_aliasing={{}: (4, {})} | custom-call | flops 1 | bytes 1 | tf_op jit(solution)/shard_map/pallas_call | solution.py:392
  (12 shorter events, 0.1 us)
Async XLA Ops:
  0.6 13.0 %copy-start = (f32[512,512]{1,0:T(8,128)S(1)}, f32[512,512]{1,0:T(8,128)}, u32[]{:S(2)}) copy-start(f32[512,512]{1,0:T(8,128)} %param.13) | copy-start | bytes 3145732
  9.5 38.3 %collective-permute-start.3 = (f32[256,512]{1,0:T(8,128)}, f32[256,512]{1,0:T(8,128)S(1)}, u32[]{:S(2)}, u32[]{:S(2)}) collective-permute-start(f32[256,512]{1,0:T(8,128)} %get-tuple-element.58), channel_id=1, source_target_pairs={{0,4},{4,0},{8,12},{12,8},{16,20},{20,16},{24,28},{28,24},{1,5},{5... | collective-permute-start | bytes 1572872 | tf_op jit(solution)/shard_map/ppermute | solution.py:422
  11.1 36.8 %collective-permute-start.4 = (f32[256,512]{1,0:T(8,128)}, f32[256,512]{1,0:T(8,128)S(1)}, u32[]{:S(2)}, u32[]{:S(2)}) collective-permute-start(f32[256,512]{1,0:T(8,128)} %get-tuple-element.61), channel_id=1, source_target_pairs={{0,16},{4,20},{8,24},{12,28},{16,0},{20,4},{24,8},{28,12},{1,17},{... | collective-permute-start | bytes 1572872 | tf_op jit(solution)/shard_map/ppermute | solution.py:422
  33.5 8.6 %collective-permute-start.2 = (f32[160,128]{1,0:T(8,128)S(1)}, f32[160,128]{1,0:T(8,128)S(1)}, u32[]{:S(2)}, u32[]{:S(2)}) collective-permute-start(f32[160,128]{1,0:T(8,128)S(1)} %get-tuple-element.65), channel_id=1, source_target_pairs={{0,24},{4,28},{8,16},{12,20},{16,8},{20,12},{24,0},{28,4},{1,25},{... | collective-permute-start | bytes 245768 | tf_op jit(solution)/shard_map/ppermute | solution.py:422
  33.6 9.3 %collective-permute-start.1 = (f32[160,128]{1,0:T(8,128)S(1)}, f32[160,128]{1,0:T(8,128)S(1)}, u32[]{:S(2)}, u32[]{:S(2)}) collective-permute-start(f32[160,128]{1,0:T(8,128)S(1)} %get-tuple-element.65), channel_id=1, source_target_pairs={{0,16},{4,20},{8,24},{12,28},{16,0},{20,4},{24,8},{28,12},{1,17},{... | collective-permute-start | bytes 245768 | tf_op jit(solution)/shard_map/ppermute | solution.py:422
  36.4 6.5 %collective-permute-start = (f32[160,128]{1,0:T(8,128)S(1)}, f32[160,128]{1,0:T(8,128)S(1)}, u32[]{:S(2)}, u32[]{:S(2)}) collective-permute-start(f32[160,128]{1,0:T(8,128)S(1)} %get-tuple-element.65), channel_id=1, source_target_pairs={{0,8},{4,12},{8,0},{12,4},{16,24},{20,28},{24,16},{28,20},{1,9},{5... | collective-permute-start | bytes 245768 | tf_op jit(solution)/shard_map/ppermute | solution.py:422
  42.9 48.9 %collective-permute-start.8 = (f32[256,512]{1,0:T(8,128)}, f32[256,512]{1,0:T(8,128)S(1)}, u32[]{:S(2)}, u32[]{:S(2)}) collective-permute-start(f32[256,512]{1,0:T(8,128)} %get-tuple-element.76), channel_id=1, source_target_pairs={{0,24},{4,28},{8,16},{12,20},{16,8},{20,12},{24,0},{28,4},{1,25},{... | collective-permute-start | bytes 1572872 | tf_op jit(solution)/shard_map/ppermute | solution.py:422
  43.8 48.0 %collective-permute-start.9 = (f32[256,512]{1,0:T(8,128)}, f32[256,512]{1,0:T(8,128)S(1)}, u32[]{:S(2)}, u32[]{:S(2)}) collective-permute-start(f32[256,512]{1,0:T(8,128)} %get-tuple-element.77), channel_id=1, source_target_pairs={{0,8},{4,12},{8,0},{12,4},{16,24},{20,28},{24,16},{28,20},{1,9},{5... | collective-permute-start | bytes 1572872 | tf_op jit(solution)/shard_map/ppermute | solution.py:422
  61.4 34.6 %collective-permute-start.6 = (f32[256,512]{1,0:T(8,128)}, f32[256,512]{1,0:T(8,128)S(1)}, u32[]{:S(2)}, u32[]{:S(2)}) collective-permute-start(f32[256,512]{1,0:T(8,128)} %get-tuple-element.72), channel_id=1, source_target_pairs={{0,12},{4,8},{8,4},{12,0},{16,28},{20,24},{24,20},{28,16},{1,13},{... | collective-permute-start | bytes 1572872 | tf_op jit(solution)/shard_map/ppermute | solution.py:422
  61.7 34.3 %collective-permute-start.7 = (f32[256,512]{1,0:T(8,128)}, f32[256,512]{1,0:T(8,128)S(1)}, u32[]{:S(2)}, u32[]{:S(2)}) collective-permute-start(f32[256,512]{1,0:T(8,128)} %get-tuple-element.73), channel_id=1, source_target_pairs={{0,20},{4,16},{8,28},{12,24},{16,4},{20,0},{24,12},{28,8},{1,21},{... | collective-permute-start | bytes 1572872 | tf_op jit(solution)/shard_map/ppermute | solution.py:422
  63.2 52.9 %collective-permute-start.5 = (f32[256,512]{1,0:T(8,128)}, f32[256,512]{1,0:T(8,128)S(1)}, u32[]{:S(2)}, u32[]{:S(2)}) collective-permute-start(f32[256,512]{1,0:T(8,128)} %get-tuple-element.71), channel_id=1, source_target_pairs={{0,28},{4,24},{8,20},{12,16},{16,12},{20,8},{24,4},{28,0},{1,29},{... | collective-permute-start | bytes 1572872 | tf_op jit(solution)/shard_map/ppermute | solution.py:422

commit v8 on v7

--- a/solution.py
+++ b/solution.py
@@ -224,20 +224,31 @@
         )
 
 
+def fetch_all(sources, held, sems):
+    copies = []
+    for n, source in enumerate(sources):
+        copy = pltpu.make_async_copy(source, held.at[n], sems.at[n])
+        copy.start()
+        copies.append(copy)
+    return copies
+
+
 def gram_kernel(groups, prior_ref, *rest):
     chunks = rest[:groups]
-    out_ref, prior_out_ref, both_ref, pair_ref = rest[groups:]
+    out_ref, prior_out_ref, both_ref, pair_ref, held, sems = rest[groups:]
     per_bucket, state = chunks[0].shape
-    for k, chunk in enumerate(chunks):
+    copies = fetch_all(chunks, held, sems)
+    high, low = split(prior_ref[...])
+    both_ref[...] = dot_rows(high, jnp.concatenate([high, low], axis=1))
+    write_gram(both_ref, state, prior_out_ref)
+    for k, copy in enumerate(copies):
         rows = slice(k * per_bucket, (k + 1) * per_bucket)
-        high, low = split(chunk[...])
+        copy.wait()
+        high, low = split(held[k])
         pair_ref[rows, :state] = high
         pair_ref[rows, state:] = low
     both_ref[...] = dot_rows(pair_ref[:, :state], pair_ref[...])
     write_gram(both_ref, state, out_ref)
-    high, low = split(prior_ref[...])
-    both_ref[...] = dot_rows(high, jnp.concatenate([high, low], axis=1))
-    write_gram(both_ref, state, prior_out_ref)
 
 
 def gram(prior_factor, chunks):
@@ -248,10 +259,15 @@
     vmem = pl.BlockSpec(memory_space=pltpu.VMEM)
     return pl.pallas_call(
         functools.partial(gram_kernel, groups),
-        in_specs=[vmem] * (groups + 1),
+        in_specs=[vmem] + [pl.BlockSpec(memory_space=pl.ANY)] * groups,
         out_specs=[vmem] * 2,
         out_shape=[jax.ShapeDtypeStruct((packed, LANES), F32)] * 2,
-        scratch_shapes=[pltpu.VMEM((state, 2 * state), F32), pltpu.VMEM((rows, 2 * state), BF16)],
+        scratch_shapes=[
+            pltpu.VMEM((state, 2 * state), F32),
+            pltpu.VMEM((rows, 2 * state), BF16),
+            pltpu.VMEM((groups, per_bucket, state), F32),
+            pltpu.SemaphoreType.DMA((groups,)),
+        ],
         compiler_params=pltpu.CompilerParams(vmem_limit_bytes=24 * MIB),
         cost_estimate=pl.CostEstimate(
             flops=4 * rows * state * state, bytes_accessed=4 * rows * state, transcendentals=0
@@ -364,12 +380,14 @@
 def whiten_kernel(steps, aliased, me_ref, high_ref, low_ref, *rest):
     count = len(steps)
     chunks = rest[:count]
-    out_ref, held, sems = rest[count + aliased :]
+    out_ref, held, given, sems, given_sems = rest[count + aliased :]
     per_bucket = chunks[0].shape[0]
-    high, low = high_ref[...], low_ref[...]
+    fetches = fetch_all(chunks, given, given_sems)
     copies = []
     for n, k in enumerate(steps):
-        rows_high, rows_low = split(chunks[n][...])
+        fetches[n].wait()
+        rows_high, rows_low = split(given[n])
+        high, low = high_ref[...], low_ref[...]
         held[n] = dot(rows_high, high) + (dot(rows_high, low) + dot(rows_low, high))
         slot = me_ref[0] ^ k
         copy = pltpu.make_async_copy(
@@ -391,20 +409,19 @@
     extra = [] if out is None else [out]
     return pl.pallas_call(
         functools.partial(whiten_kernel, tuple(steps), len(extra)),
-        in_specs=[pl.BlockSpec(memory_space=pltpu.SMEM)]
-        + [vmem] * (2 + count)
-        + [anywhere] * len(extra),
+        in_specs=[pl.BlockSpec(memory_space=pltpu.SMEM), vmem, vmem]
+        + [anywhere] * (count + len(extra)),
         out_specs=anywhere,
         out_shape=jax.ShapeDtypeStruct((rows, state), F32),
         scratch_shapes=[
             pltpu.VMEM((count, per_bucket, state), F32),
+            pltpu.VMEM((count, per_bucket, state), F32),
+            pltpu.SemaphoreType.DMA((count,)),
             pltpu.SemaphoreType.DMA((count,)),
         ],
         input_output_aliases={3 + count: 0} if extra else {},
         compiler_params=pltpu.CompilerParams(vmem_limit_bytes=16 * MIB),
-        cost_estimate=pl.CostEstimate(
-            flops=1, bytes_accessed=1, transcendentals=0
-        ),
+        cost_estimate=pl.CostEstimate(flops=1, bytes_accessed=1, transcendentals=0),
     )(me.reshape(1), high, low, *chunks, *extra)
 
 
@@ -424,8 +441,8 @@
     plane = 2 * grp
     planes = [list(range(i, i + plane)) for i in range(0, groups * grp, plane)]
     early = [k for k in (1, 4) if k < groups]
-    middle = [k for k in (6, 2) if k < groups]
-    late = [k for k in range(1, groups) if k not in early + middle]
+    middle = [k for k in (2, 6) if k < groups]
+    late = [k for k in (5, 3, *range(7, groups)) if k < groups and k not in early + middle]
     received = {0: chunks[0]}
     valid = prior_factor[0, 0] > 0
     nothing = lambda rows: jnp.full((rows, LANES), jnp.nan, F32)

time: 118 us -> 117 us (level)
  transfers between devices with their start and end apart: 10 -> 10, of which waited for: 3 -> 4; matrix products, arithmetic and copies ran while one was open for 1% -> 1% of each run, Pallas kernels for 31% -> 32%
where the time goes in v8:
time: 117 us
  Pallas kernels  48 us (41%)
  blocking collectives  26.9 us (23%)
  waiting for transfers between devices  23.4 us (20%)
  starting transfers between devices  16.3 us (14%)
  between operations  1.42 us (1%)
    pallas_call x1, Pallas kernels, factorise(): pl.pallas_call(functools.partial(factor_kernel, 1.0 / total_rows), in_spe...  25.8 us
    ppermute x10, waiting for transfers between devices, shards(): lax.ppermute(chunk, 'rows', [(i, i ^ k) for i in range(groups)])  23.4 us
    ppermute x10, starting transfers between devices, shards(): lax.ppermute(chunk, 'rows', [(i, i ^ k) for i in range(groups)])  16.3 us
    all_to_all x1, blocking collectives, gather_pieces(): lax.all_to_all(copies, axes, split_axis=0, concat_axis=0, axis_index_grou...  13.5 us
    all_to_all x1, blocking collectives, scatter_sum(): lax.all_to_all(packed, axes, split_axis=0, concat_axis=0, axis_index_grou...  13.5 us
    pallas_call x1, Pallas kernels, regroup(): pl.pallas_call(functools.partial(regroup_kernel, groups, per_bucket), in_...  8.86 us
    pallas_call x3, Pallas kernels, whiten(): pl.pallas_call(functools.partial(whiten_kernel, tuple(steps), len(extra))...  8.49 us
    pallas_call x1, Pallas kernels, gram(): pl.pallas_call(functools.partial(gram_kernel, groups), in_specs=[vmem] +...  4.83 us
  transfers between devices with their start and end apart: 10, of which 4 were waited for; matrix products, arithmetic and copies ran while one was open for 1% of the time, Pallas kernels for 32%

profile of v8, /device:TPU:8, one launch (start us, length us, event | category | flops | bytes accessed | tf_op | source)
XLA Modules:
  0.0 116.7 jit_solution(5317296872469318076)
XLA Ops:
  0.6 8.9 %shard_map.68 = (f32[256,512]{1,0:T(8,128)}, f32[256,512]{1,0:T(8,128)}, f32[256,512]{1,0:T(8,128)}, f32[256,512]{1,0:T(8,128)}, f32[256,512]{1,0:T(8,128)}, /*i...) custom-call(s32[1]{0:T(128)} %bitcast.2.me_ref, s32[16,128]{1,0:T(8,128)} %bitcast.9, s32[16,128]{1,0:T(8,128)} %bitcast.10, ...), custom_call_target="tpu_custom_call" | custom-call | flops 1543503872 | bytes 8388608 | tf_op jit(solution)/shard_map/pallas_call | solution.py:183
  9.5 1.6 %collective-permute-start.3 = (f32[256,512]{1,0:T(8,128)}, f32[256,512]{1,0:T(8,128)S(1)}, u32[]{:S(2)}, u32[]{:S(2)}) collective-permute-start(f32[256,512]{1,0:T(8,128)} %get-tuple-element.58), channel_id=1, source_target_pairs={{0,4},{4,0},{8,12},{12,8},{16,20},{20,16},{24,28},{28,24},{1,5},{5... | collective-permute-start | bytes 1572872 | tf_op jit(solution)/shard_map/ppermute | solution.py:439
  11.1 2.6 %collective-permute-start.4 = (f32[256,512]{1,0:T(8,128)}, f32[256,512]{1,0:T(8,128)S(1)}, u32[]{:S(2)}, u32[]{:S(2)}) collective-permute-start(f32[256,512]{1,0:T(8,128)} %get-tuple-element.61), channel_id=1, source_target_pairs={{0,16},{4,20},{8,24},{12,28},{16,0},{20,4},{24,8},{28,12},{1,17},{... | collective-permute-start | bytes 1572872 | tf_op jit(solution)/shard_map/ppermute | solution.py:439
  13.7 0.5 slice.3
  14.7 18.4 %conditional.2 = (f32[160,128]{1,0:T(8,128)S(1)}, f32[1280,128]{1,0:T(8,128)S(1)}) conditional(s32[]{:T(128)} %bitcast.3, () %tuple.30, (f32[512,512]{1,0:T(8,128)S(1)}, f32[256,512]{1,0:T(8,128)}, f32[256,512]{1,0:T(8,128)}, f32[256,512]{1,0:T(8,128)}, f32[256,512]{1,0:T(8,128)}, /*index=5*/f32[256,512]{1,0:T(8,128)}, f32[256,512]{1,0:T(8,128)}, ...), branch_computations={%region_0.0_spmd, %region_1.0_spmd} | conditional | flops 2147627008 | bytes 6242324 | solution.py:457
  14.8 4.8 %branch_1_fun.1 = (f32[1280,128]{1,0:T(8,128)S(1)}, f32[1280,128]{1,0:T(8,128)S(1)}) custom-call(f32[512,512]{1,0:T(8,128)S(1)} %get-tuple-element.22.prior_ref, f32[256,512]{1,0:T(8,128)} %get-tuple-element.23.rest_0_, f32[256,512]{1,0:T(8,128)} %get-tuple-element.24.rest_1_, f32[256,512]{1,0:T(8,128)} %get-tuple-element.25.rest_2_, ...), custom_call_target="tpu_custom_call" | custom-call | flops 2147483648 | bytes 4194304 | tf_op jit(solution)/shard_map/cond/branch_1_fun/pallas_call | solution.py:260
  19.6 13.5 %all_to_all.14 = f32[8,160,128]{2,1,0:T(8,128)S(1)} all-to-all(f32[8,160,128]{2,1,0:T(8,128)S(1)} %bitcast.7), channel_id=1, replica_groups={{0,1,2,3,4,5,6,7},{8,9,10,11,12,13,14,15},{16,17,18,19,20,21,22,23},{24..., dimensions={0} | all-to-all | bytes 1310720 | tf_op jit(solution)/shard_map/cond/branch_1_fun/all_to_all | solution.py:281
  33.2 2.8 %collective-permute-start.1 = (f32[160,128]{1,0:T(8,128)S(1)}, f32[160,128]{1,0:T(8,128)S(1)}, u32[]{:S(2)}, u32[]{:S(2)}) collective-permute-start(f32[160,128]{1,0:T(8,128)S(1)} %get-tuple-element.65), channel_id=1, source_target_pairs={{0,16},{4,20},{8,24},{12,28},{16,0},{20,4},{24,8},{28,12},{1,17},{... | collective-permute-start | bytes 245768 | tf_op jit(solution)/shard_map/ppermute | solution.py:439
  36.0 0.7 collective-permute-start
  36.7 5.2 %collective-permute-done.2 = f32[160,128]{1,0:T(8,128)S(1)} collective-permute-done((f32[160,128]{1,0:T(8,128)S(1)}, f32[160,128]{1,0:T(8,128)S(1)}, u32[]{:S(2)}, u32[]{:S(2)}) %collective-permute-start.2) | collective-permute-done | bytes 81952 | tf_op jit(solution)/shard_map/ppermute | solution.py:439
  41.9 1.1 collective-permute-done.1
  42.9 1.4 %collective-permute-start.8 = (f32[256,512]{1,0:T(8,128)}, f32[256,512]{1,0:T(8,128)S(1)}, u32[]{:S(2)}, u32[]{:S(2)}) collective-permute-start(f32[256,512]{1,0:T(8,128)} %get-tuple-element.76), channel_id=1, source_target_pairs={{0,8},{4,12},{8,0},{12,4},{16,24},{20,28},{24,16},{28,20},{1,9},{5... | collective-permute-start | bytes 1572872 | tf_op jit(solution)/shard_map/ppermute | solution.py:439
  44.3 2.6 %collective-permute-start.9 = (f32[256,512]{1,0:T(8,128)}, f32[256,512]{1,0:T(8,128)S(1)}, u32[]{:S(2)}, u32[]{:S(2)}) collective-permute-start(f32[256,512]{1,0:T(8,128)} %get-tuple-element.77), channel_id=1, source_target_pairs={{0,24},{4,28},{8,16},{12,20},{16,8},{20,12},{24,0},{28,4},{1,25},{... | collective-permute-start | bytes 1572872 | tf_op jit(solution)/shard_map/ppermute | solution.py:439
  47.0 13.5 %conditional.3 = (f32[1280,128]{1,0:T(8,128)S(1)}) conditional(s32[]{:T(128)} %bitcast.3, () %tuple.29, f32[160,128]{1,0:T(8,128)S(1)} %add_add_fusion), branch_computations={%region_3.0_spmd, %region_4.0_spmd} | conditional | bytes 2048008 | solution.py:470
  47.0 13.5 %all_to_all.15 = f32[8,160,128]{2,1,0:T(8,128)S(1)} all-to-all(f32[8,160,128]{2,1,0:T(8,128)S(1)} %broadcast_in_dim.2), channel_id=1, replica_groups={{0,1,2,3,4,5,6,7},{8,9,10,11,12,13,14,15},{16,17,18,19,20,21,22,23},{24..., dimensions={0} | all-to-all | bytes 1310720 | tf_op jit(solution)/shard_map/cond/branch_1_fun/all_to_all | solution.py:289
  60.5 0.7 collective-permute-start.6
  61.2 1.7 %collective-permute-start.7 = (f32[256,512]{1,0:T(8,128)}, f32[256,512]{1,0:T(8,128)S(1)}, u32[]{:S(2)}, u32[]{:S(2)}) collective-permute-start(f32[256,512]{1,0:T(8,128)} %get-tuple-element.73), channel_id=1, source_target_pairs={{0,12},{4,8},{8,4},{12,0},{16,28},{20,24},{24,20},{28,16},{1,13},{... | collective-permute-start | bytes 1572872 | tf_op jit(solution)/shard_map/ppermute | solution.py:439
  62.9 2.3 %collective-permute-start.5 = (f32[256,512]{1,0:T(8,128)}, f32[256,512]{1,0:T(8,128)S(1)}, u32[]{:S(2)}, u32[]{:S(2)}) collective-permute-start(f32[256,512]{1,0:T(8,128)} %get-tuple-element.71), channel_id=1, source_target_pairs={{0,28},{4,24},{8,20},{12,16},{16,12},{20,8},{24,4},{28,0},{1,29},{... | collective-permute-start | bytes 1572872 | tf_op jit(solution)/shard_map/ppermute | solution.py:439
  65.1 25.8 %shard_map.69 = (f32[512,512]{1,0:T(8,128)}, bf16[512,512]{1,0:T(8,128)(2,1)S(1)}, bf16[512,512]{1,0:T(8,128)(2,1)S(1)}) custom-call(f32[1280,128]{1,0:T(8,128)S(1)} %get-tuple-element.83.sum_ref, f32[1280,128]{1,0:T(8,128)S(1)} %get-tuple-element.68.prior_ref), custom_call_target="tpu_custom_call" | custom-call | flops 1 | bytes 1 | tf_op jit(solution)/shard_map/pallas_call | solution.py:363
  90.9 4.9 %shard_map.70.rest_2_ = f32[2048,512]{1,0:T(8,128)} custom-call(s32[1]{0:T(128)} %bitcast.2.me_ref, bf16[512,512]{1,0:T(8,128)(2,1)S(1)} %get-tuple-element.69.high_ref, bf16[512,512]{1,0:T(8,128)(2,1)S(1)} %get-tuple-element.70.low_ref, f32[256,512]{1,0:T(8,128)} %get-tuple-element.57.rest_0_, f32[256,512]{1,0:T(8,128)S(1)} %collective-permute-done.3.rest_1_, ...), custom_call_target="tpu_custom_call" | custom-call | flops 1 | bytes 1 | tf_op jit(solution)/shard_map/pallas_call | solution.py:410
  95.9 8.7 %collective-permute-done.6.rest_0_ = f32[256,512]{1,0:T(8,128)S(1)} collective-permute-done((f32[256,512]{1,0:T(8,128)}, f32[256,512]{1,0:T(8,128)S(1)}, u32[]{:S(2)}, u32[]{:S(2)}) %collective-permute-start.6) | collective-permute-done | bytes 524320 | tf_op jit(solution)/shard_map/ppermute | solution.py:439
  104.6 2.1 %shard_map.71.rest_1_ = f32[2048,512]{1,0:T(8,128)} custom-call(s32[1]{0:T(128)} %bitcast.2.me_ref, bf16[512,512]{1,0:T(8,128)(2,1)S(1)} %get-tuple-element.69.high_ref, bf16[512,512]{1,0:T(8,128)(2,1)S(1)} %get-tuple-element.70.low_ref, f32[256,512]{1,0:T(8,128)S(1)} %collective-permute-done.6.rest_0_, ...), custom_call_target="tpu_custom_call", output_to_operand_aliasing={{}: (5, {})} | custom-call | flops 1 | bytes 1 | tf_op jit(solution)/shard_map/pallas_call | solution.py:410
  106.7 8.5 %collective-permute-done.5.rest_0_ = f32[256,512]{1,0:T(8,128)S(1)} collective-permute-done((f32[256,512]{1,0:T(8,128)}, f32[256,512]{1,0:T(8,128)S(1)}, u32[]{:S(2)}, u32[]{:S(2)}) %collective-permute-start.5) | collective-permute-done | bytes 524320 | tf_op jit(solution)/shard_map/ppermute | solution.py:439
  115.1 1.4 %shard_map.72 = f32[2048,512]{1,0:T(8,128)} custom-call(s32[1]{0:T(128)} %bitcast.2.me_ref, bf16[512,512]{1,0:T(8,128)(2,1)S(1)} %get-tuple-element.69.high_ref, bf16[512,512]{1,0:T(8,128)(2,1)S(1)} %get-tuple-element.70.low_ref, f32[256,512]{1,0:T(8,128)S(1)} %collective-permute-done.5.rest_0_, ...), custom_call_target="tpu_custom_call", output_to_operand_aliasing={{}: (4, {})} | custom-call | flops 1 | bytes 1 | tf_op jit(solution)/shard_map/pallas_call | solution.py:410
  (12 shorter events, 0.2 us)
Async XLA Ops:
  0.6 13.0 %copy-start = (f32[512,512]{1,0:T(8,128)S(1)}, f32[512,512]{1,0:T(8,128)}, u32[]{:S(2)}) copy-start(f32[512,512]{1,0:T(8,128)} %param.13) | copy-start | bytes 3145732
  9.5 37.4 %collective-permute-start.3 = (f32[256,512]{1,0:T(8,128)}, f32[256,512]{1,0:T(8,128)S(1)}, u32[]{:S(2)}, u32[]{:S(2)}) collective-permute-start(f32[256,512]{1,0:T(8,128)} %get-tuple-element.58), channel_id=1, source_target_pairs={{0,4},{4,0},{8,12},{12,8},{16,20},{20,16},{24,28},{28,24},{1,5},{5... | collective-permute-start | bytes 1572872 | tf_op jit(solution)/shard_map/ppermute | solution.py:439
  11.1 35.9 %collective-permute-start.4 = (f32[256,512]{1,0:T(8,128)}, f32[256,512]{1,0:T(8,128)S(1)}, u32[]{:S(2)}, u32[]{:S(2)}) collective-permute-start(f32[256,512]{1,0:T(8,128)} %get-tuple-element.61), channel_id=1, source_target_pairs={{0,16},{4,20},{8,24},{12,28},{16,0},{20,4},{24,8},{28,12},{1,17},{... | collective-permute-start | bytes 1572872 | tf_op jit(solution)/shard_map/ppermute | solution.py:439
  33.1 8.8 %collective-permute-start.2 = (f32[160,128]{1,0:T(8,128)S(1)}, f32[160,128]{1,0:T(8,128)S(1)}, u32[]{:S(2)}, u32[]{:S(2)}) collective-permute-start(f32[160,128]{1,0:T(8,128)S(1)} %get-tuple-element.65), channel_id=1, source_target_pairs={{0,24},{4,28},{8,16},{12,20},{16,8},{20,12},{24,0},{28,4},{1,25},{... | collective-permute-start | bytes 245768 | tf_op jit(solution)/shard_map/ppermute | solution.py:439
  33.2 9.7 %collective-permute-start.1 = (f32[160,128]{1,0:T(8,128)S(1)}, f32[160,128]{1,0:T(8,128)S(1)}, u32[]{:S(2)}, u32[]{:S(2)}) collective-permute-start(f32[160,128]{1,0:T(8,128)S(1)} %get-tuple-element.65), channel_id=1, source_target_pairs={{0,16},{4,20},{8,24},{12,28},{16,0},{20,4},{24,8},{28,12},{1,17},{... | collective-permute-start | bytes 245768 | tf_op jit(solution)/shard_map/ppermute | solution.py:439
  36.0 6.9 %collective-permute-start = (f32[160,128]{1,0:T(8,128)S(1)}, f32[160,128]{1,0:T(8,128)S(1)}, u32[]{:S(2)}, u32[]{:S(2)}) collective-permute-start(f32[160,128]{1,0:T(8,128)S(1)} %get-tuple-element.65), channel_id=1, source_target_pairs={{0,8},{4,12},{8,0},{12,4},{16,24},{20,28},{24,16},{28,20},{1,9},{5... | collective-permute-start | bytes 245768 | tf_op jit(solution)/shard_map/ppermute | solution.py:439
  42.9 48.0 %collective-permute-start.8 = (f32[256,512]{1,0:T(8,128)}, f32[256,512]{1,0:T(8,128)S(1)}, u32[]{:S(2)}, u32[]{:S(2)}) collective-permute-start(f32[256,512]{1,0:T(8,128)} %get-tuple-element.76), channel_id=1, source_target_pairs={{0,8},{4,12},{8,0},{12,4},{16,24},{20,28},{24,16},{28,20},{1,9},{5... | collective-permute-start | bytes 1572872 | tf_op jit(solution)/shard_map/ppermute | solution.py:439
  44.3 46.6 %collective-permute-start.9 = (f32[256,512]{1,0:T(8,128)}, f32[256,512]{1,0:T(8,128)S(1)}, u32[]{:S(2)}, u32[]{:S(2)}) collective-permute-start(f32[256,512]{1,0:T(8,128)} %get-tuple-element.77), channel_id=1, source_target_pairs={{0,24},{4,28},{8,16},{12,20},{16,8},{20,12},{24,0},{28,4},{1,25},{... | collective-permute-start | bytes 1572872 | tf_op jit(solution)/shard_map/ppermute | solution.py:439
  60.5 44.1 %collective-permute-start.6 = (f32[256,512]{1,0:T(8,128)}, f32[256,512]{1,0:T(8,128)S(1)}, u32[]{:S(2)}, u32[]{:S(2)}) collective-permute-start(f32[256,512]{1,0:T(8,128)} %get-tuple-element.72), channel_id=1, source_target_pairs={{0,20},{4,16},{8,28},{12,24},{16,4},{20,0},{24,12},{28,8},{1,21},{... | collective-permute-start | bytes 1572872 | tf_op jit(solution)/shard_map/ppermute | solution.py:439
  61.2 43.4 %collective-permute-start.7 = (f32[256,512]{1,0:T(8,128)}, f32[256,512]{1,0:T(8,128)S(1)}, u32[]{:S(2)}, u32[]{:S(2)}) collective-permute-start(f32[256,512]{1,0:T(8,128)} %get-tuple-element.73), channel_id=1, source_target_pairs={{0,12},{4,8},{8,4},{12,0},{16,28},{20,24},{24,20},{28,16},{1,13},{... | collective-permute-start | bytes 1572872 | tf_op jit(solution)/shard_map/ppermute | solution.py:439
  62.9 52.3 %collective-permute-start.5 = (f32[256,512]{1,0:T(8,128)}, f32[256,512]{1,0:T(8,128)S(1)}, u32[]{:S(2)}, u32[]{:S(2)}) collective-permute-start(f32[256,512]{1,0:T(8,128)} %get-tuple-element.71), channel_id=1, source_target_pairs={{0,28},{4,24},{8,20},{12,16},{16,12},{20,8},{24,4},{28,0},{1,29},{... | collective-permute-start | bytes 1572872 | tf_op jit(solution)/shard_map/ppermute | solution.py:439

commit v9 on v7

--- a/solution.py
+++ b/solution.py
@@ -52,17 +52,49 @@
     ]
 
 
-def regroup_kernel(groups, per_bucket, me_ref, *refs):
-    given, outs, scratch = refs[:4], refs[4 : 4 + groups], refs[4 + groups :]
-    held, (place_ref, meta_ref, sorted_ref, inv_ref, meta_smem, sems) = scratch[:4], scratch[4:]
+def tile(t):
+    return pl.ds(pl.multiple_of(t * SUB, SUB), SUB)
+
+
+class Runs:
+    def __init__(self, table, groups, per_bucket, state):
+        self.table, self.groups = table, groups
+        self.most = min(7, per_bucket // SUB + 1)
+        self.sub_row = iota((SUB, state), 0)
+
+    def get(self, s, v):
+        return [self.table[s * self.groups + v, i] for i in range(4)]
+
+    def place(self, s, v, out, source, base=None):
+        kept, target, first, final = self.get(s, v)
+        first = first if base is None else base
+        old = out[tile(target), :]
+        for t in reversed(range(1, self.most)):
+            t = jnp.minimum(t, final)
+            out[tile(target + t), :] = source[tile(first + t), :]
+        out[tile(target), :] = jnp.where(self.sub_row < kept, old, source[tile(first), :])
+
+    def place_rest(self, s, v, out, source):
+        _, target, first, final = self.get(s, v)
+
+        def longer(t, carry):
+            out[tile(target + t), :] = source[tile(first + t), :]
+            return carry
+
+        lax.fori_loop(self.most, final + 1, longer, 0)
+
+
+def lead_kernel(groups, per_bucket, lead, me_ref, *refs):
+    given, (out, pair_ref, place_ref, meta_ref), scratch = refs[:4], refs[4:8], refs[8:]
+    held, (sorted_ref, small_a, small_b, inv_ref, table, sems) = scratch[:4], scratch[4:]
     buckets_ref, ids_ref, sigma_ref, obs_ref = held
     blocks, block = place_ref.shape
     wide = block // LANES
     sensors = sigma_ref.shape[1]
-    _, padded, state = sorted_ref.shape
+    padded, state = sorted_ref.shape
     cells = blocks * groups
     last_tile = per_bucket // SUB - 1
-    most = min(7, last_tile + 2)
+    runs = Runs(table, groups, per_bucket, state)
 
     small = [pltpu.make_async_copy(given[i], held[i], sems.at[i]) for i in range(3)]
     for copy in small:
@@ -100,7 +132,7 @@
     final = jnp.maximum(tiles - 1, 0)
     meta = jnp.where(lane == 2, first, final)
     meta_ref[...] = jnp.where(lane == 0, kept, jnp.where(lane == 1, target, meta))
-    copy = pltpu.make_async_copy(meta_ref, meta_smem, sems.at[3])
+    copy = pltpu.make_async_copy(meta_ref, table, sems.at[3])
     copy.start()
     local = first * SUB + odd
     local = jnp.concatenate([local] * wide, axis=1)
@@ -109,12 +141,10 @@
         [jnp.sum(spot[s * groups : (s + 1) * groups], axis=0, keepdims=True) for s in range(blocks)],
         axis=0,
     )
-    sub_row = iota((SUB, state), 0)
-    tile = lambda t: pl.ds(pl.multiple_of(t * SUB, SUB), SUB)
-
-    def sort_block(s, into):
-        place = place_ref[pl.ds(s, 1), :]
-        moves = (iota((padded, block), 0) == place).astype(F32).astype(BF16)
+    of_lead = (iota((cells, LANES), 0) & (groups - 1)) == lead
+    longest = jnp.max(jnp.where(of_lead, final, 0))
+
+    def scale_block(s):
         ids = [ids_ref[pl.ds(s * wide + i, 1), :] for i in range(wide)]
         known = iota((sensors, block), 0) == jnp.concatenate(ids, axis=1)
         inv = jnp.concatenate([inv_ref[...]] * wide, axis=1)
@@ -122,84 +152,115 @@
         scale = jnp.transpose(jnp.broadcast_to(scale_row, (LANES, block)))
         fetch(s).wait()
         rows = pl.ds(pl.multiple_of(s * block, block), block)
-        scaled = obs_ref[rows, :] * jnp.concatenate([scale] * (state // LANES), axis=1)
-        high, low = split(scaled)
-        into[...] = dot(moves, high) + dot(moves, low)
-
-    def run(cell):
-        return [meta_smem[cell, i] for i in range(4)]
-
-    def place_runs(s, source):
-        for v in range(groups):
-            kept, target, first, final = run(s * groups + v)
-            old = outs[v][tile(target), :]
-            for t in reversed(range(1, most)):
-                t = jnp.minimum(t, final)
-                outs[v][tile(target + t), :] = source[tile(first + t), :]
-            outs[v][tile(target), :] = jnp.where(sub_row < kept, old, source[tile(first), :])
-
-    def place_rest(s, source):
-        for v in range(groups):
-            _, target, first, final = run(s * groups + v)
-
-            def longer(t, carry, v=v, target=target, first=first):
-                outs[v][tile(target + t), :] = source[tile(first + t), :]
-                return carry
-
-            lax.fori_loop(most, final + 1, longer, 0)
-
-    longest = jnp.max(final)
+        high, low = split(obs_ref[rows, :] * jnp.concatenate([scale] * (state // LANES), axis=1))
+        pair_ref[rows, :state] = high
+        pair_ref[rows, state:] = low
+        return high, low
+
+    def moves(s, shape, base):
+        spots = place_ref[pl.ds(s, 1), :] - base
+        return (iota(shape, 0) == spots).astype(F32).astype(BF16)
+
+    copy.wait()
     unroll = groups <= 8
 
-    @pl.when((longest < most) & unroll)
+    @pl.when((longest < runs.most) & unroll)
     def _():
         for s in range(blocks if unroll else 0):
-            sort_block(s, sorted_ref.at[s % 2])
-            if s == 0:
-                copy.wait()
-            place_runs(s, sorted_ref.at[s % 2])
-
-    @pl.when((longest >= most) | (not unroll))
+            into = (small_a, small_b)[s % 2]
+            high, low = scale_block(s)
+            picked = moves(s, (into.shape[0], block), runs.get(s, lead)[2] * SUB)
+            into[...] = dot(picked, high) + dot(picked, low)
+            runs.place(s, lead, out, into, 0)
+
+    @pl.when((longest >= runs.most) | (not unroll))
     def _():
-        copy.wait()
-
         def body(s, carry):
-            sort_block(s, sorted_ref.at[0])
-            place_runs(s, sorted_ref.at[0])
-            place_rest(s, sorted_ref.at[0])
+            high, low = scale_block(s)
+            picked = moves(s, (padded, block), 0)
+            sorted_ref[...] = dot(picked, high) + dot(picked, low)
+            runs.place(s, lead, out, sorted_ref)
+            runs.place_rest(s, lead, out, sorted_ref)
             return carry
 
         lax.fori_loop(0, blocks, body, 0)
 
 
-def regroup(observations, sensor_ids, sensor_sigma, buckets, me, groups):
+def rest_kernel(groups, per_bucket, others, table, place_ref, pair_ref, *refs):
+    outs, (sorted_a, sorted_b) = refs[: len(others)], refs[len(others) :]
+    blocks, block = place_ref.shape
+    padded, state = sorted_a.shape
+    runs = Runs(table, groups, per_bucket, state)
+
+    def sort_block(s, into):
+        picked = (iota((padded, block), 0) == place_ref[pl.ds(s, 1), :]).astype(F32).astype(BF16)
+        rows = pl.ds(pl.multiple_of(s * block, block), block)
+        both = dot(picked, pair_ref[rows, :])
+        into[...] = both[:, :state] + both[:, state:]
+
+    longest = 0
+    for s in range(blocks):
+        for v in range(groups):
+            longest = jnp.maximum(longest, table[s * groups + v, 3])
+    unroll = groups <= 8
+
+    @pl.when((longest < runs.most) & unroll)
+    def _():
+        for s in range(blocks if unroll else 0):
+            into = (sorted_a, sorted_b)[s % 2]
+            sort_block(s, into)
+            for v, out in zip(others, outs):
+                runs.place(s, v, out, into)
+
+    @pl.when((longest >= runs.most) | (not unroll))
+    def _():
+        def body(s, carry):
+            sort_block(s, sorted_a)
+            for v, out in zip(others, outs):
+                runs.place(s, v, out, sorted_a)
+                runs.place_rest(s, v, out, sorted_a)
+            return carry
+
+        lax.fori_loop(0, blocks, body, 0)
+
+
+def sorted_rows(block, groups):
+    return -(-(block + groups * 2 * (SUB - 1)) // 16) * 16
+
+
+def regroup_lead(observations, sensor_ids, sensor_sigma, buckets, me, groups, lead):
     rows, state = observations.shape
     sensors = sensor_sigma.shape[0]
     block = 256
     blocks = rows // block
+    cells = blocks * groups
     per_bucket = rows // groups
-    padded = -(-(block + groups * 2 * (SUB - 1)) // 16) * 16
     far = pl.BlockSpec(memory_space=pltpu.HBM)
     return pl.pallas_call(
-        functools.partial(regroup_kernel, groups, per_bucket),
+        functools.partial(lead_kernel, groups, per_bucket, lead),
         in_specs=[pl.BlockSpec(memory_space=pltpu.SMEM)] + [far] * 4,
-        out_specs=[pl.BlockSpec(memory_space=pltpu.VMEM)] * groups,
+        out_specs=[pl.BlockSpec(memory_space=pltpu.VMEM)] * 4,
         scratch_shapes=[
             pltpu.VMEM((rows // LANES, LANES), I32),
             pltpu.VMEM((rows // LANES, LANES), I32),
             pltpu.VMEM((1, sensors), F32),
             pltpu.VMEM((rows, state), F32),
-            pltpu.VMEM((blocks, block), I32),
-            pltpu.VMEM((blocks * groups, LANES), I32),
-            pltpu.VMEM((2, padded, state), F32),
+            pltpu.VMEM((sorted_rows(block, groups), state), F32),
+            pltpu.VMEM((64, state), F32),
+            pltpu.VMEM((64, state), F32),
             pltpu.VMEM((sensors, LANES), F32),
-            pltpu.SMEM((blocks * groups, LANES), I32),
+            pltpu.SMEM((cells, LANES), I32),
             pltpu.SemaphoreType.DMA((4 + blocks,)),
         ],
-        out_shape=[jax.ShapeDtypeStruct((per_bucket, state), F32)] * groups,
+        out_shape=[
+            jax.ShapeDtypeStruct((per_bucket, state), F32),
+            jax.ShapeDtypeStruct((rows, 2 * state), BF16),
+            jax.ShapeDtypeStruct((blocks, block), I32),
+            jax.ShapeDtypeStruct((cells, LANES), I32),
+        ],
         compiler_params=pltpu.CompilerParams(vmem_limit_bytes=56 * MIB),
         cost_estimate=pl.CostEstimate(
-            flops=4 * rows * padded * state, bytes_accessed=8 * rows * state, transcendentals=0
+            flops=rows * state, bytes_accessed=8 * rows * state, transcendentals=0
         ),
     )(
         me.reshape(1),
@@ -210,6 +271,24 @@
     )
 
 
+def regroup_rest(table, place, pair, groups, others):
+    rows, state = pair.shape[0], pair.shape[1] // 2
+    per_bucket = rows // groups
+    padded = sorted_rows(place.shape[1], groups)
+    vmem = pl.BlockSpec(memory_space=pltpu.VMEM)
+    return pl.pallas_call(
+        functools.partial(rest_kernel, groups, per_bucket, tuple(others)),
+        in_specs=[pl.BlockSpec(memory_space=pltpu.SMEM), vmem, vmem],
+        out_specs=[vmem] * len(others),
+        scratch_shapes=[pltpu.VMEM((padded, state), F32)] * 2,
+        out_shape=[jax.ShapeDtypeStruct((per_bucket, state), F32)] * len(others),
+        compiler_params=pltpu.CompilerParams(vmem_limit_bytes=24 * MIB),
+        cost_estimate=pl.CostEstimate(
+            flops=8 * rows * padded * state, bytes_accessed=8 * rows * state, transcendentals=0
+        ),
+    )(table, place, pair)
+
+
 def block_pairs(count):
     return [(i, j) for i in range(count) for j in range(i, count)]
 
@@ -224,15 +303,8 @@
         )
 
 
-def gram_kernel(groups, prior_ref, *rest):
-    chunks = rest[:groups]
-    out_ref, prior_out_ref, both_ref, pair_ref = rest[groups:]
-    per_bucket, state = chunks[0].shape
-    for k, chunk in enumerate(chunks):
-        rows = slice(k * per_bucket, (k + 1) * per_bucket)
-        high, low = split(chunk[...])
-        pair_ref[rows, :state] = high
-        pair_ref[rows, state:] = low
+def gram_kernel(prior_ref, pair_ref, out_ref, prior_out_ref, both_ref):
+    state = prior_ref.shape[0]
     both_ref[...] = dot_rows(pair_ref[:, :state], pair_ref[...])
     write_gram(both_ref, state, out_ref)
     high, low = split(prior_ref[...])
@@ -240,23 +312,21 @@
     write_gram(both_ref, state, prior_out_ref)
 
 
-def gram(prior_factor, chunks):
-    groups = len(chunks)
-    per_bucket, state = chunks[0].shape
-    rows = groups * per_bucket
+def gram(prior_factor, pair):
+    rows, state = pair.shape[0], pair.shape[1] // 2
     packed = len(block_pairs(state // LANES)) * LANES
     vmem = pl.BlockSpec(memory_space=pltpu.VMEM)
     return pl.pallas_call(
-        functools.partial(gram_kernel, groups),
-        in_specs=[vmem] * (groups + 1),
+        gram_kernel,
+        in_specs=[vmem] * 2,
         out_specs=[vmem] * 2,
         out_shape=[jax.ShapeDtypeStruct((packed, LANES), F32)] * 2,
-        scratch_shapes=[pltpu.VMEM((state, 2 * state), F32), pltpu.VMEM((rows, 2 * state), BF16)],
+        scratch_shapes=[pltpu.VMEM((state, 2 * state), F32)],
         compiler_params=pltpu.CompilerParams(vmem_limit_bytes=24 * MIB),
         cost_estimate=pl.CostEstimate(
             flops=4 * rows * state * state, bytes_accessed=4 * rows * state, transcendentals=0
         ),
-    )(prior_factor, *chunks)
+    )(prior_factor, pair)
 
 
 def scatter_sum(packed, count, groups):
@@ -418,47 +488,59 @@
     grp = lax.axis_size("grp")
     me = lax.axis_index("rows").astype(I32)
     total_rows = rows_dev * groups * grp
-    chunks = regroup(observations, sensor_ids, sensor_sigma, buckets, me, groups)
+    lead = 4 if groups > 4 else 0
+    others = [k for k in range(groups) if k != lead]
+    chunk, pair, place, table = regroup_lead(
+        observations, sensor_ids, sensor_sigma, buckets, me, groups, lead
+    )
     move = lambda k, chunk: lax.ppermute(chunk, "rows", [(i, i ^ k) for i in range(groups)])
+    received = {lead: move(lead, chunk) if lead else chunk}
     packed_rows = len(block_pairs(state // LANES)) * LANES
     plane = 2 * grp
     planes = [list(range(i, i + plane)) for i in range(0, groups * grp, plane)]
-    early = [k for k in (1, 4) if k < groups]
-    middle = [k for k in (6, 2) if k < groups]
-    late = [k for k in range(1, groups) if k not in early + middle]
-    received = {0: chunks[0]}
+    side = [k for k in (1,) if k < groups]
+    middle = [k for k in (2, 6) if k < groups]
+    late = [k for k in (5, 3, *range(7, groups)) if k < groups]
     valid = prior_factor[0, 0] > 0
     nothing = lambda rows: jnp.full((rows, LANES), jnp.nan, F32)
 
-    for k in early:
-        received[k] = move(k, chunks[k])
-
     def first():
-        packed, prior_gram = gram(prior_factor, chunks)
-        return scatter_sum(packed, plane, planes), prior_gram
-
-    piece, prior_gram = lax.cond(
-        valid, first, lambda: (nothing(packed_rows // plane), nothing(packed_rows))
-    )
+        packed, prior_gram = gram(prior_factor, pair)
+        rest = list(regroup_rest(table, place, pair, groups, others))
+        return scatter_sum(packed, plane, planes), prior_gram, rest
+
+    def wrong():
+        return nothing(packed_rows // plane), nothing(packed_rows), [chunk] * len(others)
+
+    piece, prior_gram, rest = lax.cond(valid, first, wrong)
+    chunks = {**dict(zip(others, rest)), lead: chunk}
+    if lead:
+        received[0] = chunks[0]
     across = [piece]
     for step in range(1, groups // 2):
         across.append(move(2 * step, piece))
+    for k in side:
+        received[k] = move(k, chunks[k])
     while len(across) > 1:
         across = [across[i] + across[i + 1] for i in range(0, len(across), 2)]
     for k in middle:
         _, chunk = behind(across[0], chunks[k])
         received[k] = move(k, chunk)
-    for k in early:
-        across[0], received[k] = behind(across[0], received[k])
+    across[0], received[lead] = behind(across[0], received[lead])
     summed = lax.cond(
         valid, lambda: gather_pieces(across[0], plane, planes), lambda: nothing(packed_rows)
     )
+    for k in side:
+        summed, received[k] = behind(summed, received[k])
     for k in late:
         _, chunk = behind(summed, chunks[k])
         received[k] = move(k, chunk)
     factor, high, low = factorise(summed, prior_gram, state, total_rows)
     out = None
-    for steps in ([0] + early + middle, late[:-1], late[-1:]):
+    soon = sorted({0, lead, *side, *middle})
+    for steps in (soon, late[:-1], late[-1:]):
+        if not steps:
+            continue
         out = whiten(me, high, low, steps, [received[k] for k in steps], out, rows_dev)
     return (out, factor)
 

time: 118 us -> 114 us (0.966)
  blocking collectives: 26.9 us -> 13.9 us
  local copies, waits for them, and re-layouts: 0.56 us -> 3.25 us
  waiting for transfers between devices: 24.2 us -> 26.5 us
  Pallas kernels: 47.2 us -> 49.4 us
  starting transfers between devices: 17.2 us -> 19.1 us
    all_to_all x1 -> x0, blocking collectives: 13.5 us -> none  [scatter_sum(): lax.all_to_all(packed, axes, split_axis=0, concat_axis=0, axis_index_grou...]
    all_to_all x0 -> x1, waiting for transfers between devices: none -> 3.97 us  [scatter_sum(): lax.all_to_all(packed, axes, split_axis=0, concat_axis=0, axis_index_grou...]
    all_to_all x0 -> x1, starting transfers between devices: none -> 3.72 us  [scatter_sum(): lax.all_to_all(packed, axes, split_axis=0, concat_axis=0, axis_index_grou...]
    pallas_call x2 -> x3, Pallas kernels: 14.1 us -> 16.4 us  [the longest x1 6.28 us: regroup_rest(): pl.pallas_call(functools.partial(rest_kernel, groups, per_bucket, tuple(o...]
    cond x0 -> x2, local copies, waits for them, and re-layouts: none -> 2.01 us
    ppermute x10, starting transfers between devices: 17.2 us -> 15.3 us  [shards(): lax.ppermute(chunk, 'rows', [(i, i ^ k) for i in range(groups)])]
    ppermute x10, waiting for transfers between devices: 24.2 us -> 22.5 us  [shards(): lax.ppermute(chunk, 'rows', [(i, i ^ k) for i in range(groups)])]
  transfers between devices with their start and end apart: 10 -> 11, of which waited for: 3 -> 4; matrix products, arithmetic and copies ran while one was open for 1% -> 1% of each run, Pallas kernels for 31% -> 37%
where the time goes in v9:
time: 114 us
  Pallas kernels  49.4 us (43%)
  waiting for transfers between devices  26.5 us (23%)
  starting transfers between devices  19.1 us (17%)
  blocking collectives  13.9 us (12%)
  local copies, waits for them, and re-layouts  3.25 us (3%)
  between operations  1.49 us (1%)
    pallas_call x1, Pallas kernels, factorise(): pl.pallas_call(functools.partial(factor_kernel, 1.0 / total_rows), in_spe...  25.8 us
    ppermute x10, waiting for transfers between devices, shards(): lax.ppermute(chunk, 'rows', [(i, i ^ k) for i in range(groups)])  22.5 us
    ppermute x10, starting transfers between devices, shards(): lax.ppermute(chunk, 'rows', [(i, i ^ k) for i in range(groups)])  15.3 us
    all_to_all x1, blocking collectives, gather_pieces(): lax.all_to_all(copies, axes, split_axis=0, concat_axis=0, axis_index_grou...  13.9 us
    pallas_call x3, Pallas kernels, whiten(): pl.pallas_call(functools.partial(whiten_kernel, tuple(steps), len(extra))...  7.27 us
    pallas_call x1, Pallas kernels, regroup_rest(): pl.pallas_call(functools.partial(rest_kernel, groups, per_bucket, tuple(o...  6.28 us
    pallas_call x1, Pallas kernels, regroup_lead(): pl.pallas_call(functools.partial(lead_kernel, groups, per_bucket, lead),...  5.53 us
    pallas_call x1, Pallas kernels, gram(): pl.pallas_call(gram_kernel, in_specs=[vmem] * 2, out_specs=[vmem] * 2, ou...  4.57 us
  transfers between devices with their start and end apart: 11, of which 4 were waited for; matrix products, arithmetic and copies ran while one was open for 1% of the time, Pallas kernels for 37%

profile of v9, /device:TPU:8, one launch (start us, length us, event | category | flops | bytes accessed | tf_op | source)
XLA Modules:
  0.0 113.8 jit_solution(1643935241785051104)
XLA Ops:
  0.6 5.5 %shard_map.68 = (f32[256,512]{1,0:T(8,128)}, bf16[2048,1024]{1,0:T(8,128)(2,1)S(1)}, s32[8,256]{1,0:T(8,128)S(1)}, s32[64,128]{1,0:T(8,128)S(1)}) custom-call(s32[1]{0:T(128)} %bitcast.2.me_ref, s32[16,128]{1,0:T(8,128)} %bitcast.8, s32[16,128]{1,0:T(8,128)} %bitcast.9, f32[1,128]{1,0:T(1,128)} %bitcast.10, f32[2048,512]{1,0:T(8,128)} %refs_3_.1), custom_call_target="tpu_custom_call" | custom-call | flops 1048576 | bytes 8388608 | tf_op jit(solution)/shard_map/pallas_call | solution.py:239
  6.2 2.7 %collective-permute-start.3 = (f32[256,512]{1,0:T(8,128)}, f32[256,512]{1,0:T(8,128)S(1)}, u32[]{:S(2)}, u32[]{:S(2)}) collective-permute-start(f32[256,512]{1,0:T(8,128)} %get-tuple-element.53), channel_id=1, source_target_pairs={{0,16},{4,20},{8,24},{12,28},{16,0},{20,4},{24,8},{28,12},{1,17},{... | collective-permute-start | bytes 1572872 | tf_op jit(solution)/shard_map/ppermute | solution.py:496
  8.8 1.2 %slice.3 = f32[1,1]{1,0:T(1,128)} slice(f32[512,512]{1,0:T(8,128)} %param.13), slice={[0:1], [0:1]} | slice | bytes 8 | tf_op jit(solution)/shard_map/slice | solution.py:504
  10.7 20.6 %conditional.2 = (f32[160,128]{1,0:T(8,128)S(1)}, f32[1280,128]{1,0:T(8,128)S(1)}, f32[256,512]{1,0:T(8,128)}, f32[256,512]{1,0:T(8,128)}, f32[256,512]{1,0:T(8,...) conditional(s32[]{:T(128)} %bitcast.3, ...), branch_computations={%region_0.0_spmd, %region_1.0_spmd} | conditional | flops 5234634752 | bytes 32063624 | solution.py:515
  10.7 2.0 %copy-done = bf16[2048,1024]{1,0:T(8,128)(2,1)} copy-done((bf16[2048,1024]{1,0:T(8,128)(2,1)}, bf16[2048,1024]{1,0:T(8,128)(2,1)S(1)}, u32[]{:S(2)}) %copy-start) | copy-done | bytes 4194328 | tf_op jit(solution)/shard_map/cond
  12.7 4.6 %branch_1_fun.2 = (f32[1280,128]{1,0:T(8,128)}, f32[1280,128]{1,0:T(8,128)S(1)}) custom-call(f32[512,512]{1,0:T(8,128)} %get-tuple-element.13.prior_ref, bf16[2048,1024]{1,0:T(8,128)(2,1)S(1)} %get-tuple-element.14.pair_ref), custom_call_target="tpu_custom_call" | custom-call | flops 2147483648 | bytes 4194304 | tf_op jit(solution)/shard_map/cond/branch_1_fun/pallas_call | solution.py:319
  17.3 3.7 %all-to-all-start = ((f32[8,160,128]{2,1,0:T(8,128)}), f32[8,160,128]{2,1,0:T(8,128)S(1)}, u32[]{:S(2)}, u32[]{:S(2)}) async-start(f32[8,160,128]{2,1,0:T(8,128)} %bitcast), calls=%async_computation | async-start | bytes 1310720 | tf_op jit(solution)/shard_map/cond/branch_1_fun/all_to_all | solution.py:335
  21.0 6.3 %branch_1_fun.3 = (f32[256,512]{1,0:T(8,128)}, f32[256,512]{1,0:T(8,128)}, f32[256,512]{1,0:T(8,128)}, f32[256,512]{1,0:T(8,128)}, f32[256,512]{1,0:T(8,128)}, /*index=5*/f32[256,512]{1,0:T(8,128)}, f32[256,512]{1,0:T(8,128)}) custom-call(s32[64,128]{1,0:T(8,128)S(1)} %get-tuple-element.17.table, s32[8,256]{1,0:T(8,128)S(1)} %get-tuple-element.18.place_ref, ...), custom_call_target="tpu_custom_call" | custom-call | flops 3087007744 | bytes 8388608 | tf_op jit(solution)/shard_map/cond/branch_1_fun/pallas_call | solution.py:279
  27.3 4.0 %all-to-all-done = f32[8,160,128]{2,1,0:T(8,128)S(1)} async-done(((f32[8,160,128]{2,1,0:T(8,128)}), f32[8,160,128]{2,1,0:T(8,128)S(1)}, u32[]{:S(2)}, u32[]{:S(2)}) %all-to-all-start) | async-done | bytes 655392 | tf_op jit(solution)/shard_map/cond/branch_1_fun/all_to_all | solution.py:335
  31.3 1.5 %collective-permute-start.4 = (f32[256,512]{1,0:T(8,128)}, f32[256,512]{1,0:T(8,128)S(1)}, u32[]{:S(2)}, u32[]{:S(2)}) collective-permute-start(f32[256,512]{1,0:T(8,128)} %get-tuple-element.59), channel_id=1, source_target_pairs={{0,4},{4,0},{8,12},{12,8},{16,20},{20,16},{24,28},{28,24},{1,5},{5... | collective-permute-start | bytes 1572872 | tf_op jit(solution)/shard_map/ppermute | solution.py:496
  32.8 2.8 %collective-permute-start.1 = (f32[160,128]{1,0:T(8,128)S(1)}, f32[160,128]{1,0:T(8,128)S(1)}, u32[]{:S(2)}, u32[]{:S(2)}) collective-permute-start(f32[160,128]{1,0:T(8,128)S(1)} %get-tuple-element.57), channel_id=1, source_target_pairs={{0,16},{4,20},{8,24},{12,28},{16,0},{20,4},{24,8},{28,12},{1,17},{... | collective-permute-start | bytes 245768 | tf_op jit(solution)/shard_map/ppermute | solution.py:496
  35.6 0.7 collective-permute-start
  36.3 3.8 %collective-permute-done.2 = f32[160,128]{1,0:T(8,128)S(1)} collective-permute-done((f32[160,128]{1,0:T(8,128)S(1)}, f32[160,128]{1,0:T(8,128)S(1)}, u32[]{:S(2)}, u32[]{:S(2)}) %collective-permute-start.2) | collective-permute-done | bytes 81952 | tf_op jit(solution)/shard_map/ppermute | solution.py:496
  40.2 2.4 %collective-permute-start.8 = (f32[256,512]{1,0:T(8,128)}, f32[256,512]{1,0:T(8,128)S(1)}, u32[]{:S(2)}, u32[]{:S(2)}) collective-permute-start(f32[256,512]{1,0:T(8,128)} %get-tuple-element.73), channel_id=1, source_target_pairs={{0,8},{4,12},{8,0},{12,4},{16,24},{20,28},{24,16},{28,20},{1,9},{5... | collective-permute-start | bytes 1572872 | tf_op jit(solution)/shard_map/ppermute | solution.py:496
  43.2 14.0 %conditional.3 = (f32[1280,128]{1,0:T(8,128)S(1)}) conditional(s32[]{:T(128)} %bitcast.3, () %tuple.29, f32[160,128]{1,0:T(8,128)S(1)} %add_add_fusion), branch_computations={%region_3.0_spmd, %region_4.0_spmd} | conditional | bytes 2048008 | solution.py:530
  43.3 13.9 %all_to_all.14 = f32[8,160,128]{2,1,0:T(8,128)S(1)} all-to-all(f32[8,160,128]{2,1,0:T(8,128)S(1)} %broadcast_in_dim.2), channel_id=1, replica_groups={{0,1,2,3,4,5,6,7},{8,9,10,11,12,13,14,15},{16,17,18,19,20,21,22,23},{24..., dimensions={0} | all-to-all | bytes 1310720 | tf_op jit(solution)/shard_map/cond/branch_1_fun/all_to_all | solution.py:343
  57.2 2.3 %collective-permute-start.6 = (f32[256,512]{1,0:T(8,128)}, f32[256,512]{1,0:T(8,128)S(1)}, u32[]{:S(2)}, u32[]{:S(2)}) collective-permute-start(f32[256,512]{1,0:T(8,128)} %get-tuple-element.67), channel_id=1, source_target_pairs={{0,20},{4,16},{8,28},{12,24},{16,4},{20,0},{24,12},{28,8},{1,21},{... | collective-permute-start | bytes 1572872 | tf_op jit(solution)/shard_map/ppermute | solution.py:496
  59.5 1.7 %collective-permute-start.7 = (f32[256,512]{1,0:T(8,128)}, f32[256,512]{1,0:T(8,128)S(1)}, u32[]{:S(2)}, u32[]{:S(2)}) collective-permute-start(f32[256,512]{1,0:T(8,128)} %get-tuple-element.69), channel_id=1, source_target_pairs={{0,12},{4,8},{8,4},{12,0},{16,28},{20,24},{24,20},{28,16},{1,13},{... | collective-permute-start | bytes 1572872 | tf_op jit(solution)/shard_map/ppermute | solution.py:496
  61.8 25.8 %shard_map.69 = (f32[512,512]{1,0:T(8,128)}, bf16[512,512]{1,0:T(8,128)(2,1)S(1)}, bf16[512,512]{1,0:T(8,128)(2,1)S(1)}) custom-call(f32[1280,128]{1,0:T(8,128)S(1)} %get-tuple-element.96.sum_ref, f32[1280,128]{1,0:T(8,128)S(1)} %get-tuple-element.61.prior_ref), custom_call_target="tpu_custom_call" | custom-call | flops 1 | bytes 1 | tf_op jit(solution)/shard_map/pallas_call | solution.py:417
  87.6 4.1 %shard_map.70.rest_2_ = f32[2048,512]{1,0:T(8,128)} custom-call(s32[1]{0:T(128)} %bitcast.2.me_ref, bf16[512,512]{1,0:T(8,128)(2,1)S(1)} %get-tuple-element.62.high_ref, bf16[512,512]{1,0:T(8,128)(2,1)S(1)} %get-tuple-element.63.low_ref, f32[256,512]{1,0:T(8,128)} %get-tuple-element.70.rest_0_, f32[256,512]{1,0:T(8,128)S(1)} %collective-permute-done.4.rest_1_, ...), custom_call_target="tpu_custom_call" | custom-call | flops 1 | bytes 1 | tf_op jit(solution)/shard_map/pallas_call | solution.py:462
  91.7 8.1 %collective-permute-done.6.rest_0_ = f32[256,512]{1,0:T(8,128)S(1)} collective-permute-done((f32[256,512]{1,0:T(8,128)}, f32[256,512]{1,0:T(8,128)S(1)}, u32[]{:S(2)}, u32[]{:S(2)}) %collective-permute-start.6) | collective-permute-done | bytes 524320 | tf_op jit(solution)/shard_map/ppermute | solution.py:496
  99.8 1.8 %shard_map.71.rest_1_ = f32[2048,512]{1,0:T(8,128)} custom-call(s32[1]{0:T(128)} %bitcast.2.me_ref, bf16[512,512]{1,0:T(8,128)(2,1)S(1)} %get-tuple-element.62.high_ref, bf16[512,512]{1,0:T(8,128)(2,1)S(1)} %get-tuple-element.63.low_ref, f32[256,512]{1,0:T(8,128)S(1)} %collective-permute-done.6.rest_0_, ...), custom_call_target="tpu_custom_call", output_to_operand_aliasing={{}: (5, {})} | custom-call | flops 1 | bytes 1 | tf_op jit(solution)/shard_map/pallas_call | solution.py:462
  101.6 10.6 %collective-permute-done.5.rest_0_ = f32[256,512]{1,0:T(8,128)S(1)} collective-permute-done((f32[256,512]{1,0:T(8,128)}, f32[256,512]{1,0:T(8,128)S(1)}, u32[]{:S(2)}, u32[]{:S(2)}) %collective-permute-start.5) | collective-permute-done | bytes 524320 | tf_op jit(solution)/shard_map/ppermute | solution.py:496
  112.2 1.4 %shard_map.72 = f32[2048,512]{1,0:T(8,128)} custom-call(s32[1]{0:T(128)} %bitcast.2.me_ref, bf16[512,512]{1,0:T(8,128)(2,1)S(1)} %get-tuple-element.62.high_ref, bf16[512,512]{1,0:T(8,128)(2,1)S(1)} %get-tuple-element.63.low_ref, f32[256,512]{1,0:T(8,128)S(1)} %collective-permute-done.5.rest_0_, ...), custom_call_target="tpu_custom_call", output_to_operand_aliasing={{}: (4, {})} | custom-call | flops 1 | bytes 1 | tf_op jit(solution)/shard_map/pallas_call | solution.py:462
  (14 shorter events, 1.4 us)
Async XLA Ops:
  6.2 37.0 %collective-permute-start.3 = (f32[256,512]{1,0:T(8,128)}, f32[256,512]{1,0:T(8,128)S(1)}, u32[]{:S(2)}, u32[]{:S(2)}) collective-permute-start(f32[256,512]{1,0:T(8,128)} %get-tuple-element.53), channel_id=1, source_target_pairs={{0,16},{4,20},{8,24},{12,28},{16,0},{20,4},{24,8},{28,12},{1,17},{... | collective-permute-start | bytes 1572872 | tf_op jit(solution)/shard_map/ppermute | solution.py:496
  10.7 2.0 %copy-start = (bf16[2048,1024]{1,0:T(8,128)(2,1)}, bf16[2048,1024]{1,0:T(8,128)(2,1)S(1)}, u32[]{:S(2)}) copy-start(bf16[2048,1024]{1,0:T(8,128)(2,1)S(1)} %get-tuple-element.14.pair_ref) | copy-start | bytes 12582916 | tf_op jit(solution)/shard_map/cond
  17.3 14.0 %all-to-all-start = ((f32[8,160,128]{2,1,0:T(8,128)}), f32[8,160,128]{2,1,0:T(8,128)S(1)}, u32[]{:S(2)}, u32[]{:S(2)}) async-start(f32[8,160,128]{2,1,0:T(8,128)} %bitcast), calls=%async_computation | async-start | bytes 1310720 | tf_op jit(solution)/shard_map/cond/branch_1_fun/all_to_all | solution.py:335
  31.3 25.9 %collective-permute-start.4 = (f32[256,512]{1,0:T(8,128)}, f32[256,512]{1,0:T(8,128)S(1)}, u32[]{:S(2)}, u32[]{:S(2)}) collective-permute-start(f32[256,512]{1,0:T(8,128)} %get-tuple-element.59), channel_id=1, source_target_pairs={{0,4},{4,0},{8,12},{12,8},{16,20},{20,16},{24,28},{28,24},{1,5},{5... | collective-permute-start | bytes 1572872 | tf_op jit(solution)/shard_map/ppermute | solution.py:496
  32.8 7.3 %collective-permute-start.2 = (f32[160,128]{1,0:T(8,128)S(1)}, f32[160,128]{1,0:T(8,128)S(1)}, u32[]{:S(2)}, u32[]{:S(2)}) collective-permute-start(f32[160,128]{1,0:T(8,128)S(1)} %get-tuple-element.57), channel_id=1, source_target_pairs={{0,24},{4,28},{8,16},{12,20},{16,8},{20,12},{24,0},{28,4},{1,25},{... | collective-permute-start | bytes 245768 | tf_op jit(solution)/shard_map/ppermute | solution.py:496
  32.8 7.3 %collective-permute-start.1 = (f32[160,128]{1,0:T(8,128)S(1)}, f32[160,128]{1,0:T(8,128)S(1)}, u32[]{:S(2)}, u32[]{:S(2)}) collective-permute-start(f32[160,128]{1,0:T(8,128)S(1)} %get-tuple-element.57), channel_id=1, source_target_pairs={{0,16},{4,20},{8,24},{12,28},{16,0},{20,4},{24,8},{28,12},{1,17},{... | collective-permute-start | bytes 245768 | tf_op jit(solution)/shard_map/ppermute | solution.py:496
  35.6 4.5 %collective-permute-start = (f32[160,128]{1,0:T(8,128)S(1)}, f32[160,128]{1,0:T(8,128)S(1)}, u32[]{:S(2)}, u32[]{:S(2)}) collective-permute-start(f32[160,128]{1,0:T(8,128)S(1)} %get-tuple-element.57), channel_id=1, source_target_pairs={{0,8},{4,12},{8,0},{12,4},{16,24},{20,28},{24,16},{28,20},{1,9},{5... | collective-permute-start | bytes 245768 | tf_op jit(solution)/shard_map/ppermute | solution.py:496
  40.2 47.4 %collective-permute-start.8 = (f32[256,512]{1,0:T(8,128)}, f32[256,512]{1,0:T(8,128)S(1)}, u32[]{:S(2)}, u32[]{:S(2)}) collective-permute-start(f32[256,512]{1,0:T(8,128)} %get-tuple-element.73), channel_id=1, source_target_pairs={{0,8},{4,12},{8,0},{12,4},{16,24},{20,28},{24,16},{28,20},{1,9},{5... | collective-permute-start | bytes 1572872 | tf_op jit(solution)/shard_map/ppermute | solution.py:496
  42.6 45.0 %collective-permute-start.9 = (f32[256,512]{1,0:T(8,128)}, f32[256,512]{1,0:T(8,128)S(1)}, u32[]{:S(2)}, u32[]{:S(2)}) collective-permute-start(f32[256,512]{1,0:T(8,128)} %get-tuple-element.76), channel_id=1, source_target_pairs={{0,24},{4,28},{8,16},{12,20},{16,8},{20,12},{24,0},{28,4},{1,25},{... | collective-permute-start | bytes 1572872 | tf_op jit(solution)/shard_map/ppermute | solution.py:496
  57.2 42.6 %collective-permute-start.6 = (f32[256,512]{1,0:T(8,128)}, f32[256,512]{1,0:T(8,128)S(1)}, u32[]{:S(2)}, u32[]{:S(2)}) collective-permute-start(f32[256,512]{1,0:T(8,128)} %get-tuple-element.67), channel_id=1, source_target_pairs={{0,20},{4,16},{8,28},{12,24},{16,4},{20,0},{24,12},{28,8},{1,21},{... | collective-permute-start | bytes 1572872 | tf_op jit(solution)/shard_map/ppermute | solution.py:496
  59.5 40.3 %collective-permute-start.7 = (f32[256,512]{1,0:T(8,128)}, f32[256,512]{1,0:T(8,128)S(1)}, u32[]{:S(2)}, u32[]{:S(2)}) collective-permute-start(f32[256,512]{1,0:T(8,128)} %get-tuple-element.69), channel_id=1, source_target_pairs={{0,12},{4,8},{8,4},{12,0},{16,28},{20,24},{24,20},{28,16},{1,13},{... | collective-permute-start | bytes 1572872 | tf_op jit(solution)/shard_map/ppermute | solution.py:496
  61.2 51.0 %collective-permute-start.5 = (f32[256,512]{1,0:T(8,128)}, f32[256,512]{1,0:T(8,128)S(1)}, u32[]{:S(2)}, u32[]{:S(2)}) collective-permute-start(f32[256,512]{1,0:T(8,128)} %get-tuple-element.65), channel_id=1, source_target_pairs={{0,28},{4,24},{8,20},{12,16},{16,12},{20,8},{24,4},{28,0},{1,29},{... | collective-permute-start | bytes 1572872 | tf_op jit(solution)/shard_map/ppermute | solution.py:496

commit v10 on v9

--- a/solution.py
+++ b/solution.py
@@ -84,9 +84,10 @@
         lax.fori_loop(self.most, final + 1, longer, 0)
 
 
-def lead_kernel(groups, per_bucket, lead, me_ref, *refs):
-    given, (out, pair_ref, place_ref, meta_ref), scratch = refs[:4], refs[4:8], refs[8:]
-    held, (sorted_ref, small_a, small_b, inv_ref, table, sems) = scratch[:4], scratch[4:]
+def lead_kernel(groups, per_bucket, leads, me_ref, *refs):
+    given, outs, refs = refs[:4], refs[4 : 4 + len(leads)], refs[4 + len(leads) :]
+    (pair_ref, place_ref, meta_ref), held, scratch = refs[:3], refs[3:7], refs[7:]
+    sorted_ref, small_a, small_b, inv_ref, table, sems = scratch
     buckets_ref, ids_ref, sigma_ref, obs_ref = held
     blocks, block = place_ref.shape
     wide = block // LANES
@@ -141,25 +142,28 @@
         [jnp.sum(spot[s * groups : (s + 1) * groups], axis=0, keepdims=True) for s in range(blocks)],
         axis=0,
     )
-    of_lead = (iota((cells, LANES), 0) & (groups - 1)) == lead
+    slot = iota((cells, LANES), 0) & (groups - 1)
+    of_lead = functools.reduce(jnp.logical_or, [slot == v for v in leads])
     longest = jnp.max(jnp.where(of_lead, final, 0))
-
-    def scale_block(s):
-        ids = [ids_ref[pl.ds(s * wide + i, 1), :] for i in range(wide)]
+    inv = jnp.concatenate([inv_ref[...]] * wide, axis=1)
+    block_rows = lambda s: pl.ds(pl.multiple_of(s * block, block), block)
+
+    for s in range(blocks):
+        ids = [ids_ref[s * wide + i : s * wide + i + 1, :] for i in range(wide)]
         known = iota((sensors, block), 0) == jnp.concatenate(ids, axis=1)
-        inv = jnp.concatenate([inv_ref[...]] * wide, axis=1)
         scale_row = jnp.sum(jnp.where(known, inv, 0.0), axis=0, keepdims=True)
         scale = jnp.transpose(jnp.broadcast_to(scale_row, (LANES, block)))
         fetch(s).wait()
-        rows = pl.ds(pl.multiple_of(s * block, block), block)
+        rows = block_rows(s)
         high, low = split(obs_ref[rows, :] * jnp.concatenate([scale] * (state // LANES), axis=1))
         pair_ref[rows, :state] = high
         pair_ref[rows, state:] = low
-        return high, low
-
-    def moves(s, shape, base):
+
+    def sort_block(s, into, base):
         spots = place_ref[pl.ds(s, 1), :] - base
-        return (iota(shape, 0) == spots).astype(F32).astype(BF16)
+        picked = (iota((into.shape[0], block), 0) == spots).astype(F32).astype(BF16)
+        both = dot(picked, pair_ref[block_rows(s), :])
+        into[...] = both[:, :state] + both[:, state:]
 
     copy.wait()
     unroll = groups <= 8
@@ -167,20 +171,18 @@
     @pl.when((longest < runs.most) & unroll)
     def _():
         for s in range(blocks if unroll else 0):
-            into = (small_a, small_b)[s % 2]
-            high, low = scale_block(s)
-            picked = moves(s, (into.shape[0], block), runs.get(s, lead)[2] * SUB)
-            into[...] = dot(picked, high) + dot(picked, low)
-            runs.place(s, lead, out, into, 0)
+            for n, v in enumerate(leads):
+                into = (small_a, small_b)[(s * len(leads) + n) % 2]
+                sort_block(s, into, runs.get(s, v)[2] * SUB)
+                runs.place(s, v, outs[n], into, 0)
 
     @pl.when((longest >= runs.most) | (not unroll))
     def _():
         def body(s, carry):
-            high, low = scale_block(s)
-            picked = moves(s, (padded, block), 0)
-            sorted_ref[...] = dot(picked, high) + dot(picked, low)
-            runs.place(s, lead, out, sorted_ref)
-            runs.place_rest(s, lead, out, sorted_ref)
+            sort_block(s, sorted_ref, 0)
+            for v, out in zip(leads, outs):
+                runs.place(s, v, out, sorted_ref)
+                runs.place_rest(s, v, out, sorted_ref)
             return carry
 
         lax.fori_loop(0, blocks, body, 0)
@@ -228,7 +230,7 @@
     return -(-(block + groups * 2 * (SUB - 1)) // 16) * 16
 
 
-def regroup_lead(observations, sensor_ids, sensor_sigma, buckets, me, groups, lead):
+def regroup_lead(observations, sensor_ids, sensor_sigma, buckets, me, groups, leads):
     rows, state = observations.shape
     sensors = sensor_sigma.shape[0]
     block = 256
@@ -237,9 +239,9 @@
     per_bucket = rows // groups
     far = pl.BlockSpec(memory_space=pltpu.HBM)
     return pl.pallas_call(
-        functools.partial(lead_kernel, groups, per_bucket, lead),
+        functools.partial(lead_kernel, groups, per_bucket, tuple(leads)),
         in_specs=[pl.BlockSpec(memory_space=pltpu.SMEM)] + [far] * 4,
-        out_specs=[pl.BlockSpec(memory_space=pltpu.VMEM)] * 4,
+        out_specs=[pl.BlockSpec(memory_space=pltpu.VMEM)] * (len(leads) + 3),
         scratch_shapes=[
             pltpu.VMEM((rows // LANES, LANES), I32),
             pltpu.VMEM((rows // LANES, LANES), I32),
@@ -252,8 +254,8 @@
             pltpu.SMEM((cells, LANES), I32),
             pltpu.SemaphoreType.DMA((4 + blocks,)),
         ],
-        out_shape=[
-            jax.ShapeDtypeStruct((per_bucket, state), F32),
+        out_shape=[jax.ShapeDtypeStruct((per_bucket, state), F32)] * len(leads)
+        + [
             jax.ShapeDtypeStruct((rows, 2 * state), BF16),
             jax.ShapeDtypeStruct((blocks, block), I32),
             jax.ShapeDtypeStruct((cells, LANES), I32),
@@ -282,7 +284,7 @@
         out_specs=[vmem] * len(others),
         scratch_shapes=[pltpu.VMEM((padded, state), F32)] * 2,
         out_shape=[jax.ShapeDtypeStruct((per_bucket, state), F32)] * len(others),
-        compiler_params=pltpu.CompilerParams(vmem_limit_bytes=24 * MIB),
+        compiler_params=pltpu.CompilerParams(vmem_limit_bytes=14 * MIB),
         cost_estimate=pl.CostEstimate(
             flops=8 * rows * padded * state, bytes_accessed=8 * rows * state, transcendentals=0
         ),
@@ -322,7 +324,7 @@
         out_specs=[vmem] * 2,
         out_shape=[jax.ShapeDtypeStruct((packed, LANES), F32)] * 2,
         scratch_shapes=[pltpu.VMEM((state, 2 * state), F32)],
-        compiler_params=pltpu.CompilerParams(vmem_limit_bytes=24 * MIB),
+        compiler_params=pltpu.CompilerParams(vmem_limit_bytes=10 * MIB),
         cost_estimate=pl.CostEstimate(
             flops=4 * rows * state * state, bytes_accessed=4 * rows * state, transcendentals=0
         ),
@@ -488,20 +490,19 @@
     grp = lax.axis_size("grp")
     me = lax.axis_index("rows").astype(I32)
     total_rows = rows_dev * groups * grp
-    lead = 4 if groups > 4 else 0
-    others = [k for k in range(groups) if k != lead]
-    chunk, pair, place, table = regroup_lead(
-        observations, sensor_ids, sensor_sigma, buckets, me, groups, lead
+    leads = [k for k in (4, 1) if k < groups]
+    others = [k for k in range(groups) if k not in leads]
+    *chunks, pair, place, table = regroup_lead(
+        observations, sensor_ids, sensor_sigma, buckets, me, groups, leads
     )
     move = lambda k, chunk: lax.ppermute(chunk, "rows", [(i, i ^ k) for i in range(groups)])
-    received = {lead: move(lead, chunk) if lead else chunk}
+    received = {k: move(k, chunk) for k, chunk in zip(leads, chunks)}
     packed_rows = len(block_pairs(state // LANES)) * LANES
     plane = 2 * grp
     planes = [list(range(i, i + plane)) for i in range(0, groups * grp, plane)]
-    side = [k for k in (1,) if k < groups]
     middle = [k for k in (2, 6) if k < groups]
     late = [k for k in (5, 3, *range(7, groups)) if k < groups]
-    valid = prior_factor[0, 0] > 0
+    valid = sensor_sigma[0] > 0
     nothing = lambda rows: jnp.full((rows, LANES), jnp.nan, F32)
 
     def first():
@@ -510,34 +511,32 @@
         return scatter_sum(packed, plane, planes), prior_gram, rest
 
     def wrong():
-        return nothing(packed_rows // plane), nothing(packed_rows), [chunk] * len(others)
+        return nothing(packed_rows // plane), nothing(packed_rows), [chunks[0]] * len(others)
 
     piece, prior_gram, rest = lax.cond(valid, first, wrong)
-    chunks = {**dict(zip(others, rest)), lead: chunk}
-    if lead:
-        received[0] = chunks[0]
+    rest = dict(zip(others, rest))
+    received[0] = rest[0]
+    for k in leads[1:]:
+        piece, received[k] = behind(piece, received[k])
     across = [piece]
     for step in range(1, groups // 2):
         across.append(move(2 * step, piece))
-    for k in side:
-        received[k] = move(k, chunks[k])
+    for k in middle[:1]:
+        received[k] = move(k, behind(piece, rest[k])[1])
     while len(across) > 1:
         across = [across[i] + across[i + 1] for i in range(0, len(across), 2)]
-    for k in middle:
-        _, chunk = behind(across[0], chunks[k])
+    for k in middle[1:]:
+        received[leads[0]], chunk = behind(received[leads[0]], rest[k])
         received[k] = move(k, chunk)
-    across[0], received[lead] = behind(across[0], received[lead])
+    across[0], received[leads[0]] = behind(across[0], received[leads[0]])
     summed = lax.cond(
         valid, lambda: gather_pieces(across[0], plane, planes), lambda: nothing(packed_rows)
     )
-    for k in side:
-        summed, received[k] = behind(summed, received[k])
     for k in late:
-        _, chunk = behind(summed, chunks[k])
-        received[k] = move(k, chunk)
+        received[k] = move(k, behind(summed, rest[k])[1])
     factor, high, low = factorise(summed, prior_gram, state, total_rows)
     out = None
-    soon = sorted({0, lead, *side, *middle})
+    soon = [0, *leads, *middle]
     for steps in (soon, late[:-1], late[-1:]):
         if not steps:
             continue

time: 114 us -> 110 us (0.965)
  waiting for transfers between devices: 26.5 us -> 25.3 us
  local copies, waits for them, and re-layouts: 3.25 us -> 2.06 us
    ppermute x10, waiting for transfers between devices: 22.5 us -> 21.1 us  [shards(): lax.ppermute(chunk, 'rows', [(i, i ^ k) for i in range(groups)])]
    slice x1 -> x0, local copies, waits for them, and re-layouts: 1.2 us -> none  [shards(): valid = prior_factor[0, 0] > 0]
  transfers between devices with their start and end apart: 11 -> 11, of which waited for: 4 -> 5; matrix products, arithmetic and copies ran while one was open for 1% -> 0% of each run, Pallas kernels for 37% -> 39%
where the time goes in v10:
time: 110 us
  Pallas kernels  49.7 us (45%)
  waiting for transfers between devices  25.3 us (23%)
  starting transfers between devices  18 us (16%)
  blocking collectives  13.5 us (12%)
  local copies, waits for them, and re-layouts  2.06 us (2%)
    pallas_call x1, Pallas kernels, factorise(): pl.pallas_call(functools.partial(factor_kernel, 1.0 / total_rows), in_spe...  25.8 us
    ppermute x10, waiting for transfers between devices, shards(): lax.ppermute(chunk, 'rows', [(i, i ^ k) for i in range(groups)])  21.1 us
    ppermute x10, starting transfers between devices, shards(): lax.ppermute(chunk, 'rows', [(i, i ^ k) for i in range(groups)])  14.5 us
    all_to_all x1, blocking collectives, gather_pieces(): lax.all_to_all(copies, axes, split_axis=0, concat_axis=0, axis_index_grou...  13.5 us
    pallas_call x3, Pallas kernels, whiten(): pl.pallas_call(functools.partial(whiten_kernel, tuple(steps), len(extra))...  7.32 us
    pallas_call x1, Pallas kernels, regroup_lead(): pl.pallas_call(functools.partial(lead_kernel, groups, per_bucket, tuple(l...  6 us
    pallas_call x1, Pallas kernels, regroup_rest(): pl.pallas_call(functools.partial(rest_kernel, groups, per_bucket, tuple(o...  5.98 us
    pallas_call x1, Pallas kernels, gram(): pl.pallas_call(gram_kernel, in_specs=[vmem] * 2, out_specs=[vmem] * 2, ou...  4.57 us
  transfers between devices with their start and end apart: 11, of which 5 were waited for; matrix products, arithmetic and copies ran while one was open for 0% of the time, Pallas kernels for 39%

profile of v10, /device:TPU:8, one launch (start us, length us, event | category | flops | bytes accessed | tf_op | source)
XLA Modules:
  0.0 109.6 jit_solution(10333778206884807107)
XLA Ops:
  0.6 6.0 %shard_map.69 = (f32[256,512]{1,0:T(8,128)}, f32[256,512]{1,0:T(8,128)}, bf16[2048,1024]{1,0:T(8,128)(2,1)S(1)}, s32[8,256]{1,0:T(8,128)S(1)}, s32[64,128]{1,0:T(8,128)S(1)}) custom-call(s32[1]{0:T(128)} %bitcast.2.me_ref, s32[16,128]{1,0:T(8,128)} %bitcast.9, s32[16,128]{1,0:T(8,128)} %bitcast.10, f32[1,128]{1,0:T(1,128)} %bitcast.11, f32[2048,512]{1,0:T(8,128)} %refs_3_.1), custom_call_target="tpu_custom_call" | custom-call | flops 1048576 | bytes 8388608 | tf_op jit(solution)/shard_map/pallas_call | solution.py:241
  6.7 1.6 %collective-permute-start = (f32[256,512]{1,0:T(8,128)}, f32[256,512]{1,0:T(8,128)S(1)}, u32[]{:S(2)}, u32[]{:S(2)}) collective-permute-start(f32[256,512]{1,0:T(8,128)} %get-tuple-element.58), channel_id=1, source_target_pairs={{0,4},{4,0},{8,12},{12,8},{16,20},{20,16},{24,28},{28,24},{1,5},{5... | collective-permute-start | bytes 1572872 | tf_op jit(solution)/shard_map/ppermute | solution.py:498
  8.2 2.6 %collective-permute-start.4 = (f32[256,512]{1,0:T(8,128)}, f32[256,512]{1,0:T(8,128)S(1)}, u32[]{:S(2)}, u32[]{:S(2)}) collective-permute-start(f32[256,512]{1,0:T(8,128)} %get-tuple-element.53), channel_id=1, source_target_pairs={{0,16},{4,20},{8,24},{12,28},{16,0},{20,4},{24,8},{28,12},{1,17},{... | collective-permute-start | bytes 1572872 | tf_op jit(solution)/shard_map/ppermute | solution.py:498
  10.8 20.4 %conditional.2 = (f32[160,128]{1,0:T(8,128)S(1)}, f32[1280,128]{1,0:T(8,128)S(1)}, f32[256,512]{1,0:T(8,128)}, f32[256,512]{1,0:T(8,128)}, f32[256,512]{1,0:T(8,...) conditional(s32[]{:T(128)} %bitcast.3, f32[256,512]{1,0:T(8,128)} %get-tuple-element.53, ...), branch_computations={%region_0.0_spmd, %region_1.0_spmd} | conditional | flops 5234634752 | bytes 32063616 | solution.py:516
  10.9 2.0 %copy-done.1 = bf16[2048,1024]{1,0:T(8,128)(2,1)} copy-done((bf16[2048,1024]{1,0:T(8,128)(2,1)}, bf16[2048,1024]{1,0:T(8,128)(2,1)S(1)}, u32[]{:S(2)}) %copy-start.1) | copy-done | bytes 4194328 | tf_op jit(solution)/shard_map/cond
  12.9 4.6 %branch_1_fun.2 = (f32[1280,128]{1,0:T(8,128)}, f32[1280,128]{1,0:T(8,128)S(1)}) custom-call(f32[512,512]{1,0:T(8,128)} %get-tuple-element.80.prior_ref, bf16[2048,1024]{1,0:T(8,128)(2,1)S(1)} %get-tuple-element.14.pair_ref), custom_call_target="tpu_custom_call" | custom-call | flops 2147483648 | bytes 4194304 | tf_op jit(solution)/shard_map/cond/branch_1_fun/pallas_call | solution.py:321
  17.5 3.5 %all-to-all-start = ((f32[8,160,128]{2,1,0:T(8,128)}), f32[8,160,128]{2,1,0:T(8,128)S(1)}, u32[]{:S(2)}, u32[]{:S(2)}) async-start(f32[8,160,128]{2,1,0:T(8,128)} %bitcast), calls=%async_computation | async-start | bytes 1310720 | tf_op jit(solution)/shard_map/cond/branch_1_fun/all_to_all | solution.py:337
  21.0 6.0 %branch_1_fun.3 = (f32[256,512]{1,0:T(8,128)}, f32[256,512]{1,0:T(8,128)}, f32[256,512]{1,0:T(8,128)}, f32[256,512]{1,0:T(8,128)}, f32[256,512]{1,0:T(8,128)}, /*index=5*/f32[256,512]{1,0:T(8,128)}) custom-call(s32[64,128]{1,0:T(8,128)S(1)} %get-tuple-element.17.table, s32[8,256]{1,0:T(8,128)S(1)} %get-tuple-element.18.place_ref, bf16[2048,1024]{1,0:T(8,128)(2,1)} %copy-done.1), custom_call_target="tpu_custom_call" | custom-call | flops 3087007744 | bytes 8388608 | tf_op jit(solution)/shard_map/cond/branch_1_fun/pallas_call | solution.py:281
  27.0 4.2 %all-to-all-done = f32[8,160,128]{2,1,0:T(8,128)S(1)} async-done(((f32[8,160,128]{2,1,0:T(8,128)}), f32[8,160,128]{2,1,0:T(8,128)S(1)}, u32[]{:S(2)}, u32[]{:S(2)}) %all-to-all-start) | async-done | bytes 655392 | tf_op jit(solution)/shard_map/cond/branch_1_fun/all_to_all | solution.py:337
  31.3 2.8 %collective-permute-start.2 = (f32[160,128]{1,0:T(8,128)S(1)}, f32[160,128]{1,0:T(8,128)S(1)}, u32[]{:S(2)}, u32[]{:S(2)}) collective-permute-start(f32[160,128]{1,0:T(8,128)S(1)} %get-tuple-element.59), channel_id=1, source_target_pairs={{0,16},{4,20},{8,24},{12,28},{16,0},{20,4},{24,8},{28,12},{1,17},{... | collective-permute-start | bytes 245768 | tf_op jit(solution)/shard_map/ppermute | solution.py:498
  34.1 0.7 collective-permute-start.1
  34.8 1.3 %collective-permute-start.8 = (f32[256,512]{1,0:T(8,128)}, f32[256,512]{1,0:T(8,128)S(1)}, u32[]{:S(2)}, u32[]{:S(2)}) collective-permute-start(f32[256,512]{1,0:T(8,128)} %get-tuple-element.76), channel_id=1, source_target_pairs={{0,8},{4,12},{8,0},{12,4},{16,24},{20,28},{24,16},{28,20},{1,9},{5... | collective-permute-start | bytes 1572872 | tf_op jit(solution)/shard_map/ppermute | solution.py:498
  36.6 3.1 %collective-permute-done.3 = f32[160,128]{1,0:T(8,128)S(1)} collective-permute-done((f32[160,128]{1,0:T(8,128)S(1)}, f32[160,128]{1,0:T(8,128)S(1)}, u32[]{:S(2)}, u32[]{:S(2)}) %collective-permute-start.3) | collective-permute-done | bytes 81952 | tf_op jit(solution)/shard_map/ppermute | solution.py:498
  39.7 0.5 collective-permute-done.2
  40.2 13.6 %conditional.3 = (f32[1280,128]{1,0:T(8,128)S(1)}) conditional(s32[]{:T(128)} %bitcast.3, () %tuple.29, f32[160,128]{1,0:T(8,128)S(1)} %add_add_fusion), branch_computations={%region_3.0_spmd, %region_4.0_spmd} | conditional | bytes 2048008 | solution.py:532
  40.3 13.5 %all_to_all.14 = f32[8,160,128]{2,1,0:T(8,128)S(1)} all-to-all(f32[8,160,128]{2,1,0:T(8,128)S(1)} %broadcast_in_dim.2), channel_id=1, replica_groups={{0,1,2,3,4,5,6,7},{8,9,10,11,12,13,14,15},{16,17,18,19,20,21,22,23},{24..., dimensions={0} | all-to-all | bytes 1310720 | tf_op jit(solution)/shard_map/cond/branch_1_fun/all_to_all | solution.py:345
  53.8 3.6 %collective-permute-start.6 = (f32[256,512]{1,0:T(8,128)}, f32[256,512]{1,0:T(8,128)S(1)}, u32[]{:S(2)}, u32[]{:S(2)}) collective-permute-start(f32[256,512]{1,0:T(8,128)} %get-tuple-element.69), channel_id=1, source_target_pairs={{0,20},{4,16},{8,28},{12,24},{16,4},{20,0},{24,12},{28,8},{1,21},{... | collective-permute-start | bytes 1572872 | tf_op jit(solution)/shard_map/ppermute | solution.py:498
  57.4 1.4 %collective-permute-start.5 = (f32[256,512]{1,0:T(8,128)}, f32[256,512]{1,0:T(8,128)S(1)}, u32[]{:S(2)}, u32[]{:S(2)}) collective-permute-start(f32[256,512]{1,0:T(8,128)} %get-tuple-element.67), channel_id=1, source_target_pairs={{0,28},{4,24},{8,20},{12,16},{16,12},{20,8},{24,4},{28,0},{1,29},{... | collective-permute-start | bytes 1572872 | tf_op jit(solution)/shard_map/ppermute | solution.py:498
  58.8 25.8 %shard_map.70 = (f32[512,512]{1,0:T(8,128)}, bf16[512,512]{1,0:T(8,128)(2,1)S(1)}, bf16[512,512]{1,0:T(8,128)(2,1)S(1)}) custom-call(f32[1280,128]{1,0:T(8,128)S(1)} %get-tuple-element.97.sum_ref, f32[1280,128]{1,0:T(8,128)S(1)} %get-tuple-element.63.prior_ref), custom_call_target="tpu_custom_call" | custom-call | flops 1 | bytes 1 | tf_op jit(solution)/shard_map/pallas_call | solution.py:419
  84.6 4.1 %shard_map.71.rest_2_ = f32[2048,512]{1,0:T(8,128)} custom-call(s32[1]{0:T(128)} %bitcast.2.me_ref, bf16[512,512]{1,0:T(8,128)(2,1)S(1)} %get-tuple-element.64.high_ref, bf16[512,512]{1,0:T(8,128)(2,1)S(1)} %get-tuple-element.65.low_ref, f32[256,512]{1,0:T(8,128)} %get-tuple-element.72.rest_0_, f32[256,512]{1,0:T(8,128)S(1)} %collective-permute-done.4.rest_1_, ...), custom_call_target="tpu_custom_call" | custom-call | flops 1 | bytes 1 | tf_op jit(solution)/shard_map/pallas_call | solution.py:464
  88.7 7.7 %collective-permute-done.6.rest_0_ = f32[256,512]{1,0:T(8,128)S(1)} collective-permute-done((f32[256,512]{1,0:T(8,128)}, f32[256,512]{1,0:T(8,128)S(1)}, u32[]{:S(2)}, u32[]{:S(2)}) %collective-permute-start.6) | collective-permute-done | bytes 524320 | tf_op jit(solution)/shard_map/ppermute | solution.py:498
  96.5 1.8 %shard_map.72.rest_1_ = f32[2048,512]{1,0:T(8,128)} custom-call(s32[1]{0:T(128)} %bitcast.2.me_ref, bf16[512,512]{1,0:T(8,128)(2,1)S(1)} %get-tuple-element.64.high_ref, bf16[512,512]{1,0:T(8,128)(2,1)S(1)} %get-tuple-element.65.low_ref, f32[256,512]{1,0:T(8,128)S(1)} %collective-permute-done.6.rest_0_, ...), custom_call_target="tpu_custom_call", output_to_operand_aliasing={{}: (5, {})} | custom-call | flops 1 | bytes 1 | tf_op jit(solution)/shard_map/pallas_call | solution.py:464
  98.3 9.8 %collective-permute-done.5.rest_0_ = f32[256,512]{1,0:T(8,128)S(1)} collective-permute-done((f32[256,512]{1,0:T(8,128)}, f32[256,512]{1,0:T(8,128)S(1)}, u32[]{:S(2)}, u32[]{:S(2)}) %collective-permute-start.5) | collective-permute-done | bytes 524320 | tf_op jit(solution)/shard_map/ppermute | solution.py:498
  108.0 1.4 %shard_map.73 = f32[2048,512]{1,0:T(8,128)} custom-call(s32[1]{0:T(128)} %bitcast.2.me_ref, bf16[512,512]{1,0:T(8,128)(2,1)S(1)} %get-tuple-element.64.high_ref, bf16[512,512]{1,0:T(8,128)(2,1)S(1)} %get-tuple-element.65.low_ref, f32[256,512]{1,0:T(8,128)S(1)} %collective-permute-done.5.rest_0_, ...), custom_call_target="tpu_custom_call", output_to_operand_aliasing={{}: (4, {})} | custom-call | flops 1 | bytes 1 | tf_op jit(solution)/shard_map/pallas_call | solution.py:464
  (15 shorter events, 0.7 us)
Async XLA Ops:
  0.6 10.2 %copy-start = (f32[128]{0:T(128)S(1)}, f32[128]{0:T(128)}, u32[]{:S(2)}) copy-start(f32[128]{0:T(128)} %param.11) | copy-start | bytes 1540
  6.7 24.6 %collective-permute-start = (f32[256,512]{1,0:T(8,128)}, f32[256,512]{1,0:T(8,128)S(1)}, u32[]{:S(2)}, u32[]{:S(2)}) collective-permute-start(f32[256,512]{1,0:T(8,128)} %get-tuple-element.58), channel_id=1, source_target_pairs={{0,4},{4,0},{8,12},{12,8},{16,20},{20,16},{24,28},{28,24},{1,5},{5... | collective-permute-start | bytes 1572872 | tf_op jit(solution)/shard_map/ppermute | solution.py:498
  8.2 27.9 %collective-permute-start.4 = (f32[256,512]{1,0:T(8,128)}, f32[256,512]{1,0:T(8,128)S(1)}, u32[]{:S(2)}, u32[]{:S(2)}) collective-permute-start(f32[256,512]{1,0:T(8,128)} %get-tuple-element.53), channel_id=1, source_target_pairs={{0,16},{4,20},{8,24},{12,28},{16,0},{20,4},{24,8},{28,12},{1,17},{... | collective-permute-start | bytes 1572872 | tf_op jit(solution)/shard_map/ppermute | solution.py:498
  10.9 2.0 %copy-start.1 = (bf16[2048,1024]{1,0:T(8,128)(2,1)}, bf16[2048,1024]{1,0:T(8,128)(2,1)S(1)}, u32[]{:S(2)}) copy-start(bf16[2048,1024]{1,0:T(8,128)(2,1)S(1)} %get-tuple-element.14.pair_ref) | copy-start | bytes 12582916 | tf_op jit(solution)/shard_map/cond
  17.5 13.7 %all-to-all-start = ((f32[8,160,128]{2,1,0:T(8,128)}), f32[8,160,128]{2,1,0:T(8,128)S(1)}, u32[]{:S(2)}, u32[]{:S(2)}) async-start(f32[8,160,128]{2,1,0:T(8,128)} %bitcast), calls=%async_computation | async-start | bytes 1310720 | tf_op jit(solution)/shard_map/cond/branch_1_fun/all_to_all | solution.py:337
  31.2 8.4 %collective-permute-start.3 = (f32[160,128]{1,0:T(8,128)S(1)}, f32[160,128]{1,0:T(8,128)S(1)}, u32[]{:S(2)}, u32[]{:S(2)}) collective-permute-start(f32[160,128]{1,0:T(8,128)S(1)} %get-tuple-element.59), channel_id=1, source_target_pairs={{0,24},{4,28},{8,16},{12,20},{16,8},{20,12},{24,0},{28,4},{1,25},{... | collective-permute-start | bytes 245768 | tf_op jit(solution)/shard_map/ppermute | solution.py:498
  31.3 8.9 %collective-permute-start.2 = (f32[160,128]{1,0:T(8,128)S(1)}, f32[160,128]{1,0:T(8,128)S(1)}, u32[]{:S(2)}, u32[]{:S(2)}) collective-permute-start(f32[160,128]{1,0:T(8,128)S(1)} %get-tuple-element.59), channel_id=1, source_target_pairs={{0,16},{4,20},{8,24},{12,28},{16,0},{20,4},{24,8},{28,12},{1,17},{... | collective-permute-start | bytes 245768 | tf_op jit(solution)/shard_map/ppermute | solution.py:498
  34.1 6.1 %collective-permute-start.1 = (f32[160,128]{1,0:T(8,128)S(1)}, f32[160,128]{1,0:T(8,128)S(1)}, u32[]{:S(2)}, u32[]{:S(2)}) collective-permute-start(f32[160,128]{1,0:T(8,128)S(1)} %get-tuple-element.59), channel_id=1, source_target_pairs={{0,8},{4,12},{8,0},{12,4},{16,24},{20,28},{24,16},{28,20},{1,9},{5... | collective-permute-start | bytes 245768 | tf_op jit(solution)/shard_map/ppermute | solution.py:498
  34.8 49.8 %collective-permute-start.8 = (f32[256,512]{1,0:T(8,128)}, f32[256,512]{1,0:T(8,128)S(1)}, u32[]{:S(2)}, u32[]{:S(2)}) collective-permute-start(f32[256,512]{1,0:T(8,128)} %get-tuple-element.76), channel_id=1, source_target_pairs={{0,8},{4,12},{8,0},{12,4},{16,24},{20,28},{24,16},{28,20},{1,9},{5... | collective-permute-start | bytes 1572872 | tf_op jit(solution)/shard_map/ppermute | solution.py:498
  36.1 48.5 %collective-permute-start.9 = (f32[256,512]{1,0:T(8,128)}, f32[256,512]{1,0:T(8,128)S(1)}, u32[]{:S(2)}, u32[]{:S(2)}) collective-permute-start(f32[256,512]{1,0:T(8,128)} %get-tuple-element.77), channel_id=1, source_target_pairs={{0,24},{4,28},{8,16},{12,20},{16,8},{20,12},{24,0},{28,4},{1,25},{... | collective-permute-start | bytes 1572872 | tf_op jit(solution)/shard_map/ppermute | solution.py:498
  53.8 42.7 %collective-permute-start.6 = (f32[256,512]{1,0:T(8,128)}, f32[256,512]{1,0:T(8,128)S(1)}, u32[]{:S(2)}, u32[]{:S(2)}) collective-permute-start(f32[256,512]{1,0:T(8,128)} %get-tuple-element.69), channel_id=1, source_target_pairs={{0,20},{4,16},{8,28},{12,24},{16,4},{20,0},{24,12},{28,8},{1,21},{... | collective-permute-start | bytes 1572872 | tf_op jit(solution)/shard_map/ppermute | solution.py:498
  57.4 39.1 %collective-permute-start.7 = (f32[256,512]{1,0:T(8,128)}, f32[256,512]{1,0:T(8,128)S(1)}, u32[]{:S(2)}, u32[]{:S(2)}) collective-permute-start(f32[256,512]{1,0:T(8,128)} %get-tuple-element.71), channel_id=1, source_target_pairs={{0,12},{4,8},{8,4},{12,0},{16,28},{20,24},{24,20},{28,16},{1,13},{... | collective-permute-start | bytes 1572872 | tf_op jit(solution)/shard_map/ppermute | solution.py:498
  57.4 50.6 %collective-permute-start.5 = (f32[256,512]{1,0:T(8,128)}, f32[256,512]{1,0:T(8,128)S(1)}, u32[]{:S(2)}, u32[]{:S(2)}) collective-permute-start(f32[256,512]{1,0:T(8,128)} %get-tuple-element.67), channel_id=1, source_target_pairs={{0,28},{4,24},{8,20},{12,16},{16,12},{20,8},{24,4},{28,0},{1,29},{... | collective-permute-start | bytes 1572872 | tf_op jit(solution)/shard_map/ppermute | solution.py:498

commit v11 on v10

--- a/solution.py
+++ b/solution.py
@@ -85,9 +85,11 @@
 
 
 def lead_kernel(groups, per_bucket, leads, me_ref, *refs):
-    given, outs, refs = refs[:4], refs[4 : 4 + len(leads)], refs[4 + len(leads) :]
+    given, far_outs, refs = refs[:4], refs[4 : 4 + len(leads)], refs[4 + len(leads) :]
     (pair_ref, place_ref, meta_ref), held, scratch = refs[:3], refs[3:7], refs[7:]
-    sorted_ref, small_a, small_b, inv_ref, table, sems = scratch
+    sorted_ref, small_a, small_b, inv_ref, outs_ref, table, sems = scratch
+    outs = [outs_ref.at[n] for n in range(len(leads))]
+    some = small_a.shape[0] // len(leads)
     buckets_ref, ids_ref, sigma_ref, obs_ref = held
     blocks, block = place_ref.shape
     wide = block // LANES
@@ -132,13 +134,12 @@
     target = jnp.minimum(before >> 3, last_tile)
     final = jnp.maximum(tiles - 1, 0)
     meta = jnp.where(lane == 2, first, final)
-    meta_ref[...] = jnp.where(lane == 0, kept, jnp.where(lane == 1, target, meta))
+    meta = jnp.where(lane == 0, kept, jnp.where(lane == 1, target, meta))
     copy = pltpu.make_async_copy(meta_ref, table, sems.at[3])
-    copy.start()
     local = first * SUB + odd
     local = jnp.concatenate([local] * wide, axis=1)
     spot = jnp.where(hits, local + running.astype(I32) - 1, 0)
-    place_ref[...] = jnp.concatenate(
+    places = jnp.concatenate(
         [jnp.sum(spot[s * groups : (s + 1) * groups], axis=0, keepdims=True) for s in range(blocks)],
         axis=0,
     )
@@ -149,6 +150,10 @@
     block_rows = lambda s: pl.ds(pl.multiple_of(s * block, block), block)
 
     for s in range(blocks):
+        if s == blocks // 2:
+            meta_ref[...] = meta
+            copy.start()
+            place_ref[...] = places
         ids = [ids_ref[s * wide + i : s * wide + i + 1, :] for i in range(wide)]
         known = iota((sensors, block), 0) == jnp.concatenate(ids, axis=1)
         scale_row = jnp.sum(jnp.where(known, inv, 0.0), axis=0, keepdims=True)
@@ -159,10 +164,8 @@
         pair_ref[rows, :state] = high
         pair_ref[rows, state:] = low
 
-    def sort_block(s, into, base):
-        spots = place_ref[pl.ds(s, 1), :] - base
-        picked = (iota((into.shape[0], block), 0) == spots).astype(F32).astype(BF16)
-        both = dot(picked, pair_ref[block_rows(s), :])
+    def sort_into(s, picked, into):
+        both = dot(picked.astype(F32).astype(BF16), pair_ref[block_rows(s), :])
         into[...] = both[:, :state] + both[:, state:]
 
     copy.wait()
@@ -171,21 +174,30 @@
     @pl.when((longest < runs.most) & unroll)
     def _():
         for s in range(blocks if unroll else 0):
+            into = (small_a, small_b)[s % 2]
+            spots = place_ref[s : s + 1, :]
+            picked = [iota((some, block), 0) == spots - runs.get(s, v)[2] * SUB for v in leads]
+            sort_into(s, jnp.concatenate(picked, axis=0), into)
             for n, v in enumerate(leads):
-                into = (small_a, small_b)[(s * len(leads) + n) % 2]
-                sort_block(s, into, runs.get(s, v)[2] * SUB)
-                runs.place(s, v, outs[n], into, 0)
+                runs.place(s, v, outs[n], into, n * some // SUB)
 
     @pl.when((longest >= runs.most) | (not unroll))
     def _():
         def body(s, carry):
-            sort_block(s, sorted_ref, 0)
+            sort_into(s, iota((padded, block), 0) == place_ref[pl.ds(s, 1), :], sorted_ref)
             for v, out in zip(leads, outs):
                 runs.place(s, v, out, sorted_ref)
                 runs.place_rest(s, v, out, sorted_ref)
             return carry
 
         lax.fori_loop(0, blocks, body, 0)
+
+    copies = []
+    for n, far in enumerate(far_outs):
+        copies.append(pltpu.make_async_copy(outs_ref.at[n], far, sems.at[4 + blocks + n]))
+        copies[-1].start()
+    for copy in copies:
+        copy.wait()
 
 
 def rest_kernel(groups, per_bucket, others, table, place_ref, pair_ref, *refs):
@@ -241,18 +253,20 @@
     return pl.pallas_call(
         functools.partial(lead_kernel, groups, per_bucket, tuple(leads)),
         in_specs=[pl.BlockSpec(memory_space=pltpu.SMEM)] + [far] * 4,
-        out_specs=[pl.BlockSpec(memory_space=pltpu.VMEM)] * (len(leads) + 3),
+        out_specs=[pl.BlockSpec(memory_space=pl.ANY)] * len(leads)
+        + [pl.BlockSpec(memory_space=pltpu.VMEM)] * 3,
         scratch_shapes=[
             pltpu.VMEM((rows // LANES, LANES), I32),
             pltpu.VMEM((rows // LANES, LANES), I32),
             pltpu.VMEM((1, sensors), F32),
             pltpu.VMEM((rows, state), F32),
             pltpu.VMEM((sorted_rows(block, groups), state), F32),
-            pltpu.VMEM((64, state), F32),
-            pltpu.VMEM((64, state), F32),
+            pltpu.VMEM((64 * len(leads), state), F32),
+            pltpu.VMEM((64 * len(leads), state), F32),
             pltpu.VMEM((sensors, LANES), F32),
+            pltpu.VMEM((len(leads), per_bucket, state), F32),
             pltpu.SMEM((cells, LANES), I32),
-            pltpu.SemaphoreType.DMA((4 + blocks,)),
+            pltpu.SemaphoreType.DMA((4 + blocks + len(leads),)),
         ],
         out_shape=[jax.ShapeDtypeStruct((per_bucket, state), F32)] * len(leads)
         + [
@@ -516,31 +530,29 @@
     piece, prior_gram, rest = lax.cond(valid, first, wrong)
     rest = dict(zip(others, rest))
     received[0] = rest[0]
-    for k in leads[1:]:
-        piece, received[k] = behind(piece, received[k])
     across = [piece]
     for step in range(1, groups // 2):
         across.append(move(2 * step, piece))
+    for k in middle[1:]:
+        received[k] = move(k, behind(piece, rest[k])[1])
     for k in middle[:1]:
-        received[k] = move(k, behind(piece, rest[k])[1])
+        received[leads[0]], chunk = behind(received[leads[0]], rest[k])
+        received[k] = move(k, chunk)
     while len(across) > 1:
         across = [across[i] + across[i + 1] for i in range(0, len(across), 2)]
-    for k in middle[1:]:
-        received[leads[0]], chunk = behind(received[leads[0]], rest[k])
-        received[k] = move(k, chunk)
     across[0], received[leads[0]] = behind(across[0], received[leads[0]])
     summed = lax.cond(
         valid, lambda: gather_pieces(across[0], plane, planes), lambda: nothing(packed_rows)
     )
+    for k in leads[1:]:
+        summed, received[k] = behind(summed, received[k])
     for k in late:
         received[k] = move(k, behind(summed, rest[k])[1])
     factor, high, low = factorise(summed, prior_gram, state, total_rows)
     out = None
-    soon = [0, *leads, *middle]
-    for steps in (soon, late[:-1], late[-1:]):
-        if not steps:
-            continue
-        out = whiten(me, high, low, steps, [received[k] for k in steps], out, rows_dev)
+    for steps in ([0, *leads, *middle], late[:-1], late[-1:]):
+        if steps:
+            out = whiten(me, high, low, steps, [received[k] for k in steps], out, rows_dev)
     return (out, factor)
 
 

time: 110 us -> 117 us (1.064)
  waiting for transfers between devices: 25.3 us -> 31.6 us
  Pallas kernels: 49.7 us -> 47.7 us
  starting transfers between devices: 18 us -> 19.8 us
    ppermute x10, waiting for transfers between devices: 21.1 us -> 27.4 us  [shards(): lax.ppermute(chunk, 'rows', [(i, i ^ k) for i in range(groups)])]
    ppermute x10, starting transfers between devices: 14.5 us -> 16.3 us  [shards(): lax.ppermute(chunk, 'rows', [(i, i ^ k) for i in range(groups)])]
    pallas_call x1, Pallas kernels: 4.57 us -> 3.35 us  [gram(): pl.pallas_call(gram_kernel, in_specs=[vmem] * 2, out_specs=[vmem] * 2, ou...]
  transfers between devices with their start and end apart: 11 -> 11, of which waited for: 5 -> 3; matrix products, arithmetic and copies ran while one was open for 0% -> 0% of each run, Pallas kernels for 39% -> 35%
where the time goes in v11:
time: 117 us; the launch traced here: 116 us
  Pallas kernels  47.7 us (41%)
  waiting for transfers between devices  31.6 us (27%)
  starting transfers between devices  19.8 us (17%)
  blocking collectives  13.9 us (12%)
  local copies, waits for them, and re-layouts  2.06 us (2%)
    ppermute x10, waiting for transfers between devices, shards(): lax.ppermute(chunk, 'rows', [(i, i ^ k) for i in range(groups)])  27.4 us
    pallas_call x1, Pallas kernels, factorise(): pl.pallas_call(functools.partial(factor_kernel, 1.0 / total_rows), in_spe...  25.8 us
    ppermute x10, starting transfers between devices, shards(): lax.ppermute(chunk, 'rows', [(i, i ^ k) for i in range(groups)])  16.3 us
    all_to_all x1, blocking collectives, gather_pieces(): lax.all_to_all(copies, axes, split_axis=0, concat_axis=0, axis_index_grou...  13.9 us
    pallas_call x3, Pallas kernels, whiten(): pl.pallas_call(functools.partial(whiten_kernel, tuple(steps), len(extra))...  7.29 us
    pallas_call x1, Pallas kernels, regroup_rest(): pl.pallas_call(functools.partial(rest_kernel, groups, per_bucket, tuple(o...  5.97 us
    pallas_call x1, Pallas kernels, regroup_lead(): pl.pallas_call(functools.partial(lead_kernel, groups, per_bucket, tuple(l...  5.27 us
    all_to_all x1, waiting for transfers between devices, scatter_sum(): lax.all_to_all(packed, axes, split_axis=0, concat_axis=0, axis_index_grou...  4.19 us
  transfers between devices with their start and end apart: 11, of which 3 were waited for; matrix products, arithmetic and copies ran while one was open for 0% of the time, Pallas kernels for 35%

profile of v11, /device:TPU:8, one launch (start us, length us, event | category | flops | bytes accessed | tf_op | source)
XLA Modules:
  0.0 116.1 jit_solution(3131605475597642414)
XLA Ops:
  0.7 5.3 %shard_map.69 = (f32[256,512]{1,0:T(8,128)}, f32[256,512]{1,0:T(8,128)}, bf16[2048,1024]{1,0:T(8,128)(2,1)S(1)}, s32[8,256]{1,0:T(8,128)S(1)}, s32[64,128]{1,0:T(8,128)S(1)}) custom-call(s32[1]{0:T(128)} %bitcast.2.me_ref, s32[16,128]{1,0:T(8,128)} %bitcast.9, s32[16,128]{1,0:T(8,128)} %bitcast.10, f32[1,128]{1,0:T(1,128)} %bitcast.11, f32[2048,512]{1,0:T(8,128)} %refs_3_.1), custom_call_target="tpu_custom_call" | custom-call | flops 1048576 | bytes 8388608 | tf_op jit(solution)/shard_map/pallas_call | solution.py:253
  5.9 2.7 %collective-permute-start.3 = (f32[256,512]{1,0:T(8,128)}, f32[256,512]{1,0:T(8,128)S(1)}, u32[]{:S(2)}, u32[]{:S(2)}) collective-permute-start(f32[256,512]{1,0:T(8,128)} %get-tuple-element.53), channel_id=1, source_target_pairs={{0,16},{4,20},{8,24},{12,28},{16,0},{20,4},{24,8},{28,12},{1,17},{... | collective-permute-start | bytes 1572872 | tf_op jit(solution)/shard_map/ppermute | solution.py:512
  8.6 1.5 %collective-permute-start.4 = (f32[256,512]{1,0:T(8,128)}, f32[256,512]{1,0:T(8,128)S(1)}, u32[]{:S(2)}, u32[]{:S(2)}) collective-permute-start(f32[256,512]{1,0:T(8,128)} %get-tuple-element.61), channel_id=1, source_target_pairs={{0,4},{4,0},{8,12},{12,8},{16,20},{20,16},{24,28},{28,24},{1,5},{5... | collective-permute-start | bytes 1572872 | tf_op jit(solution)/shard_map/ppermute | solution.py:512
  10.1 19.1 %conditional.2 = (f32[160,128]{1,0:T(8,128)S(1)}, f32[1280,128]{1,0:T(8,128)S(1)}, f32[256,512]{1,0:T(8,128)}, f32[256,512]{1,0:T(8,128)}, f32[256,512]{1,0:T(8,...) conditional(s32[]{:T(128)} %bitcast.3, f32[256,512]{1,0:T(8,128)} %get-tuple-element.53, ...), branch_computations={%region_0.0_spmd, %region_1.0_spmd} | conditional | flops 5234634752 | bytes 32063616 | solution.py:530
  10.2 2.0 %copy-done.1 = bf16[2048,1024]{1,0:T(8,128)(2,1)} copy-done((bf16[2048,1024]{1,0:T(8,128)(2,1)}, bf16[2048,1024]{1,0:T(8,128)(2,1)S(1)}, u32[]{:S(2)}) %copy-start.1) | copy-done | bytes 4194328 | tf_op jit(solution)/shard_map/cond
  12.2 3.4 %branch_1_fun.2 = (f32[1280,128]{1,0:T(8,128)}, f32[1280,128]{1,0:T(8,128)S(1)}) custom-call(f32[512,512]{1,0:T(8,128)S(1)} %get-tuple-element.80.prior_ref, bf16[2048,1024]{1,0:T(8,128)(2,1)S(1)} %get-tuple-element.14.pair_ref), custom_call_target="tpu_custom_call" | custom-call | flops 2147483648 | bytes 4194304 | tf_op jit(solution)/shard_map/cond/branch_1_fun/pallas_call | solution.py:335
  15.5 3.5 %all-to-all-start = ((f32[8,160,128]{2,1,0:T(8,128)}), f32[8,160,128]{2,1,0:T(8,128)S(1)}, u32[]{:S(2)}, u32[]{:S(2)}) async-start(f32[8,160,128]{2,1,0:T(8,128)} %bitcast), calls=%async_computation | async-start | bytes 1310720 | tf_op jit(solution)/shard_map/cond/branch_1_fun/all_to_all | solution.py:351
  19.1 6.0 %branch_1_fun.3 = (f32[256,512]{1,0:T(8,128)}, f32[256,512]{1,0:T(8,128)}, f32[256,512]{1,0:T(8,128)}, f32[256,512]{1,0:T(8,128)}, f32[256,512]{1,0:T(8,128)}, /*index=5*/f32[256,512]{1,0:T(8,128)}) custom-call(s32[64,128]{1,0:T(8,128)S(1)} %get-tuple-element.17.table, s32[8,256]{1,0:T(8,128)S(1)} %get-tuple-element.18.place_ref, bf16[2048,1024]{1,0:T(8,128)(2,1)} %copy-done.1), custom_call_target="tpu_custom_call" | custom-call | flops 3087007744 | bytes 8388608 | tf_op jit(solution)/shard_map/cond/branch_1_fun/pallas_call | solution.py:295
  25.0 4.2 %all-to-all-done = f32[8,160,128]{2,1,0:T(8,128)S(1)} async-done(((f32[8,160,128]{2,1,0:T(8,128)}), f32[8,160,128]{2,1,0:T(8,128)S(1)}, u32[]{:S(2)}, u32[]{:S(2)}) %all-to-all-start) | async-done | bytes 655392 | tf_op jit(solution)/shard_map/cond/branch_1_fun/all_to_all | solution.py:351
  29.3 0.1 collective-permute-start.2
  29.4 2.8 %collective-permute-start.1 = (f32[160,128]{1,0:T(8,128)S(1)}, f32[160,128]{1,0:T(8,128)S(1)}, u32[]{:S(2)}, u32[]{:S(2)}) collective-permute-start(f32[160,128]{1,0:T(8,128)S(1)} %get-tuple-element.57), channel_id=1, source_target_pairs={{0,16},{4,20},{8,24},{12,28},{16,0},{20,4},{24,8},{28,12},{1,17},{... | collective-permute-start | bytes 245768 | tf_op jit(solution)/shard_map/ppermute | solution.py:512
  32.2 0.7 collective-permute-start
  32.8 14.8 %collective-permute-done.2 = f32[160,128]{1,0:T(8,128)S(1)} collective-permute-done((f32[160,128]{1,0:T(8,128)S(1)}, f32[160,128]{1,0:T(8,128)S(1)}, u32[]{:S(2)}, u32[]{:S(2)}) %collective-permute-start.2) | collective-permute-done | bytes 81952 | tf_op jit(solution)/shard_map/ppermute | solution.py:512
  47.6 2.5 %collective-permute-start.9 = (f32[256,512]{1,0:T(8,128)}, f32[256,512]{1,0:T(8,128)S(1)}, u32[]{:S(2)}, u32[]{:S(2)}) collective-permute-start(f32[256,512]{1,0:T(8,128)} %get-tuple-element.77), channel_id=1, source_target_pairs={{0,24},{4,28},{8,16},{12,20},{16,8},{20,12},{24,0},{28,4},{1,25},{... | collective-permute-start | bytes 1572872 | tf_op jit(solution)/shard_map/ppermute | solution.py:512
  50.2 1.2 %collective-permute-start.8 = (f32[256,512]{1,0:T(8,128)}, f32[256,512]{1,0:T(8,128)S(1)}, u32[]{:S(2)}, u32[]{:S(2)}) collective-permute-start(f32[256,512]{1,0:T(8,128)} %get-tuple-element.75), channel_id=1, source_target_pairs={{0,8},{4,12},{8,0},{12,4},{16,24},{20,28},{24,16},{28,20},{1,9},{5... | collective-permute-start | bytes 1572872 | tf_op jit(solution)/shard_map/ppermute | solution.py:512
  51.4 14.0 %conditional.3 = (f32[1280,128]{1,0:T(8,128)S(1)}) conditional(s32[]{:T(128)} %bitcast.3, () %tuple.29, f32[160,128]{1,0:T(8,128)S(1)} %add_add_fusion), branch_computations={%region_3.0_spmd, %region_4.0_spmd} | conditional | bytes 2048008 | solution.py:544
  51.4 13.9 %all_to_all.14 = f32[8,160,128]{2,1,0:T(8,128)S(1)} all-to-all(f32[8,160,128]{2,1,0:T(8,128)S(1)} %broadcast_in_dim.2), channel_id=1, replica_groups={{0,1,2,3,4,5,6,7},{8,9,10,11,12,13,14,15},{16,17,18,19,20,21,22,23},{24..., dimensions={0} | all-to-all | bytes 1310720 | tf_op jit(solution)/shard_map/cond/branch_1_fun/all_to_all | solution.py:359
  65.4 2.2 %collective-permute-start.6 = (f32[256,512]{1,0:T(8,128)}, f32[256,512]{1,0:T(8,128)S(1)}, u32[]{:S(2)}, u32[]{:S(2)}) collective-permute-start(f32[256,512]{1,0:T(8,128)} %get-tuple-element.69), channel_id=1, source_target_pairs={{0,20},{4,16},{8,28},{12,24},{16,4},{20,0},{24,12},{28,8},{1,21},{... | collective-permute-start | bytes 1572872 | tf_op jit(solution)/shard_map/ppermute | solution.py:512
  67.6 2.6 %collective-permute-start.7 = (f32[256,512]{1,0:T(8,128)}, f32[256,512]{1,0:T(8,128)S(1)}, u32[]{:S(2)}, u32[]{:S(2)}) collective-permute-start(f32[256,512]{1,0:T(8,128)} %get-tuple-element.71), channel_id=1, source_target_pairs={{0,12},{4,8},{8,4},{12,0},{16,28},{20,24},{24,20},{28,16},{1,13},{... | collective-permute-start | bytes 1572872 | tf_op jit(solution)/shard_map/ppermute | solution.py:512
  70.2 25.8 %shard_map.70 = (f32[512,512]{1,0:T(8,128)}, bf16[512,512]{1,0:T(8,128)(2,1)S(1)}, bf16[512,512]{1,0:T(8,128)(2,1)S(1)}) custom-call(f32[1280,128]{1,0:T(8,128)S(1)} %get-tuple-element.97.sum_ref, f32[1280,128]{1,0:T(8,128)S(1)} %get-tuple-element.63.prior_ref), custom_call_target="tpu_custom_call" | custom-call | flops 1 | bytes 1 | tf_op jit(solution)/shard_map/pallas_call | solution.py:433
  96.0 4.1 %shard_map.71.rest_2_ = f32[2048,512]{1,0:T(8,128)} custom-call(s32[1]{0:T(128)} %bitcast.2.me_ref, bf16[512,512]{1,0:T(8,128)(2,1)S(1)} %get-tuple-element.64.high_ref, bf16[512,512]{1,0:T(8,128)(2,1)S(1)} %get-tuple-element.65.low_ref, f32[256,512]{1,0:T(8,128)} %get-tuple-element.72.rest_0_, f32[256,512]{1,0:T(8,128)S(1)} %collective-permute-done.3.rest_1_, ...), custom_call_target="tpu_custom_call" | custom-call | flops 1 | bytes 1 | tf_op jit(solution)/shard_map/pallas_call | solution.py:478
  100.1 1.8 %shard_map.72.rest_1_ = f32[2048,512]{1,0:T(8,128)} custom-call(s32[1]{0:T(128)} %bitcast.2.me_ref, bf16[512,512]{1,0:T(8,128)(2,1)S(1)} %get-tuple-element.64.high_ref, bf16[512,512]{1,0:T(8,128)(2,1)S(1)} %get-tuple-element.65.low_ref, f32[256,512]{1,0:T(8,128)S(1)} %collective-permute-done.6.rest_0_, ...), custom_call_target="tpu_custom_call", output_to_operand_aliasing={{}: (5, {})} | custom-call | flops 1 | bytes 1 | tf_op jit(solution)/shard_map/pallas_call | solution.py:478
  102.0 12.6 %collective-permute-done.5.rest_0_ = f32[256,512]{1,0:T(8,128)S(1)} collective-permute-done((f32[256,512]{1,0:T(8,128)}, f32[256,512]{1,0:T(8,128)S(1)}, u32[]{:S(2)}, u32[]{:S(2)}) %collective-permute-start.5) | collective-permute-done | bytes 524320 | tf_op jit(solution)/shard_map/ppermute | solution.py:512
  114.5 1.4 %shard_map.73 = f32[2048,512]{1,0:T(8,128)} custom-call(s32[1]{0:T(128)} %bitcast.2.me_ref, bf16[512,512]{1,0:T(8,128)(2,1)S(1)} %get-tuple-element.64.high_ref, bf16[512,512]{1,0:T(8,128)(2,1)S(1)} %get-tuple-element.65.low_ref, f32[256,512]{1,0:T(8,128)S(1)} %collective-permute-done.5.rest_0_, ...), custom_call_target="tpu_custom_call", output_to_operand_aliasing={{}: (4, {})} | custom-call | flops 1 | bytes 1 | tf_op jit(solution)/shard_map/pallas_call | solution.py:478
  (17 shorter events, 0.1 us)
Async XLA Ops:
  0.6 9.5 %copy-start = (f32[128]{0:T(128)S(1)}, f32[128]{0:T(128)}, u32[]{:S(2)}) copy-start(f32[128]{0:T(128)} %param.11) | copy-start | bytes 1540
  0.6 9.5 %copy-start.2 = (f32[512,512]{1,0:T(8,128)S(1)}, f32[512,512]{1,0:T(8,128)}, u32[]{:S(2)}) copy-start(f32[512,512]{1,0:T(8,128)} %param.13) | copy-start | bytes 3145732
  5.9 44.3 %collective-permute-start.3 = (f32[256,512]{1,0:T(8,128)}, f32[256,512]{1,0:T(8,128)S(1)}, u32[]{:S(2)}, u32[]{:S(2)}) collective-permute-start(f32[256,512]{1,0:T(8,128)} %get-tuple-element.53), channel_id=1, source_target_pairs={{0,16},{4,20},{8,24},{12,28},{16,0},{20,4},{24,8},{28,12},{1,17},{... | collective-permute-start | bytes 1572872 | tf_op jit(solution)/shard_map/ppermute | solution.py:512
  8.6 56.8 %collective-permute-start.4 = (f32[256,512]{1,0:T(8,128)}, f32[256,512]{1,0:T(8,128)S(1)}, u32[]{:S(2)}, u32[]{:S(2)}) collective-permute-start(f32[256,512]{1,0:T(8,128)} %get-tuple-element.61), channel_id=1, source_target_pairs={{0,4},{4,0},{8,12},{12,8},{16,20},{20,16},{24,28},{28,24},{1,5},{5... | collective-permute-start | bytes 1572872 | tf_op jit(solution)/shard_map/ppermute | solution.py:512
  10.2 2.0 %copy-start.1 = (bf16[2048,1024]{1,0:T(8,128)(2,1)}, bf16[2048,1024]{1,0:T(8,128)(2,1)S(1)}, u32[]{:S(2)}) copy-start(bf16[2048,1024]{1,0:T(8,128)(2,1)S(1)} %get-tuple-element.14.pair_ref) | copy-start | bytes 12582916 | tf_op jit(solution)/shard_map/cond
  15.5 13.7 %all-to-all-start = ((f32[8,160,128]{2,1,0:T(8,128)}), f32[8,160,128]{2,1,0:T(8,128)S(1)}, u32[]{:S(2)}, u32[]{:S(2)}) async-start(f32[8,160,128]{2,1,0:T(8,128)} %bitcast), calls=%async_computation | async-start | bytes 1310720 | tf_op jit(solution)/shard_map/cond/branch_1_fun/all_to_all | solution.py:351
  29.3 18.4 %collective-permute-start.2 = (f32[160,128]{1,0:T(8,128)S(1)}, f32[160,128]{1,0:T(8,128)S(1)}, u32[]{:S(2)}, u32[]{:S(2)}) collective-permute-start(f32[160,128]{1,0:T(8,128)S(1)} %get-tuple-element.57), channel_id=1, source_target_pairs={{0,24},{4,28},{8,16},{12,20},{16,8},{20,12},{24,0},{28,4},{1,25},{... | collective-permute-start | bytes 245768 | tf_op jit(solution)/shard_map/ppermute | solution.py:512
  29.4 20.8 %collective-permute-start.1 = (f32[160,128]{1,0:T(8,128)S(1)}, f32[160,128]{1,0:T(8,128)S(1)}, u32[]{:S(2)}, u32[]{:S(2)}) collective-permute-start(f32[160,128]{1,0:T(8,128)S(1)} %get-tuple-element.57), channel_id=1, source_target_pairs={{0,16},{4,20},{8,24},{12,28},{16,0},{20,4},{24,8},{28,12},{1,17},{... | collective-permute-start | bytes 245768 | tf_op jit(solution)/shard_map/ppermute | solution.py:512
  32.2 18.0 %collective-permute-start = (f32[160,128]{1,0:T(8,128)S(1)}, f32[160,128]{1,0:T(8,128)S(1)}, u32[]{:S(2)}, u32[]{:S(2)}) collective-permute-start(f32[160,128]{1,0:T(8,128)S(1)} %get-tuple-element.57), channel_id=1, source_target_pairs={{0,8},{4,12},{8,0},{12,4},{16,24},{20,28},{24,16},{28,20},{1,9},{5... | collective-permute-start | bytes 245768 | tf_op jit(solution)/shard_map/ppermute | solution.py:512
  47.6 48.4 %collective-permute-start.9 = (f32[256,512]{1,0:T(8,128)}, f32[256,512]{1,0:T(8,128)S(1)}, u32[]{:S(2)}, u32[]{:S(2)}) collective-permute-start(f32[256,512]{1,0:T(8,128)} %get-tuple-element.77), channel_id=1, source_target_pairs={{0,24},{4,28},{8,16},{12,20},{16,8},{20,12},{24,0},{28,4},{1,25},{... | collective-permute-start | bytes 1572872 | tf_op jit(solution)/shard_map/ppermute | solution.py:512
  50.2 45.8 %collective-permute-start.8 = (f32[256,512]{1,0:T(8,128)}, f32[256,512]{1,0:T(8,128)S(1)}, u32[]{:S(2)}, u32[]{:S(2)}) collective-permute-start(f32[256,512]{1,0:T(8,128)} %get-tuple-element.75), channel_id=1, source_target_pairs={{0,8},{4,12},{8,0},{12,4},{16,24},{20,28},{24,16},{28,20},{1,9},{5... | collective-permute-start | bytes 1572872 | tf_op jit(solution)/shard_map/ppermute | solution.py:512
  65.4 34.7 %collective-permute-start.6 = (f32[256,512]{1,0:T(8,128)}, f32[256,512]{1,0:T(8,128)S(1)}, u32[]{:S(2)}, u32[]{:S(2)}) collective-permute-start(f32[256,512]{1,0:T(8,128)} %get-tuple-element.69), channel_id=1, source_target_pairs={{0,20},{4,16},{8,28},{12,24},{16,4},{20,0},{24,12},{28,8},{1,21},{... | collective-permute-start | bytes 1572872 | tf_op jit(solution)/shard_map/ppermute | solution.py:512
  67.6 32.5 %collective-permute-start.7 = (f32[256,512]{1,0:T(8,128)}, f32[256,512]{1,0:T(8,128)S(1)}, u32[]{:S(2)}, u32[]{:S(2)}) collective-permute-start(f32[256,512]{1,0:T(8,128)} %get-tuple-element.71), channel_id=1, source_target_pairs={{0,12},{4,8},{8,4},{12,0},{16,28},{20,24},{24,20},{28,16},{1,13},{... | collective-permute-start | bytes 1572872 | tf_op jit(solution)/shard_map/ppermute | solution.py:512
  70.2 44.3 %collective-permute-start.5 = (f32[256,512]{1,0:T(8,128)}, f32[256,512]{1,0:T(8,128)S(1)}, u32[]{:S(2)}, u32[]{:S(2)}) collective-permute-start(f32[256,512]{1,0:T(8,128)} %get-tuple-element.67), channel_id=1, source_target_pairs={{0,28},{4,24},{8,20},{12,16},{16,12},{20,8},{24,4},{28,0},{1,29},{... | collective-permute-start | bytes 1572872 | tf_op jit(solution)/shard_map/ppermute | solution.py:512

commit v12 on v11

--- a/solution.py
+++ b/solution.py
@@ -530,22 +530,22 @@
     piece, prior_gram, rest = lax.cond(valid, first, wrong)
     rest = dict(zip(others, rest))
     received[0] = rest[0]
+    for k in leads[1:]:
+        piece, received[k] = behind(piece, received[k])
     across = [piece]
     for step in range(1, groups // 2):
         across.append(move(2 * step, piece))
+    for k in middle[:1]:
+        received[k] = move(k, behind(piece, rest[k])[1])
+    while len(across) > 1:
+        across = [across[i] + across[i + 1] for i in range(0, len(across), 2)]
     for k in middle[1:]:
-        received[k] = move(k, behind(piece, rest[k])[1])
-    for k in middle[:1]:
         received[leads[0]], chunk = behind(received[leads[0]], rest[k])
         received[k] = move(k, chunk)
-    while len(across) > 1:
-        across = [across[i] + across[i + 1] for i in range(0, len(across), 2)]
     across[0], received[leads[0]] = behind(across[0], received[leads[0]])
     summed = lax.cond(
         valid, lambda: gather_pieces(across[0], plane, planes), lambda: nothing(packed_rows)
     )
-    for k in leads[1:]:
-        summed, received[k] = behind(summed, received[k])
     for k in late:
         received[k] = move(k, behind(summed, rest[k])[1])
     factor, high, low = factorise(summed, prior_gram, state, total_rows)

time: 117 us -> 110 us (0.940)
  waiting for transfers between devices: 31.6 us -> 25.3 us
  starting transfers between devices: 19.8 us -> 18 us
  Pallas kernels: 47.7 us -> 48.9 us
    ppermute x10, waiting for transfers between devices: 27.4 us -> 21.1 us  [shards(): lax.ppermute(chunk, 'rows', [(i, i ^ k) for i in range(groups)])]
    ppermute x10, starting transfers between devices: 16.3 us -> 14.5 us  [shards(): lax.ppermute(chunk, 'rows', [(i, i ^ k) for i in range(groups)])]
    pallas_call x1, Pallas kernels: 3.35 us -> 4.58 us  [gram(): pl.pallas_call(gram_kernel, in_specs=[vmem] * 2, out_specs=[vmem] * 2, ou...]
  transfers between devices with their start and end apart: 11 -> 11, of which waited for: 3 -> 5; matrix products, arithmetic and copies ran while one was open for 0% -> 0% of each run, Pallas kernels for 35% -> 39%
where the time goes in v12:
time: 110 us; the launch traced here: 109 us
  Pallas kernels  48.9 us (44%)
  waiting for transfers between devices  25.3 us (23%)
  starting transfers between devices  18 us (16%)
  blocking collectives  13.5 us (12%)
  local copies, waits for them, and re-layouts  2.06 us (2%)
    pallas_call x1, Pallas kernels, factorise(): pl.pallas_call(functools.partial(factor_kernel, 1.0 / total_rows), in_spe...  25.8 us
    ppermute x10, waiting for transfers between devices, shards(): lax.ppermute(chunk, 'rows', [(i, i ^ k) for i in range(groups)])  21.1 us
    ppermute x10, starting transfers between devices, shards(): lax.ppermute(chunk, 'rows', [(i, i ^ k) for i in range(groups)])  14.5 us
    all_to_all x1, blocking collectives, gather_pieces(): lax.all_to_all(copies, axes, split_axis=0, concat_axis=0, axis_index_grou...  13.5 us
    pallas_call x3, Pallas kernels, whiten(): pl.pallas_call(functools.partial(whiten_kernel, tuple(steps), len(extra))...  7.33 us
    pallas_call x1, Pallas kernels, regroup_rest(): pl.pallas_call(functools.partial(rest_kernel, groups, per_bucket, tuple(o...  5.98 us
    pallas_call x1, Pallas kernels, regroup_lead(): pl.pallas_call(functools.partial(lead_kernel, groups, per_bucket, tuple(l...  5.2 us
    pallas_call x1, Pallas kernels, gram(): pl.pallas_call(gram_kernel, in_specs=[vmem] * 2, out_specs=[vmem] * 2, ou...  4.58 us
  transfers between devices with their start and end apart: 11, of which 5 were waited for; matrix products, arithmetic and copies ran while one was open for 0% of the time, Pallas kernels for 39%

profile of v12, /device:TPU:8, one launch (start us, length us, event | category | flops | bytes accessed | tf_op | source)
XLA Modules:
  0.0 108.8 jit_solution(15251277961181820763)
XLA Ops:
  0.6 5.2 %shard_map.69 = (f32[256,512]{1,0:T(8,128)}, f32[256,512]{1,0:T(8,128)}, bf16[2048,1024]{1,0:T(8,128)(2,1)S(1)}, s32[8,256]{1,0:T(8,128)S(1)}, s32[64,128]{1,0:T(8,128)S(1)}) custom-call(s32[1]{0:T(128)} %bitcast.2.me_ref, s32[16,128]{1,0:T(8,128)} %bitcast.9, s32[16,128]{1,0:T(8,128)} %bitcast.10, f32[1,128]{1,0:T(1,128)} %bitcast.11, f32[2048,512]{1,0:T(8,128)} %refs_3_.1), custom_call_target="tpu_custom_call" | custom-call | flops 1048576 | bytes 8388608 | tf_op jit(solution)/shard_map/pallas_call | solution.py:253
  5.8 1.6 %collective-permute-start = (f32[256,512]{1,0:T(8,128)}, f32[256,512]{1,0:T(8,128)S(1)}, u32[]{:S(2)}, u32[]{:S(2)}) collective-permute-start(f32[256,512]{1,0:T(8,128)} %get-tuple-element.58), channel_id=1, source_target_pairs={{0,4},{4,0},{8,12},{12,8},{16,20},{20,16},{24,28},{28,24},{1,5},{5... | collective-permute-start | bytes 1572872 | tf_op jit(solution)/shard_map/ppermute | solution.py:512
  7.4 2.6 %collective-permute-start.4 = (f32[256,512]{1,0:T(8,128)}, f32[256,512]{1,0:T(8,128)S(1)}, u32[]{:S(2)}, u32[]{:S(2)}) collective-permute-start(f32[256,512]{1,0:T(8,128)} %get-tuple-element.53), channel_id=1, source_target_pairs={{0,16},{4,20},{8,24},{12,28},{16,0},{20,4},{24,8},{28,12},{1,17},{... | collective-permute-start | bytes 1572872 | tf_op jit(solution)/shard_map/ppermute | solution.py:512
  10.0 20.4 %conditional.2 = (f32[160,128]{1,0:T(8,128)S(1)}, f32[1280,128]{1,0:T(8,128)S(1)}, f32[256,512]{1,0:T(8,128)}, f32[256,512]{1,0:T(8,128)}, f32[256,512]{1,0:T(8,...) conditional(s32[]{:T(128)} %bitcast.3, f32[256,512]{1,0:T(8,128)} %get-tuple-element.53, ...), branch_computations={%region_0.0_spmd, %region_1.0_spmd} | conditional | flops 5234634752 | bytes 32063616 | solution.py:530
  10.1 2.0 %copy-done.1 = bf16[2048,1024]{1,0:T(8,128)(2,1)} copy-done((bf16[2048,1024]{1,0:T(8,128)(2,1)}, bf16[2048,1024]{1,0:T(8,128)(2,1)S(1)}, u32[]{:S(2)}) %copy-start.1) | copy-done | bytes 4194328 | tf_op jit(solution)/shard_map/cond
  12.1 4.6 %branch_1_fun.2 = (f32[1280,128]{1,0:T(8,128)}, f32[1280,128]{1,0:T(8,128)S(1)}) custom-call(f32[512,512]{1,0:T(8,128)} %get-tuple-element.80.prior_ref, bf16[2048,1024]{1,0:T(8,128)(2,1)S(1)} %get-tuple-element.14.pair_ref), custom_call_target="tpu_custom_call" | custom-call | flops 2147483648 | bytes 4194304 | tf_op jit(solution)/shard_map/cond/branch_1_fun/pallas_call | solution.py:335
  16.7 3.5 %all-to-all-start = ((f32[8,160,128]{2,1,0:T(8,128)}), f32[8,160,128]{2,1,0:T(8,128)S(1)}, u32[]{:S(2)}, u32[]{:S(2)}) async-start(f32[8,160,128]{2,1,0:T(8,128)} %bitcast), calls=%async_computation | async-start | bytes 1310720 | tf_op jit(solution)/shard_map/cond/branch_1_fun/all_to_all | solution.py:351
  20.2 6.0 %branch_1_fun.3 = (f32[256,512]{1,0:T(8,128)}, f32[256,512]{1,0:T(8,128)}, f32[256,512]{1,0:T(8,128)}, f32[256,512]{1,0:T(8,128)}, f32[256,512]{1,0:T(8,128)}, /*index=5*/f32[256,512]{1,0:T(8,128)}) custom-call(s32[64,128]{1,0:T(8,128)S(1)} %get-tuple-element.17.table, s32[8,256]{1,0:T(8,128)S(1)} %get-tuple-element.18.place_ref, bf16[2048,1024]{1,0:T(8,128)(2,1)} %copy-done.1), custom_call_target="tpu_custom_call" | custom-call | flops 3087007744 | bytes 8388608 | tf_op jit(solution)/shard_map/cond/branch_1_fun/pallas_call | solution.py:295
  26.2 4.2 %all-to-all-done = f32[8,160,128]{2,1,0:T(8,128)S(1)} async-done(((f32[8,160,128]{2,1,0:T(8,128)}), f32[8,160,128]{2,1,0:T(8,128)S(1)}, u32[]{:S(2)}, u32[]{:S(2)}) %all-to-all-start) | async-done | bytes 655392 | tf_op jit(solution)/shard_map/cond/branch_1_fun/all_to_all | solution.py:351
  30.5 2.8 %collective-permute-start.2 = (f32[160,128]{1,0:T(8,128)S(1)}, f32[160,128]{1,0:T(8,128)S(1)}, u32[]{:S(2)}, u32[]{:S(2)}) collective-permute-start(f32[160,128]{1,0:T(8,128)S(1)} %get-tuple-element.59), channel_id=1, source_target_pairs={{0,16},{4,20},{8,24},{12,28},{16,0},{20,4},{24,8},{28,12},{1,17},{... | collective-permute-start | bytes 245768 | tf_op jit(solution)/shard_map/ppermute | solution.py:512
  33.3 0.7 collective-permute-start.1
  34.0 1.3 %collective-permute-start.8 = (f32[256,512]{1,0:T(8,128)}, f32[256,512]{1,0:T(8,128)S(1)}, u32[]{:S(2)}, u32[]{:S(2)}) collective-permute-start(f32[256,512]{1,0:T(8,128)} %get-tuple-element.76), channel_id=1, source_target_pairs={{0,8},{4,12},{8,0},{12,4},{16,24},{20,28},{24,16},{28,20},{1,9},{5... | collective-permute-start | bytes 1572872 | tf_op jit(solution)/shard_map/ppermute | solution.py:512
  35.8 3.1 %collective-permute-done.3 = f32[160,128]{1,0:T(8,128)S(1)} collective-permute-done((f32[160,128]{1,0:T(8,128)S(1)}, f32[160,128]{1,0:T(8,128)S(1)}, u32[]{:S(2)}, u32[]{:S(2)}) %collective-permute-start.3) | collective-permute-done | bytes 81952 | tf_op jit(solution)/shard_map/ppermute | solution.py:512
  38.9 0.5 collective-permute-done.2
  39.4 13.6 %conditional.3 = (f32[1280,128]{1,0:T(8,128)S(1)}) conditional(s32[]{:T(128)} %bitcast.3, () %tuple.29, f32[160,128]{1,0:T(8,128)S(1)} %add_add_fusion), branch_computations={%region_3.0_spmd, %region_4.0_spmd} | conditional | bytes 2048008 | solution.py:546
  39.5 13.5 %all_to_all.14 = f32[8,160,128]{2,1,0:T(8,128)S(1)} all-to-all(f32[8,160,128]{2,1,0:T(8,128)S(1)} %broadcast_in_dim.2), channel_id=1, replica_groups={{0,1,2,3,4,5,6,7},{8,9,10,11,12,13,14,15},{16,17,18,19,20,21,22,23},{24..., dimensions={0} | all-to-all | bytes 1310720 | tf_op jit(solution)/shard_map/cond/branch_1_fun/all_to_all | solution.py:359
  53.0 3.6 %collective-permute-start.6 = (f32[256,512]{1,0:T(8,128)}, f32[256,512]{1,0:T(8,128)S(1)}, u32[]{:S(2)}, u32[]{:S(2)}) collective-permute-start(f32[256,512]{1,0:T(8,128)} %get-tuple-element.69), channel_id=1, source_target_pairs={{0,20},{4,16},{8,28},{12,24},{16,4},{20,0},{24,12},{28,8},{1,21},{... | collective-permute-start | bytes 1572872 | tf_op jit(solution)/shard_map/ppermute | solution.py:512
  56.6 1.4 %collective-permute-start.5 = (f32[256,512]{1,0:T(8,128)}, f32[256,512]{1,0:T(8,128)S(1)}, u32[]{:S(2)}, u32[]{:S(2)}) collective-permute-start(f32[256,512]{1,0:T(8,128)} %get-tuple-element.67), channel_id=1, source_target_pairs={{0,28},{4,24},{8,20},{12,16},{16,12},{20,8},{24,4},{28,0},{1,29},{... | collective-permute-start | bytes 1572872 | tf_op jit(solution)/shard_map/ppermute | solution.py:512
  58.0 25.8 %shard_map.70 = (f32[512,512]{1,0:T(8,128)}, bf16[512,512]{1,0:T(8,128)(2,1)S(1)}, bf16[512,512]{1,0:T(8,128)(2,1)S(1)}) custom-call(f32[1280,128]{1,0:T(8,128)S(1)} %get-tuple-element.97.sum_ref, f32[1280,128]{1,0:T(8,128)S(1)} %get-tuple-element.63.prior_ref), custom_call_target="tpu_custom_call" | custom-call | flops 1 | bytes 1 | tf_op jit(solution)/shard_map/pallas_call | solution.py:433
  83.8 4.1 %shard_map.71.rest_2_ = f32[2048,512]{1,0:T(8,128)} custom-call(s32[1]{0:T(128)} %bitcast.2.me_ref, bf16[512,512]{1,0:T(8,128)(2,1)S(1)} %get-tuple-element.64.high_ref, bf16[512,512]{1,0:T(8,128)(2,1)S(1)} %get-tuple-element.65.low_ref, f32[256,512]{1,0:T(8,128)} %get-tuple-element.72.rest_0_, f32[256,512]{1,0:T(8,128)S(1)} %collective-permute-done.4.rest_1_, ...), custom_call_target="tpu_custom_call" | custom-call | flops 1 | bytes 1 | tf_op jit(solution)/shard_map/pallas_call | solution.py:478
  87.9 7.7 %collective-permute-done.6.rest_0_ = f32[256,512]{1,0:T(8,128)S(1)} collective-permute-done((f32[256,512]{1,0:T(8,128)}, f32[256,512]{1,0:T(8,128)S(1)}, u32[]{:S(2)}, u32[]{:S(2)}) %collective-permute-start.6) | collective-permute-done | bytes 524320 | tf_op jit(solution)/shard_map/ppermute | solution.py:512
  95.7 1.8 %shard_map.72.rest_1_ = f32[2048,512]{1,0:T(8,128)} custom-call(s32[1]{0:T(128)} %bitcast.2.me_ref, bf16[512,512]{1,0:T(8,128)(2,1)S(1)} %get-tuple-element.64.high_ref, bf16[512,512]{1,0:T(8,128)(2,1)S(1)} %get-tuple-element.65.low_ref, f32[256,512]{1,0:T(8,128)S(1)} %collective-permute-done.6.rest_0_, ...), custom_call_target="tpu_custom_call", output_to_operand_aliasing={{}: (5, {})} | custom-call | flops 1 | bytes 1 | tf_op jit(solution)/shard_map/pallas_call | solution.py:478
  97.5 9.8 %collective-permute-done.5.rest_0_ = f32[256,512]{1,0:T(8,128)S(1)} collective-permute-done((f32[256,512]{1,0:T(8,128)}, f32[256,512]{1,0:T(8,128)S(1)}, u32[]{:S(2)}, u32[]{:S(2)}) %collective-permute-start.5) | collective-permute-done | bytes 524320 | tf_op jit(solution)/shard_map/ppermute | solution.py:512
  107.2 1.4 %shard_map.73 = f32[2048,512]{1,0:T(8,128)} custom-call(s32[1]{0:T(128)} %bitcast.2.me_ref, bf16[512,512]{1,0:T(8,128)(2,1)S(1)} %get-tuple-element.64.high_ref, bf16[512,512]{1,0:T(8,128)(2,1)S(1)} %get-tuple-element.65.low_ref, f32[256,512]{1,0:T(8,128)S(1)} %collective-permute-done.5.rest_0_, ...), custom_call_target="tpu_custom_call", output_to_operand_aliasing={{}: (4, {})} | custom-call | flops 1 | bytes 1 | tf_op jit(solution)/shard_map/pallas_call | solution.py:478
  (15 shorter events, 0.7 us)
Async XLA Ops:
  0.6 9.4 %copy-start = (f32[128]{0:T(128)S(1)}, f32[128]{0:T(128)}, u32[]{:S(2)}) copy-start(f32[128]{0:T(128)} %param.11) | copy-start | bytes 1540
  5.8 24.6 %collective-permute-start = (f32[256,512]{1,0:T(8,128)}, f32[256,512]{1,0:T(8,128)S(1)}, u32[]{:S(2)}, u32[]{:S(2)}) collective-permute-start(f32[256,512]{1,0:T(8,128)} %get-tuple-element.58), channel_id=1, source_target_pairs={{0,4},{4,0},{8,12},{12,8},{16,20},{20,16},{24,28},{28,24},{1,5},{5... | collective-permute-start | bytes 1572872 | tf_op jit(solution)/shard_map/ppermute | solution.py:512
  7.4 27.9 %collective-permute-start.4 = (f32[256,512]{1,0:T(8,128)}, f32[256,512]{1,0:T(8,128)S(1)}, u32[]{:S(2)}, u32[]{:S(2)}) collective-permute-start(f32[256,512]{1,0:T(8,128)} %get-tuple-element.53), channel_id=1, source_target_pairs={{0,16},{4,20},{8,24},{12,28},{16,0},{20,4},{24,8},{28,12},{1,17},{... | collective-permute-start | bytes 1572872 | tf_op jit(solution)/shard_map/ppermute | solution.py:512
  10.1 2.0 %copy-start.1 = (bf16[2048,1024]{1,0:T(8,128)(2,1)}, bf16[2048,1024]{1,0:T(8,128)(2,1)S(1)}, u32[]{:S(2)}) copy-start(bf16[2048,1024]{1,0:T(8,128)(2,1)S(1)} %get-tuple-element.14.pair_ref) | copy-start | bytes 12582916 | tf_op jit(solution)/shard_map/cond
  16.7 13.7 %all-to-all-start = ((f32[8,160,128]{2,1,0:T(8,128)}), f32[8,160,128]{2,1,0:T(8,128)S(1)}, u32[]{:S(2)}, u32[]{:S(2)}) async-start(f32[8,160,128]{2,1,0:T(8,128)} %bitcast), calls=%async_computation | async-start | bytes 1310720 | tf_op jit(solution)/shard_map/cond/branch_1_fun/all_to_all | solution.py:351
  30.4 8.4 %collective-permute-start.3 = (f32[160,128]{1,0:T(8,128)S(1)}, f32[160,128]{1,0:T(8,128)S(1)}, u32[]{:S(2)}, u32[]{:S(2)}) collective-permute-start(f32[160,128]{1,0:T(8,128)S(1)} %get-tuple-element.59), channel_id=1, source_target_pairs={{0,24},{4,28},{8,16},{12,20},{16,8},{20,12},{24,0},{28,4},{1,25},{... | collective-permute-start | bytes 245768 | tf_op jit(solution)/shard_map/ppermute | solution.py:512
  30.5 8.9 %collective-permute-start.2 = (f32[160,128]{1,0:T(8,128)S(1)}, f32[160,128]{1,0:T(8,128)S(1)}, u32[]{:S(2)}, u32[]{:S(2)}) collective-permute-start(f32[160,128]{1,0:T(8,128)S(1)} %get-tuple-element.59), channel_id=1, source_target_pairs={{0,16},{4,20},{8,24},{12,28},{16,0},{20,4},{24,8},{28,12},{1,17},{... | collective-permute-start | bytes 245768 | tf_op jit(solution)/shard_map/ppermute | solution.py:512
  33.3 6.1 %collective-permute-start.1 = (f32[160,128]{1,0:T(8,128)S(1)}, f32[160,128]{1,0:T(8,128)S(1)}, u32[]{:S(2)}, u32[]{:S(2)}) collective-permute-start(f32[160,128]{1,0:T(8,128)S(1)} %get-tuple-element.59), channel_id=1, source_target_pairs={{0,8},{4,12},{8,0},{12,4},{16,24},{20,28},{24,16},{28,20},{1,9},{5... | collective-permute-start | bytes 245768 | tf_op jit(solution)/shard_map/ppermute | solution.py:512
  34.0 49.8 %collective-permute-start.8 = (f32[256,512]{1,0:T(8,128)}, f32[256,512]{1,0:T(8,128)S(1)}, u32[]{:S(2)}, u32[]{:S(2)}) collective-permute-start(f32[256,512]{1,0:T(8,128)} %get-tuple-element.76), channel_id=1, source_target_pairs={{0,8},{4,12},{8,0},{12,4},{16,24},{20,28},{24,16},{28,20},{1,9},{5... | collective-permute-start | bytes 1572872 | tf_op jit(solution)/shard_map/ppermute | solution.py:512
  35.3 48.5 %collective-permute-start.9 = (f32[256,512]{1,0:T(8,128)}, f32[256,512]{1,0:T(8,128)S(1)}, u32[]{:S(2)}, u32[]{:S(2)}) collective-permute-start(f32[256,512]{1,0:T(8,128)} %get-tuple-element.77), channel_id=1, source_target_pairs={{0,24},{4,28},{8,16},{12,20},{16,8},{20,12},{24,0},{28,4},{1,25},{... | collective-permute-start | bytes 1572872 | tf_op jit(solution)/shard_map/ppermute | solution.py:512
  53.0 42.7 %collective-permute-start.6 = (f32[256,512]{1,0:T(8,128)}, f32[256,512]{1,0:T(8,128)S(1)}, u32[]{:S(2)}, u32[]{:S(2)}) collective-permute-start(f32[256,512]{1,0:T(8,128)} %get-tuple-element.69), channel_id=1, source_target_pairs={{0,20},{4,16},{8,28},{12,24},{16,4},{20,0},{24,12},{28,8},{1,21},{... | collective-permute-start | bytes 1572872 | tf_op jit(solution)/shard_map/ppermute | solution.py:512
  56.6 39.1 %collective-permute-start.7 = (f32[256,512]{1,0:T(8,128)}, f32[256,512]{1,0:T(8,128)S(1)}, u32[]{:S(2)}, u32[]{:S(2)}) collective-permute-start(f32[256,512]{1,0:T(8,128)} %get-tuple-element.71), channel_id=1, source_target_pairs={{0,12},{4,8},{8,4},{12,0},{16,28},{20,24},{24,20},{28,16},{1,13},{... | collective-permute-start | bytes 1572872 | tf_op jit(solution)/shard_map/ppermute | solution.py:512
  56.6 50.6 %collective-permute-start.5 = (f32[256,512]{1,0:T(8,128)}, f32[256,512]{1,0:T(8,128)S(1)}, u32[]{:S(2)}, u32[]{:S(2)}) collective-permute-start(f32[256,512]{1,0:T(8,128)} %get-tuple-element.67), channel_id=1, source_target_pairs={{0,28},{4,24},{8,20},{12,16},{16,12},{20,8},{24,4},{28,0},{1,29},{... | collective-permute-start | bytes 1572872 | tf_op jit(solution)/shard_map/ppermute | solution.py:512

commit v13 on v12

--- a/solution.py
+++ b/solution.py
@@ -543,10 +543,12 @@
         received[leads[0]], chunk = behind(received[leads[0]], rest[k])
         received[k] = move(k, chunk)
     across[0], received[leads[0]] = behind(across[0], received[leads[0]])
+    for k in late[:1]:
+        received[k] = move(k, behind(across[0], rest[k])[1])
     summed = lax.cond(
         valid, lambda: gather_pieces(across[0], plane, planes), lambda: nothing(packed_rows)
     )
-    for k in late:
+    for k in late[1:]:
         received[k] = move(k, behind(summed, rest[k])[1])
     factor, high, low = factorise(summed, prior_gram, state, total_rows)
     out = None

time: 110 us -> 110 us (level)
  waiting for transfers between devices: 25.3 us -> 23.8 us
    ppermute x10, waiting for transfers between devices: 21.1 us -> 19.6 us  [shards(): lax.ppermute(chunk, 'rows', [(i, i ^ k) for i in range(groups)])]
  transfers between devices with their start and end apart: 11 -> 11, of which waited for: 5 -> 5; matrix products, arithmetic and copies ran while one was open for 0% -> 0% of each run, Pallas kernels for 39% -> 40%
where the time goes in v13:
time: 110 us; the launch traced here: 109 us
  Pallas kernels  49.9 us (45%)
  waiting for transfers between devices  23.8 us (22%)
  starting transfers between devices  17.5 us (16%)
  blocking collectives  14.5 us (13%)
  local copies, waits for them, and re-layouts  2.06 us (2%)
    pallas_call x1, Pallas kernels, factorise(): pl.pallas_call(functools.partial(factor_kernel, 1.0 / total_rows), in_spe...  26.9 us
    ppermute x10, waiting for transfers between devices, shards(): lax.ppermute(chunk, 'rows', [(i, i ^ k) for i in range(groups)])  19.6 us
    all_to_all x1, blocking collectives, gather_pieces(): lax.all_to_all(copies, axes, split_axis=0, concat_axis=0, axis_index_grou...  14.5 us
    ppermute x10, starting transfers between devices, shards(): lax.ppermute(chunk, 'rows', [(i, i ^ k) for i in range(groups)])  14 us
    pallas_call x3, Pallas kernels, whiten(): pl.pallas_call(functools.partial(whiten_kernel, tuple(steps), len(extra))...  7.27 us
    pallas_call x1, Pallas kernels, regroup_rest(): pl.pallas_call(functools.partial(rest_kernel, groups, per_bucket, tuple(o...  5.98 us
    pallas_call x1, Pallas kernels, regroup_lead(): pl.pallas_call(functools.partial(lead_kernel, groups, per_bucket, tuple(l...  5.2 us
    pallas_call x1, Pallas kernels, gram(): pl.pallas_call(gram_kernel, in_specs=[vmem] * 2, out_specs=[vmem] * 2, ou...  4.58 us
  transfers between devices with their start and end apart: 11, of which 5 were waited for; matrix products, arithmetic and copies ran while one was open for 0% of the time, Pallas kernels for 40%

profile of v13, /device:TPU:8, one launch (start us, length us, event | category | flops | bytes accessed | tf_op | source)
XLA Modules:
  0.0 108.8 jit_solution(11510967538888284233)
XLA Ops:
  0.6 5.2 %shard_map.69 = (f32[256,512]{1,0:T(8,128)}, f32[256,512]{1,0:T(8,128)}, bf16[2048,1024]{1,0:T(8,128)(2,1)S(1)}, s32[8,256]{1,0:T(8,128)S(1)}, s32[64,128]{1,0:T(8,128)S(1)}) custom-call(s32[1]{0:T(128)} %bitcast.2.me_ref, s32[16,128]{1,0:T(8,128)} %bitcast.9, s32[16,128]{1,0:T(8,128)} %bitcast.10, f32[1,128]{1,0:T(1,128)} %bitcast.11, f32[2048,512]{1,0:T(8,128)} %refs_3_.1), custom_call_target="tpu_custom_call" | custom-call | flops 1048576 | bytes 8388608 | tf_op jit(solution)/shard_map/pallas_call | solution.py:253
  5.8 1.6 %collective-permute-start = (f32[256,512]{1,0:T(8,128)}, f32[256,512]{1,0:T(8,128)S(1)}, u32[]{:S(2)}, u32[]{:S(2)}) collective-permute-start(f32[256,512]{1,0:T(8,128)} %get-tuple-element.58), channel_id=1, source_target_pairs={{0,4},{4,0},{8,12},{12,8},{16,20},{20,16},{24,28},{28,24},{1,5},{5... | collective-permute-start | bytes 1572872 | tf_op jit(solution)/shard_map/ppermute | solution.py:512
  7.4 2.6 %collective-permute-start.4 = (f32[256,512]{1,0:T(8,128)}, f32[256,512]{1,0:T(8,128)S(1)}, u32[]{:S(2)}, u32[]{:S(2)}) collective-permute-start(f32[256,512]{1,0:T(8,128)} %get-tuple-element.53), channel_id=1, source_target_pairs={{0,16},{4,20},{8,24},{12,28},{16,0},{20,4},{24,8},{28,12},{1,17},{... | collective-permute-start | bytes 1572872 | tf_op jit(solution)/shard_map/ppermute | solution.py:512
  10.0 20.4 %conditional.2 = (f32[160,128]{1,0:T(8,128)S(1)}, f32[1280,128]{1,0:T(8,128)S(1)}, f32[256,512]{1,0:T(8,128)}, f32[256,512]{1,0:T(8,128)}, f32[256,512]{1,0:T(8,...) conditional(s32[]{:T(128)} %bitcast.3, f32[256,512]{1,0:T(8,128)} %get-tuple-element.53, ...), branch_computations={%region_0.0_spmd, %region_1.0_spmd} | conditional | flops 5234634752 | bytes 32063616 | solution.py:530
  10.1 2.0 %copy-done.1 = bf16[2048,1024]{1,0:T(8,128)(2,1)} copy-done((bf16[2048,1024]{1,0:T(8,128)(2,1)}, bf16[2048,1024]{1,0:T(8,128)(2,1)S(1)}, u32[]{:S(2)}) %copy-start.1) | copy-done | bytes 4194328 | tf_op jit(solution)/shard_map/cond
  12.1 4.6 %branch_1_fun.2 = (f32[1280,128]{1,0:T(8,128)}, f32[1280,128]{1,0:T(8,128)S(1)}) custom-call(f32[512,512]{1,0:T(8,128)} %get-tuple-element.80.prior_ref, bf16[2048,1024]{1,0:T(8,128)(2,1)S(1)} %get-tuple-element.14.pair_ref), custom_call_target="tpu_custom_call" | custom-call | flops 2147483648 | bytes 4194304 | tf_op jit(solution)/shard_map/cond/branch_1_fun/pallas_call | solution.py:335
  16.7 3.5 %all-to-all-start = ((f32[8,160,128]{2,1,0:T(8,128)}), f32[8,160,128]{2,1,0:T(8,128)S(1)}, u32[]{:S(2)}, u32[]{:S(2)}) async-start(f32[8,160,128]{2,1,0:T(8,128)} %bitcast), calls=%async_computation | async-start | bytes 1310720 | tf_op jit(solution)/shard_map/cond/branch_1_fun/all_to_all | solution.py:351
  20.2 6.0 %branch_1_fun.3 = (f32[256,512]{1,0:T(8,128)}, f32[256,512]{1,0:T(8,128)}, f32[256,512]{1,0:T(8,128)}, f32[256,512]{1,0:T(8,128)}, f32[256,512]{1,0:T(8,128)}, /*index=5*/f32[256,512]{1,0:T(8,128)}) custom-call(s32[64,128]{1,0:T(8,128)S(1)} %get-tuple-element.17.table, s32[8,256]{1,0:T(8,128)S(1)} %get-tuple-element.18.place_ref, bf16[2048,1024]{1,0:T(8,128)(2,1)} %copy-done.1), custom_call_target="tpu_custom_call" | custom-call | flops 3087007744 | bytes 8388608 | tf_op jit(solution)/shard_map/cond/branch_1_fun/pallas_call | solution.py:295
  26.2 4.2 %all-to-all-done = f32[8,160,128]{2,1,0:T(8,128)S(1)} async-done(((f32[8,160,128]{2,1,0:T(8,128)}), f32[8,160,128]{2,1,0:T(8,128)S(1)}, u32[]{:S(2)}, u32[]{:S(2)}) %all-to-all-start) | async-done | bytes 655392 | tf_op jit(solution)/shard_map/cond/branch_1_fun/all_to_all | solution.py:351
  30.5 2.8 %collective-permute-start.2 = (f32[160,128]{1,0:T(8,128)S(1)}, f32[160,128]{1,0:T(8,128)S(1)}, u32[]{:S(2)}, u32[]{:S(2)}) collective-permute-start(f32[160,128]{1,0:T(8,128)S(1)} %get-tuple-element.59), channel_id=1, source_target_pairs={{0,16},{4,20},{8,24},{12,28},{16,0},{20,4},{24,8},{28,12},{1,17},{... | collective-permute-start | bytes 245768 | tf_op jit(solution)/shard_map/ppermute | solution.py:512
  33.3 0.7 collective-permute-start.1
  34.0 1.3 %collective-permute-start.8 = (f32[256,512]{1,0:T(8,128)}, f32[256,512]{1,0:T(8,128)S(1)}, u32[]{:S(2)}, u32[]{:S(2)}) collective-permute-start(f32[256,512]{1,0:T(8,128)} %get-tuple-element.76), channel_id=1, source_target_pairs={{0,8},{4,12},{8,0},{12,4},{16,24},{20,28},{24,16},{28,20},{1,9},{5... | collective-permute-start | bytes 1572872 | tf_op jit(solution)/shard_map/ppermute | solution.py:512
  35.8 3.1 %collective-permute-done.3 = f32[160,128]{1,0:T(8,128)S(1)} collective-permute-done((f32[160,128]{1,0:T(8,128)S(1)}, f32[160,128]{1,0:T(8,128)S(1)}, u32[]{:S(2)}, u32[]{:S(2)}) %collective-permute-start.3) | collective-permute-done | bytes 81952 | tf_op jit(solution)/shard_map/ppermute | solution.py:512
  38.9 0.5 collective-permute-done.2
  39.4 3.4 %collective-permute-start.6 = (f32[256,512]{1,0:T(8,128)}, f32[256,512]{1,0:T(8,128)S(1)}, u32[]{:S(2)}, u32[]{:S(2)}) collective-permute-start(f32[256,512]{1,0:T(8,128)} %get-tuple-element.69), channel_id=1, source_target_pairs={{0,20},{4,16},{8,28},{12,24},{16,4},{20,0},{24,12},{28,8},{1,21},{... | collective-permute-start | bytes 1572872 | tf_op jit(solution)/shard_map/ppermute | solution.py:512
  42.8 14.6 %conditional.3 = (f32[1280,128]{1,0:T(8,128)}) conditional(s32[]{:T(128)} %bitcast.3, () %tuple.29, f32[160,128]{1,0:T(8,128)S(1)} %add_add_fusion), branch_computations={%region_3.0_spmd, %region_4.0_spmd} | conditional | bytes 2048008 | solution.py:548
  42.9 14.5 %all_to_all.14 = f32[8,160,128]{2,1,0:T(8,128)} all-to-all(f32[8,160,128]{2,1,0:T(8,128)S(1)} %broadcast_in_dim.2), channel_id=1, replica_groups={{0,1,2,3,4,5,6,7},{8,9,10,11,12,13,14,15},{16,17,18,19,20,21,22,23},{24..., dimensions={0} | all-to-all | bytes 1310720 | tf_op jit(solution)/shard_map/cond/branch_1_fun/all_to_all | solution.py:359
  57.5 1.0 collective-permute-start.5
  58.5 26.9 %shard_map.70 = (f32[512,512]{1,0:T(8,128)}, bf16[512,512]{1,0:T(8,128)(2,1)S(1)}, bf16[512,512]{1,0:T(8,128)(2,1)S(1)}) custom-call(f32[1280,128]{1,0:T(8,128)} %get-tuple-element.97.sum_ref, f32[1280,128]{1,0:T(8,128)S(1)} %get-tuple-element.63.prior_ref), custom_call_target="tpu_custom_call" | custom-call | flops 1 | bytes 1 | tf_op jit(solution)/shard_map/pallas_call | solution.py:433
  85.4 4.1 %shard_map.71.rest_2_ = f32[2048,512]{1,0:T(8,128)} custom-call(s32[1]{0:T(128)} %bitcast.2.me_ref, bf16[512,512]{1,0:T(8,128)(2,1)S(1)} %get-tuple-element.64.high_ref, bf16[512,512]{1,0:T(8,128)(2,1)S(1)} %get-tuple-element.65.low_ref, f32[256,512]{1,0:T(8,128)} %get-tuple-element.72.rest_0_, f32[256,512]{1,0:T(8,128)S(1)} %collective-permute-done.4.rest_1_, ...), custom_call_target="tpu_custom_call" | custom-call | flops 1 | bytes 1 | tf_op jit(solution)/shard_map/pallas_call | solution.py:478
  89.5 6.2 %collective-permute-done.6.rest_0_ = f32[256,512]{1,0:T(8,128)S(1)} collective-permute-done((f32[256,512]{1,0:T(8,128)}, f32[256,512]{1,0:T(8,128)S(1)}, u32[]{:S(2)}, u32[]{:S(2)}) %collective-permute-start.6) | collective-permute-done | bytes 524320 | tf_op jit(solution)/shard_map/ppermute | solution.py:512
  95.7 1.8 %shard_map.72.rest_1_ = f32[2048,512]{1,0:T(8,128)} custom-call(s32[1]{0:T(128)} %bitcast.2.me_ref, bf16[512,512]{1,0:T(8,128)(2,1)S(1)} %get-tuple-element.64.high_ref, bf16[512,512]{1,0:T(8,128)(2,1)S(1)} %get-tuple-element.65.low_ref, f32[256,512]{1,0:T(8,128)S(1)} %collective-permute-done.6.rest_0_, ...), custom_call_target="tpu_custom_call", output_to_operand_aliasing={{}: (5, {})} | custom-call | flops 1 | bytes 1 | tf_op jit(solution)/shard_map/pallas_call | solution.py:478
  97.5 9.8 %collective-permute-done.5.rest_0_ = f32[256,512]{1,0:T(8,128)S(1)} collective-permute-done((f32[256,512]{1,0:T(8,128)}, f32[256,512]{1,0:T(8,128)S(1)}, u32[]{:S(2)}, u32[]{:S(2)}) %collective-permute-start.5) | collective-permute-done | bytes 524320 | tf_op jit(solution)/shard_map/ppermute | solution.py:512
  107.2 1.4 %shard_map.73 = f32[2048,512]{1,0:T(8,128)} custom-call(s32[1]{0:T(128)} %bitcast.2.me_ref, bf16[512,512]{1,0:T(8,128)(2,1)S(1)} %get-tuple-element.64.high_ref, bf16[512,512]{1,0:T(8,128)(2,1)S(1)} %get-tuple-element.65.low_ref, f32[256,512]{1,0:T(8,128)S(1)} %collective-permute-done.5.rest_0_, ...), custom_call_target="tpu_custom_call", output_to_operand_aliasing={{}: (4, {})} | custom-call | flops 1 | bytes 1 | tf_op jit(solution)/shard_map/pallas_call | solution.py:478
  (15 shorter events, 0.7 us)
Async XLA Ops:
  0.6 9.4 %copy-start = (f32[128]{0:T(128)S(1)}, f32[128]{0:T(128)}, u32[]{:S(2)}) copy-start(f32[128]{0:T(128)} %param.11) | copy-start | bytes 1540
  5.8 24.6 %collective-permute-start = (f32[256,512]{1,0:T(8,128)}, f32[256,512]{1,0:T(8,128)S(1)}, u32[]{:S(2)}, u32[]{:S(2)}) collective-permute-start(f32[256,512]{1,0:T(8,128)} %get-tuple-element.58), channel_id=1, source_target_pairs={{0,4},{4,0},{8,12},{12,8},{16,20},{20,16},{24,28},{28,24},{1,5},{5... | collective-permute-start | bytes 1572872 | tf_op jit(solution)/shard_map/ppermute | solution.py:512
  7.4 27.9 %collective-permute-start.4 = (f32[256,512]{1,0:T(8,128)}, f32[256,512]{1,0:T(8,128)S(1)}, u32[]{:S(2)}, u32[]{:S(2)}) collective-permute-start(f32[256,512]{1,0:T(8,128)} %get-tuple-element.53), channel_id=1, source_target_pairs={{0,16},{4,20},{8,24},{12,28},{16,0},{20,4},{24,8},{28,12},{1,17},{... | collective-permute-start | bytes 1572872 | tf_op jit(solution)/shard_map/ppermute | solution.py:512
  10.1 2.0 %copy-start.1 = (bf16[2048,1024]{1,0:T(8,128)(2,1)}, bf16[2048,1024]{1,0:T(8,128)(2,1)S(1)}, u32[]{:S(2)}) copy-start(bf16[2048,1024]{1,0:T(8,128)(2,1)S(1)} %get-tuple-element.14.pair_ref) | copy-start | bytes 12582916 | tf_op jit(solution)/shard_map/cond
  16.7 13.7 %all-to-all-start = ((f32[8,160,128]{2,1,0:T(8,128)}), f32[8,160,128]{2,1,0:T(8,128)S(1)}, u32[]{:S(2)}, u32[]{:S(2)}) async-start(f32[8,160,128]{2,1,0:T(8,128)} %bitcast), calls=%async_computation | async-start | bytes 1310720 | tf_op jit(solution)/shard_map/cond/branch_1_fun/all_to_all | solution.py:351
  30.4 8.4 %collective-permute-start.3 = (f32[160,128]{1,0:T(8,128)S(1)}, f32[160,128]{1,0:T(8,128)S(1)}, u32[]{:S(2)}, u32[]{:S(2)}) collective-permute-start(f32[160,128]{1,0:T(8,128)S(1)} %get-tuple-element.59), channel_id=1, source_target_pairs={{0,24},{4,28},{8,16},{12,20},{16,8},{20,12},{24,0},{28,4},{1,25},{... | collective-permute-start | bytes 245768 | tf_op jit(solution)/shard_map/ppermute | solution.py:512
  30.5 8.9 %collective-permute-start.2 = (f32[160,128]{1,0:T(8,128)S(1)}, f32[160,128]{1,0:T(8,128)S(1)}, u32[]{:S(2)}, u32[]{:S(2)}) collective-permute-start(f32[160,128]{1,0:T(8,128)S(1)} %get-tuple-element.59), channel_id=1, source_target_pairs={{0,16},{4,20},{8,24},{12,28},{16,0},{20,4},{24,8},{28,12},{1,17},{... | collective-permute-start | bytes 245768 | tf_op jit(solution)/shard_map/ppermute | solution.py:512
  33.3 6.1 %collective-permute-start.1 = (f32[160,128]{1,0:T(8,128)S(1)}, f32[160,128]{1,0:T(8,128)S(1)}, u32[]{:S(2)}, u32[]{:S(2)}) collective-permute-start(f32[160,128]{1,0:T(8,128)S(1)} %get-tuple-element.59), channel_id=1, source_target_pairs={{0,8},{4,12},{8,0},{12,4},{16,24},{20,28},{24,16},{28,20},{1,9},{5... | collective-permute-start | bytes 245768 | tf_op jit(solution)/shard_map/ppermute | solution.py:512
  34.0 51.4 %collective-permute-start.8 = (f32[256,512]{1,0:T(8,128)}, f32[256,512]{1,0:T(8,128)S(1)}, u32[]{:S(2)}, u32[]{:S(2)}) collective-permute-start(f32[256,512]{1,0:T(8,128)} %get-tuple-element.76), channel_id=1, source_target_pairs={{0,8},{4,12},{8,0},{12,4},{16,24},{20,28},{24,16},{28,20},{1,9},{5... | collective-permute-start | bytes 1572872 | tf_op jit(solution)/shard_map/ppermute | solution.py:512
  35.3 50.0 %collective-permute-start.9 = (f32[256,512]{1,0:T(8,128)}, f32[256,512]{1,0:T(8,128)S(1)}, u32[]{:S(2)}, u32[]{:S(2)}) collective-permute-start(f32[256,512]{1,0:T(8,128)} %get-tuple-element.77), channel_id=1, source_target_pairs={{0,24},{4,28},{8,16},{12,20},{16,8},{20,12},{24,0},{28,4},{1,25},{... | collective-permute-start | bytes 1572872 | tf_op jit(solution)/shard_map/ppermute | solution.py:512
  39.4 56.3 %collective-permute-start.6 = (f32[256,512]{1,0:T(8,128)}, f32[256,512]{1,0:T(8,128)S(1)}, u32[]{:S(2)}, u32[]{:S(2)}) collective-permute-start(f32[256,512]{1,0:T(8,128)} %get-tuple-element.69), channel_id=1, source_target_pairs={{0,20},{4,16},{8,28},{12,24},{16,4},{20,0},{24,12},{28,8},{1,21},{... | collective-permute-start | bytes 1572872 | tf_op jit(solution)/shard_map/ppermute | solution.py:512
  57.4 38.3 %collective-permute-start.7 = (f32[256,512]{1,0:T(8,128)}, f32[256,512]{1,0:T(8,128)S(1)}, u32[]{:S(2)}, u32[]{:S(2)}) collective-permute-start(f32[256,512]{1,0:T(8,128)} %get-tuple-element.71), channel_id=1, source_target_pairs={{0,12},{4,8},{8,4},{12,0},{16,28},{20,24},{24,20},{28,16},{1,13},{... | collective-permute-start | bytes 1572872 | tf_op jit(solution)/shard_map/ppermute | solution.py:512
  57.5 49.7 %collective-permute-start.5 = (f32[256,512]{1,0:T(8,128)}, f32[256,512]{1,0:T(8,128)S(1)}, u32[]{:S(2)}, u32[]{:S(2)}) collective-permute-start(f32[256,512]{1,0:T(8,128)} %get-tuple-element.67), channel_id=1, source_target_pairs={{0,28},{4,24},{8,20},{12,16},{16,12},{20,8},{24,4},{28,0},{1,29},{... | collective-permute-start | bytes 1572872 | tf_op jit(solution)/shard_map/ppermute | solution.py:512

commit v14 on v13

--- a/solution.py
+++ b/solution.py
@@ -84,8 +84,8 @@
         lax.fori_loop(self.most, final + 1, longer, 0)
 
 
-def lead_kernel(groups, per_bucket, leads, me_ref, *refs):
-    given, far_outs, refs = refs[:4], refs[4 : 4 + len(leads)], refs[4 + len(leads) :]
+def lead_kernel(groups, per_bucket, leads, parts, me_ref, *refs):
+    given, far_outs, refs = refs[:4], refs[4 : 4 + len(parts)], refs[4 + len(parts) :]
     (pair_ref, place_ref, meta_ref), held, scratch = refs[:3], refs[3:7], refs[7:]
     sorted_ref, small_a, small_b, inv_ref, outs_ref, table, sems = scratch
     outs = [outs_ref.at[n] for n in range(len(leads))]
@@ -193,8 +193,9 @@
         lax.fori_loop(0, blocks, body, 0)
 
     copies = []
-    for n, far in enumerate(far_outs):
-        copies.append(pltpu.make_async_copy(outs_ref.at[n], far, sems.at[4 + blocks + n]))
+    for m, ((n, first_row, rows), far) in enumerate(zip(parts, far_outs)):
+        part = outs_ref.at[n, pl.ds(first_row, rows)]
+        copies.append(pltpu.make_async_copy(part, far, sems.at[4 + blocks + m]))
         copies[-1].start()
     for copy in copies:
         copy.wait()
@@ -242,7 +243,7 @@
     return -(-(block + groups * 2 * (SUB - 1)) // 16) * 16
 
 
-def regroup_lead(observations, sensor_ids, sensor_sigma, buckets, me, groups, leads):
+def regroup_lead(observations, sensor_ids, sensor_sigma, buckets, me, groups, leads, parts):
     rows, state = observations.shape
     sensors = sensor_sigma.shape[0]
     block = 256
@@ -251,9 +252,9 @@
     per_bucket = rows // groups
     far = pl.BlockSpec(memory_space=pltpu.HBM)
     return pl.pallas_call(
-        functools.partial(lead_kernel, groups, per_bucket, tuple(leads)),
+        functools.partial(lead_kernel, groups, per_bucket, tuple(leads), tuple(parts)),
         in_specs=[pl.BlockSpec(memory_space=pltpu.SMEM)] + [far] * 4,
-        out_specs=[pl.BlockSpec(memory_space=pl.ANY)] * len(leads)
+        out_specs=[pl.BlockSpec(memory_space=pl.ANY)] * len(parts)
         + [pl.BlockSpec(memory_space=pltpu.VMEM)] * 3,
         scratch_shapes=[
             pltpu.VMEM((rows // LANES, LANES), I32),
@@ -266,9 +267,9 @@
             pltpu.VMEM((sensors, LANES), F32),
             pltpu.VMEM((len(leads), per_bucket, state), F32),
             pltpu.SMEM((cells, LANES), I32),
-            pltpu.SemaphoreType.DMA((4 + blocks + len(leads),)),
+            pltpu.SemaphoreType.DMA((4 + blocks + len(parts),)),
         ],
-        out_shape=[jax.ShapeDtypeStruct((per_bucket, state), F32)] * len(leads)
+        out_shape=[jax.ShapeDtypeStruct((part[2], state), F32) for part in parts]
         + [
             jax.ShapeDtypeStruct((rows, 2 * state), BF16),
             jax.ShapeDtypeStruct((blocks, block), I32),
@@ -306,17 +307,54 @@
 
 
 def block_pairs(count):
-    return [(i, j) for i in range(count) for j in range(i, count)]
+    return [(i, j) for i in range(count) for j in range(i + 1, count)]
+
+
+def packed_rows_of(state, plane):
+    count = state // LANES
+    rows = (len(block_pairs(count)) + count // 2) * LANES + SUB
+    return -(-rows // (plane * SUB)) * plane * SUB
 
 
 def write_gram(both, state, out_ref):
-    for n, (i, j) in enumerate(block_pairs(state // LANES)):
+    count = state // LANES
+    pairs = block_pairs(count)
+    row, col = iota((LANES, LANES), 0), iota((LANES, LANES), 1)
+
+    def block(i, j):
         a, b = i * LANES, j * LANES
         cross = both[a : a + LANES, state + b : state + b + LANES]
         turned = both[b : b + LANES, state + a : state + a + LANES]
-        out_ref[n * LANES : (n + 1) * LANES, :] = both[a : a + LANES, b : b + LANES] + (
-            cross + jnp.transpose(turned)
-        )
+        return both[a : a + LANES, b : b + LANES] + (cross + jnp.transpose(turned))
+
+    for n, (i, j) in enumerate(pairs):
+        out_ref[n * LANES : (n + 1) * LANES, :] = block(i, j)
+    tail = (len(pairs) + count // 2) * LANES
+    out_ref[tail:, :] = jnp.zeros((out_ref.shape[0] - tail, LANES), F32)
+    for m in range(count // 2):
+        n = len(pairs) + m
+        second = block(2 * m + 1, 2 * m + 1)
+        out_ref[n * LANES : (n + 1) * LANES, :] = jnp.where(row <= col, block(2 * m, 2 * m), second)
+        diagonal = jnp.sum(jnp.where(row == col, second, 0.0), axis=0, keepdims=True)
+        out_ref[tail + m : tail + m + 1, :] = diagonal
+
+
+def read_gram(value, state, a_ref):
+    count = state // LANES
+    pairs = block_pairs(count)
+    row, col = iota((LANES, LANES), 0), iota((LANES, LANES), 1)
+    span = lambda i: slice(i * LANES, (i + 1) * LANES)
+    for n, (i, j) in enumerate(pairs):
+        a_ref[span(i), span(j)] = value(span(n))
+    tail = (len(pairs) + count // 2) * LANES
+    for m in range(count // 2):
+        mixed = value(span(len(pairs) + m))
+        turned = jnp.transpose(mixed)
+        i, j = span(2 * m), span(2 * m + 1)
+        a_ref[i, i] = jnp.where(row <= col, mixed, turned)
+        diagonal = value(slice(tail, tail + SUB))[m : m + 1, :]
+        second = jnp.where(row > col, mixed, turned)
+        a_ref[j, j] = jnp.where(row == col, diagonal, second)
 
 
 def gram_kernel(prior_ref, pair_ref, out_ref, prior_out_ref, both_ref):
@@ -328,9 +366,8 @@
     write_gram(both_ref, state, prior_out_ref)
 
 
-def gram(prior_factor, pair):
+def gram(prior_factor, pair, packed):
     rows, state = pair.shape[0], pair.shape[1] // 2
-    packed = len(block_pairs(state // LANES)) * LANES
     vmem = pl.BlockSpec(memory_space=pltpu.VMEM)
     return pl.pallas_call(
         gram_kernel,
@@ -402,8 +439,7 @@
     state = factor_ref.shape[0]
     count = state // LANES
     span = lambda i: slice(i * LANES, (i + 1) * LANES)
-    for n, (i, j) in enumerate(block_pairs(count)):
-        a_ref[span(i), span(j)] = prior_ref[span(n), :] + sum_ref[span(n), :] * inv_total
+    read_gram(lambda rows: prior_ref[rows, :] + sum_ref[rows, :] * inv_total, state, a_ref)
     factor_ref[...] = jnp.zeros((state, state), F32)
     x_ref[...] = jnp.zeros((state, state), F32)
     eye = (iota((LANES, LANES), 0) == iota((LANES, LANES), 1)).astype(F32)
@@ -447,20 +483,20 @@
     )(summed, prior_gram)
 
 
-def whiten_kernel(steps, aliased, me_ref, high_ref, low_ref, *rest):
+def whiten_kernel(steps, aliased, per_bucket, me_ref, high_ref, low_ref, *rest):
     count = len(steps)
     chunks = rest[:count]
     out_ref, held, sems = rest[count + aliased :]
-    per_bucket = chunks[0].shape[0]
     high, low = high_ref[...], low_ref[...]
     copies = []
-    for n, k in enumerate(steps):
+    for n, (k, offset) in enumerate(steps):
+        rows = chunks[n].shape[0]
         rows_high, rows_low = split(chunks[n][...])
-        held[n] = dot(rows_high, high) + (dot(rows_high, low) + dot(rows_low, high))
-        slot = me_ref[0] ^ k
+        held[n, :rows] = dot(rows_high, high) + (dot(rows_high, low) + dot(rows_low, high))
+        first = pl.multiple_of((me_ref[0] ^ k) * per_bucket, per_bucket) + offset
         copy = pltpu.make_async_copy(
-            held.at[n],
-            out_ref.at[pl.ds(pl.multiple_of(slot * per_bucket, per_bucket), per_bucket), :],
+            held.at[n, pl.ds(0, rows)],
+            out_ref.at[pl.ds(pl.multiple_of(first, SUB), rows), :],
             sems.at[n],
         )
         copy.start()
@@ -469,14 +505,16 @@
         copy.wait()
 
 
-def whiten(me, high, low, steps, chunks, out, rows):
-    per_bucket, state = chunks[0].shape
+def whiten(me, high, low, parts, out, rows, groups):
+    steps = tuple((k, offset) for k, offset, _ in parts)
+    chunks = [chunk for _, _, chunk in parts]
+    per_bucket, state = rows // groups, chunks[0].shape[1]
     count = len(chunks)
     vmem = pl.BlockSpec(memory_space=pltpu.VMEM)
     anywhere = pl.BlockSpec(memory_space=pl.ANY)
     extra = [] if out is None else [out]
     return pl.pallas_call(
-        functools.partial(whiten_kernel, tuple(steps), len(extra)),
+        functools.partial(whiten_kernel, steps, len(extra), per_bucket),
         in_specs=[pl.BlockSpec(memory_space=pltpu.SMEM)]
         + [vmem] * (2 + count)
         + [anywhere] * len(extra),
@@ -488,9 +526,7 @@
         ],
         input_output_aliases={3 + count: 0} if extra else {},
         compiler_params=pltpu.CompilerParams(vmem_limit_bytes=16 * MIB),
-        cost_estimate=pl.CostEstimate(
-            flops=1, bytes_accessed=1, transcendentals=0
-        ),
+        cost_estimate=pl.CostEstimate(flops=1, bytes_accessed=1, transcendentals=0),
     )(me.reshape(1), high, low, *chunks, *extra)
 
 
@@ -506,13 +542,15 @@
     total_rows = rows_dev * groups * grp
     leads = [k for k in (4, 1) if k < groups]
     others = [k for k in range(groups) if k not in leads]
+    per_bucket = rows_dev // groups
+    parts = [(n, 0, per_bucket) for n in range(len(leads))]
     *chunks, pair, place, table = regroup_lead(
-        observations, sensor_ids, sensor_sigma, buckets, me, groups, leads
+        observations, sensor_ids, sensor_sigma, buckets, me, groups, leads, parts
     )
     move = lambda k, chunk: lax.ppermute(chunk, "rows", [(i, i ^ k) for i in range(groups)])
     received = {k: move(k, chunk) for k, chunk in zip(leads, chunks)}
-    packed_rows = len(block_pairs(state // LANES)) * LANES
     plane = 2 * grp
+    packed_rows = packed_rows_of(state, plane)
     planes = [list(range(i, i + plane)) for i in range(0, groups * grp, plane)]
     middle = [k for k in (2, 6) if k < groups]
     late = [k for k in (5, 3, *range(7, groups)) if k < groups]
@@ -520,12 +558,12 @@
     nothing = lambda rows: jnp.full((rows, LANES), jnp.nan, F32)
 
     def first():
-        packed, prior_gram = gram(prior_factor, pair)
+        packed, prior_gram = gram(prior_factor, pair, packed_rows)
         rest = list(regroup_rest(table, place, pair, groups, others))
         return scatter_sum(packed, plane, planes), prior_gram, rest
 
     def wrong():
-        return nothing(packed_rows // plane), nothing(packed_rows), [chunks[0]] * len(others)
+        return nothing(packed_rows // plane), nothing(packed_rows), [jnp.full((per_bucket, state), jnp.nan, F32)] * len(others)
 
     piece, prior_gram, rest = lax.cond(valid, first, wrong)
     rest = dict(zip(others, rest))
@@ -551,10 +589,11 @@
     for k in late[1:]:
         received[k] = move(k, behind(summed, rest[k])[1])
     factor, high, low = factorise(summed, prior_gram, state, total_rows)
+    whole = lambda slots: [(k, 0, received[k]) for k in slots]
     out = None
-    for steps in ([0, *leads, *middle], late[:-1], late[-1:]):
-        if steps:
-            out = whiten(me, high, low, steps, [received[k] for k in steps], out, rows_dev)
+    for parts in (whole([0, *leads, *middle]), whole(late[:-1]), whole(late[-1:])):
+        if parts:
+            out = whiten(me, high, low, parts, out, rows_dev, groups)
     return (out, factor)
 
 

time: 110 us -> 109 us (level)
  transfers between devices with their start and end apart: 11 -> 11, of which waited for: 5 -> 6; matrix products, arithmetic and copies ran while one was open for 0% -> 0% of each run, Pallas kernels for 40% -> 40%
where the time goes in v14:
time: 109 us; the launch traced here: 107 us
  Pallas kernels  49.9 us (46%)
  waiting for transfers between devices  23.6 us (22%)
  starting transfers between devices  17 us (16%)
  blocking collectives  13.7 us (13%)
  local copies, waits for them, and re-layouts  2.05 us (2%)
    pallas_call x1, Pallas kernels, factorise(): pl.pallas_call(functools.partial(factor_kernel, 1.0 / total_rows), in_spe...  26.9 us
    ppermute x10, waiting for transfers between devices, shards(): lax.ppermute(chunk, 'rows', [(i, i ^ k) for i in range(groups)])  20.5 us
    all_to_all x1, blocking collectives, gather_pieces(): lax.all_to_all(copies, axes, split_axis=0, concat_axis=0, axis_index_grou...  13.7 us
    ppermute x10, starting transfers between devices, shards(): lax.ppermute(chunk, 'rows', [(i, i ^ k) for i in range(groups)])  13.5 us
    pallas_call x3, Pallas kernels, whiten(): pl.pallas_call(functools.partial(whiten_kernel, steps, len(extra), per_bu...  7.28 us
    pallas_call x1, Pallas kernels, regroup_rest(): pl.pallas_call(functools.partial(rest_kernel, groups, per_bucket, tuple(o...  5.98 us
    pallas_call x1, Pallas kernels, regroup_lead(): pl.pallas_call(functools.partial(lead_kernel, groups, per_bucket, tuple(l...  5.2 us
    pallas_call x1, Pallas kernels, gram(): pl.pallas_call(gram_kernel, in_specs=[vmem] * 2, out_specs=[vmem] * 2, ou...  4.56 us
  transfers between devices with their start and end apart: 11, of which 6 were waited for; matrix products, arithmetic and copies ran while one was open for 0% of the time, Pallas kernels for 40%

profile of v14, /device:TPU:8, one launch (start us, length us, event | category | flops | bytes accessed | tf_op | source)
XLA Modules:
  0.0 107.3 jit_solution(13112353070548945814)
XLA Ops:
  0.6 5.2 %shard_map.69 = (f32[256,512]{1,0:T(8,128)}, f32[256,512]{1,0:T(8,128)}, bf16[2048,1024]{1,0:T(8,128)(2,1)S(1)}, s32[8,256]{1,0:T(8,128)S(1)}, s32[64,128]{1,0:T(8,128)S(1)}) custom-call(s32[1]{0:T(128)} %bitcast.2.me_ref, s32[16,128]{1,0:T(8,128)} %bitcast.9, s32[16,128]{1,0:T(8,128)} %bitcast.10, f32[1,128]{1,0:T(1,128)} %bitcast.11, f32[2048,512]{1,0:T(8,128)} %refs_3_.1), custom_call_target="tpu_custom_call" | custom-call | flops 1048576 | bytes 8388608 | tf_op jit(solution)/shard_map/pallas_call | solution.py:254
  5.9 1.6 %collective-permute-start = (f32[256,512]{1,0:T(8,128)}, f32[256,512]{1,0:T(8,128)S(1)}, u32[]{:S(2)}, u32[]{:S(2)}) collective-permute-start(f32[256,512]{1,0:T(8,128)} %get-tuple-element.56), channel_id=1, source_target_pairs={{0,4},{4,0},{8,12},{12,8},{16,20},{20,16},{24,28},{28,24},{1,5},{5... | collective-permute-start | bytes 1572872 | tf_op jit(solution)/shard_map/ppermute | solution.py:550
  7.4 2.6 %collective-permute-start.4 = (f32[256,512]{1,0:T(8,128)}, f32[256,512]{1,0:T(8,128)S(1)}, u32[]{:S(2)}, u32[]{:S(2)}) collective-permute-start(f32[256,512]{1,0:T(8,128)} %get-tuple-element.58), channel_id=1, source_target_pairs={{0,16},{4,20},{8,24},{12,28},{16,0},{20,4},{24,8},{28,12},{1,17},{... | collective-permute-start | bytes 1572872 | tf_op jit(solution)/shard_map/ppermute | solution.py:550
  10.0 19.3 %conditional.2 = (f32[136,128]{1,0:T(8,128)S(1)}, f32[1088,128]{1,0:T(8,128)S(1)}, f32[256,512]{1,0:T(8,128)}, f32[256,512]{1,0:T(8,128)}, f32[256,512]{1,0:T(8,...) conditional(s32[]{:T(128)} %bitcast.3, () %tuple.30, (f32[512,512]{1,0:T(8,128)}, ...), branch_computations={%region_0.0_spmd, %region_1.0_spmd} | conditional | flops 5234613248 | bytes 31658112 | solution.py:568
  10.1 2.0 %copy-done.1 = bf16[2048,1024]{1,0:T(8,128)(2,1)} copy-done((bf16[2048,1024]{1,0:T(8,128)(2,1)}, bf16[2048,1024]{1,0:T(8,128)(2,1)S(1)}, u32[]{:S(2)}) %copy-start.1) | copy-done | bytes 4194328 | tf_op jit(solution)/shard_map/cond
  12.1 4.6 %branch_1_fun.2 = (f32[1088,128]{1,0:T(8,128)}, f32[1088,128]{1,0:T(8,128)S(1)}) custom-call(f32[512,512]{1,0:T(8,128)} %get-tuple-element.79.prior_ref, bf16[2048,1024]{1,0:T(8,128)(2,1)S(1)} %get-tuple-element.13.pair_ref), custom_call_target="tpu_custom_call" | custom-call | flops 2147483648 | bytes 4194304 | tf_op jit(solution)/shard_map/cond/branch_1_fun/pallas_call | solution.py:372
  16.6 3.5 %all-to-all-start = ((f32[8,136,128]{2,1,0:T(8,128)}), f32[8,136,128]{2,1,0:T(8,128)S(1)}, u32[]{:S(2)}, u32[]{:S(2)}) async-start(f32[8,136,128]{2,1,0:T(8,128)} %bitcast), calls=%async_computation | async-start | bytes 1114112 | tf_op jit(solution)/shard_map/cond/branch_1_fun/all_to_all | solution.py:388
  20.2 6.0 %branch_1_fun.3 = (f32[256,512]{1,0:T(8,128)}, f32[256,512]{1,0:T(8,128)}, f32[256,512]{1,0:T(8,128)}, f32[256,512]{1,0:T(8,128)}, f32[256,512]{1,0:T(8,128)}, /*index=5*/f32[256,512]{1,0:T(8,128)}) custom-call(s32[64,128]{1,0:T(8,128)S(1)} %get-tuple-element.16.table, s32[8,256]{1,0:T(8,128)S(1)} %get-tuple-element.17.place_ref, bf16[2048,1024]{1,0:T(8,128)(2,1)} %copy-done.1), custom_call_target="tpu_custom_call" | custom-call | flops 3087007744 | bytes 8388608 | tf_op jit(solution)/shard_map/cond/branch_1_fun/pallas_call | solution.py:296
  26.2 3.1 %all-to-all-done = f32[8,136,128]{2,1,0:T(8,128)S(1)} async-done(((f32[8,136,128]{2,1,0:T(8,128)}), f32[8,136,128]{2,1,0:T(8,128)S(1)}, u32[]{:S(2)}, u32[]{:S(2)}) %all-to-all-start) | async-done | bytes 557088 | tf_op jit(solution)/shard_map/cond/branch_1_fun/all_to_all | solution.py:388
  29.4 2.8 %collective-permute-start.2 = (f32[136,128]{1,0:T(8,128)S(1)}, f32[136,128]{1,0:T(8,128)S(1)}, u32[]{:S(2)}, u32[]{:S(2)}) collective-permute-start(f32[136,128]{1,0:T(8,128)S(1)} %get-tuple-element.57), channel_id=1, source_target_pairs={{0,16},{4,20},{8,24},{12,28},{16,0},{20,4},{24,8},{28,12},{1,17},{... | collective-permute-start | bytes 208904 | tf_op jit(solution)/shard_map/ppermute | solution.py:550
  32.9 1.3 %collective-permute-start.8 = (f32[256,512]{1,0:T(8,128)}, f32[256,512]{1,0:T(8,128)S(1)}, u32[]{:S(2)}, u32[]{:S(2)}) collective-permute-start(f32[256,512]{1,0:T(8,128)} %get-tuple-element.75), channel_id=1, source_target_pairs={{0,8},{4,12},{8,0},{12,4},{16,24},{20,28},{24,16},{28,20},{1,9},{5... | collective-permute-start | bytes 1572872 | tf_op jit(solution)/shard_map/ppermute | solution.py:550
  34.2 1.1 %collective-permute-done.4.rest_1_ = f32[256,512]{1,0:T(8,128)S(1)} collective-permute-done((f32[256,512]{1,0:T(8,128)}, f32[256,512]{1,0:T(8,128)S(1)}, u32[]{:S(2)}, u32[]{:S(2)}) %collective-permute-start.4) | collective-permute-done | bytes 524320 | tf_op jit(solution)/shard_map/ppermute | solution.py:550
  35.4 1.7 %collective-permute-done.3 = f32[136,128]{1,0:T(8,128)S(1)} collective-permute-done((f32[136,128]{1,0:T(8,128)S(1)}, f32[136,128]{1,0:T(8,128)S(1)}, u32[]{:S(2)}, u32[]{:S(2)}) %collective-permute-start.3) | collective-permute-done | bytes 69664 | tf_op jit(solution)/shard_map/ppermute | solution.py:550
  37.0 1.3 %collective-permute-done.2 = f32[136,128]{1,0:T(8,128)S(1)} collective-permute-done((f32[136,128]{1,0:T(8,128)S(1)}, f32[136,128]{1,0:T(8,128)S(1)}, u32[]{:S(2)}, u32[]{:S(2)}) %collective-permute-start.2) | collective-permute-done | bytes 69664 | tf_op jit(solution)/shard_map/ppermute | solution.py:550
  38.4 3.4 %collective-permute-start.6 = (f32[256,512]{1,0:T(8,128)}, f32[256,512]{1,0:T(8,128)S(1)}, u32[]{:S(2)}, u32[]{:S(2)}) collective-permute-start(f32[256,512]{1,0:T(8,128)} %get-tuple-element.68), channel_id=1, source_target_pairs={{0,20},{4,16},{8,28},{12,24},{16,4},{20,0},{24,12},{28,8},{1,21},{... | collective-permute-start | bytes 1572872 | tf_op jit(solution)/shard_map/ppermute | solution.py:550
  41.8 13.8 %conditional.3 = (f32[1088,128]{1,0:T(8,128)}) conditional(s32[]{:T(128)} %bitcast.3, () %tuple.29, f32[136,128]{1,0:T(8,128)S(1)} %add_add_fusion), branch_computations={%region_3.0_spmd, %region_4.0_spmd} | conditional | bytes 1740808 | solution.py:586
  41.8 13.7 %all_to_all.14 = f32[8,136,128]{2,1,0:T(8,128)} all-to-all(f32[8,136,128]{2,1,0:T(8,128)S(1)} %broadcast_in_dim.2), channel_id=1, replica_groups={{0,1,2,3,4,5,6,7},{8,9,10,11,12,13,14,15},{16,17,18,19,20,21,22,23},{24..., dimensions={0} | all-to-all | bytes 1114112 | tf_op jit(solution)/shard_map/cond/branch_1_fun/all_to_all | solution.py:396
  55.5 1.0 collective-permute-start.5
  56.6 26.9 %shard_map.70 = (f32[512,512]{1,0:T(8,128)}, bf16[512,512]{1,0:T(8,128)(2,1)S(1)}, bf16[512,512]{1,0:T(8,128)(2,1)S(1)}) custom-call(f32[1088,128]{1,0:T(8,128)} %get-tuple-element.96.sum_ref, f32[1088,128]{1,0:T(8,128)S(1)} %get-tuple-element.62.prior_ref), custom_call_target="tpu_custom_call" | custom-call | flops 1 | bytes 1 | tf_op jit(solution)/shard_map/pallas_call | solution.py:469
  83.5 4.1 %shard_map.71.rest_2_ = f32[2048,512]{1,0:T(8,128)} custom-call(s32[1]{0:T(128)} %bitcast.2.me_ref, bf16[512,512]{1,0:T(8,128)(2,1)S(1)} %get-tuple-element.63.high_ref, bf16[512,512]{1,0:T(8,128)(2,1)S(1)} %get-tuple-element.64.low_ref, f32[256,512]{1,0:T(8,128)} %get-tuple-element.71.rest_0_, f32[256,512]{1,0:T(8,128)S(1)} %collective-permute-done.4.rest_1_, ...), custom_call_target="tpu_custom_call" | custom-call | flops 1 | bytes 1 | tf_op jit(solution)/shard_map/pallas_call | solution.py:516
  87.6 7.0 %collective-permute-done.6.rest_0_ = f32[256,512]{1,0:T(8,128)S(1)} collective-permute-done((f32[256,512]{1,0:T(8,128)}, f32[256,512]{1,0:T(8,128)S(1)}, u32[]{:S(2)}, u32[]{:S(2)}) %collective-permute-start.6) | collective-permute-done | bytes 524320 | tf_op jit(solution)/shard_map/ppermute | solution.py:550
  94.6 1.8 %shard_map.72.rest_1_ = f32[2048,512]{1,0:T(8,128)} custom-call(s32[1]{0:T(128)} %bitcast.2.me_ref, bf16[512,512]{1,0:T(8,128)(2,1)S(1)} %get-tuple-element.63.high_ref, bf16[512,512]{1,0:T(8,128)(2,1)S(1)} %get-tuple-element.64.low_ref, f32[256,512]{1,0:T(8,128)S(1)} %collective-permute-done.6.rest_0_, ...), custom_call_target="tpu_custom_call", output_to_operand_aliasing={{}: (5, {})} | custom-call | flops 1 | bytes 1 | tf_op jit(solution)/shard_map/pallas_call | solution.py:516
  96.4 9.3 %collective-permute-done.5.rest_0_ = f32[256,512]{1,0:T(8,128)S(1)} collective-permute-done((f32[256,512]{1,0:T(8,128)}, f32[256,512]{1,0:T(8,128)S(1)}, u32[]{:S(2)}, u32[]{:S(2)}) %collective-permute-start.5) | collective-permute-done | bytes 524320 | tf_op jit(solution)/shard_map/ppermute | solution.py:550
  105.8 1.4 %shard_map.73 = f32[2048,512]{1,0:T(8,128)} custom-call(s32[1]{0:T(128)} %bitcast.2.me_ref, bf16[512,512]{1,0:T(8,128)(2,1)S(1)} %get-tuple-element.63.high_ref, bf16[512,512]{1,0:T(8,128)(2,1)S(1)} %get-tuple-element.64.low_ref, f32[256,512]{1,0:T(8,128)S(1)} %collective-permute-done.5.rest_0_, ...), custom_call_target="tpu_custom_call", output_to_operand_aliasing={{}: (4, {})} | custom-call | flops 1 | bytes 1 | tf_op jit(solution)/shard_map/pallas_call | solution.py:516
  (15 shorter events, 0.9 us)
Async XLA Ops:
  0.6 9.4 %copy-start = (f32[128]{0:T(128)S(1)}, f32[128]{0:T(128)}, u32[]{:S(2)}) copy-start(f32[128]{0:T(128)} %param.11) | copy-start | bytes 1540
  5.9 23.5 %collective-permute-start = (f32[256,512]{1,0:T(8,128)}, f32[256,512]{1,0:T(8,128)S(1)}, u32[]{:S(2)}, u32[]{:S(2)}) collective-permute-start(f32[256,512]{1,0:T(8,128)} %get-tuple-element.56), channel_id=1, source_target_pairs={{0,4},{4,0},{8,12},{12,8},{16,20},{20,16},{24,28},{28,24},{1,5},{5... | collective-permute-start | bytes 1572872 | tf_op jit(solution)/shard_map/ppermute | solution.py:550
  7.4 27.9 %collective-permute-start.4 = (f32[256,512]{1,0:T(8,128)}, f32[256,512]{1,0:T(8,128)S(1)}, u32[]{:S(2)}, u32[]{:S(2)}) collective-permute-start(f32[256,512]{1,0:T(8,128)} %get-tuple-element.58), channel_id=1, source_target_pairs={{0,16},{4,20},{8,24},{12,28},{16,0},{20,4},{24,8},{28,12},{1,17},{... | collective-permute-start | bytes 1572872 | tf_op jit(solution)/shard_map/ppermute | solution.py:550
  10.1 2.0 %copy-start.1 = (bf16[2048,1024]{1,0:T(8,128)(2,1)}, bf16[2048,1024]{1,0:T(8,128)(2,1)S(1)}, u32[]{:S(2)}) copy-start(bf16[2048,1024]{1,0:T(8,128)(2,1)S(1)} %get-tuple-element.13.pair_ref) | copy-start | bytes 12582916 | tf_op jit(solution)/shard_map/cond
  16.6 12.7 %all-to-all-start = ((f32[8,136,128]{2,1,0:T(8,128)}), f32[8,136,128]{2,1,0:T(8,128)S(1)}, u32[]{:S(2)}, u32[]{:S(2)}) async-start(f32[8,136,128]{2,1,0:T(8,128)} %bitcast), calls=%async_computation | async-start | bytes 1114112 | tf_op jit(solution)/shard_map/cond/branch_1_fun/all_to_all | solution.py:388
  29.3 7.7 %collective-permute-start.3 = (f32[136,128]{1,0:T(8,128)S(1)}, f32[136,128]{1,0:T(8,128)S(1)}, u32[]{:S(2)}, u32[]{:S(2)}) collective-permute-start(f32[136,128]{1,0:T(8,128)S(1)} %get-tuple-element.57), channel_id=1, source_target_pairs={{0,24},{4,28},{8,16},{12,20},{16,8},{20,12},{24,0},{28,4},{1,25},{... | collective-permute-start | bytes 208904 | tf_op jit(solution)/shard_map/ppermute | solution.py:550
  29.4 8.9 %collective-permute-start.2 = (f32[136,128]{1,0:T(8,128)S(1)}, f32[136,128]{1,0:T(8,128)S(1)}, u32[]{:S(2)}, u32[]{:S(2)}) collective-permute-start(f32[136,128]{1,0:T(8,128)S(1)} %get-tuple-element.57), channel_id=1, source_target_pairs={{0,16},{4,20},{8,24},{12,28},{16,0},{20,4},{24,8},{28,12},{1,17},{... | collective-permute-start | bytes 208904 | tf_op jit(solution)/shard_map/ppermute | solution.py:550
  32.2 6.1 %collective-permute-start.1 = (f32[136,128]{1,0:T(8,128)S(1)}, f32[136,128]{1,0:T(8,128)S(1)}, u32[]{:S(2)}, u32[]{:S(2)}) collective-permute-start(f32[136,128]{1,0:T(8,128)S(1)} %get-tuple-element.57), channel_id=1, source_target_pairs={{0,8},{4,12},{8,0},{12,4},{16,24},{20,28},{24,16},{28,20},{1,9},{5... | collective-permute-start | bytes 208904 | tf_op jit(solution)/shard_map/ppermute | solution.py:550
  32.9 50.6 %collective-permute-start.8 = (f32[256,512]{1,0:T(8,128)}, f32[256,512]{1,0:T(8,128)S(1)}, u32[]{:S(2)}, u32[]{:S(2)}) collective-permute-start(f32[256,512]{1,0:T(8,128)} %get-tuple-element.75), channel_id=1, source_target_pairs={{0,8},{4,12},{8,0},{12,4},{16,24},{20,28},{24,16},{28,20},{1,9},{5... | collective-permute-start | bytes 1572872 | tf_op jit(solution)/shard_map/ppermute | solution.py:550
  35.4 48.1 %collective-permute-start.9 = (f32[256,512]{1,0:T(8,128)}, f32[256,512]{1,0:T(8,128)S(1)}, u32[]{:S(2)}, u32[]{:S(2)}) collective-permute-start(f32[256,512]{1,0:T(8,128)} %get-tuple-element.76), channel_id=1, source_target_pairs={{0,24},{4,28},{8,16},{12,20},{16,8},{20,12},{24,0},{28,4},{1,25},{... | collective-permute-start | bytes 1572872 | tf_op jit(solution)/shard_map/ppermute | solution.py:550
  38.4 56.3 %collective-permute-start.6 = (f32[256,512]{1,0:T(8,128)}, f32[256,512]{1,0:T(8,128)S(1)}, u32[]{:S(2)}, u32[]{:S(2)}) collective-permute-start(f32[256,512]{1,0:T(8,128)} %get-tuple-element.68), channel_id=1, source_target_pairs={{0,20},{4,16},{8,28},{12,24},{16,4},{20,0},{24,12},{28,8},{1,21},{... | collective-permute-start | bytes 1572872 | tf_op jit(solution)/shard_map/ppermute | solution.py:550
  55.5 39.1 %collective-permute-start.7 = (f32[256,512]{1,0:T(8,128)}, f32[256,512]{1,0:T(8,128)S(1)}, u32[]{:S(2)}, u32[]{:S(2)}) collective-permute-start(f32[256,512]{1,0:T(8,128)} %get-tuple-element.70), channel_id=1, source_target_pairs={{0,12},{4,8},{8,4},{12,0},{16,28},{20,24},{24,20},{28,16},{1,13},{... | collective-permute-start | bytes 1572872 | tf_op jit(solution)/shard_map/ppermute | solution.py:550
  55.5 50.2 %collective-permute-start.5 = (f32[256,512]{1,0:T(8,128)}, f32[256,512]{1,0:T(8,128)S(1)}, u32[]{:S(2)}, u32[]{:S(2)}) collective-permute-start(f32[256,512]{1,0:T(8,128)} %get-tuple-element.66), channel_id=1, source_target_pairs={{0,28},{4,24},{8,20},{12,16},{16,12},{20,8},{24,4},{28,0},{1,29},{... | collective-permute-start | bytes 1572872 | tf_op jit(solution)/shard_map/ppermute | solution.py:550

commit v15 on v14

--- a/solution.py
+++ b/solution.py
@@ -505,7 +505,7 @@
         copy.wait()
 
 
-def whiten(me, high, low, parts, out, rows, groups):
+def whiten(me, high, low, parts, out, rows, groups, cost):
     steps = tuple((k, offset) for k, offset, _ in parts)
     chunks = [chunk for _, _, chunk in parts]
     per_bucket, state = rows // groups, chunks[0].shape[1]
@@ -526,8 +526,24 @@
         ],
         input_output_aliases={3 + count: 0} if extra else {},
         compiler_params=pltpu.CompilerParams(vmem_limit_bytes=16 * MIB),
-        cost_estimate=pl.CostEstimate(flops=1, bytes_accessed=1, transcendentals=0),
+        cost_estimate=pl.CostEstimate(flops=cost, bytes_accessed=1, transcendentals=0),
     )(me.reshape(1), high, low, *chunks, *extra)
+
+
+def add_kernel(left, right, out):
+    out[...] = left[...] + right[...]
+
+
+def add(left, right, cost):
+    vmem = pl.BlockSpec(memory_space=pltpu.VMEM)
+    return pl.pallas_call(
+        add_kernel,
+        in_specs=[vmem] * 2,
+        out_specs=vmem,
+        out_shape=jax.ShapeDtypeStruct(left.shape, F32),
+        compiler_params=pltpu.CompilerParams(vmem_limit_bytes=4 * MIB),
+        cost_estimate=pl.CostEstimate(flops=cost, bytes_accessed=1, transcendentals=0),
+    )(left, right)
 
 
 def behind(value, *arrays):
@@ -552,8 +568,7 @@
     plane = 2 * grp
     packed_rows = packed_rows_of(state, plane)
     planes = [list(range(i, i + plane)) for i in range(0, groups * grp, plane)]
-    middle = [k for k in (2, 6) if k < groups]
-    late = [k for k in (5, 3, *range(7, groups)) if k < groups]
+    after = [k for k in (3, *range(7, groups)) if k < groups]
     valid = sensor_sigma[0] > 0
     nothing = lambda rows: jnp.full((rows, LANES), jnp.nan, F32)
 
@@ -568,32 +583,41 @@
     piece, prior_gram, rest = lax.cond(valid, first, wrong)
     rest = dict(zip(others, rest))
     received[0] = rest[0]
+    half = per_bucket // 2 // SUB * SUB
     for k in leads[1:]:
         piece, received[k] = behind(piece, received[k])
-    across = [piece]
-    for step in range(1, groups // 2):
-        across.append(move(2 * step, piece))
-    for k in middle[:1]:
-        received[k] = move(k, behind(piece, rest[k])[1])
-    while len(across) > 1:
-        across = [across[i] + across[i + 1] for i in range(0, len(across), 2)]
-    for k in middle[1:]:
-        received[leads[0]], chunk = behind(received[leads[0]], rest[k])
-        received[k] = move(k, chunk)
-    across[0], received[leads[0]] = behind(across[0], received[leads[0]])
-    for k in late[:1]:
-        received[k] = move(k, behind(across[0], rest[k])[1])
+    step = 1
+    if groups > 6:
+        across = move(2, piece)
+        received[2] = move(2, behind(piece, rest[2])[1])
+        received[leads[0]], chunk = behind(received[leads[0]], rest[6][:half])
+        six = [move(6, chunk)]
+        piece = add(piece, across, 1441250001)
+        step = 2
+        chunk = behind(piece, rest[6][half:])[1]
+    while step < groups // 2:
+        piece = add(piece, move(2 * step, piece), 1441250001)
+        step = 2 * step
+    if groups > 6:
+        six.append(move(6, chunk))
+        received[5] = move(5, behind(chunk, rest[5])[1])
     summed = lax.cond(
-        valid, lambda: gather_pieces(across[0], plane, planes), lambda: nothing(packed_rows)
+        valid, lambda: gather_pieces(piece, plane, planes), lambda: nothing(packed_rows)
     )
-    for k in late[1:]:
+    if groups > 6:
+        summed, six[0] = behind(summed, six[0])
+    for k in after:
         received[k] = move(k, behind(summed, rest[k])[1])
     factor, high, low = factorise(summed, prior_gram, state, total_rows)
-    whole = lambda slots: [(k, 0, received[k]) for k in slots]
+    whole = lambda *slots: [(k, 0, received[k]) for k in slots if k in received]
+    soon, last = whole(0, 1, 4, 2), []
+    if groups > 6:
+        soon.append((6, 0, six[0]))
+        last.append((6, half, six[1]))
     out = None
-    for parts in (whole([0, *leads, *middle]), whole(late[:-1]), whole(late[-1:])):
+    for parts, cost in ((soon, 4612000001), (whole(5), 576500001), (whole(*after), 1), (last, 1)):
         if parts:
-            out = whiten(me, high, low, parts, out, rows_dev, groups)
+            out = whiten(me, high, low, parts, out, rows_dev, groups, cost)
     return (out, factor)
 
 

time: 109 us -> 120 us (1.10); the launches traced: 107 us -> 120 us
  starting transfers between devices: 17 us -> 22.9 us
  waiting for transfers between devices: 23.6 us -> 26.8 us
  blocking collectives: 13.7 us -> 16.8 us
    ppermute x10, starting transfers between devices: 13.5 us -> 19.4 us  [shards(): lax.ppermute(chunk, 'rows', [(i, i ^ k) for i in range(groups)])]
    ppermute x10, waiting for transfers between devices: 20.5 us -> 23.6 us  [shards(): lax.ppermute(chunk, 'rows', [(i, i ^ k) for i in range(groups)])]
    all_to_all x1, blocking collectives: 13.7 us -> 16.8 us  [gather_pieces(): lax.all_to_all(copies, axes, split_axis=0, concat_axis=0, axis_index_grou...]
    pallas_call x3 -> x4, Pallas kernels: 7.28 us -> 8.14 us  [whiten(): pl.pallas_call(functools.partial(whiten_kernel, steps, len(extra), per_bu...]
  transfers between devices with their start and end apart: 11 -> 11, of which waited for: 6 -> 6; matrix products, arithmetic and copies ran while one was open for 0% -> 1% of each run, Pallas kernels for 40% -> 36%
where the time goes in v15:
time: 120 us
  Pallas kernels  49.6 us (41%)
  waiting for transfers between devices  26.8 us (22%)
  starting transfers between devices  22.9 us (19%)
  blocking collectives  16.8 us (14%)
  local copies, waits for them, and re-layouts  2.87 us (2%)
    pallas_call x1, Pallas kernels, factorise(): pl.pallas_call(functools.partial(factor_kernel, 1.0 / total_rows), in_spe...  25.9 us
    ppermute x10, waiting for transfers between devices, shards(): lax.ppermute(chunk, 'rows', [(i, i ^ k) for i in range(groups)])  23.6 us
    ppermute x10, starting transfers between devices, shards(): lax.ppermute(chunk, 'rows', [(i, i ^ k) for i in range(groups)])  19.4 us
    all_to_all x1, blocking collectives, gather_pieces(): lax.all_to_all(copies, axes, split_axis=0, concat_axis=0, axis_index_grou...  16.8 us
    pallas_call x4, Pallas kernels, whiten(): pl.pallas_call(functools.partial(whiten_kernel, steps, len(extra), per_bu...  8.14 us
    pallas_call x1, Pallas kernels, regroup_rest(): pl.pallas_call(functools.partial(rest_kernel, groups, per_bucket, tuple(o...  5.83 us
    pallas_call x1, Pallas kernels, regroup_lead(): pl.pallas_call(functools.partial(lead_kernel, groups, per_bucket, tuple(l...  5.19 us
    pallas_call x1, Pallas kernels, gram(): pl.pallas_call(gram_kernel, in_specs=[vmem] * 2, out_specs=[vmem] * 2, ou...  4.56 us
  transfers between devices with their start and end apart: 11, of which 6 were waited for; matrix products, arithmetic and copies ran while one was open for 1% of the time, Pallas kernels for 36%

profile of v15, /device:TPU:8, one launch (start us, length us, event | category | flops | bytes accessed | tf_op | source)
XLA Modules:
  0.0 120.1 jit_solution(12448440480736886611)
XLA Ops:
  0.6 5.2 %shard_map.69 = (f32[256,512]{1,0:T(8,128)}, f32[256,512]{1,0:T(8,128)}, bf16[2048,1024]{1,0:T(8,128)(2,1)S(1)}, s32[8,256]{1,0:T(8,128)S(1)}, s32[64,128]{1,0:T(8,128)S(1)}) custom-call(s32[1]{0:T(128)} %bitcast.2.me_ref, s32[16,128]{1,0:T(8,128)} %bitcast.9, s32[16,128]{1,0:T(8,128)} %bitcast.10, f32[1,128]{1,0:T(1,128)} %bitcast.11, f32[2048,512]{1,0:T(8,128)} %refs_3_.1), custom_call_target="tpu_custom_call" | custom-call | flops 1048576 | bytes 8388608 | tf_op jit(solution)/shard_map/pallas_call | solution.py:254
  5.8 1.6 %collective-permute-start = (f32[256,512]{1,0:T(8,128)}, f32[256,512]{1,0:T(8,128)S(1)}, u32[]{:S(2)}, u32[]{:S(2)}) collective-permute-start(f32[256,512]{1,0:T(8,128)} %get-tuple-element.57), channel_id=1, source_target_pairs={{0,4},{4,0},{8,12},{12,8},{16,20},{20,16},{24,28},{28,24},{1,5},{5... | collective-permute-start | bytes 1572872 | tf_op jit(solution)/shard_map/ppermute | solution.py:566
  7.4 2.6 %collective-permute-start.3 = (f32[256,512]{1,0:T(8,128)}, f32[256,512]{1,0:T(8,128)S(1)}, u32[]{:S(2)}, u32[]{:S(2)}) collective-permute-start(f32[256,512]{1,0:T(8,128)} %get-tuple-element.59), channel_id=1, source_target_pairs={{0,16},{4,20},{8,24},{12,28},{16,0},{20,4},{24,8},{28,12},{1,17},{... | collective-permute-start | bytes 1572872 | tf_op jit(solution)/shard_map/ppermute | solution.py:566
  10.0 19.3 %conditional.2 = (f32[136,128]{1,0:T(8,128)S(1)}, f32[1088,128]{1,0:T(8,128)S(1)}, f32[256,512]{1,0:T(8,128)}, f32[256,512]{1,0:T(8,128)}, f32[256,512]{1,0:T(8,...) conditional(s32[]{:T(128)} %bitcast.3, () %tuple.31, (f32[512,512]{1,0:T(8,128)}, ...), branch_computations={%region_0.0_spmd, %region_1.0_spmd} | conditional | flops 5234613248 | bytes 31658112 | solution.py:583
  10.1 2.0 %copy-done.1 = bf16[2048,1024]{1,0:T(8,128)(2,1)} copy-done((bf16[2048,1024]{1,0:T(8,128)(2,1)}, bf16[2048,1024]{1,0:T(8,128)(2,1)S(1)}, u32[]{:S(2)}) %copy-start.1) | copy-done | bytes 4194328 | tf_op jit(solution)/shard_map/cond
  12.1 4.6 %branch_1_fun.2 = (f32[1088,128]{1,0:T(8,128)}, f32[1088,128]{1,0:T(8,128)S(1)}) custom-call(f32[512,512]{1,0:T(8,128)} %get-tuple-element.81.prior_ref, bf16[2048,1024]{1,0:T(8,128)(2,1)S(1)} %get-tuple-element.13.pair_ref), custom_call_target="tpu_custom_call" | custom-call | flops 2147483648 | bytes 4194304 | tf_op jit(solution)/shard_map/cond/branch_1_fun/pallas_call | solution.py:372
  16.6 3.5 %all-to-all-start = ((f32[8,136,128]{2,1,0:T(8,128)}), f32[8,136,128]{2,1,0:T(8,128)S(1)}, u32[]{:S(2)}, u32[]{:S(2)}) async-start(f32[8,136,128]{2,1,0:T(8,128)} %bitcast), calls=%async_computation | async-start | bytes 1114112 | tf_op jit(solution)/shard_map/cond/branch_1_fun/all_to_all | solution.py:388
  20.2 5.8 %branch_1_fun.3 = (f32[256,512]{1,0:T(8,128)}, f32[256,512]{1,0:T(8,128)}, f32[256,512]{1,0:T(8,128)}, f32[256,512]{1,0:T(8,128)}, f32[256,512]{1,0:T(8,128)S(1)}, /*index=5*/f32[256,512]{1,0:T(8,128)}) custom-call(s32[64,128]{1,0:T(8,128)S(1)} %get-tuple-element.16.table, s32[8,256]{1,0:T(8,128)S(1)} %get-tuple-element.17.place_ref, ...), custom_call_target="tpu_custom_call" | custom-call | flops 3087007744 | bytes 8388608 | tf_op jit(solution)/shard_map/cond/branch_1_fun/pallas_call | solution.py:296
  26.0 3.3 %all-to-all-done = f32[8,136,128]{2,1,0:T(8,128)S(1)} async-done(((f32[8,136,128]{2,1,0:T(8,128)}), f32[8,136,128]{2,1,0:T(8,128)S(1)}, u32[]{:S(2)}, u32[]{:S(2)}) %all-to-all-start) | async-done | bytes 557088 | tf_op jit(solution)/shard_map/cond/branch_1_fun/all_to_all | solution.py:388
  29.8 1.6 %collective-permute-start.9 = (f32[256,512]{1,0:T(8,128)}, f32[256,512]{1,0:T(8,128)S(1)}, u32[]{:S(2)}, u32[]{:S(2)}) collective-permute-start(f32[256,512]{1,0:T(8,128)} %get-tuple-element.77), channel_id=1, source_target_pairs={{0,8},{4,12},{8,0},{12,4},{16,24},{20,28},{24,16},{28,20},{1,9},{5... | collective-permute-start | bytes 1572872 | tf_op jit(solution)/shard_map/ppermute | solution.py:566
  32.4 2.1 %collective-permute-done.1.right = f32[136,128]{1,0:T(8,128)S(1)} collective-permute-done((f32[136,128]{1,0:T(8,128)S(1)}, f32[136,128]{1,0:T(8,128)S(1)}, u32[]{:S(2)}, u32[]{:S(2)}) %collective-permute-start.1) | collective-permute-done | bytes 69664 | tf_op jit(solution)/shard_map/ppermute | solution.py:566
  34.5 2.8 %collective-permute-start.2 = (f32[136,128]{1,0:T(8,128)S(1)}, f32[136,128]{1,0:T(8,128)S(1)}, u32[]{:S(2)}, u32[]{:S(2)}) collective-permute-start(f32[136,128]{1,0:T(8,128)S(1)} %shard_map.70.left), channel_id=1, source_target_pairs={{0,16},{4,20},{8,24},{12,28},{16,0},{20,4},{24,8},{28,12},{1,17},{... | collective-permute-start | bytes 208904 | tf_op jit(solution)/shard_map/ppermute | solution.py:566
  37.3 1.2 collective-permute-start.8
  38.4 13.5 %collective-permute-done.2.right = f32[136,128]{1,0:T(8,128)S(1)} collective-permute-done((f32[136,128]{1,0:T(8,128)S(1)}, f32[136,128]{1,0:T(8,128)S(1)}, u32[]{:S(2)}, u32[]{:S(2)}) %collective-permute-start.2) | collective-permute-done | bytes 69664 | tf_op jit(solution)/shard_map/ppermute | solution.py:566
  51.9 16.9 %conditional.3 = (f32[1088,128]{1,0:T(8,128)S(1)}) conditional(s32[]{:T(128)} %bitcast.3, () %tuple.30, f32[136,128]{1,0:T(8,128)S(1)} %shard_map.71), branch_computations={%region_3.0_spmd, %region_4.0_spmd} | conditional | bytes 1740808 | solution.py:604
  52.0 16.8 %all_to_all.14 = f32[8,136,128]{2,1,0:T(8,128)S(1)} all-to-all(f32[8,136,128]{2,1,0:T(8,128)S(1)} %broadcast_in_dim.2), channel_id=1, replica_groups={{0,1,2,3,4,5,6,7},{8,9,10,11,12,13,14,15},{16,17,18,19,20,21,22,23},{24..., dimensions={0} | all-to-all | bytes 1114112 | tf_op jit(solution)/shard_map/cond/branch_1_fun/all_to_all | solution.py:396
  68.8 3.2 %collective-permute-start.7 = (f32[256,512]{1,0:T(8,128)}, f32[256,512]{1,0:T(8,128)S(1)}, u32[]{:S(2)}, u32[]{:S(2)}) collective-permute-start(f32[256,512]{1,0:T(8,128)} %get-tuple-element.70), channel_id=1, source_target_pairs={{0,28},{4,24},{8,20},{12,16},{16,12},{20,8},{24,4},{28,0},{1,29},{... | collective-permute-start | bytes 1572872 | tf_op jit(solution)/shard_map/ppermute | solution.py:566
  72.0 6.0 %collective-permute-start.5 = (f32[128,512]{1,0:T(8,128)}, f32[128,512]{1,0:T(8,128)S(1)}, u32[]{:S(2)}, u32[]{:S(2)}) collective-permute-start(f32[128,512]{1,0:T(8,128)} %get-tuple-element.66), channel_id=1, source_target_pairs={{0,24},{4,28},{8,16},{12,20},{16,8},{20,12},{24,0},{28,4},{1,25},{... | collective-permute-start | bytes 786440 | tf_op jit(solution)/shard_map/ppermute | solution.py:566
  78.0 25.9 %shard_map.72 = (f32[512,512]{1,0:T(8,128)}, bf16[512,512]{1,0:T(8,128)(2,1)S(1)}, bf16[512,512]{1,0:T(8,128)(2,1)S(1)}) custom-call(f32[1088,128]{1,0:T(8,128)S(1)} %get-tuple-element.100.sum_ref, f32[1088,128]{1,0:T(8,128)S(1)} %get-tuple-element.63.prior_ref), custom_call_target="tpu_custom_call" | custom-call | flops 1 | bytes 1 | tf_op jit(solution)/shard_map/pallas_call | solution.py:469
  103.9 3.8 %shard_map.73.rest_1_ = f32[2048,512]{1,0:T(8,128)} custom-call(s32[1]{0:T(128)} %bitcast.2.me_ref, bf16[512,512]{1,0:T(8,128)(2,1)S(1)} %get-tuple-element.64.high_ref, bf16[512,512]{1,0:T(8,128)(2,1)S(1)} %get-tuple-element.65.low_ref, f32[256,512]{1,0:T(8,128)} %get-tuple-element.73.rest_0_, f32[256,512]{1,0:T(8,128)S(1)} %collective-permute-done.rest_1_, ...), custom_call_target="tpu_custom_call" | custom-call | flops 4612000256 | bytes 1 | tf_op jit(solution)/shard_map/pallas_call | solution.py:516
  107.8 1.4 %shard_map.74.rest_2_ = f32[2048,512]{1,0:T(8,128)} custom-call(s32[1]{0:T(128)} %bitcast.2.me_ref, bf16[512,512]{1,0:T(8,128)(2,1)S(1)} %get-tuple-element.64.high_ref, bf16[512,512]{1,0:T(8,128)(2,1)S(1)} %get-tuple-element.65.low_ref, f32[256,512]{1,0:T(8,128)S(1)} %collective-permute-done.8.rest_0_, ...), custom_call_target="tpu_custom_call", output_to_operand_aliasing={{}: (4, {})} | custom-call | flops 576500032 | bytes 1 | tf_op jit(solution)/shard_map/pallas_call | solution.py:516
  109.2 1.8 %shard_map.75.rest_1_ = f32[2048,512]{1,0:T(8,128)} custom-call(s32[1]{0:T(128)} %bitcast.2.me_ref, bf16[512,512]{1,0:T(8,128)(2,1)S(1)} %get-tuple-element.64.high_ref, bf16[512,512]{1,0:T(8,128)(2,1)S(1)} %get-tuple-element.65.low_ref, f32[256,512]{1,0:T(8,128)S(1)} %collective-permute-done.6.rest_0_, ...), custom_call_target="tpu_custom_call", output_to_operand_aliasing={{}: (5, {})} | custom-call | flops 1 | bytes 1 | tf_op jit(solution)/shard_map/pallas_call | solution.py:516
  111.0 7.8 %collective-permute-done.5.rest_0_ = f32[128,512]{1,0:T(8,128)S(1)} collective-permute-done((f32[128,512]{1,0:T(8,128)}, f32[128,512]{1,0:T(8,128)S(1)}, u32[]{:S(2)}, u32[]{:S(2)}) %collective-permute-start.5) | collective-permute-done | bytes 262176 | tf_op jit(solution)/shard_map/ppermute | solution.py:566
  118.8 1.1 shard_map.76
  (18 shorter events, 1.6 us)
Async XLA Ops:
  0.6 9.4 %copy-start = (f32[128]{0:T(128)S(1)}, f32[128]{0:T(128)}, u32[]{:S(2)}) copy-start(f32[128]{0:T(128)} %param.11) | copy-start | bytes 1540
  5.8 23.5 %collective-permute-start = (f32[256,512]{1,0:T(8,128)}, f32[256,512]{1,0:T(8,128)S(1)}, u32[]{:S(2)}, u32[]{:S(2)}) collective-permute-start(f32[256,512]{1,0:T(8,128)} %get-tuple-element.57), channel_id=1, source_target_pairs={{0,4},{4,0},{8,12},{12,8},{16,20},{20,16},{24,28},{28,24},{1,5},{5... | collective-permute-start | bytes 1572872 | tf_op jit(solution)/shard_map/ppermute | solution.py:566
  7.4 25.0 %collective-permute-start.3 = (f32[256,512]{1,0:T(8,128)}, f32[256,512]{1,0:T(8,128)S(1)}, u32[]{:S(2)}, u32[]{:S(2)}) collective-permute-start(f32[256,512]{1,0:T(8,128)} %get-tuple-element.59), channel_id=1, source_target_pairs={{0,16},{4,20},{8,24},{12,28},{16,0},{20,4},{24,8},{28,12},{1,17},{... | collective-permute-start | bytes 1572872 | tf_op jit(solution)/shard_map/ppermute | solution.py:566
  10.1 2.0 %copy-start.1 = (bf16[2048,1024]{1,0:T(8,128)(2,1)}, bf16[2048,1024]{1,0:T(8,128)(2,1)S(1)}, u32[]{:S(2)}) copy-start(bf16[2048,1024]{1,0:T(8,128)(2,1)S(1)} %get-tuple-element.13.pair_ref) | copy-start | bytes 12582916 | tf_op jit(solution)/shard_map/cond
  16.6 12.7 %all-to-all-start = ((f32[8,136,128]{2,1,0:T(8,128)}), f32[8,136,128]{2,1,0:T(8,128)S(1)}, u32[]{:S(2)}, u32[]{:S(2)}) async-start(f32[8,136,128]{2,1,0:T(8,128)} %bitcast), calls=%async_computation | async-start | bytes 1114112 | tf_op jit(solution)/shard_map/cond/branch_1_fun/all_to_all | solution.py:388
  29.3 5.2 %collective-permute-start.1 = (f32[136,128]{1,0:T(8,128)S(1)}, f32[136,128]{1,0:T(8,128)S(1)}, u32[]{:S(2)}, u32[]{:S(2)}) collective-permute-start(f32[136,128]{1,0:T(8,128)S(1)} %get-tuple-element.58.left), channel_id=1, source_target_pairs={{0,8},{4,12},{8,0},{12,4},{16,24},{20,28},{24,16},{28,20},{1,9},{5... | collective-permute-start | bytes 208904 | tf_op jit(solution)/shard_map/ppermute | solution.py:566
  29.8 74.0 %collective-permute-start.9 = (f32[256,512]{1,0:T(8,128)}, f32[256,512]{1,0:T(8,128)S(1)}, u32[]{:S(2)}, u32[]{:S(2)}) collective-permute-start(f32[256,512]{1,0:T(8,128)} %get-tuple-element.77), channel_id=1, source_target_pairs={{0,8},{4,12},{8,0},{12,4},{16,24},{20,28},{24,16},{28,20},{1,9},{5... | collective-permute-start | bytes 1572872 | tf_op jit(solution)/shard_map/ppermute | solution.py:566
  32.4 36.4 %collective-permute-start.4 = (f32[128,512]{1,0:T(8,128)}, f32[128,512]{1,0:T(8,128)S(1)}, u32[]{:S(2)}, u32[]{:S(2)}) collective-permute-start(f32[128,512]{1,0:T(8,128)} %get-tuple-element.61), channel_id=1, source_target_pairs={{0,24},{4,28},{8,16},{12,20},{16,8},{20,12},{24,0},{28,4},{1,25},{... | collective-permute-start | bytes 786440 | tf_op jit(solution)/shard_map/ppermute | solution.py:566
  34.5 17.4 %collective-permute-start.2 = (f32[136,128]{1,0:T(8,128)S(1)}, f32[136,128]{1,0:T(8,128)S(1)}, u32[]{:S(2)}, u32[]{:S(2)}) collective-permute-start(f32[136,128]{1,0:T(8,128)S(1)} %shard_map.70.left), channel_id=1, source_target_pairs={{0,16},{4,20},{8,24},{12,28},{16,0},{20,4},{24,8},{28,12},{1,17},{... | collective-permute-start | bytes 208904 | tf_op jit(solution)/shard_map/ppermute | solution.py:566
  37.3 70.5 %collective-permute-start.8 = (f32[256,512]{1,0:T(8,128)}, f32[256,512]{1,0:T(8,128)S(1)}, u32[]{:S(2)}, u32[]{:S(2)}) collective-permute-start(f32[256,512]{1,0:T(8,128)} %get-tuple-element.72), channel_id=1, source_target_pairs={{0,20},{4,16},{8,28},{12,24},{16,4},{20,0},{24,12},{28,8},{1,21},{... | collective-permute-start | bytes 1572872 | tf_op jit(solution)/shard_map/ppermute | solution.py:566
  68.8 40.4 %collective-permute-start.6 = (f32[256,512]{1,0:T(8,128)}, f32[256,512]{1,0:T(8,128)S(1)}, u32[]{:S(2)}, u32[]{:S(2)}) collective-permute-start(f32[256,512]{1,0:T(8,128)} %get-tuple-element.68), channel_id=1, source_target_pairs={{0,12},{4,8},{8,4},{12,0},{16,28},{20,24},{24,20},{28,16},{1,13},{... | collective-permute-start | bytes 1572872 | tf_op jit(solution)/shard_map/ppermute | solution.py:566
  68.8 40.5 %collective-permute-start.7 = (f32[256,512]{1,0:T(8,128)}, f32[256,512]{1,0:T(8,128)S(1)}, u32[]{:S(2)}, u32[]{:S(2)}) collective-permute-start(f32[256,512]{1,0:T(8,128)} %get-tuple-element.70), channel_id=1, source_target_pairs={{0,28},{4,24},{8,20},{12,16},{16,12},{20,8},{24,4},{28,0},{1,29},{... | collective-permute-start | bytes 1572872 | tf_op jit(solution)/shard_map/ppermute | solution.py:566
  72.0 46.8 %collective-permute-start.5 = (f32[128,512]{1,0:T(8,128)}, f32[128,512]{1,0:T(8,128)S(1)}, u32[]{:S(2)}, u32[]{:S(2)}) collective-permute-start(f32[128,512]{1,0:T(8,128)} %get-tuple-element.66), channel_id=1, source_target_pairs={{0,24},{4,28},{8,16},{12,20},{16,8},{20,12},{24,0},{28,4},{1,25},{... | collective-permute-start | bytes 786440 | tf_op jit(solution)/shard_map/ppermute | solution.py:566

commit v16 on v14

--- a/solution.py
+++ b/solution.py
@@ -104,10 +104,10 @@
         copy.start()
 
     def fetch(s):
-        rows = pl.ds(pl.multiple_of(s * block, block), block)
+        rows = pl.ds(s * block, 2 * block)
         return pltpu.make_async_copy(given[3].at[rows, :], obs_ref.at[rows, :], sems.at[4 + s])
 
-    for s in range(blocks):
+    for s in range(0, blocks, 2):
         fetch(s).start()
     for copy in small:
         copy.wait()
@@ -149,16 +149,26 @@
     inv = jnp.concatenate([inv_ref[...]] * wide, axis=1)
     block_rows = lambda s: pl.ds(pl.multiple_of(s * block, block), block)
 
+    scales = []
+    for s in range(blocks):
+        ids = [ids_ref[s * wide + i : s * wide + i + 1, :] for i in range(wide)]
+        known = iota((sensors, block), 0) == jnp.concatenate(ids, axis=1)
+        scale_row = jnp.sum(jnp.where(known, inv, 0.0), axis=0, keepdims=True)
+        scales += [scale_row[:, i * LANES : (i + 1) * LANES] for i in range(wide)]
+    scales.append(jnp.zeros((-len(scales) % LANES, LANES), F32))
+    turned = jnp.transpose(jnp.concatenate(scales, axis=0))
     for s in range(blocks):
         if s == blocks // 2:
             meta_ref[...] = meta
             copy.start()
             place_ref[...] = places
-        ids = [ids_ref[s * wide + i : s * wide + i + 1, :] for i in range(wide)]
-        known = iota((sensors, block), 0) == jnp.concatenate(ids, axis=1)
-        scale_row = jnp.sum(jnp.where(known, inv, 0.0), axis=0, keepdims=True)
-        scale = jnp.transpose(jnp.broadcast_to(scale_row, (LANES, block)))
-        fetch(s).wait()
+        if s % 2 == 0:
+            fetch(s).wait()
+        spread = [
+            jnp.broadcast_to(turned[:, c : c + 1], (LANES, LANES))
+            for c in range(s * wide, (s + 1) * wide)
+        ]
+        scale = jnp.concatenate(spread, axis=0)
         rows = block_rows(s)
         high, low = split(obs_ref[rows, :] * jnp.concatenate([scale] * (state // LANES), axis=1))
         pair_ref[rows, :state] = high

time: 109 us -> 108 us (level)
  transfers between devices with their start and end apart: 11 -> 11, of which waited for: 6 -> 6; matrix products, arithmetic and copies ran while one was open for 0% -> 0% of each run, Pallas kernels for 40% -> 41%
where the time goes in v16:
time: 108 us; the launch traced here: 107 us
  Pallas kernels  49.3 us (46%)
  waiting for transfers between devices  23.6 us (22%)
  starting transfers between devices  17 us (16%)
  blocking collectives  13.7 us (13%)
  local copies, waits for them, and re-layouts  2.05 us (2%)
    pallas_call x1, Pallas kernels, factorise(): pl.pallas_call(functools.partial(factor_kernel, 1.0 / total_rows), in_spe...  26.9 us
    ppermute x10, waiting for transfers between devices, shards(): lax.ppermute(chunk, 'rows', [(i, i ^ k) for i in range(groups)])  20.5 us
    all_to_all x1, blocking collectives, gather_pieces(): lax.all_to_all(copies, axes, split_axis=0, concat_axis=0, axis_index_grou...  13.7 us
    ppermute x10, starting transfers between devices, shards(): lax.ppermute(chunk, 'rows', [(i, i ^ k) for i in range(groups)])  13.5 us
    pallas_call x3, Pallas kernels, whiten(): pl.pallas_call(functools.partial(whiten_kernel, steps, len(extra), per_bu...  7.27 us
    pallas_call x1, Pallas kernels, regroup_rest(): pl.pallas_call(functools.partial(rest_kernel, groups, per_bucket, tuple(o...  5.97 us
    pallas_call x1, Pallas kernels, gram(): pl.pallas_call(gram_kernel, in_specs=[vmem] * 2, out_specs=[vmem] * 2, ou...  4.56 us
    pallas_call x1, Pallas kernels, regroup_lead(): pl.pallas_call(functools.partial(lead_kernel, groups, per_bucket, tuple(l...  4.56 us
  transfers between devices with their start and end apart: 11, of which 6 were waited for; matrix products, arithmetic and copies ran while one was open for 0% of the time, Pallas kernels for 41%

profile of v16, /device:TPU:8, one launch (start us, length us, event | category | flops | bytes accessed | tf_op | source)
XLA Modules:
  0.0 106.7 jit_solution(15498791277795839688)
XLA Ops:
  0.6 4.6 %shard_map.69 = (f32[256,512]{1,0:T(8,128)}, f32[256,512]{1,0:T(8,128)}, bf16[2048,1024]{1,0:T(8,128)(2,1)S(1)}, s32[8,256]{1,0:T(8,128)S(1)}, s32[64,128]{1,0:T(8,128)S(1)}) custom-call(s32[1]{0:T(128)} %bitcast.2.me_ref, s32[16,128]{1,0:T(8,128)} %bitcast.9, s32[16,128]{1,0:T(8,128)} %bitcast.10, f32[1,128]{1,0:T(1,128)} %bitcast.11, f32[2048,512]{1,0:T(8,128)} %refs_3_.1), custom_call_target="tpu_custom_call" | custom-call | flops 1048576 | bytes 8388608 | tf_op jit(solution)/shard_map/pallas_call | solution.py:264
  5.2 1.6 %collective-permute-start = (f32[256,512]{1,0:T(8,128)}, f32[256,512]{1,0:T(8,128)S(1)}, u32[]{:S(2)}, u32[]{:S(2)}) collective-permute-start(f32[256,512]{1,0:T(8,128)} %get-tuple-element.56), channel_id=1, source_target_pairs={{0,4},{4,0},{8,12},{12,8},{16,20},{20,16},{24,28},{28,24},{1,5},{5... | collective-permute-start | bytes 1572872 | tf_op jit(solution)/shard_map/ppermute | solution.py:560
  6.8 2.6 %collective-permute-start.4 = (f32[256,512]{1,0:T(8,128)}, f32[256,512]{1,0:T(8,128)S(1)}, u32[]{:S(2)}, u32[]{:S(2)}) collective-permute-start(f32[256,512]{1,0:T(8,128)} %get-tuple-element.58), channel_id=1, source_target_pairs={{0,16},{4,20},{8,24},{12,28},{16,0},{20,4},{24,8},{28,12},{1,17},{... | collective-permute-start | bytes 1572872 | tf_op jit(solution)/shard_map/ppermute | solution.py:560
  9.4 19.3 %conditional.2 = (f32[136,128]{1,0:T(8,128)S(1)}, f32[1088,128]{1,0:T(8,128)S(1)}, f32[256,512]{1,0:T(8,128)}, f32[256,512]{1,0:T(8,128)}, f32[256,512]{1,0:T(8,...) conditional(s32[]{:T(128)} %bitcast.3, () %tuple.30, (f32[512,512]{1,0:T(8,128)}, ...), branch_computations={%region_0.0_spmd, %region_1.0_spmd} | conditional | flops 5234613248 | bytes 31658112 | solution.py:578
  9.4 2.0 %copy-done.1 = bf16[2048,1024]{1,0:T(8,128)(2,1)} copy-done((bf16[2048,1024]{1,0:T(8,128)(2,1)}, bf16[2048,1024]{1,0:T(8,128)(2,1)S(1)}, u32[]{:S(2)}) %copy-start.1) | copy-done | bytes 4194328 | tf_op jit(solution)/shard_map/cond
  11.4 4.6 %branch_1_fun.2 = (f32[1088,128]{1,0:T(8,128)}, f32[1088,128]{1,0:T(8,128)S(1)}) custom-call(f32[512,512]{1,0:T(8,128)} %get-tuple-element.79.prior_ref, bf16[2048,1024]{1,0:T(8,128)(2,1)S(1)} %get-tuple-element.13.pair_ref), custom_call_target="tpu_custom_call" | custom-call | flops 2147483648 | bytes 4194304 | tf_op jit(solution)/shard_map/cond/branch_1_fun/pallas_call | solution.py:382
  16.0 3.5 %all-to-all-start = ((f32[8,136,128]{2,1,0:T(8,128)}), f32[8,136,128]{2,1,0:T(8,128)S(1)}, u32[]{:S(2)}, u32[]{:S(2)}) async-start(f32[8,136,128]{2,1,0:T(8,128)} %bitcast), calls=%async_computation | async-start | bytes 1114112 | tf_op jit(solution)/shard_map/cond/branch_1_fun/all_to_all | solution.py:398
  19.5 6.0 %branch_1_fun.3 = (f32[256,512]{1,0:T(8,128)}, f32[256,512]{1,0:T(8,128)}, f32[256,512]{1,0:T(8,128)}, f32[256,512]{1,0:T(8,128)}, f32[256,512]{1,0:T(8,128)}, /*index=5*/f32[256,512]{1,0:T(8,128)}) custom-call(s32[64,128]{1,0:T(8,128)S(1)} %get-tuple-element.16.table, s32[8,256]{1,0:T(8,128)S(1)} %get-tuple-element.17.place_ref, bf16[2048,1024]{1,0:T(8,128)(2,1)} %copy-done.1), custom_call_target="tpu_custom_call" | custom-call | flops 3087007744 | bytes 8388608 | tf_op jit(solution)/shard_map/cond/branch_1_fun/pallas_call | solution.py:306
  25.5 3.1 %all-to-all-done = f32[8,136,128]{2,1,0:T(8,128)S(1)} async-done(((f32[8,136,128]{2,1,0:T(8,128)}), f32[8,136,128]{2,1,0:T(8,128)S(1)}, u32[]{:S(2)}, u32[]{:S(2)}) %all-to-all-start) | async-done | bytes 557088 | tf_op jit(solution)/shard_map/cond/branch_1_fun/all_to_all | solution.py:398
  28.8 2.8 %collective-permute-start.2 = (f32[136,128]{1,0:T(8,128)S(1)}, f32[136,128]{1,0:T(8,128)S(1)}, u32[]{:S(2)}, u32[]{:S(2)}) collective-permute-start(f32[136,128]{1,0:T(8,128)S(1)} %get-tuple-element.57), channel_id=1, source_target_pairs={{0,16},{4,20},{8,24},{12,28},{16,0},{20,4},{24,8},{28,12},{1,17},{... | collective-permute-start | bytes 208904 | tf_op jit(solution)/shard_map/ppermute | solution.py:560
  32.3 1.4 %collective-permute-start.8 = (f32[256,512]{1,0:T(8,128)}, f32[256,512]{1,0:T(8,128)S(1)}, u32[]{:S(2)}, u32[]{:S(2)}) collective-permute-start(f32[256,512]{1,0:T(8,128)} %get-tuple-element.75), channel_id=1, source_target_pairs={{0,8},{4,12},{8,0},{12,4},{16,24},{20,28},{24,16},{28,20},{1,9},{5... | collective-permute-start | bytes 1572872 | tf_op jit(solution)/shard_map/ppermute | solution.py:560
  33.6 1.1 %collective-permute-done.4.rest_1_ = f32[256,512]{1,0:T(8,128)S(1)} collective-permute-done((f32[256,512]{1,0:T(8,128)}, f32[256,512]{1,0:T(8,128)S(1)}, u32[]{:S(2)}, u32[]{:S(2)}) %collective-permute-start.4) | collective-permute-done | bytes 524320 | tf_op jit(solution)/shard_map/ppermute | solution.py:560
  34.7 1.7 %collective-permute-done.3 = f32[136,128]{1,0:T(8,128)S(1)} collective-permute-done((f32[136,128]{1,0:T(8,128)S(1)}, f32[136,128]{1,0:T(8,128)S(1)}, u32[]{:S(2)}, u32[]{:S(2)}) %collective-permute-start.3) | collective-permute-done | bytes 69664 | tf_op jit(solution)/shard_map/ppermute | solution.py:560
  36.4 1.3 %collective-permute-done.2 = f32[136,128]{1,0:T(8,128)S(1)} collective-permute-done((f32[136,128]{1,0:T(8,128)S(1)}, f32[136,128]{1,0:T(8,128)S(1)}, u32[]{:S(2)}, u32[]{:S(2)}) %collective-permute-start.2) | collective-permute-done | bytes 69664 | tf_op jit(solution)/shard_map/ppermute | solution.py:560
  37.7 3.4 %collective-permute-start.6 = (f32[256,512]{1,0:T(8,128)}, f32[256,512]{1,0:T(8,128)S(1)}, u32[]{:S(2)}, u32[]{:S(2)}) collective-permute-start(f32[256,512]{1,0:T(8,128)} %get-tuple-element.68), channel_id=1, source_target_pairs={{0,20},{4,16},{8,28},{12,24},{16,4},{20,0},{24,12},{28,8},{1,21},{... | collective-permute-start | bytes 1572872 | tf_op jit(solution)/shard_map/ppermute | solution.py:560
  41.1 13.8 %conditional.3 = (f32[1088,128]{1,0:T(8,128)}) conditional(s32[]{:T(128)} %bitcast.3, () %tuple.29, f32[136,128]{1,0:T(8,128)S(1)} %add_add_fusion), branch_computations={%region_3.0_spmd, %region_4.0_spmd} | conditional | bytes 1740808 | solution.py:596
  41.2 13.7 %all_to_all.14 = f32[8,136,128]{2,1,0:T(8,128)} all-to-all(f32[8,136,128]{2,1,0:T(8,128)S(1)} %broadcast_in_dim.2), channel_id=1, replica_groups={{0,1,2,3,4,5,6,7},{8,9,10,11,12,13,14,15},{16,17,18,19,20,21,22,23},{24..., dimensions={0} | all-to-all | bytes 1114112 | tf_op jit(solution)/shard_map/cond/branch_1_fun/all_to_all | solution.py:406
  54.9 1.0 collective-permute-start.5
  55.9 26.9 %shard_map.70 = (f32[512,512]{1,0:T(8,128)}, bf16[512,512]{1,0:T(8,128)(2,1)S(1)}, bf16[512,512]{1,0:T(8,128)(2,1)S(1)}) custom-call(f32[1088,128]{1,0:T(8,128)} %get-tuple-element.96.sum_ref, f32[1088,128]{1,0:T(8,128)S(1)} %get-tuple-element.62.prior_ref), custom_call_target="tpu_custom_call" | custom-call | flops 1 | bytes 1 | tf_op jit(solution)/shard_map/pallas_call | solution.py:479
  82.8 4.1 %shard_map.71.rest_2_ = f32[2048,512]{1,0:T(8,128)} custom-call(s32[1]{0:T(128)} %bitcast.2.me_ref, bf16[512,512]{1,0:T(8,128)(2,1)S(1)} %get-tuple-element.63.high_ref, bf16[512,512]{1,0:T(8,128)(2,1)S(1)} %get-tuple-element.64.low_ref, f32[256,512]{1,0:T(8,128)} %get-tuple-element.71.rest_0_, f32[256,512]{1,0:T(8,128)S(1)} %collective-permute-done.4.rest_1_, ...), custom_call_target="tpu_custom_call" | custom-call | flops 1 | bytes 1 | tf_op jit(solution)/shard_map/pallas_call | solution.py:526
  86.9 7.0 %collective-permute-done.6.rest_0_ = f32[256,512]{1,0:T(8,128)S(1)} collective-permute-done((f32[256,512]{1,0:T(8,128)}, f32[256,512]{1,0:T(8,128)S(1)}, u32[]{:S(2)}, u32[]{:S(2)}) %collective-permute-start.6) | collective-permute-done | bytes 524320 | tf_op jit(solution)/shard_map/ppermute | solution.py:560
  94.0 1.8 %shard_map.72.rest_1_ = f32[2048,512]{1,0:T(8,128)} custom-call(s32[1]{0:T(128)} %bitcast.2.me_ref, bf16[512,512]{1,0:T(8,128)(2,1)S(1)} %get-tuple-element.63.high_ref, bf16[512,512]{1,0:T(8,128)(2,1)S(1)} %get-tuple-element.64.low_ref, f32[256,512]{1,0:T(8,128)S(1)} %collective-permute-done.6.rest_0_, ...), custom_call_target="tpu_custom_call", output_to_operand_aliasing={{}: (5, {})} | custom-call | flops 1 | bytes 1 | tf_op jit(solution)/shard_map/pallas_call | solution.py:526
  95.8 9.3 %collective-permute-done.5.rest_0_ = f32[256,512]{1,0:T(8,128)S(1)} collective-permute-done((f32[256,512]{1,0:T(8,128)}, f32[256,512]{1,0:T(8,128)S(1)}, u32[]{:S(2)}, u32[]{:S(2)}) %collective-permute-start.5) | collective-permute-done | bytes 524320 | tf_op jit(solution)/shard_map/ppermute | solution.py:560
  105.1 1.4 %shard_map.73 = f32[2048,512]{1,0:T(8,128)} custom-call(s32[1]{0:T(128)} %bitcast.2.me_ref, bf16[512,512]{1,0:T(8,128)(2,1)S(1)} %get-tuple-element.63.high_ref, bf16[512,512]{1,0:T(8,128)(2,1)S(1)} %get-tuple-element.64.low_ref, f32[256,512]{1,0:T(8,128)S(1)} %collective-permute-done.5.rest_0_, ...), custom_call_target="tpu_custom_call", output_to_operand_aliasing={{}: (4, {})} | custom-call | flops 1 | bytes 1 | tf_op jit(solution)/shard_map/pallas_call | solution.py:526
  (15 shorter events, 0.9 us)
Async XLA Ops:
  0.6 8.7 %copy-start = (f32[128]{0:T(128)S(1)}, f32[128]{0:T(128)}, u32[]{:S(2)}) copy-start(f32[128]{0:T(128)} %param.11) | copy-start | bytes 1540
  5.2 23.5 %collective-permute-start = (f32[256,512]{1,0:T(8,128)}, f32[256,512]{1,0:T(8,128)S(1)}, u32[]{:S(2)}, u32[]{:S(2)}) collective-permute-start(f32[256,512]{1,0:T(8,128)} %get-tuple-element.56), channel_id=1, source_target_pairs={{0,4},{4,0},{8,12},{12,8},{16,20},{20,16},{24,28},{28,24},{1,5},{5... | collective-permute-start | bytes 1572872 | tf_op jit(solution)/shard_map/ppermute | solution.py:560
  6.8 27.9 %collective-permute-start.4 = (f32[256,512]{1,0:T(8,128)}, f32[256,512]{1,0:T(8,128)S(1)}, u32[]{:S(2)}, u32[]{:S(2)}) collective-permute-start(f32[256,512]{1,0:T(8,128)} %get-tuple-element.58), channel_id=1, source_target_pairs={{0,16},{4,20},{8,24},{12,28},{16,0},{20,4},{24,8},{28,12},{1,17},{... | collective-permute-start | bytes 1572872 | tf_op jit(solution)/shard_map/ppermute | solution.py:560
  9.4 2.0 %copy-start.1 = (bf16[2048,1024]{1,0:T(8,128)(2,1)}, bf16[2048,1024]{1,0:T(8,128)(2,1)S(1)}, u32[]{:S(2)}) copy-start(bf16[2048,1024]{1,0:T(8,128)(2,1)S(1)} %get-tuple-element.13.pair_ref) | copy-start | bytes 12582916 | tf_op jit(solution)/shard_map/cond
  16.0 12.7 %all-to-all-start = ((f32[8,136,128]{2,1,0:T(8,128)}), f32[8,136,128]{2,1,0:T(8,128)S(1)}, u32[]{:S(2)}, u32[]{:S(2)}) async-start(f32[8,136,128]{2,1,0:T(8,128)} %bitcast), calls=%async_computation | async-start | bytes 1114112 | tf_op jit(solution)/shard_map/cond/branch_1_fun/all_to_all | solution.py:398
  28.7 7.7 %collective-permute-start.3 = (f32[136,128]{1,0:T(8,128)S(1)}, f32[136,128]{1,0:T(8,128)S(1)}, u32[]{:S(2)}, u32[]{:S(2)}) collective-permute-start(f32[136,128]{1,0:T(8,128)S(1)} %get-tuple-element.57), channel_id=1, source_target_pairs={{0,24},{4,28},{8,16},{12,20},{16,8},{20,12},{24,0},{28,4},{1,25},{... | collective-permute-start | bytes 208904 | tf_op jit(solution)/shard_map/ppermute | solution.py:560
  28.8 8.9 %collective-permute-start.2 = (f32[136,128]{1,0:T(8,128)S(1)}, f32[136,128]{1,0:T(8,128)S(1)}, u32[]{:S(2)}, u32[]{:S(2)}) collective-permute-start(f32[136,128]{1,0:T(8,128)S(1)} %get-tuple-element.57), channel_id=1, source_target_pairs={{0,16},{4,20},{8,24},{12,28},{16,0},{20,4},{24,8},{28,12},{1,17},{... | collective-permute-start | bytes 208904 | tf_op jit(solution)/shard_map/ppermute | solution.py:560
  31.6 6.1 %collective-permute-start.1 = (f32[136,128]{1,0:T(8,128)S(1)}, f32[136,128]{1,0:T(8,128)S(1)}, u32[]{:S(2)}, u32[]{:S(2)}) collective-permute-start(f32[136,128]{1,0:T(8,128)S(1)} %get-tuple-element.57), channel_id=1, source_target_pairs={{0,8},{4,12},{8,0},{12,4},{16,24},{20,28},{24,16},{28,20},{1,9},{5... | collective-permute-start | bytes 208904 | tf_op jit(solution)/shard_map/ppermute | solution.py:560
  32.3 50.6 %collective-permute-start.8 = (f32[256,512]{1,0:T(8,128)}, f32[256,512]{1,0:T(8,128)S(1)}, u32[]{:S(2)}, u32[]{:S(2)}) collective-permute-start(f32[256,512]{1,0:T(8,128)} %get-tuple-element.75), channel_id=1, source_target_pairs={{0,8},{4,12},{8,0},{12,4},{16,24},{20,28},{24,16},{28,20},{1,9},{5... | collective-permute-start | bytes 1572872 | tf_op jit(solution)/shard_map/ppermute | solution.py:560
  34.7 48.1 %collective-permute-start.9 = (f32[256,512]{1,0:T(8,128)}, f32[256,512]{1,0:T(8,128)S(1)}, u32[]{:S(2)}, u32[]{:S(2)}) collective-permute-start(f32[256,512]{1,0:T(8,128)} %get-tuple-element.76), channel_id=1, source_target_pairs={{0,24},{4,28},{8,16},{12,20},{16,8},{20,12},{24,0},{28,4},{1,25},{... | collective-permute-start | bytes 1572872 | tf_op jit(solution)/shard_map/ppermute | solution.py:560
  37.7 56.3 %collective-permute-start.6 = (f32[256,512]{1,0:T(8,128)}, f32[256,512]{1,0:T(8,128)S(1)}, u32[]{:S(2)}, u32[]{:S(2)}) collective-permute-start(f32[256,512]{1,0:T(8,128)} %get-tuple-element.68), channel_id=1, source_target_pairs={{0,20},{4,16},{8,28},{12,24},{16,4},{20,0},{24,12},{28,8},{1,21},{... | collective-permute-start | bytes 1572872 | tf_op jit(solution)/shard_map/ppermute | solution.py:560
  54.9 39.1 %collective-permute-start.7 = (f32[256,512]{1,0:T(8,128)}, f32[256,512]{1,0:T(8,128)S(1)}, u32[]{:S(2)}, u32[]{:S(2)}) collective-permute-start(f32[256,512]{1,0:T(8,128)} %get-tuple-element.70), channel_id=1, source_target_pairs={{0,12},{4,8},{8,4},{12,0},{16,28},{20,24},{24,20},{28,16},{1,13},{... | collective-permute-start | bytes 1572872 | tf_op jit(solution)/shard_map/ppermute | solution.py:560
  54.9 50.2 %collective-permute-start.5 = (f32[256,512]{1,0:T(8,128)}, f32[256,512]{1,0:T(8,128)S(1)}, u32[]{:S(2)}, u32[]{:S(2)}) collective-permute-start(f32[256,512]{1,0:T(8,128)} %get-tuple-element.66), channel_id=1, source_target_pairs={{0,28},{4,24},{8,20},{12,16},{16,12},{20,8},{24,4},{28,0},{1,29},{... | collective-permute-start | bytes 1572872 | tf_op jit(solution)/shard_map/ppermute | solution.py:560

commit v17 on v16

--- a/solution.py
+++ b/solution.py
@@ -562,7 +562,7 @@
     plane = 2 * grp
     packed_rows = packed_rows_of(state, plane)
     planes = [list(range(i, i + plane)) for i in range(0, groups * grp, plane)]
-    middle = [k for k in (2, 6) if k < groups]
+    middle = [k for k in (6, 2) if k < groups]
     late = [k for k in (5, 3, *range(7, groups)) if k < groups]
     valid = sensor_sigma[0] > 0
     nothing = lambda rows: jnp.full((rows, LANES), jnp.nan, F32)

time: 108 us -> 117 us (1.083)
  the two profiles are of different devices: /device:TPU:8 before, /device:TPU:0 now
where the time goes in v17:
time: 117 us; the launch traced here: 116 us
  Pallas kernels  49.3 us (42%)
  starting transfers between devices  33 us (28%)
  waiting for transfers between devices  16.6 us (14%)
  blocking collectives  14.3 us (12%)
  local copies, waits for them, and re-layouts  2.05 us (2%)
    ppermute x10, starting transfers between devices, shards(): lax.ppermute(chunk, 'rows', [(i, i ^ k) for i in range(groups)])  29.4 us
    pallas_call x1, Pallas kernels, factorise(): pl.pallas_call(functools.partial(factor_kernel, 1.0 / total_rows), in_spe...  26.9 us
    all_to_all x1, blocking collectives, gather_pieces(): lax.all_to_all(copies, axes, split_axis=0, concat_axis=0, axis_index_grou...  14.3 us
    ppermute x10, waiting for transfers between devices, shards(): lax.ppermute(chunk, 'rows', [(i, i ^ k) for i in range(groups)])  13.5 us
    pallas_call x3, Pallas kernels, whiten(): pl.pallas_call(functools.partial(whiten_kernel, steps, len(extra), per_bu...  7.29 us
    pallas_call x1, Pallas kernels, regroup_rest(): pl.pallas_call(functools.partial(rest_kernel, groups, per_bucket, tuple(o...  5.98 us
    pallas_call x1, Pallas kernels, gram(): pl.pallas_call(gram_kernel, in_specs=[vmem] * 2, out_specs=[vmem] * 2, ou...  4.56 us
    pallas_call x1, Pallas kernels, regroup_lead(): pl.pallas_call(functools.partial(lead_kernel, groups, per_bucket, tuple(l...  4.55 us
  transfers between devices with their start and end apart: 11, of which 3 were waited for; matrix products, arithmetic and copies ran while one was open for 0% of the time, Pallas kernels for 37%

profile of v17, /device:TPU:0, one launch (start us, length us, event | category | flops | bytes accessed | tf_op | source)
XLA Modules:
  0.0 116.2 jit_solution(14946761117779931349)
XLA Ops:
  0.6 4.6 %shard_map.69 = (f32[256,512]{1,0:T(8,128)}, f32[256,512]{1,0:T(8,128)}, bf16[2048,1024]{1,0:T(8,128)(2,1)S(1)}, s32[8,256]{1,0:T(8,128)S(1)}, s32[64,128]{1,0:T(8,128)S(1)}) custom-call(s32[1]{0:T(128)} %bitcast.2.me_ref, s32[16,128]{1,0:T(8,128)} %bitcast.9, s32[16,128]{1,0:T(8,128)} %bitcast.10, f32[1,128]{1,0:T(1,128)} %bitcast.11, f32[2048,512]{1,0:T(8,128)} %refs_3_.1), custom_call_target="tpu_custom_call" | custom-call | flops 1048576 | bytes 8388608 | tf_op jit(solution)/shard_map/pallas_call | solution.py:264
  5.2 3.0 %collective-permute-start = (f32[256,512]{1,0:T(8,128)}, f32[256,512]{1,0:T(8,128)S(1)}, u32[]{:S(2)}, u32[]{:S(2)}) collective-permute-start(f32[256,512]{1,0:T(8,128)} %get-tuple-element.56), channel_id=1, source_target_pairs={{0,4},{4,0},{8,12},{12,8},{16,20},{20,16},{24,28},{28,24},{1,5},{5... | collective-permute-start | bytes 1572872 | tf_op jit(solution)/shard_map/ppermute | solution.py:560
  8.2 2.6 %collective-permute-start.4 = (f32[256,512]{1,0:T(8,128)}, f32[256,512]{1,0:T(8,128)S(1)}, u32[]{:S(2)}, u32[]{:S(2)}) collective-permute-start(f32[256,512]{1,0:T(8,128)} %get-tuple-element.58), channel_id=1, source_target_pairs={{0,16},{4,20},{8,24},{12,28},{16,0},{20,4},{24,8},{28,12},{1,17},{... | collective-permute-start | bytes 1572872 | tf_op jit(solution)/shard_map/ppermute | solution.py:560
  10.9 19.3 %conditional.2 = (f32[136,128]{1,0:T(8,128)S(1)}, f32[1088,128]{1,0:T(8,128)S(1)}, f32[256,512]{1,0:T(8,128)}, f32[256,512]{1,0:T(8,128)}, f32[256,512]{1,0:T(8,...) conditional(s32[]{:T(128)} %bitcast.3, () %tuple.30, (f32[512,512]{1,0:T(8,128)}, ...), branch_computations={%region_0.0_spmd, %region_1.0_spmd} | conditional | flops 5234613248 | bytes 31658112 | solution.py:578
  10.9 2.0 %copy-done.1 = bf16[2048,1024]{1,0:T(8,128)(2,1)} copy-done((bf16[2048,1024]{1,0:T(8,128)(2,1)}, bf16[2048,1024]{1,0:T(8,128)(2,1)S(1)}, u32[]{:S(2)}) %copy-start.1) | copy-done | bytes 4194328 | tf_op jit(solution)/shard_map/cond
  12.9 4.6 %branch_1_fun.2 = (f32[1088,128]{1,0:T(8,128)}, f32[1088,128]{1,0:T(8,128)S(1)}) custom-call(f32[512,512]{1,0:T(8,128)} %get-tuple-element.79.prior_ref, bf16[2048,1024]{1,0:T(8,128)(2,1)S(1)} %get-tuple-element.13.pair_ref), custom_call_target="tpu_custom_call" | custom-call | flops 2147483648 | bytes 4194304 | tf_op jit(solution)/shard_map/cond/branch_1_fun/pallas_call | solution.py:382
  17.4 3.5 %all-to-all-start = ((f32[8,136,128]{2,1,0:T(8,128)}), f32[8,136,128]{2,1,0:T(8,128)S(1)}, u32[]{:S(2)}, u32[]{:S(2)}) async-start(f32[8,136,128]{2,1,0:T(8,128)} %bitcast), calls=%async_computation | async-start | bytes 1114112 | tf_op jit(solution)/shard_map/cond/branch_1_fun/all_to_all | solution.py:398
  21.0 6.0 %branch_1_fun.3 = (f32[256,512]{1,0:T(8,128)}, f32[256,512]{1,0:T(8,128)}, f32[256,512]{1,0:T(8,128)}, f32[256,512]{1,0:T(8,128)}, f32[256,512]{1,0:T(8,128)}, /*index=5*/f32[256,512]{1,0:T(8,128)}) custom-call(s32[64,128]{1,0:T(8,128)S(1)} %get-tuple-element.16.table, s32[8,256]{1,0:T(8,128)S(1)} %get-tuple-element.17.place_ref, bf16[2048,1024]{1,0:T(8,128)(2,1)} %copy-done.1), custom_call_target="tpu_custom_call" | custom-call | flops 3087007744 | bytes 8388608 | tf_op jit(solution)/shard_map/cond/branch_1_fun/pallas_call | solution.py:306
  27.0 3.1 %all-to-all-done = f32[8,136,128]{2,1,0:T(8,128)S(1)} async-done(((f32[8,136,128]{2,1,0:T(8,128)}), f32[8,136,128]{2,1,0:T(8,128)S(1)}, u32[]{:S(2)}, u32[]{:S(2)}) %all-to-all-start) | async-done | bytes 557088 | tf_op jit(solution)/shard_map/cond/branch_1_fun/all_to_all | solution.py:398
  30.1 1.4 %collective-permute-start.3 = (f32[136,128]{1,0:T(8,128)S(1)}, f32[136,128]{1,0:T(8,128)S(1)}, u32[]{:S(2)}, u32[]{:S(2)}) collective-permute-start(f32[136,128]{1,0:T(8,128)S(1)} %get-tuple-element.57), channel_id=1, source_target_pairs={{0,24},{4,28},{8,16},{12,20},{16,8},{20,12},{24,0},{28,4},{1,25},{... | collective-permute-start | bytes 208904 | tf_op jit(solution)/shard_map/ppermute | solution.py:560
  31.6 1.7 %collective-permute-start.2 = (f32[136,128]{1,0:T(8,128)S(1)}, f32[136,128]{1,0:T(8,128)S(1)}, u32[]{:S(2)}, u32[]{:S(2)}) collective-permute-start(f32[136,128]{1,0:T(8,128)S(1)} %get-tuple-element.57), channel_id=1, source_target_pairs={{0,16},{4,20},{8,24},{12,28},{16,0},{20,4},{24,8},{28,12},{1,17},{... | collective-permute-start | bytes 208904 | tf_op jit(solution)/shard_map/ppermute | solution.py:560
  33.2 1.4 %collective-permute-start.1 = (f32[136,128]{1,0:T(8,128)S(1)}, f32[136,128]{1,0:T(8,128)S(1)}, u32[]{:S(2)}, u32[]{:S(2)}) collective-permute-start(f32[136,128]{1,0:T(8,128)S(1)} %get-tuple-element.57), channel_id=1, source_target_pairs={{0,8},{4,12},{8,0},{12,4},{16,24},{20,28},{24,16},{28,20},{1,9},{5... | collective-permute-start | bytes 208904 | tf_op jit(solution)/shard_map/ppermute | solution.py:560
  34.6 1.3 %collective-permute-start.8 = (f32[256,512]{1,0:T(8,128)}, f32[256,512]{1,0:T(8,128)S(1)}, u32[]{:S(2)}, u32[]{:S(2)}) collective-permute-start(f32[256,512]{1,0:T(8,128)} %get-tuple-element.75), channel_id=1, source_target_pairs={{0,24},{4,28},{8,16},{12,20},{16,8},{20,12},{24,0},{28,4},{1,25},{... | collective-permute-start | bytes 1572872 | tf_op jit(solution)/shard_map/ppermute | solution.py:560
  36.1 2.2 %collective-permute-start.9 = (f32[256,512]{1,0:T(8,128)}, f32[256,512]{1,0:T(8,128)S(1)}, u32[]{:S(2)}, u32[]{:S(2)}) collective-permute-start(f32[256,512]{1,0:T(8,128)} %get-tuple-element.76), channel_id=1, source_target_pairs={{0,8},{4,12},{8,0},{12,4},{16,24},{20,28},{24,16},{28,20},{1,9},{5... | collective-permute-start | bytes 1572872 | tf_op jit(solution)/shard_map/ppermute | solution.py:560
  38.2 13.3 %collective-permute-done.2 = f32[136,128]{1,0:T(8,128)S(1)} collective-permute-done((f32[136,128]{1,0:T(8,128)S(1)}, f32[136,128]{1,0:T(8,128)S(1)}, u32[]{:S(2)}, u32[]{:S(2)}) %collective-permute-start.2) | collective-permute-done | bytes 69664 | tf_op jit(solution)/shard_map/ppermute | solution.py:560
  51.6 0.2 collective-permute-start.6
  51.8 14.4 %conditional.3 = (f32[1088,128]{1,0:T(8,128)}) conditional(s32[]{:T(128)} %bitcast.3, () %tuple.29, f32[136,128]{1,0:T(8,128)S(1)} %add_add_fusion), branch_computations={%region_3.0_spmd, %region_4.0_spmd} | conditional | bytes 1740808 | solution.py:596
  51.8 14.3 %all_to_all.14 = f32[8,136,128]{2,1,0:T(8,128)} all-to-all(f32[8,136,128]{2,1,0:T(8,128)S(1)} %broadcast_in_dim.2), channel_id=1, replica_groups={{0,1,2,3,4,5,6,7},{8,9,10,11,12,13,14,15},{16,17,18,19,20,21,22,23},{24..., dimensions={0} | all-to-all | bytes 1114112 | tf_op jit(solution)/shard_map/cond/branch_1_fun/all_to_all | solution.py:406
  66.2 13.6 %collective-permute-start.7 = (f32[256,512]{1,0:T(8,128)}, f32[256,512]{1,0:T(8,128)S(1)}, u32[]{:S(2)}, u32[]{:S(2)}) collective-permute-start(f32[256,512]{1,0:T(8,128)} %get-tuple-element.70), channel_id=1, source_target_pairs={{0,12},{4,8},{8,4},{12,0},{16,28},{20,24},{24,20},{28,16},{1,13},{... | collective-permute-start | bytes 1572872 | tf_op jit(solution)/shard_map/ppermute | solution.py:560
  79.8 2.0 %collective-permute-start.5 = (f32[256,512]{1,0:T(8,128)}, f32[256,512]{1,0:T(8,128)S(1)}, u32[]{:S(2)}, u32[]{:S(2)}) collective-permute-start(f32[256,512]{1,0:T(8,128)} %get-tuple-element.66), channel_id=1, source_target_pairs={{0,28},{4,24},{8,20},{12,16},{16,12},{20,8},{24,4},{28,0},{1,29},{... | collective-permute-start | bytes 1572872 | tf_op jit(solution)/shard_map/ppermute | solution.py:560
  81.8 26.9 %shard_map.70 = (f32[512,512]{1,0:T(8,128)}, bf16[512,512]{1,0:T(8,128)(2,1)S(1)}, bf16[512,512]{1,0:T(8,128)(2,1)S(1)}) custom-call(f32[1088,128]{1,0:T(8,128)} %get-tuple-element.96.sum_ref, f32[1088,128]{1,0:T(8,128)S(1)} %get-tuple-element.62.prior_ref), custom_call_target="tpu_custom_call" | custom-call | flops 1 | bytes 1 | tf_op jit(solution)/shard_map/pallas_call | solution.py:479
  108.8 4.1 %shard_map.71.rest_2_ = f32[2048,512]{1,0:T(8,128)} custom-call(s32[1]{0:T(128)} %bitcast.2.me_ref, bf16[512,512]{1,0:T(8,128)(2,1)S(1)} %get-tuple-element.63.high_ref, bf16[512,512]{1,0:T(8,128)(2,1)S(1)} %get-tuple-element.64.low_ref, f32[256,512]{1,0:T(8,128)} %get-tuple-element.71.rest_0_, f32[256,512]{1,0:T(8,128)S(1)} %collective-permute-done.4.rest_1_, ...), custom_call_target="tpu_custom_call" | custom-call | flops 1 | bytes 1 | tf_op jit(solution)/shard_map/pallas_call | solution.py:526
  112.9 1.8 %shard_map.72.rest_1_ = f32[2048,512]{1,0:T(8,128)} custom-call(s32[1]{0:T(128)} %bitcast.2.me_ref, bf16[512,512]{1,0:T(8,128)(2,1)S(1)} %get-tuple-element.63.high_ref, bf16[512,512]{1,0:T(8,128)(2,1)S(1)} %get-tuple-element.64.low_ref, f32[256,512]{1,0:T(8,128)S(1)} %collective-permute-done.6.rest_0_, ...), custom_call_target="tpu_custom_call", output_to_operand_aliasing={{}: (5, {})} | custom-call | flops 1 | bytes 1 | tf_op jit(solution)/shard_map/pallas_call | solution.py:526
  114.7 1.4 %shard_map.73 = f32[2048,512]{1,0:T(8,128)} custom-call(s32[1]{0:T(128)} %bitcast.2.me_ref, bf16[512,512]{1,0:T(8,128)(2,1)S(1)} %get-tuple-element.63.high_ref, bf16[512,512]{1,0:T(8,128)(2,1)S(1)} %get-tuple-element.64.low_ref, f32[256,512]{1,0:T(8,128)S(1)} %collective-permute-done.5.rest_0_, ...), custom_call_target="tpu_custom_call", output_to_operand_aliasing={{}: (4, {})} | custom-call | flops 1 | bytes 1 | tf_op jit(solution)/shard_map/pallas_call | solution.py:526
  (15 shorter events, 0.2 us)
Async XLA Ops:
  0.6 10.2 %copy-start = (f32[128]{0:T(128)S(1)}, f32[128]{0:T(128)}, u32[]{:S(2)}) copy-start(f32[128]{0:T(128)} %param.11) | copy-start | bytes 1540
  5.2 24.9 %collective-permute-start = (f32[256,512]{1,0:T(8,128)}, f32[256,512]{1,0:T(8,128)S(1)}, u32[]{:S(2)}, u32[]{:S(2)}) collective-permute-start(f32[256,512]{1,0:T(8,128)} %get-tuple-element.56), channel_id=1, source_target_pairs={{0,4},{4,0},{8,12},{12,8},{16,20},{20,16},{24,28},{28,24},{1,5},{5... | collective-permute-start | bytes 1572872 | tf_op jit(solution)/shard_map/ppermute | solution.py:560
  8.2 27.9 %collective-permute-start.4 = (f32[256,512]{1,0:T(8,128)}, f32[256,512]{1,0:T(8,128)S(1)}, u32[]{:S(2)}, u32[]{:S(2)}) collective-permute-start(f32[256,512]{1,0:T(8,128)} %get-tuple-element.58), channel_id=1, source_target_pairs={{0,16},{4,20},{8,24},{12,28},{16,0},{20,4},{24,8},{28,12},{1,17},{... | collective-permute-start | bytes 1572872 | tf_op jit(solution)/shard_map/ppermute | solution.py:560
  10.9 2.0 %copy-start.1 = (bf16[2048,1024]{1,0:T(8,128)(2,1)}, bf16[2048,1024]{1,0:T(8,128)(2,1)S(1)}, u32[]{:S(2)}) copy-start(bf16[2048,1024]{1,0:T(8,128)(2,1)S(1)} %get-tuple-element.13.pair_ref) | copy-start | bytes 12582916 | tf_op jit(solution)/shard_map/cond
  17.4 12.7 %all-to-all-start = ((f32[8,136,128]{2,1,0:T(8,128)}), f32[8,136,128]{2,1,0:T(8,128)S(1)}, u32[]{:S(2)}, u32[]{:S(2)}) async-start(f32[8,136,128]{2,1,0:T(8,128)} %bitcast), calls=%async_computation | async-start | bytes 1114112 | tf_op jit(solution)/shard_map/cond/branch_1_fun/all_to_all | solution.py:398
  30.1 8.1 %collective-permute-start.3 = (f32[136,128]{1,0:T(8,128)S(1)}, f32[136,128]{1,0:T(8,128)S(1)}, u32[]{:S(2)}, u32[]{:S(2)}) collective-permute-start(f32[136,128]{1,0:T(8,128)S(1)} %get-tuple-element.57), channel_id=1, source_target_pairs={{0,24},{4,28},{8,16},{12,20},{16,8},{20,12},{24,0},{28,4},{1,25},{... | collective-permute-start | bytes 208904 | tf_op jit(solution)/shard_map/ppermute | solution.py:560
  31.6 20.0 %collective-permute-start.2 = (f32[136,128]{1,0:T(8,128)S(1)}, f32[136,128]{1,0:T(8,128)S(1)}, u32[]{:S(2)}, u32[]{:S(2)}) collective-permute-start(f32[136,128]{1,0:T(8,128)S(1)} %get-tuple-element.57), channel_id=1, source_target_pairs={{0,16},{4,20},{8,24},{12,28},{16,0},{20,4},{24,8},{28,12},{1,17},{... | collective-permute-start | bytes 208904 | tf_op jit(solution)/shard_map/ppermute | solution.py:560
  33.2 18.3 %collective-permute-start.1 = (f32[136,128]{1,0:T(8,128)S(1)}, f32[136,128]{1,0:T(8,128)S(1)}, u32[]{:S(2)}, u32[]{:S(2)}) collective-permute-start(f32[136,128]{1,0:T(8,128)S(1)} %get-tuple-element.57), channel_id=1, source_target_pairs={{0,8},{4,12},{8,0},{12,4},{16,24},{20,28},{24,16},{28,20},{1,9},{5... | collective-permute-start | bytes 208904 | tf_op jit(solution)/shard_map/ppermute | solution.py:560
  34.6 74.1 %collective-permute-start.8 = (f32[256,512]{1,0:T(8,128)}, f32[256,512]{1,0:T(8,128)S(1)}, u32[]{:S(2)}, u32[]{:S(2)}) collective-permute-start(f32[256,512]{1,0:T(8,128)} %get-tuple-element.75), channel_id=1, source_target_pairs={{0,24},{4,28},{8,16},{12,20},{16,8},{20,12},{24,0},{28,4},{1,25},{... | collective-permute-start | bytes 1572872 | tf_op jit(solution)/shard_map/ppermute | solution.py:560
  36.1 72.7 %collective-permute-start.9 = (f32[256,512]{1,0:T(8,128)}, f32[256,512]{1,0:T(8,128)S(1)}, u32[]{:S(2)}, u32[]{:S(2)}) collective-permute-start(f32[256,512]{1,0:T(8,128)} %get-tuple-element.76), channel_id=1, source_target_pairs={{0,8},{4,12},{8,0},{12,4},{16,24},{20,28},{24,16},{28,20},{1,9},{5... | collective-permute-start | bytes 1572872 | tf_op jit(solution)/shard_map/ppermute | solution.py:560
  51.6 61.3 %collective-permute-start.6 = (f32[256,512]{1,0:T(8,128)}, f32[256,512]{1,0:T(8,128)S(1)}, u32[]{:S(2)}, u32[]{:S(2)}) collective-permute-start(f32[256,512]{1,0:T(8,128)} %get-tuple-element.68), channel_id=1, source_target_pairs={{0,20},{4,16},{8,28},{12,24},{16,4},{20,0},{24,12},{28,8},{1,21},{... | collective-permute-start | bytes 1572872 | tf_op jit(solution)/shard_map/ppermute | solution.py:560
  66.2 46.7 %collective-permute-start.7 = (f32[256,512]{1,0:T(8,128)}, f32[256,512]{1,0:T(8,128)S(1)}, u32[]{:S(2)}, u32[]{:S(2)}) collective-permute-start(f32[256,512]{1,0:T(8,128)} %get-tuple-element.70), channel_id=1, source_target_pairs={{0,12},{4,8},{8,4},{12,0},{16,28},{20,24},{24,20},{28,16},{1,13},{... | collective-permute-start | bytes 1572872 | tf_op jit(solution)/shard_map/ppermute | solution.py:560
  79.8 34.9 %collective-permute-start.5 = (f32[256,512]{1,0:T(8,128)}, f32[256,512]{1,0:T(8,128)S(1)}, u32[]{:S(2)}, u32[]{:S(2)}) collective-permute-start(f32[256,512]{1,0:T(8,128)} %get-tuple-element.66), channel_id=1, source_target_pairs={{0,28},{4,24},{8,20},{12,16},{16,12},{20,8},{24,4},{28,0},{1,29},{... | collective-permute-start | bytes 1572872 | tf_op jit(solution)/shard_map/ppermute | solution.py:560

commit v18 on v16

--- a/solution.py
+++ b/solution.py
@@ -158,7 +158,7 @@
     scales.append(jnp.zeros((-len(scales) % LANES, LANES), F32))
     turned = jnp.transpose(jnp.concatenate(scales, axis=0))
     for s in range(blocks):
-        if s == blocks // 2:
+        if s == blocks // 4:
             meta_ref[...] = meta
             copy.start()
             place_ref[...] = places
@@ -498,19 +498,22 @@
     chunks = rest[:count]
     out_ref, held, sems = rest[count + aliased :]
     high, low = high_ref[...], low_ref[...]
+    pieces = 2 if count == 1 else 1
     copies = []
     for n, (k, offset) in enumerate(steps):
-        rows = chunks[n].shape[0]
-        rows_high, rows_low = split(chunks[n][...])
-        held[n, :rows] = dot(rows_high, high) + (dot(rows_high, low) + dot(rows_low, high))
-        first = pl.multiple_of((me_ref[0] ^ k) * per_bucket, per_bucket) + offset
-        copy = pltpu.make_async_copy(
-            held.at[n, pl.ds(0, rows)],
-            out_ref.at[pl.ds(pl.multiple_of(first, SUB), rows), :],
-            sems.at[n],
-        )
-        copy.start()
-        copies.append(copy)
+        rows = chunks[n].shape[0] // pieces
+        for i in range(pieces):
+            rows_high, rows_low = split(chunks[n][i * rows : (i + 1) * rows, :])
+            product = dot(rows_high, high) + (dot(rows_high, low) + dot(rows_low, high))
+            held[n, i * rows : (i + 1) * rows] = product
+            first = pl.multiple_of((me_ref[0] ^ k) * per_bucket, per_bucket) + offset + i * rows
+            copy = pltpu.make_async_copy(
+                held.at[n, pl.ds(i * rows, rows)],
+                out_ref.at[pl.ds(pl.multiple_of(first, SUB), rows), :],
+                sems.at[n * pieces + i],
+            )
+            copy.start()
+            copies.append(copy)
     for copy in copies:
         copy.wait()
 
@@ -532,7 +535,7 @@
         out_shape=jax.ShapeDtypeStruct((rows, state), F32),
         scratch_shapes=[
             pltpu.VMEM((count, per_bucket, state), F32),
-            pltpu.SemaphoreType.DMA((count,)),
+            pltpu.SemaphoreType.DMA((count + 1,)),
         ],
         input_output_aliases={3 + count: 0} if extra else {},
         compiler_params=pltpu.CompilerParams(vmem_limit_bytes=16 * MIB),

time: 108 us -> 108 us (level)
  no operation moved by 1% of the time
where the time goes in v18:
time: 108 us; the launch traced here: 106 us
  Pallas kernels  49 us (45%)
  waiting for transfers between devices  23.6 us (22%)
  starting transfers between devices  17 us (16%)
  blocking collectives  13.7 us (13%)
  local copies, waits for them, and re-layouts  2.05 us (2%)
    pallas_call x1, Pallas kernels, factorise(): pl.pallas_call(functools.partial(factor_kernel, 1.0 / total_rows), in_spe...  26.9 us
    ppermute x10, waiting for transfers between devices, shards(): lax.ppermute(chunk, 'rows', [(i, i ^ k) for i in range(groups)])  20.4 us
    all_to_all x1, blocking collectives, gather_pieces(): lax.all_to_all(copies, axes, split_axis=0, concat_axis=0, axis_index_grou...  13.7 us
    ppermute x10, starting transfers between devices, shards(): lax.ppermute(chunk, 'rows', [(i, i ^ k) for i in range(groups)])  13.5 us
    pallas_call x3, Pallas kernels, whiten(): pl.pallas_call(functools.partial(whiten_kernel, steps, len(extra), per_bu...  7.22 us
    pallas_call x1, Pallas kernels, regroup_rest(): pl.pallas_call(functools.partial(rest_kernel, groups, per_bucket, tuple(o...  5.98 us
    pallas_call x1, Pallas kernels, gram(): pl.pallas_call(gram_kernel, in_specs=[vmem] * 2, out_specs=[vmem] * 2, ou...  4.56 us
    pallas_call x1, Pallas kernels, regroup_lead(): pl.pallas_call(functools.partial(lead_kernel, groups, per_bucket, tuple(l...  4.34 us
  transfers between devices with their start and end apart: 11, of which 6 were waited for; matrix products, arithmetic and copies ran while one was open for 0% of the time, Pallas kernels for 41%

profile of v18, /device:TPU:8, one launch (start us, length us, event | category | flops | bytes accessed | tf_op | source)
XLA Modules:
  0.0 106.4 jit_solution(17288954724555763199)
XLA Ops:
  0.6 4.3 %shard_map.69 = (f32[256,512]{1,0:T(8,128)}, f32[256,512]{1,0:T(8,128)}, bf16[2048,1024]{1,0:T(8,128)(2,1)S(1)}, s32[8,256]{1,0:T(8,128)S(1)}, s32[64,128]{1,0:T(8,128)S(1)}) custom-call(s32[1]{0:T(128)} %bitcast.2.me_ref, s32[16,128]{1,0:T(8,128)} %bitcast.9, s32[16,128]{1,0:T(8,128)} %bitcast.10, f32[1,128]{1,0:T(1,128)} %bitcast.11, f32[2048,512]{1,0:T(8,128)} %refs_3_.1), custom_call_target="tpu_custom_call" | custom-call | flops 1048576 | bytes 8388608 | tf_op jit(solution)/shard_map/pallas_call | solution.py:264
  5.0 1.6 %collective-permute-start = (f32[256,512]{1,0:T(8,128)}, f32[256,512]{1,0:T(8,128)S(1)}, u32[]{:S(2)}, u32[]{:S(2)}) collective-permute-start(f32[256,512]{1,0:T(8,128)} %get-tuple-element.56), channel_id=1, source_target_pairs={{0,4},{4,0},{8,12},{12,8},{16,20},{20,16},{24,28},{28,24},{1,5},{5... | collective-permute-start | bytes 1572872 | tf_op jit(solution)/shard_map/ppermute | solution.py:563
  6.5 2.6 %collective-permute-start.4 = (f32[256,512]{1,0:T(8,128)}, f32[256,512]{1,0:T(8,128)S(1)}, u32[]{:S(2)}, u32[]{:S(2)}) collective-permute-start(f32[256,512]{1,0:T(8,128)} %get-tuple-element.58), channel_id=1, source_target_pairs={{0,16},{4,20},{8,24},{12,28},{16,0},{20,4},{24,8},{28,12},{1,17},{... | collective-permute-start | bytes 1572872 | tf_op jit(solution)/shard_map/ppermute | solution.py:563
  9.2 19.3 %conditional.2 = (f32[136,128]{1,0:T(8,128)S(1)}, f32[1088,128]{1,0:T(8,128)S(1)}, f32[256,512]{1,0:T(8,128)}, f32[256,512]{1,0:T(8,128)}, f32[256,512]{1,0:T(8,...) conditional(s32[]{:T(128)} %bitcast.3, () %tuple.30, (f32[512,512]{1,0:T(8,128)}, ...), branch_computations={%region_0.0_spmd, %region_1.0_spmd} | conditional | flops 5234613248 | bytes 31658112 | solution.py:581
  9.2 2.0 %copy-done.1 = bf16[2048,1024]{1,0:T(8,128)(2,1)} copy-done((bf16[2048,1024]{1,0:T(8,128)(2,1)}, bf16[2048,1024]{1,0:T(8,128)(2,1)S(1)}, u32[]{:S(2)}) %copy-start.1) | copy-done | bytes 4194328 | tf_op jit(solution)/shard_map/cond
  11.2 4.6 %branch_1_fun.2 = (f32[1088,128]{1,0:T(8,128)}, f32[1088,128]{1,0:T(8,128)S(1)}) custom-call(f32[512,512]{1,0:T(8,128)} %get-tuple-element.79.prior_ref, bf16[2048,1024]{1,0:T(8,128)(2,1)S(1)} %get-tuple-element.13.pair_ref), custom_call_target="tpu_custom_call" | custom-call | flops 2147483648 | bytes 4194304 | tf_op jit(solution)/shard_map/cond/branch_1_fun/pallas_call | solution.py:382
  15.8 3.5 %all-to-all-start = ((f32[8,136,128]{2,1,0:T(8,128)}), f32[8,136,128]{2,1,0:T(8,128)S(1)}, u32[]{:S(2)}, u32[]{:S(2)}) async-start(f32[8,136,128]{2,1,0:T(8,128)} %bitcast), calls=%async_computation | async-start | bytes 1114112 | tf_op jit(solution)/shard_map/cond/branch_1_fun/all_to_all | solution.py:398
  19.3 6.0 %branch_1_fun.3 = (f32[256,512]{1,0:T(8,128)}, f32[256,512]{1,0:T(8,128)}, f32[256,512]{1,0:T(8,128)}, f32[256,512]{1,0:T(8,128)}, f32[256,512]{1,0:T(8,128)}, /*index=5*/f32[256,512]{1,0:T(8,128)}) custom-call(s32[64,128]{1,0:T(8,128)S(1)} %get-tuple-element.16.table, s32[8,256]{1,0:T(8,128)S(1)} %get-tuple-element.17.place_ref, bf16[2048,1024]{1,0:T(8,128)(2,1)} %copy-done.1), custom_call_target="tpu_custom_call" | custom-call | flops 3087007744 | bytes 8388608 | tf_op jit(solution)/shard_map/cond/branch_1_fun/pallas_call | solution.py:306
  25.3 3.1 %all-to-all-done = f32[8,136,128]{2,1,0:T(8,128)S(1)} async-done(((f32[8,136,128]{2,1,0:T(8,128)}), f32[8,136,128]{2,1,0:T(8,128)S(1)}, u32[]{:S(2)}, u32[]{:S(2)}) %all-to-all-start) | async-done | bytes 557088 | tf_op jit(solution)/shard_map/cond/branch_1_fun/all_to_all | solution.py:398
  28.6 2.8 %collective-permute-start.2 = (f32[136,128]{1,0:T(8,128)S(1)}, f32[136,128]{1,0:T(8,128)S(1)}, u32[]{:S(2)}, u32[]{:S(2)}) collective-permute-start(f32[136,128]{1,0:T(8,128)S(1)} %get-tuple-element.57), channel_id=1, source_target_pairs={{0,16},{4,20},{8,24},{12,28},{16,0},{20,4},{24,8},{28,12},{1,17},{... | collective-permute-start | bytes 208904 | tf_op jit(solution)/shard_map/ppermute | solution.py:563
  32.0 1.3 %collective-permute-start.8 = (f32[256,512]{1,0:T(8,128)}, f32[256,512]{1,0:T(8,128)S(1)}, u32[]{:S(2)}, u32[]{:S(2)}) collective-permute-start(f32[256,512]{1,0:T(8,128)} %get-tuple-element.75), channel_id=1, source_target_pairs={{0,8},{4,12},{8,0},{12,4},{16,24},{20,28},{24,16},{28,20},{1,9},{5... | collective-permute-start | bytes 1572872 | tf_op jit(solution)/shard_map/ppermute | solution.py:563
  33.4 1.1 %collective-permute-done.4.rest_1_ = f32[256,512]{1,0:T(8,128)S(1)} collective-permute-done((f32[256,512]{1,0:T(8,128)}, f32[256,512]{1,0:T(8,128)S(1)}, u32[]{:S(2)}, u32[]{:S(2)}) %collective-permute-start.4) | collective-permute-done | bytes 524320 | tf_op jit(solution)/shard_map/ppermute | solution.py:563
  34.5 1.7 %collective-permute-done.3 = f32[136,128]{1,0:T(8,128)S(1)} collective-permute-done((f32[136,128]{1,0:T(8,128)S(1)}, f32[136,128]{1,0:T(8,128)S(1)}, u32[]{:S(2)}, u32[]{:S(2)}) %collective-permute-start.3) | collective-permute-done | bytes 69664 | tf_op jit(solution)/shard_map/ppermute | solution.py:563
  36.2 1.3 %collective-permute-done.2 = f32[136,128]{1,0:T(8,128)S(1)} collective-permute-done((f32[136,128]{1,0:T(8,128)S(1)}, f32[136,128]{1,0:T(8,128)S(1)}, u32[]{:S(2)}, u32[]{:S(2)}) %collective-permute-start.2) | collective-permute-done | bytes 69664 | tf_op jit(solution)/shard_map/ppermute | solution.py:563
  37.5 3.4 %collective-permute-start.6 = (f32[256,512]{1,0:T(8,128)}, f32[256,512]{1,0:T(8,128)S(1)}, u32[]{:S(2)}, u32[]{:S(2)}) collective-permute-start(f32[256,512]{1,0:T(8,128)} %get-tuple-element.68), channel_id=1, source_target_pairs={{0,20},{4,16},{8,28},{12,24},{16,4},{20,0},{24,12},{28,8},{1,21},{... | collective-permute-start | bytes 1572872 | tf_op jit(solution)/shard_map/ppermute | solution.py:563
  40.9 13.8 %conditional.3 = (f32[1088,128]{1,0:T(8,128)}) conditional(s32[]{:T(128)} %bitcast.3, () %tuple.29, f32[136,128]{1,0:T(8,128)S(1)} %add_add_fusion), branch_computations={%region_3.0_spmd, %region_4.0_spmd} | conditional | bytes 1740808 | solution.py:599
  41.0 13.7 %all_to_all.14 = f32[8,136,128]{2,1,0:T(8,128)} all-to-all(f32[8,136,128]{2,1,0:T(8,128)S(1)} %broadcast_in_dim.2), channel_id=1, replica_groups={{0,1,2,3,4,5,6,7},{8,9,10,11,12,13,14,15},{16,17,18,19,20,21,22,23},{24..., dimensions={0} | all-to-all | bytes 1114112 | tf_op jit(solution)/shard_map/cond/branch_1_fun/all_to_all | solution.py:406
  54.7 1.0 collective-permute-start.5
  55.7 26.9 %shard_map.70 = (f32[512,512]{1,0:T(8,128)}, bf16[512,512]{1,0:T(8,128)(2,1)S(1)}, bf16[512,512]{1,0:T(8,128)(2,1)S(1)}) custom-call(f32[1088,128]{1,0:T(8,128)} %get-tuple-element.96.sum_ref, f32[1088,128]{1,0:T(8,128)S(1)} %get-tuple-element.62.prior_ref), custom_call_target="tpu_custom_call" | custom-call | flops 1 | bytes 1 | tf_op jit(solution)/shard_map/pallas_call | solution.py:479
  82.6 4.1 %shard_map.71.rest_2_ = f32[2048,512]{1,0:T(8,128)} custom-call(s32[1]{0:T(128)} %bitcast.2.me_ref, bf16[512,512]{1,0:T(8,128)(2,1)S(1)} %get-tuple-element.63.high_ref, bf16[512,512]{1,0:T(8,128)(2,1)S(1)} %get-tuple-element.64.low_ref, f32[256,512]{1,0:T(8,128)} %get-tuple-element.71.rest_0_, f32[256,512]{1,0:T(8,128)S(1)} %collective-permute-done.4.rest_1_, ...), custom_call_target="tpu_custom_call" | custom-call | flops 1 | bytes 1 | tf_op jit(solution)/shard_map/pallas_call | solution.py:529
  86.7 7.0 %collective-permute-done.6.rest_0_ = f32[256,512]{1,0:T(8,128)S(1)} collective-permute-done((f32[256,512]{1,0:T(8,128)}, f32[256,512]{1,0:T(8,128)S(1)}, u32[]{:S(2)}, u32[]{:S(2)}) %collective-permute-start.6) | collective-permute-done | bytes 524320 | tf_op jit(solution)/shard_map/ppermute | solution.py:563
  93.8 1.8 %shard_map.72.rest_1_ = f32[2048,512]{1,0:T(8,128)} custom-call(s32[1]{0:T(128)} %bitcast.2.me_ref, bf16[512,512]{1,0:T(8,128)(2,1)S(1)} %get-tuple-element.63.high_ref, bf16[512,512]{1,0:T(8,128)(2,1)S(1)} %get-tuple-element.64.low_ref, f32[256,512]{1,0:T(8,128)S(1)} %collective-permute-done.6.rest_0_, ...), custom_call_target="tpu_custom_call", output_to_operand_aliasing={{}: (5, {})} | custom-call | flops 1 | bytes 1 | tf_op jit(solution)/shard_map/pallas_call | solution.py:529
  95.6 9.3 %collective-permute-done.5.rest_0_ = f32[256,512]{1,0:T(8,128)S(1)} collective-permute-done((f32[256,512]{1,0:T(8,128)}, f32[256,512]{1,0:T(8,128)S(1)}, u32[]{:S(2)}, u32[]{:S(2)}) %collective-permute-start.5) | collective-permute-done | bytes 524320 | tf_op jit(solution)/shard_map/ppermute | solution.py:563
  104.9 1.3 %shard_map.73 = f32[2048,512]{1,0:T(8,128)} custom-call(s32[1]{0:T(128)} %bitcast.2.me_ref, bf16[512,512]{1,0:T(8,128)(2,1)S(1)} %get-tuple-element.63.high_ref, bf16[512,512]{1,0:T(8,128)(2,1)S(1)} %get-tuple-element.64.low_ref, f32[256,512]{1,0:T(8,128)S(1)} %collective-permute-done.5.rest_0_, ...), custom_call_target="tpu_custom_call", output_to_operand_aliasing={{}: (4, {})} | custom-call | flops 1 | bytes 1 | tf_op jit(solution)/shard_map/pallas_call | solution.py:529
  (15 shorter events, 0.9 us)
Async XLA Ops:
  0.6 8.5 %copy-start = (f32[128]{0:T(128)S(1)}, f32[128]{0:T(128)}, u32[]{:S(2)}) copy-start(f32[128]{0:T(128)} %param.11) | copy-start | bytes 1540
  5.0 23.5 %collective-permute-start = (f32[256,512]{1,0:T(8,128)}, f32[256,512]{1,0:T(8,128)S(1)}, u32[]{:S(2)}, u32[]{:S(2)}) collective-permute-start(f32[256,512]{1,0:T(8,128)} %get-tuple-element.56), channel_id=1, source_target_pairs={{0,4},{4,0},{8,12},{12,8},{16,20},{20,16},{24,28},{28,24},{1,5},{5... | collective-permute-start | bytes 1572872 | tf_op jit(solution)/shard_map/ppermute | solution.py:563
  6.5 27.9 %collective-permute-start.4 = (f32[256,512]{1,0:T(8,128)}, f32[256,512]{1,0:T(8,128)S(1)}, u32[]{:S(2)}, u32[]{:S(2)}) collective-permute-start(f32[256,512]{1,0:T(8,128)} %get-tuple-element.58), channel_id=1, source_target_pairs={{0,16},{4,20},{8,24},{12,28},{16,0},{20,4},{24,8},{28,12},{1,17},{... | collective-permute-start | bytes 1572872 | tf_op jit(solution)/shard_map/ppermute | solution.py:563
  9.2 2.0 %copy-start.1 = (bf16[2048,1024]{1,0:T(8,128)(2,1)}, bf16[2048,1024]{1,0:T(8,128)(2,1)S(1)}, u32[]{:S(2)}) copy-start(bf16[2048,1024]{1,0:T(8,128)(2,1)S(1)} %get-tuple-element.13.pair_ref) | copy-start | bytes 12582916 | tf_op jit(solution)/shard_map/cond
  15.8 12.7 %all-to-all-start = ((f32[8,136,128]{2,1,0:T(8,128)}), f32[8,136,128]{2,1,0:T(8,128)S(1)}, u32[]{:S(2)}, u32[]{:S(2)}) async-start(f32[8,136,128]{2,1,0:T(8,128)} %bitcast), calls=%async_computation | async-start | bytes 1114112 | tf_op jit(solution)/shard_map/cond/branch_1_fun/all_to_all | solution.py:398
  28.5 7.7 %collective-permute-start.3 = (f32[136,128]{1,0:T(8,128)S(1)}, f32[136,128]{1,0:T(8,128)S(1)}, u32[]{:S(2)}, u32[]{:S(2)}) collective-permute-start(f32[136,128]{1,0:T(8,128)S(1)} %get-tuple-element.57), channel_id=1, source_target_pairs={{0,24},{4,28},{8,16},{12,20},{16,8},{20,12},{24,0},{28,4},{1,25},{... | collective-permute-start | bytes 208904 | tf_op jit(solution)/shard_map/ppermute | solution.py:563
  28.6 8.9 %collective-permute-start.2 = (f32[136,128]{1,0:T(8,128)S(1)}, f32[136,128]{1,0:T(8,128)S(1)}, u32[]{:S(2)}, u32[]{:S(2)}) collective-permute-start(f32[136,128]{1,0:T(8,128)S(1)} %get-tuple-element.57), channel_id=1, source_target_pairs={{0,16},{4,20},{8,24},{12,28},{16,0},{20,4},{24,8},{28,12},{1,17},{... | collective-permute-start | bytes 208904 | tf_op jit(solution)/shard_map/ppermute | solution.py:563
  31.4 6.1 %collective-permute-start.1 = (f32[136,128]{1,0:T(8,128)S(1)}, f32[136,128]{1,0:T(8,128)S(1)}, u32[]{:S(2)}, u32[]{:S(2)}) collective-permute-start(f32[136,128]{1,0:T(8,128)S(1)} %get-tuple-element.57), channel_id=1, source_target_pairs={{0,8},{4,12},{8,0},{12,4},{16,24},{20,28},{24,16},{28,20},{1,9},{5... | collective-permute-start | bytes 208904 | tf_op jit(solution)/shard_map/ppermute | solution.py:563
  32.0 50.6 %collective-permute-start.8 = (f32[256,512]{1,0:T(8,128)}, f32[256,512]{1,0:T(8,128)S(1)}, u32[]{:S(2)}, u32[]{:S(2)}) collective-permute-start(f32[256,512]{1,0:T(8,128)} %get-tuple-element.75), channel_id=1, source_target_pairs={{0,8},{4,12},{8,0},{12,4},{16,24},{20,28},{24,16},{28,20},{1,9},{5... | collective-permute-start | bytes 1572872 | tf_op jit(solution)/shard_map/ppermute | solution.py:563
  34.5 48.1 %collective-permute-start.9 = (f32[256,512]{1,0:T(8,128)}, f32[256,512]{1,0:T(8,128)S(1)}, u32[]{:S(2)}, u32[]{:S(2)}) collective-permute-start(f32[256,512]{1,0:T(8,128)} %get-tuple-element.76), channel_id=1, source_target_pairs={{0,24},{4,28},{8,16},{12,20},{16,8},{20,12},{24,0},{28,4},{1,25},{... | collective-permute-start | bytes 1572872 | tf_op jit(solution)/shard_map/ppermute | solution.py:563
  37.5 56.3 %collective-permute-start.6 = (f32[256,512]{1,0:T(8,128)}, f32[256,512]{1,0:T(8,128)S(1)}, u32[]{:S(2)}, u32[]{:S(2)}) collective-permute-start(f32[256,512]{1,0:T(8,128)} %get-tuple-element.68), channel_id=1, source_target_pairs={{0,20},{4,16},{8,28},{12,24},{16,4},{20,0},{24,12},{28,8},{1,21},{... | collective-permute-start | bytes 1572872 | tf_op jit(solution)/shard_map/ppermute | solution.py:563
  54.7 39.1 %collective-permute-start.7 = (f32[256,512]{1,0:T(8,128)}, f32[256,512]{1,0:T(8,128)S(1)}, u32[]{:S(2)}, u32[]{:S(2)}) collective-permute-start(f32[256,512]{1,0:T(8,128)} %get-tuple-element.70), channel_id=1, source_target_pairs={{0,12},{4,8},{8,4},{12,0},{16,28},{20,24},{24,20},{28,16},{1,13},{... | collective-permute-start | bytes 1572872 | tf_op jit(solution)/shard_map/ppermute | solution.py:563
  54.7 50.2 %collective-permute-start.5 = (f32[256,512]{1,0:T(8,128)}, f32[256,512]{1,0:T(8,128)S(1)}, u32[]{:S(2)}, u32[]{:S(2)}) collective-permute-start(f32[256,512]{1,0:T(8,128)} %get-tuple-element.66), channel_id=1, source_target_pairs={{0,28},{4,24},{8,20},{12,16},{16,12},{20,8},{24,4},{28,0},{1,29},{... | collective-permute-start | bytes 1572872 | tf_op jit(solution)/shard_map/ppermute | solution.py:563

commit v19 on v18

--- a/solution.py
+++ b/solution.py
@@ -566,7 +566,7 @@
     packed_rows = packed_rows_of(state, plane)
     planes = [list(range(i, i + plane)) for i in range(0, groups * grp, plane)]
     middle = [k for k in (2, 6) if k < groups]
-    late = [k for k in (5, 3, *range(7, groups)) if k < groups]
+    late = [k for k in (5, *range(7, groups), 3) if k < groups]
     valid = sensor_sigma[0] > 0
     nothing = lambda rows: jnp.full((rows, LANES), jnp.nan, F32)
 

time: 108 us -> 110 us (1.019)
  transfers between devices with their start and end apart: 11 -> 11, of which waited for: 6 -> 6; matrix products, arithmetic and copies ran while one was open for 0% -> 0% of each run, Pallas kernels for 41% -> 40%
where the time goes in v19:
time: 110 us; the launch traced here: 108 us
  Pallas kernels  49 us (45%)
  waiting for transfers between devices  24.5 us (22%)
  starting transfers between devices  17.9 us (16%)
  blocking collectives  13.7 us (12%)
  local copies, waits for them, and re-layouts  2.05 us (2%)
    pallas_call x1, Pallas kernels, factorise(): pl.pallas_call(functools.partial(factor_kernel, 1.0 / total_rows), in_spe...  26.9 us
    ppermute x10, waiting for transfers between devices, shards(): lax.ppermute(chunk, 'rows', [(i, i ^ k) for i in range(groups)])  21.4 us
    ppermute x10, starting transfers between devices, shards(): lax.ppermute(chunk, 'rows', [(i, i ^ k) for i in range(groups)])  14.4 us
    all_to_all x1, blocking collectives, gather_pieces(): lax.all_to_all(copies, axes, split_axis=0, concat_axis=0, axis_index_grou...  13.7 us
    pallas_call x3, Pallas kernels, whiten(): pl.pallas_call(functools.partial(whiten_kernel, steps, len(extra), per_bu...  7.21 us
    pallas_call x1, Pallas kernels, regroup_rest(): pl.pallas_call(functools.partial(rest_kernel, groups, per_bucket, tuple(o...  5.98 us
    pallas_call x1, Pallas kernels, gram(): pl.pallas_call(gram_kernel, in_specs=[vmem] * 2, out_specs=[vmem] * 2, ou...  4.56 us
    pallas_call x1, Pallas kernels, regroup_lead(): pl.pallas_call(functools.partial(lead_kernel, groups, per_bucket, tuple(l...  4.34 us
  transfers between devices with their start and end apart: 11, of which 6 were waited for; matrix products, arithmetic and copies ran while one was open for 0% of the time, Pallas kernels for 40%

profile of v19, /device:TPU:8, one launch (start us, length us, event | category | flops | bytes accessed | tf_op | source)
XLA Modules:
  0.0 108.2 jit_solution(6553101847520867407)
XLA Ops:
  0.6 4.3 %shard_map.69 = (f32[256,512]{1,0:T(8,128)}, f32[256,512]{1,0:T(8,128)}, bf16[2048,1024]{1,0:T(8,128)(2,1)S(1)}, s32[8,256]{1,0:T(8,128)S(1)}, s32[64,128]{1,0:T(8,128)S(1)}) custom-call(s32[1]{0:T(128)} %bitcast.2.me_ref, s32[16,128]{1,0:T(8,128)} %bitcast.9, s32[16,128]{1,0:T(8,128)} %bitcast.10, f32[1,128]{1,0:T(1,128)} %bitcast.11, f32[2048,512]{1,0:T(8,128)} %refs_3_.1), custom_call_target="tpu_custom_call" | custom-call | flops 1048576 | bytes 8388608 | tf_op jit(solution)/shard_map/pallas_call | solution.py:264
  5.0 1.6 %collective-permute-start = (f32[256,512]{1,0:T(8,128)}, f32[256,512]{1,0:T(8,128)S(1)}, u32[]{:S(2)}, u32[]{:S(2)}) collective-permute-start(f32[256,512]{1,0:T(8,128)} %get-tuple-element.56), channel_id=1, source_target_pairs={{0,4},{4,0},{8,12},{12,8},{16,20},{20,16},{24,28},{28,24},{1,5},{5... | collective-permute-start | bytes 1572872 | tf_op jit(solution)/shard_map/ppermute | solution.py:563
  6.5 2.6 %collective-permute-start.4 = (f32[256,512]{1,0:T(8,128)}, f32[256,512]{1,0:T(8,128)S(1)}, u32[]{:S(2)}, u32[]{:S(2)}) collective-permute-start(f32[256,512]{1,0:T(8,128)} %get-tuple-element.58), channel_id=1, source_target_pairs={{0,16},{4,20},{8,24},{12,28},{16,0},{20,4},{24,8},{28,12},{1,17},{... | collective-permute-start | bytes 1572872 | tf_op jit(solution)/shard_map/ppermute | solution.py:563
  9.2 19.3 %conditional.2 = (f32[136,128]{1,0:T(8,128)S(1)}, f32[1088,128]{1,0:T(8,128)S(1)}, f32[256,512]{1,0:T(8,128)}, f32[256,512]{1,0:T(8,128)}, f32[256,512]{1,0:T(8,...) conditional(s32[]{:T(128)} %bitcast.3, () %tuple.30, (f32[512,512]{1,0:T(8,128)}, ...), branch_computations={%region_0.0_spmd, %region_1.0_spmd} | conditional | flops 5234613248 | bytes 31658112 | solution.py:581
  9.2 2.0 %copy-done.1 = bf16[2048,1024]{1,0:T(8,128)(2,1)} copy-done((bf16[2048,1024]{1,0:T(8,128)(2,1)}, bf16[2048,1024]{1,0:T(8,128)(2,1)S(1)}, u32[]{:S(2)}) %copy-start.1) | copy-done | bytes 4194328 | tf_op jit(solution)/shard_map/cond
  11.2 4.6 %branch_1_fun.2 = (f32[1088,128]{1,0:T(8,128)}, f32[1088,128]{1,0:T(8,128)S(1)}) custom-call(f32[512,512]{1,0:T(8,128)} %get-tuple-element.79.prior_ref, bf16[2048,1024]{1,0:T(8,128)(2,1)S(1)} %get-tuple-element.13.pair_ref), custom_call_target="tpu_custom_call" | custom-call | flops 2147483648 | bytes 4194304 | tf_op jit(solution)/shard_map/cond/branch_1_fun/pallas_call | solution.py:382
  15.8 3.5 %all-to-all-start = ((f32[8,136,128]{2,1,0:T(8,128)}), f32[8,136,128]{2,1,0:T(8,128)S(1)}, u32[]{:S(2)}, u32[]{:S(2)}) async-start(f32[8,136,128]{2,1,0:T(8,128)} %bitcast), calls=%async_computation | async-start | bytes 1114112 | tf_op jit(solution)/shard_map/cond/branch_1_fun/all_to_all | solution.py:398
  19.3 6.0 %branch_1_fun.3 = (f32[256,512]{1,0:T(8,128)}, f32[256,512]{1,0:T(8,128)}, f32[256,512]{1,0:T(8,128)}, f32[256,512]{1,0:T(8,128)}, f32[256,512]{1,0:T(8,128)}, /*index=5*/f32[256,512]{1,0:T(8,128)}) custom-call(s32[64,128]{1,0:T(8,128)S(1)} %get-tuple-element.16.table, s32[8,256]{1,0:T(8,128)S(1)} %get-tuple-element.17.place_ref, bf16[2048,1024]{1,0:T(8,128)(2,1)} %copy-done.1), custom_call_target="tpu_custom_call" | custom-call | flops 3087007744 | bytes 8388608 | tf_op jit(solution)/shard_map/cond/branch_1_fun/pallas_call | solution.py:306
  25.3 3.1 %all-to-all-done = f32[8,136,128]{2,1,0:T(8,128)S(1)} async-done(((f32[8,136,128]{2,1,0:T(8,128)}), f32[8,136,128]{2,1,0:T(8,128)S(1)}, u32[]{:S(2)}, u32[]{:S(2)}) %all-to-all-start) | async-done | bytes 557088 | tf_op jit(solution)/shard_map/cond/branch_1_fun/all_to_all | solution.py:398
  28.6 2.8 %collective-permute-start.2 = (f32[136,128]{1,0:T(8,128)S(1)}, f32[136,128]{1,0:T(8,128)S(1)}, u32[]{:S(2)}, u32[]{:S(2)}) collective-permute-start(f32[136,128]{1,0:T(8,128)S(1)} %get-tuple-element.57), channel_id=1, source_target_pairs={{0,16},{4,20},{8,24},{12,28},{16,0},{20,4},{24,8},{28,12},{1,17},{... | collective-permute-start | bytes 208904 | tf_op jit(solution)/shard_map/ppermute | solution.py:563
  32.0 1.3 %collective-permute-start.8 = (f32[256,512]{1,0:T(8,128)}, f32[256,512]{1,0:T(8,128)S(1)}, u32[]{:S(2)}, u32[]{:S(2)}) collective-permute-start(f32[256,512]{1,0:T(8,128)} %get-tuple-element.75), channel_id=1, source_target_pairs={{0,8},{4,12},{8,0},{12,4},{16,24},{20,28},{24,16},{28,20},{1,9},{5... | collective-permute-start | bytes 1572872 | tf_op jit(solution)/shard_map/ppermute | solution.py:563
  33.4 1.1 %collective-permute-done.4.rest_1_ = f32[256,512]{1,0:T(8,128)S(1)} collective-permute-done((f32[256,512]{1,0:T(8,128)}, f32[256,512]{1,0:T(8,128)S(1)}, u32[]{:S(2)}, u32[]{:S(2)}) %collective-permute-start.4) | collective-permute-done | bytes 524320 | tf_op jit(solution)/shard_map/ppermute | solution.py:563
  34.5 1.7 %collective-permute-done.3 = f32[136,128]{1,0:T(8,128)S(1)} collective-permute-done((f32[136,128]{1,0:T(8,128)S(1)}, f32[136,128]{1,0:T(8,128)S(1)}, u32[]{:S(2)}, u32[]{:S(2)}) %collective-permute-start.3) | collective-permute-done | bytes 69664 | tf_op jit(solution)/shard_map/ppermute | solution.py:563
  36.2 1.3 %collective-permute-done.2 = f32[136,128]{1,0:T(8,128)S(1)} collective-permute-done((f32[136,128]{1,0:T(8,128)S(1)}, f32[136,128]{1,0:T(8,128)S(1)}, u32[]{:S(2)}, u32[]{:S(2)}) %collective-permute-start.2) | collective-permute-done | bytes 69664 | tf_op jit(solution)/shard_map/ppermute | solution.py:563
  37.5 3.4 %collective-permute-start.6 = (f32[256,512]{1,0:T(8,128)}, f32[256,512]{1,0:T(8,128)S(1)}, u32[]{:S(2)}, u32[]{:S(2)}) collective-permute-start(f32[256,512]{1,0:T(8,128)} %get-tuple-element.68), channel_id=1, source_target_pairs={{0,20},{4,16},{8,28},{12,24},{16,4},{20,0},{24,12},{28,8},{1,21},{... | collective-permute-start | bytes 1572872 | tf_op jit(solution)/shard_map/ppermute | solution.py:563
  40.9 13.8 %conditional.3 = (f32[1088,128]{1,0:T(8,128)}) conditional(s32[]{:T(128)} %bitcast.3, () %tuple.29, f32[136,128]{1,0:T(8,128)S(1)} %add_add_fusion), branch_computations={%region_3.0_spmd, %region_4.0_spmd} | conditional | bytes 1740808 | solution.py:599
  41.0 13.7 %all_to_all.14 = f32[8,136,128]{2,1,0:T(8,128)} all-to-all(f32[8,136,128]{2,1,0:T(8,128)S(1)} %broadcast_in_dim.2), channel_id=1, replica_groups={{0,1,2,3,4,5,6,7},{8,9,10,11,12,13,14,15},{16,17,18,19,20,21,22,23},{24..., dimensions={0} | all-to-all | bytes 1114112 | tf_op jit(solution)/shard_map/cond/branch_1_fun/all_to_all | solution.py:406
  54.7 1.9 %collective-permute-start.5 = (f32[256,512]{1,0:T(8,128)}, f32[256,512]{1,0:T(8,128)S(1)}, u32[]{:S(2)}, u32[]{:S(2)}) collective-permute-start(f32[256,512]{1,0:T(8,128)} %get-tuple-element.66), channel_id=1, source_target_pairs={{0,12},{4,8},{8,4},{12,0},{16,28},{20,24},{24,20},{28,16},{1,13},{... | collective-permute-start | bytes 1572872 | tf_op jit(solution)/shard_map/ppermute | solution.py:563
  56.6 26.9 %shard_map.70 = (f32[512,512]{1,0:T(8,128)}, bf16[512,512]{1,0:T(8,128)(2,1)S(1)}, bf16[512,512]{1,0:T(8,128)(2,1)S(1)}) custom-call(f32[1088,128]{1,0:T(8,128)} %get-tuple-element.96.sum_ref, f32[1088,128]{1,0:T(8,128)S(1)} %get-tuple-element.62.prior_ref), custom_call_target="tpu_custom_call" | custom-call | flops 1 | bytes 1 | tf_op jit(solution)/shard_map/pallas_call | solution.py:479
  83.5 4.1 %shard_map.71.rest_2_ = f32[2048,512]{1,0:T(8,128)} custom-call(s32[1]{0:T(128)} %bitcast.2.me_ref, bf16[512,512]{1,0:T(8,128)(2,1)S(1)} %get-tuple-element.63.high_ref, bf16[512,512]{1,0:T(8,128)(2,1)S(1)} %get-tuple-element.64.low_ref, f32[256,512]{1,0:T(8,128)} %get-tuple-element.71.rest_0_, f32[256,512]{1,0:T(8,128)S(1)} %collective-permute-done.4.rest_1_, ...), custom_call_target="tpu_custom_call" | custom-call | flops 1 | bytes 1 | tf_op jit(solution)/shard_map/pallas_call | solution.py:529
  87.6 6.1 %collective-permute-done.6.rest_0_ = f32[256,512]{1,0:T(8,128)S(1)} collective-permute-done((f32[256,512]{1,0:T(8,128)}, f32[256,512]{1,0:T(8,128)S(1)}, u32[]{:S(2)}, u32[]{:S(2)}) %collective-permute-start.6) | collective-permute-done | bytes 524320 | tf_op jit(solution)/shard_map/ppermute | solution.py:563
  93.8 11.1 %collective-permute-done.7.rest_1_ = f32[256,512]{1,0:T(8,128)S(1)} collective-permute-done((f32[256,512]{1,0:T(8,128)}, f32[256,512]{1,0:T(8,128)S(1)}, u32[]{:S(2)}, u32[]{:S(2)}) %collective-permute-start.7) | collective-permute-done | bytes 524320 | tf_op jit(solution)/shard_map/ppermute | solution.py:563
  104.9 1.8 %shard_map.72.rest_1_ = f32[2048,512]{1,0:T(8,128)} custom-call(s32[1]{0:T(128)} %bitcast.2.me_ref, bf16[512,512]{1,0:T(8,128)(2,1)S(1)} %get-tuple-element.63.high_ref, bf16[512,512]{1,0:T(8,128)(2,1)S(1)} %get-tuple-element.64.low_ref, f32[256,512]{1,0:T(8,128)S(1)} %collective-permute-done.6.rest_0_, ...), custom_call_target="tpu_custom_call", output_to_operand_aliasing={{}: (5, {})} | custom-call | flops 1 | bytes 1 | tf_op jit(solution)/shard_map/pallas_call | solution.py:529
  106.7 1.3 %shard_map.73 = f32[2048,512]{1,0:T(8,128)} custom-call(s32[1]{0:T(128)} %bitcast.2.me_ref, bf16[512,512]{1,0:T(8,128)(2,1)S(1)} %get-tuple-element.63.high_ref, bf16[512,512]{1,0:T(8,128)(2,1)S(1)} %get-tuple-element.64.low_ref, f32[256,512]{1,0:T(8,128)S(1)} %collective-permute-done.5.rest_0_, ...), custom_call_target="tpu_custom_call", output_to_operand_aliasing={{}: (4, {})} | custom-call | flops 1 | bytes 1 | tf_op jit(solution)/shard_map/pallas_call | solution.py:529
  (15 shorter events, 0.9 us)
Async XLA Ops:
  0.6 8.5 %copy-start = (f32[128]{0:T(128)S(1)}, f32[128]{0:T(128)}, u32[]{:S(2)}) copy-start(f32[128]{0:T(128)} %param.11) | copy-start | bytes 1540
  5.0 23.5 %collective-permute-start = (f32[256,512]{1,0:T(8,128)}, f32[256,512]{1,0:T(8,128)S(1)}, u32[]{:S(2)}, u32[]{:S(2)}) collective-permute-start(f32[256,512]{1,0:T(8,128)} %get-tuple-element.56), channel_id=1, source_target_pairs={{0,4},{4,0},{8,12},{12,8},{16,20},{20,16},{24,28},{28,24},{1,5},{5... | collective-permute-start | bytes 1572872 | tf_op jit(solution)/shard_map/ppermute | solution.py:563
  6.5 27.9 %collective-permute-start.4 = (f32[256,512]{1,0:T(8,128)}, f32[256,512]{1,0:T(8,128)S(1)}, u32[]{:S(2)}, u32[]{:S(2)}) collective-permute-start(f32[256,512]{1,0:T(8,128)} %get-tuple-element.58), channel_id=1, source_target_pairs={{0,16},{4,20},{8,24},{12,28},{16,0},{20,4},{24,8},{28,12},{1,17},{... | collective-permute-start | bytes 1572872 | tf_op jit(solution)/shard_map/ppermute | solution.py:563
  9.2 2.0 %copy-start.1 = (bf16[2048,1024]{1,0:T(8,128)(2,1)}, bf16[2048,1024]{1,0:T(8,128)(2,1)S(1)}, u32[]{:S(2)}) copy-start(bf16[2048,1024]{1,0:T(8,128)(2,1)S(1)} %get-tuple-element.13.pair_ref) | copy-start | bytes 12582916 | tf_op jit(solution)/shard_map/cond
  15.8 12.7 %all-to-all-start = ((f32[8,136,128]{2,1,0:T(8,128)}), f32[8,136,128]{2,1,0:T(8,128)S(1)}, u32[]{:S(2)}, u32[]{:S(2)}) async-start(f32[8,136,128]{2,1,0:T(8,128)} %bitcast), calls=%async_computation | async-start | bytes 1114112 | tf_op jit(solution)/shard_map/cond/branch_1_fun/all_to_all | solution.py:398
  28.5 7.7 %collective-permute-start.3 = (f32[136,128]{1,0:T(8,128)S(1)}, f32[136,128]{1,0:T(8,128)S(1)}, u32[]{:S(2)}, u32[]{:S(2)}) collective-permute-start(f32[136,128]{1,0:T(8,128)S(1)} %get-tuple-element.57), channel_id=1, source_target_pairs={{0,24},{4,28},{8,16},{12,20},{16,8},{20,12},{24,0},{28,4},{1,25},{... | collective-permute-start | bytes 208904 | tf_op jit(solution)/shard_map/ppermute | solution.py:563
  28.6 8.9 %collective-permute-start.2 = (f32[136,128]{1,0:T(8,128)S(1)}, f32[136,128]{1,0:T(8,128)S(1)}, u32[]{:S(2)}, u32[]{:S(2)}) collective-permute-start(f32[136,128]{1,0:T(8,128)S(1)} %get-tuple-element.57), channel_id=1, source_target_pairs={{0,16},{4,20},{8,24},{12,28},{16,0},{20,4},{24,8},{28,12},{1,17},{... | collective-permute-start | bytes 208904 | tf_op jit(solution)/shard_map/ppermute | solution.py:563
  31.4 6.1 %collective-permute-start.1 = (f32[136,128]{1,0:T(8,128)S(1)}, f32[136,128]{1,0:T(8,128)S(1)}, u32[]{:S(2)}, u32[]{:S(2)}) collective-permute-start(f32[136,128]{1,0:T(8,128)S(1)} %get-tuple-element.57), channel_id=1, source_target_pairs={{0,8},{4,12},{8,0},{12,4},{16,24},{20,28},{24,16},{28,20},{1,9},{5... | collective-permute-start | bytes 208904 | tf_op jit(solution)/shard_map/ppermute | solution.py:563
  32.0 51.5 %collective-permute-start.8 = (f32[256,512]{1,0:T(8,128)}, f32[256,512]{1,0:T(8,128)S(1)}, u32[]{:S(2)}, u32[]{:S(2)}) collective-permute-start(f32[256,512]{1,0:T(8,128)} %get-tuple-element.75), channel_id=1, source_target_pairs={{0,8},{4,12},{8,0},{12,4},{16,24},{20,28},{24,16},{28,20},{1,9},{5... | collective-permute-start | bytes 1572872 | tf_op jit(solution)/shard_map/ppermute | solution.py:563
  34.5 49.0 %collective-permute-start.9 = (f32[256,512]{1,0:T(8,128)}, f32[256,512]{1,0:T(8,128)S(1)}, u32[]{:S(2)}, u32[]{:S(2)}) collective-permute-start(f32[256,512]{1,0:T(8,128)} %get-tuple-element.76), channel_id=1, source_target_pairs={{0,24},{4,28},{8,16},{12,20},{16,8},{20,12},{24,0},{28,4},{1,25},{... | collective-permute-start | bytes 1572872 | tf_op jit(solution)/shard_map/ppermute | solution.py:563
  37.5 56.3 %collective-permute-start.6 = (f32[256,512]{1,0:T(8,128)}, f32[256,512]{1,0:T(8,128)S(1)}, u32[]{:S(2)}, u32[]{:S(2)}) collective-permute-start(f32[256,512]{1,0:T(8,128)} %get-tuple-element.68), channel_id=1, source_target_pairs={{0,20},{4,16},{8,28},{12,24},{16,4},{20,0},{24,12},{28,8},{1,21},{... | collective-permute-start | bytes 1572872 | tf_op jit(solution)/shard_map/ppermute | solution.py:563
  54.7 50.2 %collective-permute-start.7 = (f32[256,512]{1,0:T(8,128)}, f32[256,512]{1,0:T(8,128)S(1)}, u32[]{:S(2)}, u32[]{:S(2)}) collective-permute-start(f32[256,512]{1,0:T(8,128)} %get-tuple-element.70), channel_id=1, source_target_pairs={{0,28},{4,24},{8,20},{12,16},{16,12},{20,8},{24,4},{28,0},{1,29},{... | collective-permute-start | bytes 1572872 | tf_op jit(solution)/shard_map/ppermute | solution.py:563
  54.7 52.0 %collective-permute-start.5 = (f32[256,512]{1,0:T(8,128)}, f32[256,512]{1,0:T(8,128)S(1)}, u32[]{:S(2)}, u32[]{:S(2)}) collective-permute-start(f32[256,512]{1,0:T(8,128)} %get-tuple-element.66), channel_id=1, source_target_pairs={{0,12},{4,8},{8,4},{12,0},{16,28},{20,24},{24,20},{28,16},{1,13},{... | collective-permute-start | bytes 1572872 | tf_op jit(solution)/shard_map/ppermute | solution.py:563
